TPU v7x, 32 devices: a whole 2x2x4 slice. The times are simulated.
32 devices in a mesh: row: 8 (over z, x), col: 4 (over y, core).
Axes of the slice: x: 2, y: 2, z: 4, core: 2. Of those that a mesh axis runs over, the one named last changes fastest.
Arguments:
- feats: bfloat16 [4096, 1024], P(('row', 'col')), may hold values from -6 to 6
- weight: bfloat16 [1024, 1024], replicated, may hold values from -0.1875 to 0.1875
- tile_vals: bfloat16 [8, 4, 32, 128, 128], P('row', 'col'), may hold values from -0.25 to 0.25
- tile_rows: int32 [8, 4, 32], P('row', 'col'), may hold values from 0 to 3, as said below
- tile_cols: int32 [8, 4, 32], P('row', 'col'), may hold values from 0 to 7
- tile_count: int32 [8, 4], P('row', 'col'), may hold values from 4 to 32, as said below
- grad_out: bfloat16 [4096, 1024], P(('row', 'col')), may hold values from -6 to 6
Outputs:
- activated: bfloat16 [4096, 1024], P(('row', 'col'))
- grad_feats: bfloat16 [4096, 1024], P(('row', 'col'))
- grad_weight: float32 [1024, 1024], replicated
Inputs may be any that keep to these rules, and one draw needn't show every extreme that they name: On each grid block the 32 slots name distinct tile positions (tile_rows, tile_cols); only the first tile_count slots are live. `tile_count`: some grid block has all 32 slots live.
All inputs are finite; a program needn't handle non-finite values.
Results may differ from a plain program's by a relative error of at most 0.029.
Values may be sent and summed in bfloat16 or wider, within the bound.
No kernel may reach another device: no remote copies, remote signals or barrier semaphores. Data moves between devices by JAX's collectives and lax.ppermute only.
A program may use at most 128 MiB of HBM per device.

v0:
```python
import jax
import jax.numpy as jnp
from jax import lax
from jax.sharding import PartitionSpec as P


def dense_block(block_vals, block_rows, block_cols, live_count, out_tiles, in_tiles):
    slots = block_vals.shape[0]
    tile_side = block_vals.shape[1]
    live_slots = jnp.arange(slots, dtype=jnp.int32) < live_count
    masked_vals = jnp.where(live_slots[:, None, None], block_vals, jnp.zeros_like(block_vals))
    empty = jnp.zeros((out_tiles, tile_side, in_tiles, tile_side), jnp.bfloat16)
    filled = empty.at[block_rows, :, block_cols, :].add(masked_vals)
    return filled.reshape(out_tiles * tile_side, in_tiles * tile_side)


def body(feats, weight, tile_vals, tile_rows, tile_cols, tile_count, grad_out):
    block_vals = tile_vals[0, 0]
    block_rows = tile_rows[0, 0]
    block_cols = tile_cols[0, 0]
    live_count = tile_count[0, 0]
    tile_side = block_vals.shape[1]
    rows_here = feats.shape[0]
    grid_r = lax.axis_size("row")
    grid_c = lax.axis_size("col")
    row_tiles_count = grid_c * rows_here // tile_side
    col_tiles_count = grid_r * rows_here // tile_side
    gathered = lax.all_gather(feats, "row", axis=0, tiled=True)
    adjacency = dense_block(
        block_vals, block_rows, block_cols, live_count, row_tiles_count, col_tiles_count
    )
    partial_value = jnp.dot(adjacency, gathered, preferred_element_type=jnp.float32)
    partial_half = partial_value.astype(jnp.bfloat16)
    aggregated = (
        lax.psum_scatter(partial_half, "col", scatter_dimension=0, tiled=True)
        .astype(jnp.float32)
        .astype(jnp.bfloat16)
    )
    pre_act = jnp.dot(aggregated, weight, preferred_element_type=jnp.float32)
    activated = jax.nn.silu(pre_act).astype(jnp.bfloat16)
    sigmoid_val = jax.nn.sigmoid(pre_act)
    slope_val = sigmoid_val * (1.0 + pre_act * (1.0 - sigmoid_val))
    grad_pre = (grad_out.astype(jnp.float32) * slope_val).astype(jnp.bfloat16)
    local_term = lax.dot_general(
        aggregated, grad_pre, (((0,), (0,)), ((), ())), preferred_element_type=jnp.float32
    )
    grad_weight = lax.psum(local_term, ("row", "col"))
    back_rows = lax.dot_general(
        grad_pre, weight, (((1,), (1,)), ((), ())), preferred_element_type=jnp.float32
    ).astype(jnp.bfloat16)
    row_gathered = lax.all_gather(back_rows, "col", axis=0, tiled=True)
    partial_back = lax.dot_general(
        adjacency, row_gathered, (((0,), (0,)), ((), ())), preferred_element_type=jnp.float32
    )
    back_half = partial_back.astype(jnp.bfloat16)
    grad_feats = (
        lax.psum_scatter(back_half, "row", scatter_dimension=0, tiled=True)
        .astype(jnp.float32)
        .astype(jnp.bfloat16)
    )
    return (activated, grad_feats, grad_weight)


def solution(mesh):
    placed = (
        P(("row", "col"), None),
        P(),
        P("row", "col", None, None, None),
        P("row", "col", None),
        P("row", "col", None),
        P("row", "col"),
        P(("row", "col"), None),
    )
    return jax.shard_map(
        body,
        mesh=mesh,
        in_specs=placed,
        out_specs=(P(("row", "col"), None), P(("row", "col"), None), P()),
        check_vma=False,
    )
```

profile of v0, /device:TPU:0, one launch (start us, length us, event | category | flops | bytes accessed | tf_op | source)
XLA Modules:
  0.0 341.5 jit_solution(6954291644694238686)
XLA Ops:
  7.2 0.0 copy-start
  7.2 0.0 all-gather.3.cloned.1.call-start
  7.2 0.7 all-gather.3.cloned.1.call-update
  7.9 0.0 reduce-scatter.3.cloned.1.call-start
  8.6 0.7 fusion.5
  9.3 2.3 bitcast_select_fusion
  11.6 0.2 broadcast_in_dim.17
  11.9 5.5 %scatter_fusion = bf16[4,128,8,128]{3,1,2,0:T(8,128)(2,1)S(1)} fusion(bf16[4,128,8,128]{3,1,2,0:T(8,128)(2,1)S(1)} %broadcast_in_dim.17, s32[32]{0:T(128)S(1)} %fusion.5, bf16[32,128,128]{2,1,0:T(8,128)(2,1)} %bitcast_select_fusion), kind=kCustom, calls=%fused_computation | custom fusion | flops 524288 | bytes 3145984 | tf_op jit(solution)/shard_map/scatter-add | solution.py:13
  17.4 1.6 copy.10
  19.1 43.1 %all-gather.3.cloned.1.call-done = bf16[1024,1024]{1,0:T(8,128)(2,1)} async-done(((bf16[128,1024]{1,0:T(8,128)(2,1)}), bf16[1024,1024]{1,0:T(8,128)(2,1)}) %all-gather.3.cloned.1.call-update) | async-done | bytes 2097168 | tf_op jit(solution)/shard_map/all_gather | solution.py:28
  62.2 4.1 %convolution_convert_fusion.1 = bf16[512,1024]{1,0:T(8,128)(2,1)} fusion(bf16[1024,1024]{1,0:T(8,128)(2,1)} %all-gather.3.cloned.1.call-done, bf16[64,8,8,128]{3,2,1,0:T(8,128)(2,1)} %bitcast.27), kind=kOutput, calls=%fused_computation.2 | convolution fusion | flops 1074266112 | bytes 4194304 | tf_op jit(solution)/shard_map/dot_general | solution.py:32
  66.3 0.0 reduce-scatter.3.cloned.1.call-update
  66.3 0.0 copy-start.2
  66.3 0.0 all-gather.5.cloned.1.call-start
  66.4 23.5 %reduce-scatter.3.cloned.1.call-done = bf16[128,1024]{1,0:T(8,128)(2,1)} async-done(((bf16[512,1024]{1,0:T(8,128)(2,1)}), bf16[128,1024]{1,0:T(8,128)(2,1)}) %reduce-scatter.3.cloned.1.call-update) | async-done | bytes 262160 | tf_op jit(solution)/shard_map/reduce_scatter | solution.py:35
  89.9 0.0 copy-done
  89.9 2.1 multiply_convert_fusion.1
  92.0 0.0 copy-done.2
  92.0 1.5 convolution_convert_fusion.2
  93.6 0.0 all-gather.5.cloned.1.call-update
  93.6 0.0 all-reduce.2.cloned.1.call-start
  93.6 0.0 copy-done.3
  93.6 2.8 fusion.6
  96.5 0.0 all-reduce.2.cloned.1.call-update
  96.5 0.0 reduce-scatter.5.cloned.1.call-start
  96.5 13.9 %all-gather.5.cloned.1.call-done = bf16[512,1024]{1,0:T(8,128)(2,1)} async-done(((bf16[128,1024]{1,0:T(8,128)(2,1)}), bf16[512,1024]{1,0:T(8,128)(2,1)}) %all-gather.5.cloned.1.call-update) | async-done | bytes 1048592 | tf_op jit(solution)/shard_map/all_gather | solution.py:51
  110.5 0.0 copy-done.1
  110.5 3.8 %convolution_convert_fusion = bf16[1024,1024]{1,0:T(8,128)(2,1)} fusion(bf16[512,1024]{1,0:T(8,128)(2,1)} %all-gather.5.cloned.1.call-done, bf16[64,8,8,128]{3,2,1,0:T(8,128)(2,1)S(1)} %bitcast.28), kind=kOutput, calls=%fused_computation.1 | convolution fusion | flops 1074790400 | bytes 4194304 | tf_op jit(solution)/shard_map/dot_general | solution.py:52
  114.3 0.0 reduce-scatter.5.cloned.1.call-update
  114.3 144.8 %all-reduce.2.cloned.1.call-done = f32[1024,1024]{1,0:T(8,128)} async-done(((f32[1024,1024]{1,0:T(8,128)}), f32[1024,1024]{1,0:T(8,128)}) %all-reduce.2.cloned.1.call-update) | async-done | bytes 4194320 | tf_op jit(solution)/shard_map/psum | solution.py:47
  259.1 71.1 %reduce-scatter.5.cloned.1.call-done = bf16[128,1024]{1,0:T(8,128)(2,1)} async-done(((bf16[1024,1024]{1,0:T(8,128)(2,1)}), bf16[128,1024]{1,0:T(8,128)(2,1)}) %reduce-scatter.5.cloned.1.call-update) | async-done | bytes 262160 | tf_op jit(solution)/shard_map/reduce_scatter | solution.py:57
  330.2 4.8 %copy.23 = f32[1024,1024]{1,0:T(8,128)} copy(f32[1024,1024]{1,0:T(8,128)} %all-reduce.2.cloned.1.call-done) | data formatting | bytes 8388608
  (3 shorter events, 0.0 us)
Async XLA Ops:
  7.2 82.7 %copy-start = (bf16[1024,1024]{1,0:T(8,128)(2,1)S(1)}, bf16[1024,1024]{1,0:T(8,128)(2,1)}, u32[]{:S(2)}) copy-start(bf16[1024,1024]{1,0:T(8,128)(2,1)} %param.8) | copy-start | bytes 6291460
  7.2 55.0 %all-gather.3.cloned.1.call-start = ((), (), s32[]{:S(2)}) async-start(), calls=%async_computation.2 | async-start | bytes 2359296 | tf_op jit(solution)/shard_map/all_gather | solution.py:28
  7.9 81.9 %reduce-scatter.3.cloned.1.call-start = ((), (), s32[]{:S(2)}) async-start(), calls=%async_computation.3 | async-start | bytes 1310720 | tf_op jit(solution)/shard_map/reduce_scatter | solution.py:35
  66.3 25.7 %copy-start.2 = (bf16[128,1024]{1,0:T(8,128)(2,1)S(1)}, bf16[128,1024]{1,0:T(8,128)(2,1)}, u32[]{:S(2)}) copy-start(bf16[128,1024]{1,0:T(8,128)(2,1)} %param.13) | copy-start | bytes 786436
  66.3 44.1 %all-gather.5.cloned.1.call-start = ((), (), s32[]{:S(2)}) async-start(), calls=%async_computation.4 | async-start | bytes 1310720 | tf_op jit(solution)/shard_map/all_gather | solution.py:51
  92.0 1.6 copy-start.3
  93.6 165.5 %all-reduce.2.cloned.1.call-start = ((), (), s32[]{:S(2)}) async-start(), calls=%async_computation.6 | async-start | bytes 8388608 | tf_op jit(solution)/shard_map/psum | solution.py:47
  96.5 14.0 %copy-start.1 = (bf16[4,128,8,128]{3,2,1,0:T(8,128)(2,1)S(1)}, bf16[4,128,8,128]{3,2,1,0:T(8,128)(2,1)}, u32[]{:S(2)}) copy-start(bf16[4,128,8,128]{3,2,1,0:T(8,128)(2,1)} %copy.10) | copy-start | bytes 3145732
  96.5 233.7 %reduce-scatter.5.cloned.1.call-start = ((), (), s32[]{:S(2)}) async-start(), calls=%async_computation.5 | async-start | bytes 2359296 | tf_op jit(solution)/shard_map/reduce_scatter | solution.py:57
Sparse Core Ops, SparseCore 0:
  10.1 51.9 all-gather.2
  66.4 23.3 reduce-scatter.2
  93.7 16.7 all-gather.4
  117.4 141.7 all-reduce.1
  263.5 66.6 reduce-scatter.4
where the time goes:
time: 342 us
  waiting for transfers between devices  297 us (87%)
  matrix products  14.5 us (4%)
  between operations  14.5 us (4%)
  other arithmetic  8.55 us (3%)
  local copies, waits for them, and re-layouts  6.68 us (2%)
    psum x1, waiting for transfers between devices, body(): grad_weight = lax.psum(local_term, ('row', 'col'))  145 us
    reduce_scatter x1, waiting for transfers between devices, body(): lax.psum_scatter(back_half, 'row', scatter_dimension=0, tiled=True)  71.1 us
    all_gather x1, waiting for transfers between devices, body(): gathered = lax.all_gather(feats, 'row', axis=0, tiled=True)  43.1 us
    reduce_scatter x1, waiting for transfers between devices, body(): lax.psum_scatter(partial_half, 'col', scatter_dimension=0, tiled=True)  23.5 us
    all_gather x1, waiting for transfers between devices, body(): row_gathered = lax.all_gather(back_rows, 'col', axis=0, tiled=True)  13.9 us
  transfers between devices with their start and end apart: 5, of which 5 were waited for; matrix products, arithmetic and copies ran while one was open for 5% of the time, Pallas kernels for 0%

commit v1 on v0

v1 whole, which is shorter than its diff:
```python
import functools

import jax
import jax.numpy as jnp
from jax import lax
from jax.experimental import pallas as pl
from jax.experimental.pallas import tpu as pltpu
from jax.sharding import PartitionSpec as P

CHUNKS = 2
VMEM_LIMIT = 48 * 1024 * 1024


def ring_of(count, width):
    height = count // width
    if count % width or width % 2 or height < 2:
        return list(range(count))
    walk = [(0, x) for x in range(width)]
    for turn, x in enumerate(reversed(range(width))):
        down = range(1, height) if turn % 2 == 0 else range(height - 1, 0, -1)
        walk += [(z, x) for z in down]
    return [z * width + x for z, x in walk]


def vmem_call(kernel, out_shapes, scratch=(), smem=0, inputs=0, flops=0, moved=0):
    specs = [pl.BlockSpec(memory_space=pltpu.SMEM)] * smem + [pl.BlockSpec(memory_space=pltpu.VMEM)] * inputs
    return pl.pallas_call(
        kernel,
        out_shape=out_shapes,
        in_specs=specs,
        out_specs=jax.tree.map(lambda _: pl.BlockSpec(memory_space=pltpu.VMEM), out_shapes),
        scratch_shapes=list(scratch),
        compiler_params=pltpu.CompilerParams(vmem_limit_bytes=VMEM_LIMIT),
        cost_estimate=pl.CostEstimate(flops=flops, bytes_accessed=moved, transcendentals=0),
    )


def place_tiles(vals, row_at, col_at, live, rows, cols):
    side = vals.shape[1]

    def kernel(row_ref, col_ref, live_ref, vals_ref, out_ref):
        out_ref[...] = jnp.zeros_like(out_ref)

        def put(slot, carry):
            top = pl.multiple_of(row_ref[slot] * side, side)
            left = pl.multiple_of(col_ref[slot] * side, side)
            out_ref[pl.ds(top, side), pl.ds(left, side)] = vals_ref[slot]
            return carry

        lax.fori_loop(0, live_ref[0], put, 0)

    shape = jax.ShapeDtypeStruct((rows * side, cols * side), vals.dtype)
    call = vmem_call(kernel, shape, smem=3, inputs=1, moved=2 * vals.size * 2)
    return call(row_at, col_at, live, vals)


def aggregate(adjacency, pieces, ends):
    rows, depth = adjacency.shape
    height, width = pieces[0].shape
    half = rows // 2

    def kernel(*refs):
        adj_ref = refs[0]
        piece_refs = refs[1 : 1 + len(pieces)]
        right_ref, left_ref, near_ref, far_ref, held = refs[1 + len(pieces) :]
        for place, piece_ref in enumerate(piece_refs):
            held[place * height : (place + 1) * height] = piece_ref[...]
        held[depth - height :, : width // 2] = right_ref[...]
        held[depth - height :, width // 2 :] = left_ref[...]
        far_ref[...] = jnp.dot(adj_ref[half:], held[...], preferred_element_type=jnp.float32).astype(jnp.bfloat16)
        near_ref[...] = jnp.dot(adj_ref[:half], held[...], preferred_element_type=jnp.float32)

    shapes = (
        jax.ShapeDtypeStruct((half, width), jnp.float32),
        jax.ShapeDtypeStruct((half, width), jnp.bfloat16),
    )
    call = vmem_call(
        kernel,
        shapes,
        scratch=[pltpu.VMEM((depth, width), jnp.bfloat16)],
        inputs=3 + len(pieces),
        flops=2 * rows * depth * width,
        moved=2 * (rows * depth + depth * width + rows * width),
    )
    return call(adjacency, *pieces, *ends)


def dense(where, held, arrived, weight, cotangents):
    chunks = len(held)
    rows, width = held[0].shape
    depth, cols = weight.shape
    groups = len(cotangents)
    side = rows // groups
    part = depth // groups
    quarter = part // 2

    def kernel(*refs):
        refs = list(refs)
        where_ref = refs.pop(0)
        held_refs = [refs.pop(0) for _ in range(chunks)]
        arrived_refs = [[refs.pop(0) for _ in range(chunks)] for _ in range(groups - 1)]
        weight_ref = refs.pop(0)
        cot_refs = [refs.pop(0) for _ in range(groups)]
        act_ref, near_ref, far_ref = refs[:3]
        back_refs = refs[3 : 3 + chunks]
        agg = refs[-2]
        grad = refs[-1]
        for h in range(chunks):
            for g in range(groups):
                total = held_refs[h][g * side : (g + 1) * side].astype(jnp.float32)
                for s in range(1, groups):
                    at = (g + s) % groups
                    total = total + arrived_refs[s - 1][h][at * side : (at + 1) * side].astype(jnp.float32)
                agg[g * side : (g + 1) * side, h * width : (h + 1) * width] = total.astype(jnp.bfloat16)
        for g in range(groups):
            value = jnp.dot(agg[g * side : (g + 1) * side], weight_ref[...], preferred_element_type=jnp.float32)
            gate = jax.nn.sigmoid(value)
            if g == 0:
                act_ref[...] = (value * gate).astype(jnp.bfloat16)
            slope = gate * (1.0 + value * (1.0 - gate))
            cot = cot_refs[(groups - g) % groups][...].astype(jnp.float32)
            grad[g * side : (g + 1) * side] = (cot * slope).astype(jnp.bfloat16)
        for h in range(chunks):
            back_refs[h][...] = lax.dot_general(
                grad[...], weight_ref[h * width : (h + 1) * width], (((1,), (1,)), ((), ())), preferred_element_type=jnp.float32
            ).astype(jnp.bfloat16)
        first = where_ref[0] * part
        near_at = pl.multiple_of(first + where_ref[1] * quarter, 128)
        far_at = pl.multiple_of(first + (1 - where_ref[1]) * quarter, 128)
        far_ref[...] = lax.dot_general(
            agg[:, pl.ds(far_at, quarter)], grad[...], (((0,), (0,)), ((), ())), preferred_element_type=jnp.float32
        ).astype(jnp.bfloat16)
        near_ref[...] = lax.dot_general(
            agg[:, pl.ds(near_at, quarter)], grad[...], (((0,), (0,)), ((), ())), preferred_element_type=jnp.float32
        )

    shapes = [
        jax.ShapeDtypeStruct((side, cols), jnp.bfloat16),
        jax.ShapeDtypeStruct((quarter, cols), jnp.float32),
        jax.ShapeDtypeStruct((quarter, cols), jnp.bfloat16),
    ] + [jax.ShapeDtypeStruct((rows, width), jnp.bfloat16)] * chunks
    call = vmem_call(
        kernel,
        shapes,
        scratch=[pltpu.VMEM((rows, depth), jnp.bfloat16), pltpu.VMEM((rows, cols), jnp.bfloat16)],
        smem=1,
        inputs=chunks * groups + 1 + groups,
        flops=2 * rows * cols * (2 * depth + part),
        moved=2 * (depth * cols + 6 * rows * depth),
    )
    outs = call(where, *held, *[a for step in arrived for a in step], weight, *cotangents)
    return outs[0], outs[1], outs[2], outs[3:]


def back_blocks(adjacency, near, far, count):
    rows, depth = adjacency.shape
    half, width = near.shape
    height = depth // count

    def kernel(adj_ref, near_ref, far_ref, *out_refs):
        held = out_refs[-1]
        held[:half] = near_ref[...]
        held[half:] = far_ref[...]
        for place in reversed(range(count)):
            block = lax.dot_general(
                adj_ref[:, place * height : (place + 1) * height],
                held[...],
                (((0,), (0,)), ((), ())),
                preferred_element_type=jnp.float32,
            ).astype(jnp.bfloat16)
            if place == count - 1:
                out_refs[place][...] = block[:, : width // 2]
                out_refs[place + 1][...] = block[:, width // 2 :]
            else:
                out_refs[place][...] = block

    shapes = [jax.ShapeDtypeStruct((height, width), jnp.bfloat16)] * (count - 1)
    shapes += [jax.ShapeDtypeStruct((height, width // 2), jnp.bfloat16)] * 2
    call = vmem_call(
        kernel,
        shapes,
        scratch=[pltpu.VMEM((rows, width), jnp.bfloat16)],
        inputs=3,
        flops=2 * rows * depth * width,
        moved=2 * (rows * depth + depth * width + rows * width),
    )
    return call(adjacency, near, far)


def weight_blocks(where, near, arrived, count):
    rows, cols = near.shape
    height = rows // count

    def kernel(where_ref, near_ref, arrived_ref, *out_refs):
        for place in range(count):
            step = (place + 1) // 2
            away = step if place % 2 == 0 or place == count - 1 else count - step
            at = pl.multiple_of(lax.rem(where_ref[0] + away, count) * height, height)
            block = near_ref[pl.ds(at, height)] + arrived_ref[pl.ds(at, height)].astype(jnp.float32)
            block = block.astype(jnp.bfloat16)
            if place == count - 1:
                out_refs[place][...] = block[:, : cols // 2]
                out_refs[place + 1][...] = block[:, cols // 2 :]
            else:
                out_refs[place][...] = block

    shapes = [jax.ShapeDtypeStruct((height, cols), jnp.bfloat16)] * (count - 1)
    shapes += [jax.ShapeDtypeStruct((height, cols // 2), jnp.bfloat16)] * 2
    call = vmem_call(kernel, shapes, smem=1, inputs=2, flops=rows * cols, moved=8 * rows * cols)
    return call(where, near, arrived)


def add_pair(right, left, from_left, from_right, halves):
    height, width = right.shape

    def kernel(right_ref, left_ref, first_ref, second_ref, out_right, out_left):
        if halves:
            middle = width // 2
            out_right[:, middle:] = right_ref[:, middle:]
            out_right[:, :middle] = right_ref[:, :middle] + first_ref[...]
            out_left[:, :middle] = left_ref[:, :middle]
            out_left[:, middle:] = left_ref[:, middle:] + second_ref[...]
        else:
            out_right[...] = right_ref[...] + first_ref[...]
            out_left[...] = left_ref[...] + second_ref[...]

    shapes = (jax.ShapeDtypeStruct(right.shape, right.dtype),) * 2
    call = vmem_call(kernel, shapes, inputs=4, flops=2 * right.size, moved=12 * right.size)
    return call(right, left, from_left, from_right)


def join_ring(where, pieces, ends, count):
    height, cols = pieces[0].shape

    def kernel(where_ref, *refs):
        out_ref = refs[-1]
        for place in range(count):
            step = (place + 1) // 2
            away = step if place % 2 == 0 or place == count - 1 else count - step
            at = pl.multiple_of(lax.rem(where_ref[0] + away, count) * height, height)
            if place == count - 1:
                out_ref[pl.ds(at, height), : cols // 2] = refs[place][...]
                out_ref[pl.ds(at, height), cols // 2 :] = refs[place + 1][...]
            else:
                out_ref[pl.ds(at, height)] = refs[place][...]

    shape = jax.ShapeDtypeStruct((height * count, cols), pieces[0].dtype)
    call = vmem_call(kernel, shape, smem=1, inputs=len(pieces) + 2, moved=4 * height * count * cols)
    return call(where, *pieces, *ends)


def join_weight(where, near, far):
    quarter, cols = near[0].shape
    groups = len(near)

    def kernel(where_ref, *refs):
        out_ref = refs[-1]
        for s in range(groups):
            group = lax.rem(where_ref[0] + groups - s, groups)
            for other in range(2):
                core = where_ref[1] if other == 0 else 1 - where_ref[1]
                at = pl.multiple_of((group * 2 + core) * quarter, quarter)
                out_ref[pl.ds(at, quarter)] = refs[other * groups + s][...].astype(jnp.float32)

    shape = jax.ShapeDtypeStruct((quarter * 2 * groups, cols), jnp.float32)
    call = vmem_call(kernel, shape, smem=1, inputs=2 * groups, moved=12 * quarter * groups * cols)
    return call(where, *near, *far)


def body(width, feats, weight, tile_vals, tile_rows, tile_cols, tile_count, grad_out):
    side = tile_vals.shape[-1]
    count = lax.axis_size("row")
    columns = lax.axis_size("col")
    groups = columns // 2
    ring = ring_of(count, width)
    spot = [0] * count
    for place, row in enumerate(ring):
        spot[row] = place
    spot = jnp.array(spot, jnp.int32)
    me = spot[lax.axis_index("row")]
    core = lax.axis_index("col") % 2
    group = lax.axis_index("col") // 2

    to_right = [(ring[k], ring[(k + 1) % count]) for k in range(count)]
    to_left = [(ring[k], ring[(k - 1) % count]) for k in range(count)]
    swap = [(k, k ^ 1) for k in range(columns)]

    def go_right(value):
        return lax.ppermute(value, "row", to_right)

    def go_left(value):
        return lax.ppermute(value, "row", to_left)

    def swap_core(value):
        return lax.ppermute(value, "col", swap)

    def from_group(value, steps):
        return lax.ppermute(value, "col", [(k, (k + 2 * steps) % columns) for k in range(columns)])

    def gather_ring(piece):
        pieces = [piece]
        right = left = piece
        for _ in range(count // 2 - 1):
            right, left = go_right(right), go_left(left)
            pieces += [right, left]
        middle = piece.shape[1] // 2
        return pieces, [go_right(right[:, :middle]), go_left(left[:, middle:])]

    def scatter_ring(blocks):
        right, left = go_right(blocks[count - 1]), go_left(blocks[count])
        for step in range(count // 2 - 1, 0, -1):
            right, left = add_pair(blocks[2 * step], blocks[2 * step - 1], right, left, step == count // 2 - 1)
            right, left = go_right(right), go_left(left)
        return (blocks[0].astype(jnp.float32) + right.astype(jnp.float32) + left.astype(jnp.float32)).astype(jnp.bfloat16)

    rows = tile_rows[0, 0]
    row_at = (rows % 2 ^ core) * groups + (rows // 2 - group) % groups
    away = (spot[tile_cols[0, 0]] - me) % count
    col_at = jnp.where(away < count // 2, 2 * away, 2 * (count - away) - 1)
    adjacency = place_tiles(tile_vals[0, 0], row_at, col_at, tile_count[0], columns, count)

    chunk = feats.shape[1] // CHUNKS
    cotangents = [grad_out] + [from_group(grad_out, s) for s in range(1, groups)]
    held = []
    arrived = [[] for _ in range(groups - 1)]
    for h in range(CHUNKS):
        pieces, ends = gather_ring(feats[:, h * chunk : (h + 1) * chunk])
        near, far = aggregate(adjacency, pieces, ends)
        total = (near + swap_core(far).astype(jnp.float32)).astype(jnp.bfloat16)
        held.append(total)
        for s in range(1, groups):
            arrived[s - 1].append(from_group(total, s))

    where = jnp.stack([group, core]).astype(jnp.int32)
    activated, near_weight, far_weight, back = dense(where, held, arrived, weight, cotangents)

    place = me.reshape(1).astype(jnp.int32)
    terms = weight_blocks(place, near_weight, swap_core(far_weight), count)
    own = scatter_ring(terms)
    pieces, ends = gather_ring(own)
    near_quarters = [join_ring(place, pieces, ends, count)]
    near_quarters += [from_group(near_quarters[0], s) for s in range(1, groups)]
    far_quarters = [swap_core(q) for q in near_quarters]
    grad_weight = join_weight(where, near_quarters, far_quarters)

    grads = []
    for h in range(CHUNKS):
        blocks = back_blocks(adjacency, back[h], swap_core(back[h]), count)
        grads.append(scatter_ring(blocks))
    grad_feats = jnp.concatenate(grads, axis=1)
    return (activated, grad_feats, grad_weight)


def solution(mesh):
    spread = {d.coords[0] for d in mesh.devices.flat if hasattr(d, "coords")}
    placed = (
        P(("row", "col"), None),
        P(),
        P("row", "col", None, None, None),
        P("row", "col", None),
        P("row", "col", None),
        P("row", "col"),
        P(("row", "col"), None),
    )
    return jax.shard_map(
        functools.partial(body, max(1, len(spread))),
        mesh=mesh,
        in_specs=placed,
        out_specs=(P(("row", "col"), None), P(("row", "col"), None), P()),
        check_vma=False,
    )
```

time: 342 us -> 147 us (0.43)
  waiting for transfers between devices: 297 us -> 69.7 us
  starting transfers between devices: 0.2 us -> 57 us
  matrix products: 14.5 us -> 0 us
  between operations: 14.5 us -> 1.54 us
  Pallas kernels: 0 us -> 10.9 us
  other arithmetic: 8.55 us -> 3.07 us
    psum x1 -> x0, waiting for transfers between devices: 145 us -> none  [body(): grad_weight = lax.psum(local_term, ('row', 'col'))]
    reduce_scatter x2 -> x0, waiting for transfers between devices: 94.5 us -> none  [the longest x1 71.1 us: body(): lax.psum_scatter(back_half, 'row', scatter_dimension=0, tiled=True)]
    ppermute x0 -> x59, waiting for transfers between devices: none -> 69.7 us  [the longest x24 30.1 us: go_left(): return lax.ppermute(value, 'row', to_left)]
    all_gather x2 -> x0, waiting for transfers between devices: 57.1 us -> none  [the longest x1 43.1 us: body(): gathered = lax.all_gather(feats, 'row', axis=0, tiled=True)]
    ppermute x0 -> x59, starting transfers between devices: none -> 57 us  [the longest x24 30 us: go_left(): return lax.ppermute(value, 'row', to_left)]
    dot_general x5 -> x0, matrix products: 14.5 us -> none  [the longest x1 4.14 us: body(): jnp.dot(adjacency, gathered, preferred_element_type=jnp.float32)]
    pallas_call x0 -> x18, Pallas kernels: none -> 10.9 us  [the longest x1 2.83 us: join_weight(): return call(where, *near, *far)]
    scatter-add x1 -> x0, other arithmetic: 5.53 us -> none  [dense_block(): filled = empty.at[block_rows, :, block_cols, :].add(masked_vals)]
  transfers between devices with their start and end apart: 5 -> 59, of which waited for: 5 -> 32; matrix products, arithmetic and copies ran while one was open for 5% -> 4% of each run, Pallas kernels for 0% -> 3%
where the time goes in v1:
time: 147 us
  waiting for transfers between devices  69.7 us (47%)
  starting transfers between devices  57 us (39%)
  Pallas kernels  10.9 us (7%)
  local copies, waits for them, and re-layouts  4.87 us (3%)
  other arithmetic  3.07 us (2%)
  between operations  1.54 us (1%)
    ppermute x24, waiting for transfers between devices, go_left(): return lax.ppermute(value, 'row', to_left)  30.1 us
    ppermute x24, starting transfers between devices, go_left(): return lax.ppermute(value, 'row', to_left)  30 us
    ppermute x24, waiting for transfers between devices, go_right(): return lax.ppermute(value, 'row', to_right)  21.7 us
    ppermute x24, starting transfers between devices, go_right(): return lax.ppermute(value, 'row', to_right)  20.6 us
    ppermute x4, waiting for transfers between devices, from_group(): lax.ppermute(value, 'col', [(k, (k + 2 * steps) % columns) for k in range...  16 us
    ppermute x4, starting transfers between devices, from_group(): lax.ppermute(value, 'col', [(k, (k + 2 * steps) % columns) for k in range...  5.75 us
  transfers between devices with their start and end apart: 59, of which 32 were waited for; matrix products, arithmetic and copies ran while one was open for 4% of the time, Pallas kernels for 3%

profile of v1, /device:TPU:0, one launch (start us, length us, event | category | flops | bytes accessed | tf_op | source)
XLA Modules:
  0.0 147.2 jit_solution(13038995889377915632)
XLA Ops:
  1.7 3.1 %collective-permute-start.10 = (bf16[128,512]{1,0:T(8,128)(2,1)S(1)}, bf16[128,512]{1,0:T(8,128)(2,1)S(1)}, u32[]{:S(2)}, u32[]{:S(2)}) collective-permute-start(bf16[128,512]{1,0:T(8,128)(2,1)S(1)} %get-tuple-element.111.refs_1_), channel_id=1, source_target_pairs={{0,8},{4,0},{12,4},{20,12},{28,20},{24,28},{16,24},{8,16},{1,9},{5... | collective-permute-start | bytes 393224 | tf_op jit(solution)/shard_map/ppermute | solution.py:292
  4.8 3.4 %collective-permute-done.10.refs_3_ = bf16[128,512]{1,0:T(8,128)(2,1)S(1)} collective-permute-done((bf16[128,512]{1,0:T(8,128)(2,1)S(1)}, bf16[128,512]{1,0:T(8,128)(2,1)S(1)}, u32[]{:S(2)}, u32[]{:S(2)}) %collective-permute-start.10) | collective-permute-done | bytes 131104 | tf_op jit(solution)/shard_map/ppermute | solution.py:292
  8.2 1.8 %collective-permute-start.12 = (bf16[128,512]{1,0:T(8,128)(2,1)S(1)}, bf16[128,512]{1,0:T(8,128)(2,1)S(1)}, u32[]{:S(2)}, u32[]{:S(2)}) collective-permute-start(bf16[128,512]{1,0:T(8,128)(2,1)S(1)} %collective-permute-done.10.refs_3_), channel_id=1, source_target_pairs={{0,8},{4,0},{12,4},{20,12},{28,20},{24,28},{16,24},{8,16},{1,9},{5... | collective-permute-start | bytes 393224 | tf_op jit(solution)/shard_map/ppermute | solution.py:292
  10.2 1.8 %collective-permute-start.1 = (bf16[128,512]{1,0:T(8,128)(2,1)S(1)}, bf16[128,512]{1,0:T(8,128)(2,1)S(1)}, u32[]{:S(2)}, u32[]{:S(2)}) collective-permute-start(bf16[128,512]{1,0:T(8,128)(2,1)S(1)} %get-tuple-element.112.refs_1_), channel_id=1, source_target_pairs={{0,8},{4,0},{12,4},{20,12},{28,20},{24,28},{16,24},{8,16},{1,9},{5... | collective-permute-start | bytes 393224 | tf_op jit(solution)/shard_map/ppermute | solution.py:292
  12.2 2.3 %collective-permute-done.12.refs_5_ = bf16[128,512]{1,0:T(8,128)(2,1)S(1)} collective-permute-done((bf16[128,512]{1,0:T(8,128)(2,1)S(1)}, bf16[128,512]{1,0:T(8,128)(2,1)S(1)}, u32[]{:S(2)}, u32[]{:S(2)}) %collective-permute-start.12) | collective-permute-done | bytes 131104 | tf_op jit(solution)/shard_map/ppermute | solution.py:292
  19.8 1.8 %collective-permute-start.3 = (bf16[128,512]{1,0:T(8,128)(2,1)S(1)}, bf16[128,512]{1,0:T(8,128)(2,1)S(1)}, u32[]{:S(2)}, u32[]{:S(2)}) collective-permute-start(bf16[128,512]{1,0:T(8,128)(2,1)S(1)} %collective-permute-done.1.refs_3_), channel_id=1, source_target_pairs={{0,8},{4,0},{12,4},{20,12},{28,20},{24,28},{16,24},{8,16},{1,9},{5... | collective-permute-start | bytes 393224 | tf_op jit(solution)/shard_map/ppermute | solution.py:292
  21.9 1.8 %collective-permute-start.16 = (bf16[128,256]{1,0:T(8,128)(2,1)S(1)}, bf16[128,256]{1,0:T(8,128)(2,1)S(1)}, u32[]{:S(2)}, u32[]{:S(2)}) collective-permute-start(bf16[128,256]{1,0:T(8,128)(2,1)S(1)} %slice.37), channel_id=1, source_target_pairs={{0,8},{4,0},{12,4},{20,12},{28,20},{24,28},{16,24},{8,16},{1,9},{5... | collective-permute-start | bytes 196616 | tf_op jit(solution)/shard_map/ppermute | solution.py:292
  28.9 1.8 %collective-permute-start.5 = (bf16[128,512]{1,0:T(8,128)(2,1)S(1)}, bf16[128,512]{1,0:T(8,128)(2,1)S(1)}, u32[]{:S(2)}, u32[]{:S(2)}) collective-permute-start(bf16[128,512]{1,0:T(8,128)(2,1)S(1)} %collective-permute-done.3.refs_5_), channel_id=1, source_target_pairs={{0,8},{4,0},{12,4},{20,12},{28,20},{24,28},{16,24},{8,16},{1,9},{5... | collective-permute-start | bytes 393224 | tf_op jit(solution)/shard_map/ppermute | solution.py:292
  31.0 3.8 %collective-permute-done.5.refs_7_ = bf16[128,512]{1,0:T(8,128)(2,1)S(1)} collective-permute-done((bf16[128,512]{1,0:T(8,128)(2,1)S(1)}, bf16[128,512]{1,0:T(8,128)(2,1)S(1)}, u32[]{:S(2)}, u32[]{:S(2)}) %collective-permute-start.5) | collective-permute-done | bytes 131104 | tf_op jit(solution)/shard_map/ppermute | solution.py:292
  36.9 2.2 %collective-permute-done.7.refs_9_ = bf16[128,256]{1,0:T(8,128)(2,1)S(1)} collective-permute-done((bf16[128,256]{1,0:T(8,128)(2,1)S(1)}, bf16[128,256]{1,0:T(8,128)(2,1)S(1)}, u32[]{:S(2)}, u32[]{:S(2)}) %collective-permute-start.7) | collective-permute-done | bytes 65568 | tf_op jit(solution)/shard_map/ppermute | solution.py:292
  39.1 1.8 %collective-permute-done.6.refs_8_ = bf16[128,256]{1,0:T(8,128)(2,1)S(1)} collective-permute-done((bf16[128,256]{1,0:T(8,128)(2,1)S(1)}, bf16[128,256]{1,0:T(8,128)(2,1)S(1)}, u32[]{:S(2)}, u32[]{:S(2)}) %collective-permute-start.6) | collective-permute-done | bytes 65568 | tf_op jit(solution)/shard_map/ppermute | solution.py:289
  45.6 5.2 %collective-permute-done.20.refs_7_ = bf16[128,1024]{1,0:T(8,128)(2,1)S(1)} collective-permute-done((bf16[128,1024]{1,0:T(8,128)(2,1)S(1)}, bf16[128,1024]{1,0:T(8,128)(2,1)S(1)}, u32[]{:S(2)}, u32[]{:S(2)}) %collective-permute-start.20) | collective-permute-done | bytes 262176 | tf_op jit(solution)/shard_map/ppermute | solution.py:298
  50.9 5.6 %collective-permute-done.19.refs_4_ = bf16[256,512]{1,0:T(8,128)(2,1)S(1)} collective-permute-done((bf16[256,512]{1,0:T(8,128)(2,1)S(1)}, bf16[256,512]{1,0:T(8,128)(2,1)S(1)}, u32[]{:S(2)}, u32[]{:S(2)}) %collective-permute-start.19) | collective-permute-done | bytes 262176 | tf_op jit(solution)/shard_map/ppermute | solution.py:298
  56.5 5.2 %collective-permute-done.18.refs_3_ = bf16[256,512]{1,0:T(8,128)(2,1)S(1)} collective-permute-done((bf16[256,512]{1,0:T(8,128)(2,1)S(1)}, bf16[256,512]{1,0:T(8,128)(2,1)S(1)}, u32[]{:S(2)}, u32[]{:S(2)}) %collective-permute-start.18) | collective-permute-done | bytes 262176 | tf_op jit(solution)/shard_map/ppermute | solution.py:298
  61.7 2.6 %shard_map.106 = (bf16[128,1024]{1,0:T(8,128)(2,1)}, f32[256,1024]{1,0:T(8,128)S(1)}, bf16[256,1024]{1,0:T(8,128)(2,1)S(1)}, bf16[256,512]{1,0:T(8,128)(2,1)S(1)}, bf16[256,512]{1,0:T(8,128)(2,1)S(1)}) custom-call(s32[2]{0:T(128)S(1)} %pad_add_fusion.refs_0_.where_ref, bf16[256,512]{1,0:T(8,128)(2,1)S(1)} %add_convert_fusion.1.refs_1_, ...), custom_call_target="tpu_custom_call" | custom-call | flops 1342177280 | bytes 5242880 | tf_op jit(solution)/shard_map/pallas_call | solution.py:151
  64.3 1.9 %collective-permute-done.39.arrived_ref = bf16[256,1024]{1,0:T(8,128)(2,1)S(1)} collective-permute-done((bf16[256,1024]{1,0:T(8,128)(2,1)S(1)}, bf16[256,1024]{1,0:T(8,128)(2,1)S(1)}, u32[]{:S(2)}, u32[]{:S(2)}) %collective-permute-start.39) | collective-permute-done | bytes 524320 | tf_op jit(solution)/shard_map/ppermute | solution.py:295
  69.0 1.9 %collective-permute-done.40.first_ref = bf16[32,512]{1,0:T(8,128)(2,1)S(1)} collective-permute-done((bf16[32,512]{1,0:T(8,128)(2,1)S(1)}, bf16[32,512]{1,0:T(8,128)(2,1)S(1)}, u32[]{:S(2)}, u32[]{:S(2)}) %collective-permute-start.40) | collective-permute-done | bytes 32800 | tf_op jit(solution)/shard_map/ppermute | solution.py:289
  73.3 2.2 %collective-permute-done.42.first_ref = bf16[32,1024]{1,0:T(8,128)(2,1)S(1)} collective-permute-done((bf16[32,1024]{1,0:T(8,128)(2,1)S(1)}, bf16[32,1024]{1,0:T(8,128)(2,1)S(1)}, u32[]{:S(2)}, u32[]{:S(2)}) %collective-permute-start.42) | collective-permute-done | bytes 65568 | tf_op jit(solution)/shard_map/ppermute | solution.py:289
  79.3 2.2 %collective-permute-done.44.first_ref = bf16[32,1024]{1,0:T(8,128)(2,1)S(1)} collective-permute-done((bf16[32,1024]{1,0:T(8,128)(2,1)S(1)}, bf16[32,1024]{1,0:T(8,128)(2,1)S(1)}, u32[]{:S(2)}, u32[]{:S(2)}) %collective-permute-start.44) | collective-permute-done | bytes 65568 | tf_op jit(solution)/shard_map/ppermute | solution.py:289
  85.3 2.2 %collective-permute-done.46 = bf16[32,1024]{1,0:T(8,128)(2,1)S(1)} collective-permute-done((bf16[32,1024]{1,0:T(8,128)(2,1)S(1)}, bf16[32,1024]{1,0:T(8,128)(2,1)S(1)}, u32[]{:S(2)}, u32[]{:S(2)}) %collective-permute-start.46) | collective-permute-done | bytes 65568 | tf_op jit(solution)/shard_map/ppermute | solution.py:289
  87.5 2.1 %collective-permute-done.47 = bf16[32,1024]{1,0:T(8,128)(2,1)S(1)} collective-permute-done((bf16[32,1024]{1,0:T(8,128)(2,1)S(1)}, bf16[32,1024]{1,0:T(8,128)(2,1)S(1)}, u32[]{:S(2)}, u32[]{:S(2)}) %collective-permute-start.47) | collective-permute-done | bytes 65568 | tf_op jit(solution)/shard_map/ppermute | solution.py:292
  91.8 2.2 %collective-permute-done.49.refs_2_ = bf16[32,1024]{1,0:T(8,128)(2,1)S(1)} collective-permute-done((bf16[32,1024]{1,0:T(8,128)(2,1)S(1)}, bf16[32,1024]{1,0:T(8,128)(2,1)S(1)}, u32[]{:S(2)}, u32[]{:S(2)}) %collective-permute-start.49) | collective-permute-done | bytes 65568 | tf_op jit(solution)/shard_map/ppermute | solution.py:292
  96.1 2.2 %collective-permute-done.51.refs_4_ = bf16[32,1024]{1,0:T(8,128)(2,1)S(1)} collective-permute-done((bf16[32,1024]{1,0:T(8,128)(2,1)S(1)}, bf16[32,1024]{1,0:T(8,128)(2,1)S(1)}, u32[]{:S(2)}, u32[]{:S(2)}) %collective-permute-start.51) | collective-permute-done | bytes 65568 | tf_op jit(solution)/shard_map/ppermute | solution.py:292
  100.3 2.6 %collective-permute-done.53.refs_6_ = bf16[32,1024]{1,0:T(8,128)(2,1)S(1)} collective-permute-done((bf16[32,1024]{1,0:T(8,128)(2,1)S(1)}, bf16[32,1024]{1,0:T(8,128)(2,1)S(1)}, u32[]{:S(2)}, u32[]{:S(2)}) %collective-permute-start.53) | collective-permute-done | bytes 65568 | tf_op jit(solution)/shard_map/ppermute | solution.py:292
  104.9 1.9 %collective-permute-done.55.refs_8_ = bf16[32,512]{1,0:T(8,128)(2,1)S(1)} collective-permute-done((bf16[32,512]{1,0:T(8,128)(2,1)S(1)}, bf16[32,512]{1,0:T(8,128)(2,1)S(1)}, u32[]{:S(2)}, u32[]{:S(2)}) %collective-permute-start.55) | collective-permute-done | bytes 32800 | tf_op jit(solution)/shard_map/ppermute | solution.py:292
  107.8 2.1 %collective-permute-start.56 = (bf16[256,1024]{1,0:T(8,128)(2,1)S(1)}, bf16[256,1024]{1,0:T(8,128)(2,1)S(1)}, u32[]{:S(2)}, u32[]{:S(2)}) collective-permute-start(bf16[256,1024]{1,0:T(8,128)(2,1)S(1)} %shard_map.119.refs_0_), channel_id=1, source_target_pairs={{0,2},{1,3},{2,0},{3,1},{4,6},{5,7},{6,4},{7,5},{8,10},{9,11},{10,... | collective-permute-start | bytes 1572872 | tf_op jit(solution)/shard_map/ppermute | solution.py:298
  112.7 2.5 %collective-permute-done.22.first_ref = bf16[128,256]{1,0:T(8,128)(2,1)S(1)} collective-permute-done((bf16[128,256]{1,0:T(8,128)(2,1)S(1)}, bf16[128,256]{1,0:T(8,128)(2,1)S(1)}, u32[]{:S(2)}, u32[]{:S(2)}) %collective-permute-start.22) | collective-permute-done | bytes 65568 | tf_op jit(solution)/shard_map/ppermute | solution.py:289
  121.6 3.0 %collective-permute-done.31.first_ref = bf16[128,256]{1,0:T(8,128)(2,1)S(1)} collective-permute-done((bf16[128,256]{1,0:T(8,128)(2,1)S(1)}, bf16[128,256]{1,0:T(8,128)(2,1)S(1)}, u32[]{:S(2)}, u32[]{:S(2)}) %collective-permute-start.31) | collective-permute-done | bytes 65568 | tf_op jit(solution)/shard_map/ppermute | solution.py:289
  130.3 2.2 %collective-permute-done.33.first_ref = bf16[128,512]{1,0:T(8,128)(2,1)S(1)} collective-permute-done((bf16[128,512]{1,0:T(8,128)(2,1)S(1)}, bf16[128,512]{1,0:T(8,128)(2,1)S(1)}, u32[]{:S(2)}, u32[]{:S(2)}) %collective-permute-start.33) | collective-permute-done | bytes 131104 | tf_op jit(solution)/shard_map/ppermute | solution.py:289
  138.6 2.0 %collective-permute-start.38 = (bf16[128,512]{1,0:T(8,128)(2,1)S(1)}, bf16[128,512]{1,0:T(8,128)(2,1)S(1)}, u32[]{:S(2)}, u32[]{:S(2)}) collective-permute-start(bf16[128,512]{1,0:T(8,128)(2,1)S(1)} %get-tuple-element.93), channel_id=1, source_target_pairs={{0,8},{4,0},{12,4},{20,12},{28,20},{24,28},{16,24},{8,16},{1,9},{5... | collective-permute-start | bytes 393224 | tf_op jit(solution)/shard_map/ppermute | solution.py:292
  141.1 2.4 %collective-permute-done.37 = bf16[128,512]{1,0:T(8,128)(2,1)S(1)} collective-permute-done((bf16[128,512]{1,0:T(8,128)(2,1)S(1)}, bf16[128,512]{1,0:T(8,128)(2,1)S(1)}, u32[]{:S(2)}, u32[]{:S(2)}) %collective-permute-start.37) | collective-permute-done | bytes 131104 | tf_op jit(solution)/shard_map/ppermute | solution.py:289
  144.3 2.8 %shard_map.120 = f32[1024,1024]{1,0:T(8,128)} custom-call(s32[2]{0:T(128)S(1)} %pad_add_fusion.refs_0_.where_ref, bf16[256,1024]{1,0:T(8,128)(2,1)S(1)} %shard_map.119.refs_0_, bf16[256,1024]{1,0:T(8,128)(2,1)S(1)} %collective-permute-done.56.refs_1_, bf16[256,1024]{1,0:T(8,128)(2,1)S(1)} %collective-permute-done.57.refs_2_, ...), custom_call_target="tpu_custom_call" | custom-call | bytes 6291456 | tf_op jit(solution)/shard_map/pallas_call | solution.py:267
  (129 shorter events, 62.8 us)
Async XLA Ops:
  1.7 6.5 %collective-permute-start.10 = (bf16[128,512]{1,0:T(8,128)(2,1)S(1)}, bf16[128,512]{1,0:T(8,128)(2,1)S(1)}, u32[]{:S(2)}, u32[]{:S(2)}) collective-permute-start(bf16[128,512]{1,0:T(8,128)(2,1)S(1)} %get-tuple-element.111.refs_1_), channel_id=1, source_target_pairs={{0,8},{4,0},{12,4},{20,12},{28,20},{24,28},{16,24},{8,16},{1,9},{5... | collective-permute-start | bytes 393224 | tf_op jit(solution)/shard_map/ppermute | solution.py:292
  4.7 5.2 %collective-permute-start.9 = (bf16[128,512]{1,0:T(8,128)(2,1)S(1)}, bf16[128,512]{1,0:T(8,128)(2,1)S(1)}, u32[]{:S(2)}, u32[]{:S(2)}) collective-permute-start(bf16[128,512]{1,0:T(8,128)(2,1)S(1)} %get-tuple-element.111.refs_1_), channel_id=1, source_target_pairs={{0,4},{4,12},{12,20},{20,28},{28,24},{24,16},{16,8},{8,0},{1,5},{5... | collective-permute-start | bytes 393224 | tf_op jit(solution)/shard_map/ppermute | solution.py:289
  8.2 6.4 %collective-permute-start.12 = (bf16[128,512]{1,0:T(8,128)(2,1)S(1)}, bf16[128,512]{1,0:T(8,128)(2,1)S(1)}, u32[]{:S(2)}, u32[]{:S(2)}) collective-permute-start(bf16[128,512]{1,0:T(8,128)(2,1)S(1)} %collective-permute-done.10.refs_3_), channel_id=1, source_target_pairs={{0,8},{4,0},{12,4},{20,12},{28,20},{24,28},{16,24},{8,16},{1,9},{5... | collective-permute-start | bytes 393224 | tf_op jit(solution)/shard_map/ppermute | solution.py:292
  10.0 6.3 %collective-permute-start.11 = (bf16[128,512]{1,0:T(8,128)(2,1)S(1)}, bf16[128,512]{1,0:T(8,128)(2,1)S(1)}, u32[]{:S(2)}, u32[]{:S(2)}) collective-permute-start(bf16[128,512]{1,0:T(8,128)(2,1)S(1)} %collective-permute-done.9.refs_2_), channel_id=1, source_target_pairs={{0,4},{4,12},{12,20},{20,28},{28,24},{24,16},{16,8},{8,0},{1,5},{5... | collective-permute-start | bytes 393224 | tf_op jit(solution)/shard_map/ppermute | solution.py:289
  10.2 9.6 %collective-permute-start.1 = (bf16[128,512]{1,0:T(8,128)(2,1)S(1)}, bf16[128,512]{1,0:T(8,128)(2,1)S(1)}, u32[]{:S(2)}, u32[]{:S(2)}) collective-permute-start(bf16[128,512]{1,0:T(8,128)(2,1)S(1)} %get-tuple-element.112.refs_1_), channel_id=1, source_target_pairs={{0,8},{4,0},{12,4},{20,12},{28,20},{24,28},{16,24},{8,16},{1,9},{5... | collective-permute-start | bytes 393224 | tf_op jit(solution)/shard_map/ppermute | solution.py:292
  12.0 9.6 %collective-permute-start = (bf16[128,512]{1,0:T(8,128)(2,1)S(1)}, bf16[128,512]{1,0:T(8,128)(2,1)S(1)}, u32[]{:S(2)}, u32[]{:S(2)}) collective-permute-start(bf16[128,512]{1,0:T(8,128)(2,1)S(1)} %get-tuple-element.112.refs_1_), channel_id=1, source_target_pairs={{0,4},{4,12},{12,20},{20,28},{28,24},{24,16},{16,8},{8,0},{1,5},{5... | collective-permute-start | bytes 393224 | tf_op jit(solution)/shard_map/ppermute | solution.py:289
  14.5 7.4 %collective-permute-start.14 = (bf16[128,512]{1,0:T(8,128)(2,1)S(1)}, bf16[128,512]{1,0:T(8,128)(2,1)S(1)}, u32[]{:S(2)}, u32[]{:S(2)}) collective-permute-start(bf16[128,512]{1,0:T(8,128)(2,1)S(1)} %collective-permute-done.12.refs_5_), channel_id=1, source_target_pairs={{0,8},{4,0},{12,4},{20,12},{28,20},{24,28},{16,24},{8,16},{1,9},{5... | collective-permute-start | bytes 393224 | tf_op jit(solution)/shard_map/ppermute | solution.py:292
  16.3 7.4 %collective-permute-start.13 = (bf16[128,512]{1,0:T(8,128)(2,1)S(1)}, bf16[128,512]{1,0:T(8,128)(2,1)S(1)}, u32[]{:S(2)}, u32[]{:S(2)}) collective-permute-start(bf16[128,512]{1,0:T(8,128)(2,1)S(1)} %collective-permute-done.11.refs_4_), channel_id=1, source_target_pairs={{0,4},{4,12},{12,20},{20,28},{28,24},{24,16},{16,8},{8,0},{1,5},{5... | collective-permute-start | bytes 393224 | tf_op jit(solution)/shard_map/ppermute | solution.py:289
  19.8 9.1 %collective-permute-start.3 = (bf16[128,512]{1,0:T(8,128)(2,1)S(1)}, bf16[128,512]{1,0:T(8,128)(2,1)S(1)}, u32[]{:S(2)}, u32[]{:S(2)}) collective-permute-start(bf16[128,512]{1,0:T(8,128)(2,1)S(1)} %collective-permute-done.1.refs_3_), channel_id=1, source_target_pairs={{0,8},{4,0},{12,4},{20,12},{28,20},{24,28},{16,24},{8,16},{1,9},{5... | collective-permute-start | bytes 393224 | tf_op jit(solution)/shard_map/ppermute | solution.py:292
  21.6 9.1 %collective-permute-start.2 = (bf16[128,512]{1,0:T(8,128)(2,1)S(1)}, bf16[128,512]{1,0:T(8,128)(2,1)S(1)}, u32[]{:S(2)}, u32[]{:S(2)}) collective-permute-start(bf16[128,512]{1,0:T(8,128)(2,1)S(1)} %collective-permute-done.refs_2_), channel_id=1, source_target_pairs={{0,4},{4,12},{12,20},{20,28},{28,24},{24,16},{16,8},{8,0},{1,5},{5... | collective-permute-start | bytes 393224 | tf_op jit(solution)/shard_map/ppermute | solution.py:289
  21.9 6.1 %collective-permute-start.16 = (bf16[128,256]{1,0:T(8,128)(2,1)S(1)}, bf16[128,256]{1,0:T(8,128)(2,1)S(1)}, u32[]{:S(2)}, u32[]{:S(2)}) collective-permute-start(bf16[128,256]{1,0:T(8,128)(2,1)S(1)} %slice.37), channel_id=1, source_target_pairs={{0,8},{4,0},{12,4},{20,12},{28,20},{24,28},{16,24},{8,16},{1,9},{5... | collective-permute-start | bytes 196616 | tf_op jit(solution)/shard_map/ppermute | solution.py:292
  28.8 14.4 %collective-permute-start.17 = (bf16[256,512]{1,0:T(8,128)(2,1)S(1)}, bf16[256,512]{1,0:T(8,128)(2,1)S(1)}, u32[]{:S(2)}, u32[]{:S(2)}) collective-permute-start(bf16[256,512]{1,0:T(8,128)(2,1)S(1)} %get-tuple-element.60), channel_id=1, source_target_pairs={{0,1},{1,0},{2,3},{3,2},{4,5},{5,4},{6,7},{7,6},{8,9},{9,8},{10,11... | collective-permute-start | bytes 786440 | tf_op jit(solution)/shard_map/ppermute | solution.py:295
  28.9 5.9 %collective-permute-start.5 = (bf16[128,512]{1,0:T(8,128)(2,1)S(1)}, bf16[128,512]{1,0:T(8,128)(2,1)S(1)}, u32[]{:S(2)}, u32[]{:S(2)}) collective-permute-start(bf16[128,512]{1,0:T(8,128)(2,1)S(1)} %collective-permute-done.3.refs_5_), channel_id=1, source_target_pairs={{0,8},{4,0},{12,4},{20,12},{28,20},{24,28},{16,24},{8,16},{1,9},{5... | collective-permute-start | bytes 393224 | tf_op jit(solution)/shard_map/ppermute | solution.py:292
  30.7 5.8 %collective-permute-start.4 = (bf16[128,512]{1,0:T(8,128)(2,1)S(1)}, bf16[128,512]{1,0:T(8,128)(2,1)S(1)}, u32[]{:S(2)}, u32[]{:S(2)}) collective-permute-start(bf16[128,512]{1,0:T(8,128)(2,1)S(1)} %collective-permute-done.2.refs_4_), channel_id=1, source_target_pairs={{0,4},{4,12},{12,20},{20,28},{28,24},{24,16},{16,8},{8,0},{1,5},{5... | collective-permute-start | bytes 393224 | tf_op jit(solution)/shard_map/ppermute | solution.py:289
  41.7 9.2 %collective-permute-start.20 = (bf16[128,1024]{1,0:T(8,128)(2,1)S(1)}, bf16[128,1024]{1,0:T(8,128)(2,1)S(1)}, u32[]{:S(2)}, u32[]{:S(2)}) collective-permute-start(bf16[128,1024]{1,0:T(8,128)(2,1)S(1)} %copy-done.2), channel_id=1, source_target_pairs={{0,2},{1,3},{2,0},{3,1},{4,6},{5,7},{6,4},{7,5},{8,10},{9,11},{10,... | collective-permute-start | bytes 786440 | tf_op jit(solution)/shard_map/ppermute | solution.py:298
  43.3 13.2 %collective-permute-start.19 = (bf16[256,512]{1,0:T(8,128)(2,1)S(1)}, bf16[256,512]{1,0:T(8,128)(2,1)S(1)}, u32[]{:S(2)}, u32[]{:S(2)}) collective-permute-start(bf16[256,512]{1,0:T(8,128)(2,1)S(1)} %add_convert_fusion.refs_2_), channel_id=1, source_target_pairs={{0,2},{1,3},{2,0},{3,1},{4,6},{5,7},{6,4},{7,5},{8,10},{9,11},{10,... | collective-permute-start | bytes 786440 | tf_op jit(solution)/shard_map/ppermute | solution.py:298
  44.0 17.6 %collective-permute-start.18 = (bf16[256,512]{1,0:T(8,128)(2,1)S(1)}, bf16[256,512]{1,0:T(8,128)(2,1)S(1)}, u32[]{:S(2)}, u32[]{:S(2)}) collective-permute-start(bf16[256,512]{1,0:T(8,128)(2,1)S(1)} %add_convert_fusion.1.refs_1_), channel_id=1, source_target_pairs={{0,2},{1,3},{2,0},{3,1},{4,6},{5,7},{6,4},{7,5},{8,10},{9,11},{10,... | collective-permute-start | bytes 786440 | tf_op jit(solution)/shard_map/ppermute | solution.py:298
  85.3 24.6 %collective-permute-start.21 = (bf16[256,512]{1,0:T(8,128)(2,1)S(1)}, bf16[256,512]{1,0:T(8,128)(2,1)S(1)}, u32[]{:S(2)}, u32[]{:S(2)}) collective-permute-start(bf16[256,512]{1,0:T(8,128)(2,1)S(1)} %get-tuple-element.62.near_ref), channel_id=1, source_target_pairs={{0,1},{1,0},{2,3},{3,2},{4,5},{5,4},{6,7},{7,6},{8,9},{9,8},{10,11... | collective-permute-start | bytes 786440 | tf_op jit(solution)/shard_map/ppermute | solution.py:295
  96.1 22.7 %collective-permute-start.30 = (bf16[256,512]{1,0:T(8,128)(2,1)S(1)}, bf16[256,512]{1,0:T(8,128)(2,1)S(1)}, u32[]{:S(2)}, u32[]{:S(2)}) collective-permute-start(bf16[256,512]{1,0:T(8,128)(2,1)S(1)} %get-tuple-element.78.near_ref), channel_id=1, source_target_pairs={{0,1},{1,0},{2,3},{3,2},{4,5},{5,4},{6,7},{7,6},{8,9},{9,8},{10,11... | collective-permute-start | bytes 786440 | tf_op jit(solution)/shard_map/ppermute | solution.py:295
  107.8 32.7 %collective-permute-start.56 = (bf16[256,1024]{1,0:T(8,128)(2,1)S(1)}, bf16[256,1024]{1,0:T(8,128)(2,1)S(1)}, u32[]{:S(2)}, u32[]{:S(2)}) collective-permute-start(bf16[256,1024]{1,0:T(8,128)(2,1)S(1)} %shard_map.119.refs_0_), channel_id=1, source_target_pairs={{0,2},{1,3},{2,0},{3,1},{4,6},{5,7},{6,4},{7,5},{8,10},{9,11},{10,... | collective-permute-start | bytes 1572872 | tf_op jit(solution)/shard_map/ppermute | solution.py:298
  116.7 11.5 %collective-permute-start.24 = (bf16[128,512]{1,0:T(8,128)(2,1)S(1)}, bf16[128,512]{1,0:T(8,128)(2,1)S(1)}, u32[]{:S(2)}, u32[]{:S(2)}) collective-permute-start(bf16[128,512]{1,0:T(8,128)(2,1)S(1)} %get-tuple-element.72), channel_id=1, source_target_pairs={{0,4},{4,12},{12,20},{20,28},{28,24},{24,16},{16,8},{8,0},{1,5},{5... | collective-permute-start | bytes 393224 | tf_op jit(solution)/shard_map/ppermute | solution.py:289
  118.4 9.8 %collective-permute-start.25 = (bf16[128,512]{1,0:T(8,128)(2,1)S(1)}, bf16[128,512]{1,0:T(8,128)(2,1)S(1)}, u32[]{:S(2)}, u32[]{:S(2)}) collective-permute-start(bf16[128,512]{1,0:T(8,128)(2,1)S(1)} %get-tuple-element.73), channel_id=1, source_target_pairs={{0,8},{4,0},{12,4},{20,12},{28,20},{24,28},{16,24},{8,16},{1,9},{5... | collective-permute-start | bytes 393224 | tf_op jit(solution)/shard_map/ppermute | solution.py:292
  119.6 5.1 %collective-permute-start.31 = (bf16[128,256]{1,0:T(8,128)(2,1)S(1)}, bf16[128,256]{1,0:T(8,128)(2,1)S(1)}, u32[]{:S(2)}, u32[]{:S(2)}) collective-permute-start(bf16[128,256]{1,0:T(8,128)(2,1)S(1)} %get-tuple-element.86), channel_id=1, source_target_pairs={{0,4},{4,12},{12,20},{20,28},{28,24},{24,16},{16,8},{8,0},{1,5},{5... | collective-permute-start | bytes 196616 | tf_op jit(solution)/shard_map/ppermute | solution.py:289
  126.1 6.4 %collective-permute-start.33 = (bf16[128,512]{1,0:T(8,128)(2,1)S(1)}, bf16[128,512]{1,0:T(8,128)(2,1)S(1)}, u32[]{:S(2)}, u32[]{:S(2)}) collective-permute-start(bf16[128,512]{1,0:T(8,128)(2,1)S(1)} %get-tuple-element.88), channel_id=1, source_target_pairs={{0,4},{4,12},{12,20},{20,28},{28,24},{24,16},{16,8},{8,0},{1,5},{5... | collective-permute-start | bytes 393224 | tf_op jit(solution)/shard_map/ppermute | solution.py:289
  126.6 6.3 %collective-permute-start.34 = (bf16[128,512]{1,0:T(8,128)(2,1)S(1)}, bf16[128,512]{1,0:T(8,128)(2,1)S(1)}, u32[]{:S(2)}, u32[]{:S(2)}) collective-permute-start(bf16[128,512]{1,0:T(8,128)(2,1)S(1)} %get-tuple-element.89), channel_id=1, source_target_pairs={{0,8},{4,0},{12,4},{20,12},{28,20},{24,28},{16,24},{8,16},{1,9},{5... | collective-permute-start | bytes 393224 | tf_op jit(solution)/shard_map/ppermute | solution.py:292
  128.2 6.8 %collective-permute-start.26 = (bf16[128,512]{1,0:T(8,128)(2,1)S(1)}, bf16[128,512]{1,0:T(8,128)(2,1)S(1)}, u32[]{:S(2)}, u32[]{:S(2)}) collective-permute-start(bf16[128,512]{1,0:T(8,128)(2,1)S(1)} %get-tuple-element.74), channel_id=1, source_target_pairs={{0,4},{4,12},{12,20},{20,28},{28,24},{24,16},{16,8},{8,0},{1,5},{5... | collective-permute-start | bytes 393224 | tf_op jit(solution)/shard_map/ppermute | solution.py:289
  128.7 6.3 %collective-permute-start.27 = (bf16[128,512]{1,0:T(8,128)(2,1)S(1)}, bf16[128,512]{1,0:T(8,128)(2,1)S(1)}, u32[]{:S(2)}, u32[]{:S(2)}) collective-permute-start(bf16[128,512]{1,0:T(8,128)(2,1)S(1)} %get-tuple-element.75), channel_id=1, source_target_pairs={{0,8},{4,0},{12,4},{20,12},{28,20},{24,28},{16,24},{8,16},{1,9},{5... | collective-permute-start | bytes 393224 | tf_op jit(solution)/shard_map/ppermute | solution.py:292
  132.9 5.0 %collective-permute-start.35 = (bf16[128,512]{1,0:T(8,128)(2,1)S(1)}, bf16[128,512]{1,0:T(8,128)(2,1)S(1)}, u32[]{:S(2)}, u32[]{:S(2)}) collective-permute-start(bf16[128,512]{1,0:T(8,128)(2,1)S(1)} %get-tuple-element.90), channel_id=1, source_target_pairs={{0,4},{4,12},{12,20},{20,28},{28,24},{24,16},{16,8},{8,0},{1,5},{5... | collective-permute-start | bytes 393224 | tf_op jit(solution)/shard_map/ppermute | solution.py:289
  133.4 5.0 %collective-permute-start.36 = (bf16[128,512]{1,0:T(8,128)(2,1)S(1)}, bf16[128,512]{1,0:T(8,128)(2,1)S(1)}, u32[]{:S(2)}, u32[]{:S(2)}) collective-permute-start(bf16[128,512]{1,0:T(8,128)(2,1)S(1)} %get-tuple-element.91), channel_id=1, source_target_pairs={{0,8},{4,0},{12,4},{20,12},{28,20},{24,28},{16,24},{8,16},{1,9},{5... | collective-permute-start | bytes 393224 | tf_op jit(solution)/shard_map/ppermute | solution.py:292
  135.0 5.5 %collective-permute-start.28 = (bf16[128,512]{1,0:T(8,128)(2,1)S(1)}, bf16[128,512]{1,0:T(8,128)(2,1)S(1)}, u32[]{:S(2)}, u32[]{:S(2)}) collective-permute-start(bf16[128,512]{1,0:T(8,128)(2,1)S(1)} %get-tuple-element.76), channel_id=1, source_target_pairs={{0,4},{4,12},{12,20},{20,28},{28,24},{24,16},{16,8},{8,0},{1,5},{5... | collective-permute-start | bytes 393224 | tf_op jit(solution)/shard_map/ppermute | solution.py:289
  135.5 5.5 %collective-permute-start.29 = (bf16[128,512]{1,0:T(8,128)(2,1)S(1)}, bf16[128,512]{1,0:T(8,128)(2,1)S(1)}, u32[]{:S(2)}, u32[]{:S(2)}) collective-permute-start(bf16[128,512]{1,0:T(8,128)(2,1)S(1)} %get-tuple-element.77), channel_id=1, source_target_pairs={{0,8},{4,0},{12,4},{20,12},{28,20},{24,28},{16,24},{8,16},{1,9},{5... | collective-permute-start | bytes 393224 | tf_op jit(solution)/shard_map/ppermute | solution.py:292
  138.4 5.0 %collective-permute-start.37 = (bf16[128,512]{1,0:T(8,128)(2,1)S(1)}, bf16[128,512]{1,0:T(8,128)(2,1)S(1)}, u32[]{:S(2)}, u32[]{:S(2)}) collective-permute-start(bf16[128,512]{1,0:T(8,128)(2,1)S(1)} %get-tuple-element.92), channel_id=1, source_target_pairs={{0,4},{4,12},{12,20},{20,28},{28,24},{24,16},{16,8},{8,0},{1,5},{5... | collective-permute-start | bytes 393224 | tf_op jit(solution)/shard_map/ppermute | solution.py:289
  (30 other events, 189.2 us)

commit v2 on v1

v2 whole, which is shorter than its diff:
```python
import functools

import jax
import jax.numpy as jnp
from jax import lax
from jax.experimental import pallas as pl
from jax.experimental.pallas import tpu as pltpu
from jax.sharding import PartitionSpec as P

CHUNKS = 2
VMEM_LIMIT = 48 * 1024 * 1024


def ring_of(count, width):
    height = count // width
    if count % width or width % 2 or height < 2:
        return list(range(count))
    walk = [(0, x) for x in range(width)]
    for turn, x in enumerate(reversed(range(width))):
        down = range(1, height) if turn % 2 == 0 else range(height - 1, 0, -1)
        walk += [(z, x) for z in down]
    return [z * width + x for z, x in walk]


def ring_slots(count):
    return [0] + [away for step in range(1, count // 2) for away in (count - step, step)] + [count // 2]


def pick(index, table):
    value = jnp.int32(table[0])
    for at in range(1, len(table)):
        value = jnp.where(index == at, jnp.int32(table[at]), value)
    return value


def position(spot):
    column = lax.axis_index("col")
    return pick(lax.axis_index("row"), spot), lax.div(column, jnp.int32(2)), lax.rem(column, jnp.int32(2))


class Tiling:
    def __init__(self, rows, cols, count):
        self.split = max(1, 16 * count // rows)
        self.height = rows * self.split // count
        self.width = cols // self.split
        self.shape = (self.height, self.width)

    def at(self, block, base=0):
        top = pl.multiple_of(base + lax.div(block, jnp.int32(self.split)) * self.height, self.height)
        if self.split == 1:
            return pl.ds(top, self.height), slice(None)
        return pl.ds(top, self.height), pl.ds(pl.multiple_of(lax.rem(block, jnp.int32(self.split)) * self.width, 128), self.width)


def vmem_call(kernel, out_shapes, args, scratch=(), smem=0, hbm=0, hbm_out=False, after=(), flops=0, moved=0):
    vmem = pl.BlockSpec(memory_space=pltpu.VMEM)
    anywhere = pl.BlockSpec(memory_space=pl.ANY)
    specs = [pl.BlockSpec(memory_space=pltpu.SMEM)] * smem + [anywhere] * hbm
    specs += [vmem] * (len(args) - smem - hbm) + [anywhere] * len(after)
    count = len(args)

    def inner(*refs):
        kernel(*refs[:count], *refs[count + len(after) :])

    return pl.pallas_call(
        inner,
        out_shape=out_shapes,
        in_specs=specs,
        out_specs=jax.tree.map(lambda _: anywhere if hbm_out else vmem, out_shapes),
        scratch_shapes=list(scratch),
        compiler_params=pltpu.CompilerParams(vmem_limit_bytes=VMEM_LIMIT),
        cost_estimate=pl.CostEstimate(flops=flops, bytes_accessed=moved, transcendentals=0),
    )(*args, *after)


def place_tiles(spot, groups, vals, tile_rows, tile_cols, tile_count, feats, first):
    slots, side = vals.shape[2], vals.shape[-1]
    count = len(spot)

    def kernel(row_ref, col_ref, live_ref, vals_hbm, feats_hbm, out_ref, rest_ref, held, sems):
        feats_copy = pltpu.make_async_copy(feats_hbm.at[:, first:], rest_ref, sems.at[0])
        feats_copy.start()
        vals_copy = pltpu.make_async_copy(vals_hbm.at[0, 0], held, sems.at[1])
        vals_copy.start()
        me, group, core = position(spot)
        out_ref[...] = jnp.zeros_like(out_ref)
        vals_copy.wait()

        def put(slot, carry):
            row = row_ref[0, 0, slot]
            other = lax.rem(row, 2) ^ core
            along = lax.rem(lax.div(row, 2) + groups - group, groups)
            top = pl.multiple_of((other * groups + along) * side, side)
            away = lax.rem(pick(col_ref[0, 0, slot], spot) + count - me, count)
            col = jnp.where(away < count // 2, 2 * away, 2 * (count - away) - 1)
            left = pl.multiple_of(col * side, side)
            out_ref[pl.ds(top, side), pl.ds(left, side)] = held[slot]
            return carry

        lax.fori_loop(0, live_ref[0, 0], put, 0)
        feats_copy.wait()

    shapes = (
        jax.ShapeDtypeStruct((2 * groups * side, count * side), vals.dtype),
        jax.ShapeDtypeStruct((feats.shape[0], feats.shape[1] - first), feats.dtype),
    )
    scratch = [pltpu.VMEM((slots, side, side), vals.dtype), pltpu.SemaphoreType.DMA((2,))]
    args = (tile_rows, tile_cols, tile_count, vals, feats)
    return vmem_call(kernel, shapes, args, scratch=scratch, smem=3, hbm=2, moved=4 * vals.size)


def aggregate(adjacency, pieces, ends, after):
    rows, depth = adjacency.shape
    height, width = pieces[0].shape
    half = rows // 2

    def kernel(*refs):
        adj_ref = refs[0]
        piece_refs = refs[1 : 1 + len(pieces)]
        right_ref, left_ref, near_ref, far_ref, held = refs[1 + len(pieces) :]
        for place, piece_ref in enumerate(piece_refs):
            held[place * height : (place + 1) * height] = piece_ref[...]
        held[depth - height :, : width // 2] = right_ref[...]
        held[depth - height :, width // 2 :] = left_ref[...]
        far_ref[...] = jnp.dot(adj_ref[half:], held[...], preferred_element_type=jnp.float32).astype(jnp.bfloat16)
        near_ref[...] = jnp.dot(adj_ref[:half], held[...], preferred_element_type=jnp.float32)

    shapes = (
        jax.ShapeDtypeStruct((half, width), jnp.float32),
        jax.ShapeDtypeStruct((half, width), jnp.bfloat16),
    )
    return vmem_call(
        kernel,
        shapes,
        (adjacency, *pieces, *ends),
        scratch=[pltpu.VMEM((depth, width), jnp.bfloat16)],
        after=after,
        flops=2 * rows * depth * width,
        moved=2 * (rows * depth + depth * width + rows * width),
    )


def dense(spot, held, arrived, weight, cotangents):
    chunks = len(held)
    rows, width = held[0].shape
    depth, cols = weight.shape
    groups = len(cotangents)
    side = rows // groups
    part = depth // groups
    quarter = part // 2

    def kernel(*refs):
        refs = list(refs)
        _, group, core = position(spot)
        held_refs = [refs.pop(0) for _ in range(chunks)]
        arrived_refs = [[refs.pop(0) for _ in range(chunks)] for _ in range(groups - 1)]
        weight_ref = refs.pop(0)
        cot_refs = [refs.pop(0) for _ in range(groups)]
        act_ref, near_ref, far_ref = refs[:3]
        back_refs = refs[3 : 3 + chunks]
        agg = refs[-2]
        grad = refs[-1]
        for h in range(chunks):
            for g in range(groups):
                total = held_refs[h][g * side : (g + 1) * side].astype(jnp.float32)
                for s in range(1, groups):
                    at = (g + s) % groups
                    total = total + arrived_refs[s - 1][h][at * side : (at + 1) * side].astype(jnp.float32)
                agg[g * side : (g + 1) * side, h * width : (h + 1) * width] = total.astype(jnp.bfloat16)
        for g in range(groups):
            value = jnp.dot(agg[g * side : (g + 1) * side], weight_ref[...], preferred_element_type=jnp.float32)
            gate = jax.nn.sigmoid(value)
            if g == 0:
                act_ref[...] = (value * gate).astype(jnp.bfloat16)
            slope = gate * (1.0 + value * (1.0 - gate))
            cot = cot_refs[(groups - g) % groups][...].astype(jnp.float32)
            grad[g * side : (g + 1) * side] = (cot * slope).astype(jnp.bfloat16)
        for h in range(chunks):
            back_refs[h][...] = lax.dot_general(
                grad[...], weight_ref[h * width : (h + 1) * width], (((1,), (1,)), ((), ())), preferred_element_type=jnp.float32
            ).astype(jnp.bfloat16)
        first = group * part
        near_at = pl.multiple_of(first + core * quarter, 128)
        far_at = pl.multiple_of(first + (1 - core) * quarter, 128)
        far_ref[...] = lax.dot_general(
            agg[:, pl.ds(far_at, quarter)], grad[...], (((0,), (0,)), ((), ())), preferred_element_type=jnp.float32
        ).astype(jnp.bfloat16)
        near_ref[...] = lax.dot_general(
            agg[:, pl.ds(near_at, quarter)], grad[...], (((0,), (0,)), ((), ())), preferred_element_type=jnp.float32
        )

    shapes = [
        jax.ShapeDtypeStruct((side, cols), jnp.bfloat16),
        jax.ShapeDtypeStruct((quarter, cols), jnp.float32),
        jax.ShapeDtypeStruct((quarter, cols), jnp.bfloat16),
    ] + [jax.ShapeDtypeStruct((rows, width), jnp.bfloat16)] * chunks
    outs = vmem_call(
        kernel,
        shapes,
        (*held, *[a for step in arrived for a in step], weight, *cotangents),
        scratch=[pltpu.VMEM((rows, depth), jnp.bfloat16), pltpu.VMEM((rows, cols), jnp.bfloat16)],
        flops=2 * rows * cols * (2 * depth + part),
        moved=2 * (depth * cols + 6 * rows * depth),
    )
    return outs[0], outs[1], outs[2], outs[3:]


def back_blocks(adjacency, near, far, count):
    rows, depth = adjacency.shape
    half, width = near.shape
    height = depth // count

    def kernel(adj_ref, near_ref, far_ref, *out_refs):
        held = out_refs[-1]
        held[:half] = near_ref[...]
        held[half:] = far_ref[...]
        for place in reversed(range(count)):
            block = lax.dot_general(
                adj_ref[:, place * height : (place + 1) * height],
                held[...],
                (((0,), (0,)), ((), ())),
                preferred_element_type=jnp.float32,
            ).astype(jnp.bfloat16)
            if place == count - 1:
                out_refs[place][...] = block[:, : width // 2]
                out_refs[place + 1][...] = block[:, width // 2 :]
            else:
                out_refs[place][...] = block

    shapes = [jax.ShapeDtypeStruct((height, width), jnp.bfloat16)] * (count - 1)
    shapes += [jax.ShapeDtypeStruct((height, width // 2), jnp.bfloat16)] * 2
    return vmem_call(
        kernel,
        shapes,
        (adjacency, near, far),
        scratch=[pltpu.VMEM((rows, width), jnp.bfloat16)],
        flops=2 * rows * depth * width,
        moved=2 * (rows * depth + depth * width + rows * width),
    )


def weight_blocks(spot, near, arrived, tiling):
    count = len(spot)
    middle = tiling.width // 2

    def kernel(near_ref, arrived_ref, *out_refs):
        me, _, _ = position(spot)
        for place, away in enumerate(ring_slots(count)):
            at = tiling.at(lax.rem(me + away, count))
            block = (near_ref[at] + arrived_ref[at].astype(jnp.float32)).astype(jnp.bfloat16)
            if place == count - 1:
                out_refs[place][...] = block[:, :middle]
                out_refs[place + 1][...] = block[:, middle:]
            else:
                out_refs[place][...] = block

    shapes = [jax.ShapeDtypeStruct(tiling.shape, jnp.bfloat16)] * (count - 1)
    shapes += [jax.ShapeDtypeStruct((tiling.height, middle), jnp.bfloat16)] * 2
    return vmem_call(kernel, shapes, (near, arrived), flops=near.size, moved=8 * near.size)


def add_round(pairs, finals, after=()):
    args = [a for group in pairs + finals for a in group]

    def kernel(*refs):
        ins, outs = list(refs[: len(args)]), list(refs[len(args) :])
        for _ in pairs:
            right, left, first, second = (ins.pop(0) for _ in range(4))
            width, part = right.shape[1], first.shape[1]
            out_right, out_left = outs.pop(0), outs.pop(0)
            out_right[:, :part] = right[:, :part] + first[...]
            out_left[:, width - part :] = left[:, width - part :] + second[...]
            if part < width:
                out_right[:, part:] = right[:, part:]
                out_left[:, : width - part] = left[:, : width - part]
        for _ in finals:
            own, first, second = (ins.pop(0)[...].astype(jnp.float32) for _ in range(3))
            outs.pop(0)[...] = (own + first + second).astype(jnp.bfloat16)

    shapes = [jax.ShapeDtypeStruct(g[0].shape, jnp.bfloat16) for g in pairs for _ in range(2)]
    shapes += [jax.ShapeDtypeStruct(g[0].shape, jnp.bfloat16) for g in finals]
    moved = sum(2 * a.size for a in args)
    outs = vmem_call(kernel, shapes, args, after=after, flops=moved, moved=2 * moved)
    return [tuple(outs[2 * k : 2 * k + 2]) for k in range(len(pairs))], outs[2 * len(pairs) :]


def stack_blocks(blocks, ends):
    height, width = (blocks or ends)[0].shape
    if not blocks:
        width *= 2

    def kernel(*refs):
        out_ref = refs[-1]
        for place in range(len(blocks)):
            out_ref[place * height : (place + 1) * height] = refs[place][...]
        for side in range(len(ends)):
            half = width // 2
            out_ref[len(blocks) * height :, side * half : (side + 1) * half] = refs[len(blocks) + side][...]

    total = len(blocks) + len(ends) // 2
    shape = jax.ShapeDtypeStruct((total * height, width), jnp.bfloat16)
    return vmem_call(kernel, shape, (*blocks, *ends), moved=4 * total * height * width)


def join_weight(spot, groups, tiling, shape, stacks):
    count = len(spot)
    quarter = shape[0] // (2 * groups)
    total = 2 * groups * count

    def kernel(*refs):
        stack_refs, out_ref, wide, sems = refs[: len(stacks)], refs[-3], refs[-2], refs[-1]
        me, group, core = position(spot)
        copies = []
        for ref, (_, aways, steps, other) in zip(stack_refs, stacks):
            back = lax.rem(group + groups - steps, groups)
            base = (back * 2 + (1 - core if other else core)) * quarter
            for place, away in enumerate(aways):
                slot = len(copies)
                wide[slot] = ref[place * tiling.height : (place + 1) * tiling.height].astype(jnp.float32)
                at = tiling.at(lax.rem(me + away, count), base)
                copies.append(pltpu.make_async_copy(wide.at[slot], out_ref.at[at], sems.at[slot]))
                copies[-1].start()
        for copy in copies:
            copy.wait()

    out = jax.ShapeDtypeStruct(shape, jnp.float32)
    scratch = [pltpu.VMEM((total, *tiling.shape), jnp.float32), pltpu.SemaphoreType.DMA((total,))]
    return vmem_call(kernel, out, [s[0] for s in stacks], scratch=scratch, hbm_out=True, moved=6 * shape[0] * shape[1])


def body(width, feats, weight, tile_vals, tile_rows, tile_cols, tile_count, grad_out):
    count = lax.axis_size("row")
    columns = lax.axis_size("col")
    groups = columns // 2
    rounds = count // 2
    ring = ring_of(count, width)
    spot = [0] * count
    for place, row in enumerate(ring):
        spot[row] = place

    to_right = [(ring[k], ring[(k + 1) % count]) for k in range(count)]
    to_left = [(ring[k], ring[(k - 1) % count]) for k in range(count)]
    swap = [(k, k ^ 1) for k in range(columns)]

    def go(right, left):
        return lax.ppermute(right, "row", to_right), lax.ppermute(left, "row", to_left)

    def go_halves(right, left):
        middle = right.shape[1] // 2
        return go(right[:, :middle], left[:, middle:])

    def swap_core(value):
        return lax.ppermute(value, "col", swap)

    def from_group(value, steps):
        return lax.ppermute(value, "col", [(k, (k + 2 * steps) % columns) for k in range(columns)])

    def gather_ring(piece):
        pieces = [piece]
        right = left = piece
        for _ in range(rounds - 1):
            right, left = go(right, left)
            pieces += [right, left]
        return pieces, go_halves(right, left)

    chunk = feats.shape[1] // CHUNKS
    adjacency, second = place_tiles(spot, groups, tile_vals, tile_rows, tile_cols, tile_count, feats, chunk)
    cotangents = [grad_out] + [from_group(grad_out, s) for s in range(1, groups)]
    held = []
    arrived = [[] for _ in range(groups - 1)]
    for h, piece in enumerate((feats[:, :chunk], second)):
        pieces, ends = gather_ring(piece)
        after = cotangents[1:] if h == 0 else [step[0] for step in arrived]
        near, far = aggregate(adjacency, pieces, ends, after)
        total = (near + swap_core(far).astype(jnp.float32)).astype(jnp.bfloat16)
        held.append(total)
        for s in range(1, groups):
            arrived[s - 1].append(from_group(total, s))

    activated, near_weight, far_weight, back = dense(spot, held, arrived, weight, cotangents)

    tiling = Tiling(*near_weight.shape, count)
    blocks = [back_blocks(adjacency, b, swap_core(b), count) for b in back]
    terms = weight_blocks(spot, near_weight, swap_core(far_weight), tiling)
    moving = [None] * CHUNKS
    weight_moving = go(terms[count - 1], terms[count])
    weight_pieces = []
    for slot in range(2 * rounds):
        j, h = divmod(slot, 2)
        pairs, finals, after = [], [], []
        if 0 < slot < rounds:
            step = 2 * (rounds - slot)
            pairs.append((terms[step], terms[step - 1], *weight_moving))
        elif slot == rounds:
            finals.append((terms[0], *weight_moving))
        elif slot > rounds:
            weight_pieces += weight_moving
            after = weight_moving
        if j > 0:
            step = 2 * (rounds - j)
            pairs.append((blocks[h][step], blocks[h][step - 1], *moving[h]))
        sums, ends = add_round(pairs, finals, after) if pairs or finals else ([], [])
        if 0 < slot < rounds:
            weight_moving = go(*sums[0])
        elif slot == rounds:
            weight_pieces.append(ends[0])
            weight_moving = go(ends[0], ends[0])
        elif rounds < slot < 2 * rounds - 1:
            weight_moving = go(*weight_moving)
        elif slot == 2 * rounds - 1:
            weight_moving = go_halves(*weight_moving)
        moving[h] = go(*sums[-1]) if j > 0 else go(blocks[h][count - 1], blocks[h][count])

    _, grads = add_round([], [(blocks[h][0], *moving[h]) for h in range(CHUNKS)])
    grad_feats = jnp.concatenate(grads, axis=1)

    slots = ring_slots(count)
    early = 1 + 2 * (rounds // 2)
    stacks = []
    for first, last in ((0, early), (early, count)):
        stack = stack_blocks(weight_pieces[first:last], weight_moving if last == count else ())
        for s in range(groups):
            value = stack if s == 0 else from_group(stack, s)
            stacks.append((value, slots[first:last], s, False))
            stacks.append((swap_core(value), slots[first:last], s, True))
    grad_weight = join_weight(spot, groups, tiling, weight.shape, stacks)
    return (activated, grad_feats, grad_weight)


def solution(mesh):
    spread = {d.coords[0] for d in mesh.devices.flat if hasattr(d, "coords")}
    placed = (
        P(("row", "col"), None),
        P(),
        P("row", "col", None, None, None),
        P("row", "col", None),
        P("row", "col", None),
        P("row", "col"),
        P(("row", "col"), None),
    )
    return jax.shard_map(
        functools.partial(body, max(1, len(spread))),
        mesh=mesh,
        in_specs=placed,
        out_specs=(P(("row", "col"), None), P(("row", "col"), None), P()),
        check_vma=False,
    )
```

time: 147 us -> 130 us (0.88)
  waiting for transfers between devices: 69.7 us -> 53.6 us
  starting transfers between devices: 57 us -> 60.8 us
  other arithmetic: 3.07 us -> 0.87 us
  Pallas kernels: 10.9 us -> 8.87 us
    ppermute x4 -> x5, waiting for transfers between devices: 16 us -> 6.89 us  [from_group(): lax.ppermute(value, 'col', [(k, (k + 2 * steps) % columns) for k in range...]
    ppermute x48, waiting for transfers between devices: 51.8 us -> 43.8 us  [the longest x24 35.1 us: go(): lax.ppermute(left, 'row', to_left)]
    ppermute x4 -> x5, starting transfers between devices: 5.75 us -> 8.8 us  [from_group(): lax.ppermute(value, 'col', [(k, (k + 2 * steps) % columns) for k in range...]
    unnamed x6 -> x12, local copies, waits for them, and re-layouts: 1.23 us -> 3.49 us
    pallas_call x18, Pallas kernels: 10.9 us -> 8.87 us  [vmem_call(): pl.pallas_call(inner, out_shape=out_shapes, in_specs=specs, out_specs=jax...]
    select_n x2 -> x0, other arithmetic: 1.98 us -> none  [the longest x1 1.32 us: body(): col_at = jnp.where(away < count // 2, 2 * away, 2 * (count - away) - 1)]
  transfers between devices with their start and end apart: 59 -> 62, of which waited for: 32 -> 26; matrix products, arithmetic and copies ran while one was open for 4% -> 1% of each run, Pallas kernels for 3% -> 2%
where the time goes in v2:
time: 130 us
  starting transfers between devices  60.8 us (47%)
  waiting for transfers between devices  53.6 us (41%)
  Pallas kernels  8.87 us (7%)
  local copies, waits for them, and re-layouts  4.43 us (3%)
  between operations  1.53 us (1%)
    ppermute x24, waiting for transfers between devices, go(): lax.ppermute(left, 'row', to_left)  35.1 us
    ppermute x24, starting transfers between devices, go(): lax.ppermute(left, 'row', to_left)  25.2 us
    ppermute x24, starting transfers between devices, go(): lax.ppermute(right, 'row', to_right)  25.1 us
    pallas_call x18, Pallas kernels, vmem_call(): pl.pallas_call(inner, out_shape=out_shapes, in_specs=specs, out_specs=jax...  8.87 us
    ppermute x5, starting transfers between devices, from_group(): lax.ppermute(value, 'col', [(k, (k + 2 * steps) % columns) for k in range...  8.8 us
    ppermute x24, waiting for transfers between devices, go(): lax.ppermute(right, 'row', to_right)  8.74 us
    ppermute x5, waiting for transfers between devices, from_group(): lax.ppermute(value, 'col', [(k, (k + 2 * steps) % columns) for k in range...  6.89 us
    unnamed x12, local copies, waits for them, and re-layouts  3.49 us
  transfers between devices with their start and end apart: 62, of which 26 were waited for; matrix products, arithmetic and copies ran while one was open for 1% of the time, Pallas kernels for 2%

profile of v2, /device:TPU:0, one launch (start us, length us, event | category | flops | bytes accessed | tf_op | source)
XLA Modules:
  0.0 130.1 jit_solution(7649086329404051320)
XLA Ops:
  1.5 3.1 %collective-permute-start.1 = (bf16[128,512]{1,0:T(8,128)(2,1)S(1)}, bf16[128,512]{1,0:T(8,128)(2,1)S(1)}, u32[]{:S(2)}, u32[]{:S(2)}) collective-permute-start(bf16[128,512]{1,0:T(8,128)(2,1)S(1)} %slice.21.refs_1_), channel_id=1, source_target_pairs={{0,8},{4,0},{12,4},{20,12},{28,20},{24,28},{16,24},{8,16},{1,9},{5... | collective-permute-start | bytes 393224 | tf_op jit(solution)/shard_map/ppermute | solution.py:346
  4.6 3.4 %collective-permute-done.1.refs_3_ = bf16[128,512]{1,0:T(8,128)(2,1)S(1)} collective-permute-done((bf16[128,512]{1,0:T(8,128)(2,1)S(1)}, bf16[128,512]{1,0:T(8,128)(2,1)S(1)}, u32[]{:S(2)}, u32[]{:S(2)}) %collective-permute-start.1) | collective-permute-done | bytes 131104 | tf_op jit(solution)/shard_map/ppermute | solution.py:346
  8.0 1.8 %collective-permute-start.3 = (bf16[128,512]{1,0:T(8,128)(2,1)S(1)}, bf16[128,512]{1,0:T(8,128)(2,1)S(1)}, u32[]{:S(2)}, u32[]{:S(2)}) collective-permute-start(bf16[128,512]{1,0:T(8,128)(2,1)S(1)} %collective-permute-done.1.refs_3_), channel_id=1, source_target_pairs={{0,8},{4,0},{12,4},{20,12},{28,20},{24,28},{16,24},{8,16},{1,9},{5... | collective-permute-start | bytes 393224 | tf_op jit(solution)/shard_map/ppermute | solution.py:346
  10.1 1.8 %collective-permute-start.8 = (bf16[128,1024]{1,0:T(8,128)(2,1)}, bf16[128,1024]{1,0:T(8,128)(2,1)S(1)}, u32[]{:S(2)}, u32[]{:S(2)}) collective-permute-start(bf16[128,1024]{1,0:T(8,128)(2,1)} %refs_5_.1), channel_id=1, source_target_pairs={{0,2},{1,3},{2,0},{3,1},{4,6},{5,7},{6,4},{7,5},{8,10},{9,11},{10,... | collective-permute-start | bytes 786440 | tf_op jit(solution)/shard_map/ppermute | solution.py:356
  13.0 1.8 %collective-permute-start.5 = (bf16[128,512]{1,0:T(8,128)(2,1)S(1)}, bf16[128,512]{1,0:T(8,128)(2,1)S(1)}, u32[]{:S(2)}, u32[]{:S(2)}) collective-permute-start(bf16[128,512]{1,0:T(8,128)(2,1)S(1)} %collective-permute-done.3.refs_5_), channel_id=1, source_target_pairs={{0,8},{4,0},{12,4},{20,12},{28,20},{24,28},{16,24},{8,16},{1,9},{5... | collective-permute-start | bytes 393224 | tf_op jit(solution)/shard_map/ppermute | solution.py:346
  15.0 3.0 %collective-permute-done.5.refs_7_ = bf16[128,512]{1,0:T(8,128)(2,1)S(1)} collective-permute-done((bf16[128,512]{1,0:T(8,128)(2,1)S(1)}, bf16[128,512]{1,0:T(8,128)(2,1)S(1)}, u32[]{:S(2)}, u32[]{:S(2)}) %collective-permute-start.5) | collective-permute-done | bytes 131104 | tf_op jit(solution)/shard_map/ppermute | solution.py:346
  18.1 2.2 %collective-permute-start.7 = (bf16[128,256]{1,0:T(8,128)(2,1)S(1)}, bf16[128,256]{1,0:T(8,128)(2,1)S(1)}, u32[]{:S(2)}, u32[]{:S(2)}) collective-permute-start(bf16[128,256]{1,0:T(8,128)(2,1)S(1)} %slice.29), channel_id=1, source_target_pairs={{0,8},{4,0},{12,4},{20,12},{28,20},{24,28},{16,24},{8,16},{1,9},{5... | collective-permute-start | bytes 196616 | tf_op jit(solution)/shard_map/ppermute | solution.py:346
  26.5 1.8 %collective-permute-start.11 = (bf16[128,512]{1,0:T(8,128)(2,1)S(1)}, bf16[128,512]{1,0:T(8,128)(2,1)S(1)}, u32[]{:S(2)}, u32[]{:S(2)}) collective-permute-start(bf16[128,512]{1,0:T(8,128)(2,1)S(1)} %get-tuple-element.65.refs_1_), channel_id=1, source_target_pairs={{0,8},{4,0},{12,4},{20,12},{28,20},{24,28},{16,24},{8,16},{1,9},{5... | collective-permute-start | bytes 393224 | tf_op jit(solution)/shard_map/ppermute | solution.py:346
  28.6 3.9 %collective-permute-done.11.refs_3_ = bf16[128,512]{1,0:T(8,128)(2,1)S(1)} collective-permute-done((bf16[128,512]{1,0:T(8,128)(2,1)S(1)}, bf16[128,512]{1,0:T(8,128)(2,1)S(1)}, u32[]{:S(2)}, u32[]{:S(2)}) %collective-permute-start.11) | collective-permute-done | bytes 131104 | tf_op jit(solution)/shard_map/ppermute | solution.py:346
  32.4 1.6 %collective-permute-start.13 = (bf16[128,512]{1,0:T(8,128)(2,1)S(1)}, bf16[128,512]{1,0:T(8,128)(2,1)S(1)}, u32[]{:S(2)}, u32[]{:S(2)}) collective-permute-start(bf16[128,512]{1,0:T(8,128)(2,1)S(1)} %collective-permute-done.11.refs_3_), channel_id=1, source_target_pairs={{0,8},{4,0},{12,4},{20,12},{28,20},{24,28},{16,24},{8,16},{1,9},{5... | collective-permute-start | bytes 393224 | tf_op jit(solution)/shard_map/ppermute | solution.py:346
  34.6 1.9 %collective-permute-start.18 = (bf16[256,512]{1,0:T(8,128)(2,1)S(1)}, bf16[256,512]{1,0:T(8,128)(2,1)S(1)}, u32[]{:S(2)}, u32[]{:S(2)}) collective-permute-start(bf16[256,512]{1,0:T(8,128)(2,1)S(1)} %add_convert_fusion.1.refs_0_), channel_id=1, source_target_pairs={{0,2},{1,3},{2,0},{3,1},{4,6},{5,7},{6,4},{7,5},{8,10},{9,11},{10,... | collective-permute-start | bytes 786440 | tf_op jit(solution)/shard_map/ppermute | solution.py:356
  39.6 2.9 %collective-permute-done.15.refs_7_ = bf16[128,512]{1,0:T(8,128)(2,1)S(1)} collective-permute-done((bf16[128,512]{1,0:T(8,128)(2,1)S(1)}, bf16[128,512]{1,0:T(8,128)(2,1)S(1)}, u32[]{:S(2)}, u32[]{:S(2)}) %collective-permute-start.15) | collective-permute-done | bytes 131104 | tf_op jit(solution)/shard_map/ppermute | solution.py:346
  44.6 2.2 %collective-permute-done.17.refs_9_ = bf16[128,256]{1,0:T(8,128)(2,1)S(1)} collective-permute-done((bf16[128,256]{1,0:T(8,128)(2,1)S(1)}, bf16[128,256]{1,0:T(8,128)(2,1)S(1)}, u32[]{:S(2)}, u32[]{:S(2)}) %collective-permute-start.17) | collective-permute-done | bytes 65568 | tf_op jit(solution)/shard_map/ppermute | solution.py:346
  52.4 6.9 %collective-permute-done.20.refs_3_ = bf16[256,512]{1,0:T(8,128)(2,1)S(1)} collective-permute-done((bf16[256,512]{1,0:T(8,128)(2,1)S(1)}, bf16[256,512]{1,0:T(8,128)(2,1)S(1)}, u32[]{:S(2)}, u32[]{:S(2)}) %collective-permute-start.20) | collective-permute-done | bytes 262176 | tf_op jit(solution)/shard_map/ppermute | solution.py:356
  59.3 2.0 %shard_map.97 = (bf16[128,1024]{1,0:T(8,128)(2,1)}, f32[256,1024]{1,0:T(8,128)S(1)}, bf16[256,1024]{1,0:T(8,128)(2,1)S(1)}, bf16[256,512]{1,0:T(8,128)(2,1)S(1)}, bf16[256,512]{1,0:T(8,128)(2,1)S(1)}) custom-call(bf16[256,512]{1,0:T(8,128)(2,1)S(1)} %add_convert_fusion.1.refs_0_, bf16[256,512]{1,0:T(8,128)(2,1)S(1)} %add_convert_fusion.refs_1_, ...), custom_call_target="tpu_custom_call" | custom-call | flops 1342177280 | bytes 5242880 | tf_op jit(solution)/shard_map/pallas_call | solution.py:65
  74.3 1.8 %collective-permute-start.31 = (bf16[32,1024]{1,0:T(8,128)(2,1)S(1)}, bf16[32,1024]{1,0:T(8,128)(2,1)S(1)}, u32[]{:S(2)}, u32[]{:S(2)}) collective-permute-start(bf16[32,1024]{1,0:T(8,128)(2,1)S(1)} %get-tuple-element.94), channel_id=1, source_target_pairs={{0,4},{4,12},{12,20},{20,28},{28,24},{24,16},{16,8},{8,0},{1,5},{5... | collective-permute-start | bytes 196616 | tf_op jit(solution)/shard_map/ppermute | solution.py:346
  76.4 1.7 %collective-permute-start.29 = (bf16[128,512]{1,0:T(8,128)(2,1)S(1)}, bf16[128,512]{1,0:T(8,128)(2,1)S(1)}, u32[]{:S(2)}, u32[]{:S(2)}) collective-permute-start(bf16[128,512]{1,0:T(8,128)(2,1)S(1)} %get-tuple-element.89), channel_id=1, source_target_pairs={{0,4},{4,12},{12,20},{20,28},{28,24},{24,16},{16,8},{8,0},{1,5},{5... | collective-permute-start | bytes 393224 | tf_op jit(solution)/shard_map/ppermute | solution.py:346
  78.7 1.7 %collective-permute-done.32.refs_3_ = bf16[32,1024]{1,0:T(8,128)(2,1)S(1)} collective-permute-done((bf16[32,1024]{1,0:T(8,128)(2,1)S(1)}, bf16[32,1024]{1,0:T(8,128)(2,1)S(1)}, u32[]{:S(2)}, u32[]{:S(2)}) %collective-permute-start.32) | collective-permute-done | bytes 65568 | tf_op jit(solution)/shard_map/ppermute | solution.py:346
  80.4 1.7 %collective-permute-start.36 = (bf16[32,1024]{1,0:T(8,128)(2,1)S(1)}, bf16[32,1024]{1,0:T(8,128)(2,1)S(1)}, u32[]{:S(2)}, u32[]{:S(2)}) collective-permute-start(bf16[32,1024]{1,0:T(8,128)(2,1)S(1)} %get-tuple-element.101), channel_id=1, source_target_pairs={{0,4},{4,12},{12,20},{20,28},{28,24},{24,16},{16,8},{8,0},{1,5},{5... | collective-permute-start | bytes 196616 | tf_op jit(solution)/shard_map/ppermute | solution.py:346
  82.5 2.2 %collective-permute-done.36.refs_5_ = bf16[32,1024]{1,0:T(8,128)(2,1)S(1)} collective-permute-done((bf16[32,1024]{1,0:T(8,128)(2,1)S(1)}, bf16[32,1024]{1,0:T(8,128)(2,1)S(1)}, u32[]{:S(2)}, u32[]{:S(2)}) %collective-permute-start.36) | collective-permute-done | bytes 65568 | tf_op jit(solution)/shard_map/ppermute | solution.py:346
  84.8 2.2 %collective-permute-done.37.refs_6_ = bf16[32,1024]{1,0:T(8,128)(2,1)S(1)} collective-permute-done((bf16[32,1024]{1,0:T(8,128)(2,1)S(1)}, bf16[32,1024]{1,0:T(8,128)(2,1)S(1)}, u32[]{:S(2)}, u32[]{:S(2)}) %collective-permute-start.37) | collective-permute-done | bytes 65568 | tf_op jit(solution)/shard_map/ppermute | solution.py:346
  87.4 1.7 %collective-permute-start.40 = (bf16[32,1024]{1,0:T(8,128)(2,1)S(1)}, bf16[32,1024]{1,0:T(8,128)(2,1)S(1)}, u32[]{:S(2)}, u32[]{:S(2)}) collective-permute-start(bf16[32,1024]{1,0:T(8,128)(2,1)S(1)} %get-tuple-element.105.refs_0_), channel_id=1, source_target_pairs={{0,4},{4,12},{12,20},{20,28},{28,24},{24,16},{16,8},{8,0},{1,5},{5... | collective-permute-start | bytes 196616 | tf_op jit(solution)/shard_map/ppermute | solution.py:346
  89.1 2.2 %collective-permute-done.42.refs_5_.refs_2_ = bf16[32,1024]{1,0:T(8,128)(2,1)S(1)} collective-permute-done((bf16[32,1024]{1,0:T(8,128)(2,1)S(1)}, bf16[32,1024]{1,0:T(8,128)(2,1)S(1)}, u32[]{:S(2)}, u32[]{:S(2)}) %collective-permute-start.42) | collective-permute-done | bytes 65568 | tf_op jit(solution)/shard_map/ppermute | solution.py:346
  92.2 1.9 %collective-permute-start.41 = (bf16[32,1024]{1,0:T(8,128)(2,1)S(1)}, bf16[32,1024]{1,0:T(8,128)(2,1)S(1)}, u32[]{:S(2)}, u32[]{:S(2)}) collective-permute-start(bf16[32,1024]{1,0:T(8,128)(2,1)S(1)} %collective-permute-done.40.refs_4_.refs_1_), channel_id=1, source_target_pairs={{0,4},{4,12},{12,20},{20,28},{28,24},{24,16},{16,8},{8,0},{1,5},{5... | collective-permute-start | bytes 196616 | tf_op jit(solution)/shard_map/ppermute | solution.py:346
  97.0 2.1 %collective-permute-start.55 = (bf16[160,1024]{1,0:T(8,128)(2,1)S(1)}, bf16[160,1024]{1,0:T(8,128)(2,1)S(1)}, u32[]{:S(2)}, u32[]{:S(2)}) collective-permute-start(bf16[160,1024]{1,0:T(8,128)(2,1)S(1)} %shard_map.109.refs_0_), channel_id=1, source_target_pairs={{0,2},{1,3},{2,0},{3,1},{4,6},{5,7},{6,4},{7,5},{8,10},{9,11},{10,... | collective-permute-start | bytes 983048 | tf_op jit(solution)/shard_map/ppermute | solution.py:356
  101.3 1.8 %collective-permute-start.50 = (bf16[32,1024]{1,0:T(8,128)(2,1)S(1)}, bf16[32,1024]{1,0:T(8,128)(2,1)S(1)}, u32[]{:S(2)}, u32[]{:S(2)}) collective-permute-start(bf16[32,1024]{1,0:T(8,128)(2,1)S(1)} %collective-permute-done.41.refs_4_.refs_3_), channel_id=1, source_target_pairs={{0,4},{4,12},{12,20},{20,28},{28,24},{24,16},{16,8},{8,0},{1,5},{5... | collective-permute-start | bytes 196616 | tf_op jit(solution)/shard_map/ppermute | solution.py:346
  108.2 3.4 %collective-permute-done.58.refs_3_ = bf16[32,512]{1,0:T(8,128)(2,1)S(1)} collective-permute-done((bf16[32,512]{1,0:T(8,128)(2,1)S(1)}, bf16[32,512]{1,0:T(8,128)(2,1)S(1)}, u32[]{:S(2)}, u32[]{:S(2)}) %collective-permute-start.58) | collective-permute-done | bytes 32800 | tf_op jit(solution)/shard_map/ppermute | solution.py:346
  113.2 2.3 %collective-permute-done.57.refs_2_ = bf16[32,512]{1,0:T(8,128)(2,1)S(1)} collective-permute-done((bf16[32,512]{1,0:T(8,128)(2,1)S(1)}, bf16[32,512]{1,0:T(8,128)(2,1)S(1)}, u32[]{:S(2)}, u32[]{:S(2)}) %collective-permute-start.57) | collective-permute-done | bytes 32800 | tf_op jit(solution)/shard_map/ppermute | solution.py:346
  117.4 1.8 %collective-permute-start.52 = (bf16[128,512]{1,0:T(8,128)(2,1)S(1)}, bf16[128,512]{1,0:T(8,128)(2,1)S(1)}, u32[]{:S(2)}, u32[]{:S(2)}) collective-permute-start(bf16[128,512]{1,0:T(8,128)(2,1)S(1)} %get-tuple-element.117), channel_id=1, source_target_pairs={{0,4},{4,12},{12,20},{20,28},{28,24},{24,16},{16,8},{8,0},{1,5},{5... | collective-permute-start | bytes 393224 | tf_op jit(solution)/shard_map/ppermute | solution.py:346
  119.7 2.3 %collective-permute-done.45.refs_2_ = bf16[128,512]{1,0:T(8,128)(2,1)S(1)} collective-permute-done((bf16[128,512]{1,0:T(8,128)(2,1)S(1)}, bf16[128,512]{1,0:T(8,128)(2,1)S(1)}, u32[]{:S(2)}, u32[]{:S(2)}) %collective-permute-start.45) | collective-permute-done | bytes 131104 | tf_op jit(solution)/shard_map/ppermute | solution.py:346
  122.9 4.0 %collective-permute-done.53.refs_5_ = bf16[128,512]{1,0:T(8,128)(2,1)S(1)} collective-permute-done((bf16[128,512]{1,0:T(8,128)(2,1)S(1)}, bf16[128,512]{1,0:T(8,128)(2,1)S(1)}, u32[]{:S(2)}, u32[]{:S(2)}) %collective-permute-start.53) | collective-permute-done | bytes 131104 | tf_op jit(solution)/shard_map/ppermute | solution.py:346
  127.8 2.3 %shard_map.111 = f32[1024,1024]{1,0:T(8,128)} custom-call(bf16[160,1024]{1,0:T(8,128)(2,1)S(1)} %shard_map.109.refs_0_, bf16[160,1024]{1,0:T(8,128)(2,1)S(1)} %collective-permute-done.54.refs_1_, bf16[160,1024]{1,0:T(8,128)(2,1)S(1)} %collective-permute-done.55.refs_2_, bf16[160,1024]{1,0:T(8,128)(2,1)S(1)} %collective-permute-done.56.refs_3_, ...), custom_call_target="tpu_custom_call" | custom-call | bytes 6291456 | tf_op jit(solution)/shard_map/pallas_call | solution.py:65
  (132 shorter events, 51.0 us)
Async XLA Ops:
  1.5 6.5 %collective-permute-start.1 = (bf16[128,512]{1,0:T(8,128)(2,1)S(1)}, bf16[128,512]{1,0:T(8,128)(2,1)S(1)}, u32[]{:S(2)}, u32[]{:S(2)}) collective-permute-start(bf16[128,512]{1,0:T(8,128)(2,1)S(1)} %slice.21.refs_1_), channel_id=1, source_target_pairs={{0,8},{4,0},{12,4},{20,12},{28,20},{24,28},{16,24},{8,16},{1,9},{5... | collective-permute-start | bytes 393224 | tf_op jit(solution)/shard_map/ppermute | solution.py:346
  4.6 5.2 %collective-permute-start = (bf16[128,512]{1,0:T(8,128)(2,1)S(1)}, bf16[128,512]{1,0:T(8,128)(2,1)S(1)}, u32[]{:S(2)}, u32[]{:S(2)}) collective-permute-start(bf16[128,512]{1,0:T(8,128)(2,1)S(1)} %slice.21.refs_1_), channel_id=1, source_target_pairs={{0,4},{4,12},{12,20},{20,28},{28,24},{24,16},{16,8},{8,0},{1,5},{5... | collective-permute-start | bytes 393224 | tf_op jit(solution)/shard_map/ppermute | solution.py:346
  10.1 15.6 %collective-permute-start.8 = (bf16[128,1024]{1,0:T(8,128)(2,1)}, bf16[128,1024]{1,0:T(8,128)(2,1)S(1)}, u32[]{:S(2)}, u32[]{:S(2)}) collective-permute-start(bf16[128,1024]{1,0:T(8,128)(2,1)} %refs_5_.1), channel_id=1, source_target_pairs={{0,2},{1,3},{2,0},{3,1},{4,6},{5,7},{6,4},{7,5},{8,10},{9,11},{10,... | collective-permute-start | bytes 786440 | tf_op jit(solution)/shard_map/ppermute | solution.py:356
  14.8 5.4 %collective-permute-start.4 = (bf16[128,512]{1,0:T(8,128)(2,1)S(1)}, bf16[128,512]{1,0:T(8,128)(2,1)S(1)}, u32[]{:S(2)}, u32[]{:S(2)}) collective-permute-start(bf16[128,512]{1,0:T(8,128)(2,1)S(1)} %collective-permute-done.2.refs_4_), channel_id=1, source_target_pairs={{0,4},{4,12},{12,20},{20,28},{28,24},{24,16},{16,8},{8,0},{1,5},{5... | collective-permute-start | bytes 393224 | tf_op jit(solution)/shard_map/ppermute | solution.py:346
  18.1 7.6 %collective-permute-start.7 = (bf16[128,256]{1,0:T(8,128)(2,1)S(1)}, bf16[128,256]{1,0:T(8,128)(2,1)S(1)}, u32[]{:S(2)}, u32[]{:S(2)}) collective-permute-start(bf16[128,256]{1,0:T(8,128)(2,1)S(1)} %slice.29), channel_id=1, source_target_pairs={{0,8},{4,0},{12,4},{20,12},{28,20},{24,28},{16,24},{8,16},{1,9},{5... | collective-permute-start | bytes 196616 | tf_op jit(solution)/shard_map/ppermute | solution.py:346
  20.3 5.4 %collective-permute-start.6 = (bf16[128,256]{1,0:T(8,128)(2,1)S(1)}, bf16[128,256]{1,0:T(8,128)(2,1)S(1)}, u32[]{:S(2)}, u32[]{:S(2)}) collective-permute-start(bf16[128,256]{1,0:T(8,128)(2,1)S(1)} %slice.28), channel_id=1, source_target_pairs={{0,4},{4,12},{12,20},{20,28},{28,24},{24,16},{16,8},{8,0},{1,5},{5... | collective-permute-start | bytes 196616 | tf_op jit(solution)/shard_map/ppermute | solution.py:346
  26.4 8.1 %collective-permute-start.9 = (bf16[256,512]{1,0:T(8,128)(2,1)S(1)}, bf16[256,512]{1,0:T(8,128)(2,1)S(1)}, u32[]{:S(2)}, u32[]{:S(2)}) collective-permute-start(bf16[256,512]{1,0:T(8,128)(2,1)S(1)} %get-tuple-element.64), channel_id=1, source_target_pairs={{0,1},{1,0},{2,3},{3,2},{4,5},{5,4},{6,7},{7,6},{8,9},{9,8},{10,11... | collective-permute-start | bytes 786440 | tf_op jit(solution)/shard_map/ppermute | solution.py:353
  26.5 6.0 %collective-permute-start.11 = (bf16[128,512]{1,0:T(8,128)(2,1)S(1)}, bf16[128,512]{1,0:T(8,128)(2,1)S(1)}, u32[]{:S(2)}, u32[]{:S(2)}) collective-permute-start(bf16[128,512]{1,0:T(8,128)(2,1)S(1)} %get-tuple-element.65.refs_1_), channel_id=1, source_target_pairs={{0,8},{4,0},{12,4},{20,12},{28,20},{24,28},{16,24},{8,16},{1,9},{5... | collective-permute-start | bytes 393224 | tf_op jit(solution)/shard_map/ppermute | solution.py:346
  28.2 5.8 %collective-permute-start.10 = (bf16[128,512]{1,0:T(8,128)(2,1)S(1)}, bf16[128,512]{1,0:T(8,128)(2,1)S(1)}, u32[]{:S(2)}, u32[]{:S(2)}) collective-permute-start(bf16[128,512]{1,0:T(8,128)(2,1)S(1)} %get-tuple-element.65.refs_1_), channel_id=1, source_target_pairs={{0,4},{4,12},{12,20},{20,28},{28,24},{24,16},{16,8},{8,0},{1,5},{5... | collective-permute-start | bytes 393224 | tf_op jit(solution)/shard_map/ppermute | solution.py:346
  32.4 5.1 %collective-permute-start.13 = (bf16[128,512]{1,0:T(8,128)(2,1)S(1)}, bf16[128,512]{1,0:T(8,128)(2,1)S(1)}, u32[]{:S(2)}, u32[]{:S(2)}) collective-permute-start(bf16[128,512]{1,0:T(8,128)(2,1)S(1)} %collective-permute-done.11.refs_3_), channel_id=1, source_target_pairs={{0,8},{4,0},{12,4},{20,12},{28,20},{24,28},{16,24},{8,16},{1,9},{5... | collective-permute-start | bytes 393224 | tf_op jit(solution)/shard_map/ppermute | solution.py:346
  34.6 13.9 %collective-permute-start.18 = (bf16[256,512]{1,0:T(8,128)(2,1)S(1)}, bf16[256,512]{1,0:T(8,128)(2,1)S(1)}, u32[]{:S(2)}, u32[]{:S(2)}) collective-permute-start(bf16[256,512]{1,0:T(8,128)(2,1)S(1)} %add_convert_fusion.1.refs_0_), channel_id=1, source_target_pairs={{0,2},{1,3},{2,0},{3,1},{4,6},{5,7},{6,4},{7,5},{8,10},{9,11},{10,... | collective-permute-start | bytes 786440 | tf_op jit(solution)/shard_map/ppermute | solution.py:356
  50.8 8.4 %collective-permute-start.20 = (bf16[256,512]{1,0:T(8,128)(2,1)S(1)}, bf16[256,512]{1,0:T(8,128)(2,1)S(1)}, u32[]{:S(2)}, u32[]{:S(2)}) collective-permute-start(bf16[256,512]{1,0:T(8,128)(2,1)S(1)} %add_convert_fusion.refs_1_), channel_id=1, source_target_pairs={{0,2},{1,3},{2,0},{3,1},{4,6},{5,7},{6,4},{7,5},{8,10},{9,11},{10,... | collective-permute-start | bytes 786440 | tf_op jit(solution)/shard_map/ppermute | solution.py:356
  61.8 8.5 %collective-permute-start.33 = (bf16[256,512]{1,0:T(8,128)(2,1)S(1)}, bf16[256,512]{1,0:T(8,128)(2,1)S(1)}, u32[]{:S(2)}, u32[]{:S(2)}) collective-permute-start(bf16[256,512]{1,0:T(8,128)(2,1)S(1)} %get-tuple-element.96.refs_1_), channel_id=1, source_target_pairs={{0,1},{1,0},{2,3},{3,2},{4,5},{5,4},{6,7},{7,6},{8,9},{9,8},{10,11... | collective-permute-start | bytes 786440 | tf_op jit(solution)/shard_map/ppermute | solution.py:353
  66.1 6.3 %collective-permute-start.27 = (bf16[128,256]{1,0:T(8,128)(2,1)S(1)}, bf16[128,256]{1,0:T(8,128)(2,1)S(1)}, u32[]{:S(2)}, u32[]{:S(2)}) collective-permute-start(bf16[128,256]{1,0:T(8,128)(2,1)S(1)} %get-tuple-element.87), channel_id=1, source_target_pairs={{0,4},{4,12},{12,20},{20,28},{28,24},{24,16},{16,8},{8,0},{1,5},{5... | collective-permute-start | bytes 196616 | tf_op jit(solution)/shard_map/ppermute | solution.py:346
  66.7 6.5 %collective-permute-start.28 = (bf16[128,256]{1,0:T(8,128)(2,1)S(1)}, bf16[128,256]{1,0:T(8,128)(2,1)S(1)}, u32[]{:S(2)}, u32[]{:S(2)}) collective-permute-start(bf16[128,256]{1,0:T(8,128)(2,1)S(1)} %get-tuple-element.88), channel_id=1, source_target_pairs={{0,8},{4,0},{12,4},{20,12},{28,20},{24,28},{16,24},{8,16},{1,9},{5... | collective-permute-start | bytes 196616 | tf_op jit(solution)/shard_map/ppermute | solution.py:346
  71.1 7.1 %collective-permute-start.34 = (bf16[128,256]{1,0:T(8,128)(2,1)S(1)}, bf16[128,256]{1,0:T(8,128)(2,1)S(1)}, u32[]{:S(2)}, u32[]{:S(2)}) collective-permute-start(bf16[128,256]{1,0:T(8,128)(2,1)S(1)} %get-tuple-element.99), channel_id=1, source_target_pairs={{0,4},{4,12},{12,20},{20,28},{28,24},{24,16},{16,8},{8,0},{1,5},{5... | collective-permute-start | bytes 196616 | tf_op jit(solution)/shard_map/ppermute | solution.py:346
  72.4 6.0 %collective-permute-start.35 = (bf16[128,256]{1,0:T(8,128)(2,1)S(1)}, bf16[128,256]{1,0:T(8,128)(2,1)S(1)}, u32[]{:S(2)}, u32[]{:S(2)}) collective-permute-start(bf16[128,256]{1,0:T(8,128)(2,1)S(1)} %get-tuple-element.100), channel_id=1, source_target_pairs={{0,8},{4,0},{12,4},{20,12},{28,20},{24,28},{16,24},{8,16},{1,9},{5... | collective-permute-start | bytes 196616 | tf_op jit(solution)/shard_map/ppermute | solution.py:346
  76.4 10.6 %collective-permute-start.29 = (bf16[128,512]{1,0:T(8,128)(2,1)S(1)}, bf16[128,512]{1,0:T(8,128)(2,1)S(1)}, u32[]{:S(2)}, u32[]{:S(2)}) collective-permute-start(bf16[128,512]{1,0:T(8,128)(2,1)S(1)} %get-tuple-element.89), channel_id=1, source_target_pairs={{0,4},{4,12},{12,20},{20,28},{28,24},{24,16},{16,8},{8,0},{1,5},{5... | collective-permute-start | bytes 393224 | tf_op jit(solution)/shard_map/ppermute | solution.py:346
  78.2 8.8 %collective-permute-start.30 = (bf16[128,512]{1,0:T(8,128)(2,1)S(1)}, bf16[128,512]{1,0:T(8,128)(2,1)S(1)}, u32[]{:S(2)}, u32[]{:S(2)}) collective-permute-start(bf16[128,512]{1,0:T(8,128)(2,1)S(1)} %get-tuple-element.90), channel_id=1, source_target_pairs={{0,8},{4,0},{12,4},{20,12},{28,20},{24,28},{16,24},{8,16},{1,9},{5... | collective-permute-start | bytes 393224 | tf_op jit(solution)/shard_map/ppermute | solution.py:346
  94.1 7.0 %collective-permute-start.46 = (bf16[128,512]{1,0:T(8,128)(2,1)S(1)}, bf16[128,512]{1,0:T(8,128)(2,1)S(1)}, u32[]{:S(2)}, u32[]{:S(2)}) collective-permute-start(bf16[128,512]{1,0:T(8,128)(2,1)S(1)} %get-tuple-element.113), channel_id=1, source_target_pairs={{0,4},{4,12},{12,20},{20,28},{28,24},{24,16},{16,8},{8,0},{1,5},{5... | collective-permute-start | bytes 393224 | tf_op jit(solution)/shard_map/ppermute | solution.py:346
  95.5 5.8 %collective-permute-start.47 = (bf16[128,512]{1,0:T(8,128)(2,1)S(1)}, bf16[128,512]{1,0:T(8,128)(2,1)S(1)}, u32[]{:S(2)}, u32[]{:S(2)}) collective-permute-start(bf16[128,512]{1,0:T(8,128)(2,1)S(1)} %get-tuple-element.114), channel_id=1, source_target_pairs={{0,8},{4,0},{12,4},{20,12},{28,20},{24,28},{16,24},{8,16},{1,9},{5... | collective-permute-start | bytes 393224 | tf_op jit(solution)/shard_map/ppermute | solution.py:346
  97.0 22.2 %collective-permute-start.55 = (bf16[160,1024]{1,0:T(8,128)(2,1)S(1)}, bf16[160,1024]{1,0:T(8,128)(2,1)S(1)}, u32[]{:S(2)}, u32[]{:S(2)}) collective-permute-start(bf16[160,1024]{1,0:T(8,128)(2,1)S(1)} %shard_map.109.refs_0_), channel_id=1, source_target_pairs={{0,2},{1,3},{2,0},{3,1},{4,6},{5,7},{6,4},{7,5},{8,10},{9,11},{10,... | collective-permute-start | bytes 983048 | tf_op jit(solution)/shard_map/ppermute | solution.py:356
  101.3 5.4 %collective-permute-start.50 = (bf16[32,1024]{1,0:T(8,128)(2,1)S(1)}, bf16[32,1024]{1,0:T(8,128)(2,1)S(1)}, u32[]{:S(2)}, u32[]{:S(2)}) collective-permute-start(bf16[32,1024]{1,0:T(8,128)(2,1)S(1)} %collective-permute-done.41.refs_4_.refs_3_), channel_id=1, source_target_pairs={{0,4},{4,12},{12,20},{20,28},{28,24},{24,16},{16,8},{8,0},{1,5},{5... | collective-permute-start | bytes 196616 | tf_op jit(solution)/shard_map/ppermute | solution.py:346
  104.0 13.0 %collective-permute-start.48 = (bf16[128,512]{1,0:T(8,128)(2,1)S(1)}, bf16[128,512]{1,0:T(8,128)(2,1)S(1)}, u32[]{:S(2)}, u32[]{:S(2)}) collective-permute-start(bf16[128,512]{1,0:T(8,128)(2,1)S(1)} %get-tuple-element.115), channel_id=1, source_target_pairs={{0,4},{4,12},{12,20},{20,28},{28,24},{24,16},{16,8},{8,0},{1,5},{5... | collective-permute-start | bytes 393224 | tf_op jit(solution)/shard_map/ppermute | solution.py:346
  105.2 12.2 %collective-permute-start.49 = (bf16[128,512]{1,0:T(8,128)(2,1)S(1)}, bf16[128,512]{1,0:T(8,128)(2,1)S(1)}, u32[]{:S(2)}, u32[]{:S(2)}) collective-permute-start(bf16[128,512]{1,0:T(8,128)(2,1)S(1)} %get-tuple-element.116), channel_id=1, source_target_pairs={{0,8},{4,0},{12,4},{20,12},{28,20},{24,28},{16,24},{8,16},{1,9},{5... | collective-permute-start | bytes 393224 | tf_op jit(solution)/shard_map/ppermute | solution.py:346
  106.1 5.5 %collective-permute-start.58 = (bf16[32,512]{1,0:T(8,128)(2,1)S(1)}, bf16[32,512]{1,0:T(8,128)(2,1)S(1)}, u32[]{:S(2)}, u32[]{:S(2)}) collective-permute-start(bf16[32,512]{1,0:T(8,128)(2,1)S(1)} %slice.33), channel_id=1, source_target_pairs={{0,8},{4,0},{12,4},{20,12},{28,20},{24,28},{16,24},{8,16},{1,9},{5... | collective-permute-start | bytes 98312 | tf_op jit(solution)/shard_map/ppermute | solution.py:346
  106.7 12.4 %collective-permute-start.44 = (bf16[128,512]{1,0:T(8,128)(2,1)S(1)}, bf16[128,512]{1,0:T(8,128)(2,1)S(1)}, u32[]{:S(2)}, u32[]{:S(2)}) collective-permute-start(bf16[128,512]{1,0:T(8,128)(2,1)S(1)} %get-tuple-element.106), channel_id=1, source_target_pairs={{0,4},{4,12},{12,20},{20,28},{28,24},{24,16},{16,8},{8,0},{1,5},{5... | collective-permute-start | bytes 393224 | tf_op jit(solution)/shard_map/ppermute | solution.py:346
  115.5 6.9 %collective-permute-start.60 = (bf16[96,1024]{1,0:T(8,128)(2,1)S(1)}, bf16[96,1024]{1,0:T(8,128)(2,1)S(1)}, u32[]{:S(2)}, u32[]{:S(2)}) collective-permute-start(bf16[96,1024]{1,0:T(8,128)(2,1)S(1)} %shard_map.110.refs_4_), channel_id=1, source_target_pairs={{0,2},{1,3},{2,0},{3,1},{4,6},{5,7},{6,4},{7,5},{8,10},{9,11},{10,... | collective-permute-start | bytes 589832 | tf_op jit(solution)/shard_map/ppermute | solution.py:356
  119.1 8.7 %collective-permute-start.54 = (bf16[160,1024]{1,0:T(8,128)(2,1)S(1)}, bf16[160,1024]{1,0:T(8,128)(2,1)S(1)}, u32[]{:S(2)}, u32[]{:S(2)}) collective-permute-start(bf16[160,1024]{1,0:T(8,128)(2,1)S(1)} %shard_map.109.refs_0_), channel_id=1, source_target_pairs={{0,1},{1,0},{2,3},{3,2},{4,5},{5,4},{6,7},{7,6},{8,9},{9,8},{10,11... | collective-permute-start | bytes 983048 | tf_op jit(solution)/shard_map/ppermute | solution.py:353
  119.1 8.7 %collective-permute-start.56 = (bf16[160,1024]{1,0:T(8,128)(2,1)S(1)}, bf16[160,1024]{1,0:T(8,128)(2,1)S(1)}, u32[]{:S(2)}, u32[]{:S(2)}) collective-permute-start(bf16[160,1024]{1,0:T(8,128)(2,1)S(1)} %collective-permute-done.55.refs_2_), channel_id=1, source_target_pairs={{0,1},{1,0},{2,3},{3,2},{4,5},{5,4},{6,7},{7,6},{8,9},{9,8},{10,11... | collective-permute-start | bytes 983048 | tf_op jit(solution)/shard_map/ppermute | solution.py:353
  122.4 5.4 %collective-permute-start.59 = (bf16[96,1024]{1,0:T(8,128)(2,1)S(1)}, bf16[96,1024]{1,0:T(8,128)(2,1)S(1)}, u32[]{:S(2)}, u32[]{:S(2)}) collective-permute-start(bf16[96,1024]{1,0:T(8,128)(2,1)S(1)} %shard_map.110.refs_4_), channel_id=1, source_target_pairs={{0,1},{1,0},{2,3},{3,2},{4,5},{5,4},{6,7},{7,6},{8,9},{9,8},{10,11... | collective-permute-start | bytes 589832 | tf_op jit(solution)/shard_map/ppermute | solution.py:353
  122.4 5.4 %collective-permute-start.61 = (bf16[96,1024]{1,0:T(8,128)(2,1)S(1)}, bf16[96,1024]{1,0:T(8,128)(2,1)S(1)}, u32[]{:S(2)}, u32[]{:S(2)}) collective-permute-start(bf16[96,1024]{1,0:T(8,128)(2,1)S(1)} %collective-permute-done.60.refs_6_), channel_id=1, source_target_pairs={{0,1},{1,0},{2,3},{3,2},{4,5},{5,4},{6,7},{7,6},{8,9},{9,8},{10,11... | collective-permute-start | bytes 589832 | tf_op jit(solution)/shard_map/ppermute | solution.py:353
  (36 other events, 208.3 us)

commit v3 on v2

v3 whole, which is shorter than its diff:
```python
import functools

import jax
import jax.numpy as jnp
from jax import lax
from jax.experimental import pallas as pl
from jax.experimental.pallas import tpu as pltpu
from jax.sharding import PartitionSpec as P

STRIPS = 2
HEAVY = 20_000_000_000
VMEM_LIMIT = 48 * 1024 * 1024


def ring_of(count, width):
    height = count // width
    if count % width or width % 2 or height < 2:
        return list(range(count))
    walk = [(0, x) for x in range(width)]
    for turn, x in enumerate(reversed(range(width))):
        down = range(1, height) if turn % 2 == 0 else range(height - 1, 0, -1)
        walk += [(z, x) for z in down]
    return [z * width + x for z, x in walk]


def ring_slots(count):
    return [0] + [away for step in range(1, count // 2) for away in (count - step, step)] + [count // 2]


def pick(index, table):
    value = jnp.int32(table[0])
    for at in range(1, len(table)):
        value = jnp.where(index == at, jnp.int32(table[at]), value)
    return value


def position(spot):
    column = lax.axis_index("col")
    return pick(lax.axis_index("row"), spot), lax.div(column, jnp.int32(2)), lax.rem(column, jnp.int32(2))


def vmem_call(name, kernel, out_shapes, args, scratch=(), hbm=0, hbm_out=False, after=(), aliases=None, flops=0, moved=0):
    vmem = pl.BlockSpec(memory_space=pltpu.VMEM)
    anywhere = pl.BlockSpec(memory_space=pl.ANY)
    far = pl.BlockSpec(memory_space=pltpu.HBM)
    specs = [far] * hbm + [vmem] * (len(args) - hbm) + [anywhere] * len(after)
    count = len(args)

    def inner(*refs):
        kernel(*refs[:count], *refs[count + len(after) :])

    return pl.pallas_call(
        inner,
        out_shape=out_shapes,
        in_specs=specs,
        out_specs=jax.tree.map(lambda _: far if hbm_out else vmem, out_shapes),
        scratch_shapes=list(scratch),
        input_output_aliases=aliases or {},
        name=name,
        compiler_params=pltpu.CompilerParams(vmem_limit_bytes=VMEM_LIMIT),
        cost_estimate=pl.CostEstimate(flops=flops, bytes_accessed=moved, transcendentals=0),
    )(*args, *after)


def place_tiles(spot, groups, vals, tile_rows, tile_cols, tile_count, feats):
    slots, side = vals.shape[2], vals.shape[-1]
    count = len(spot)

    def kernel(row_hbm, col_hbm, live_hbm, vals_hbm, feats_hbm, out_ref, feats_ref, row_ref, col_ref, live_ref, held, sems):
        sources = (row_hbm, col_hbm, live_hbm, vals_hbm.at[0, 0], feats_hbm)
        targets = (row_ref, col_ref, live_ref, held, feats_ref)
        copies = [pltpu.make_async_copy(a, b, sems.at[k]) for k, (a, b) in enumerate(zip(sources, targets))]
        for copy in copies:
            copy.start()
        me, group, core = position(spot)
        out_ref[...] = jnp.zeros_like(out_ref)
        for copy in copies:
            copy.wait()

        def put(slot, carry):
            row = row_ref[0, 0, slot]
            other = lax.rem(row, 2) ^ core
            along = lax.rem(lax.div(row, 2) + groups - group, groups)
            top = pl.multiple_of((other * groups + along) * side, side)
            away = lax.rem(pick(col_ref[0, 0, slot], spot) + count - me, count)
            col = jnp.where(away < count // 2, 2 * away, 2 * (count - away) - 1)
            left = pl.multiple_of(col * side, side)
            out_ref[pl.ds(top, side), pl.ds(left, side)] = held[slot]
            return carry

        lax.fori_loop(0, live_ref[0, 0], put, 0)

    shapes = (
        jax.ShapeDtypeStruct((2 * groups * side, count * side), vals.dtype),
        jax.ShapeDtypeStruct(feats.shape, feats.dtype),
    )
    args = (tile_rows, tile_cols, tile_count, vals, feats)
    scratch = [pltpu.SMEM(a.shape, a.dtype) for a in args[:3]]
    scratch += [pltpu.VMEM((slots, side, side), vals.dtype), pltpu.SemaphoreType.DMA((5,))]
    return vmem_call("place_tiles", kernel, shapes, args, scratch=scratch, hbm=5, moved=4 * vals.size)


def gate(values, after, flops=0):
    def kernel(*refs):
        del refs

    shapes = [jax.ShapeDtypeStruct(v.shape, v.dtype) for v in values]
    return vmem_call("gate", kernel, shapes, values, after=after, flops=flops, aliases={k: k for k in range(len(values))})


def aggregate(adjacency, pieces, ends, part, parts, after):
    rows, depth = adjacency.shape
    height, width = pieces[0].shape
    half, strip = rows // 2, width // parts
    columns = slice(part * strip, (part + 1) * strip)

    def kernel(*refs):
        adj_ref = refs[0]
        piece_refs = refs[1 : 1 + len(pieces)]
        right_ref, left_ref, near_ref, far_ref, held = refs[1 + len(pieces) :]
        for place, piece_ref in enumerate(piece_refs):
            held[place * height : (place + 1) * height] = piece_ref[:, columns]
        held[depth - height :] = jnp.concatenate([right_ref[...], left_ref[...]], axis=1)[:, columns]
        far_ref[...] = jnp.dot(adj_ref[half:], held[...], preferred_element_type=jnp.float32).astype(jnp.bfloat16)
        near_ref[...] = jnp.dot(adj_ref[:half], held[...], preferred_element_type=jnp.float32)

    shapes = (
        jax.ShapeDtypeStruct((half, strip), jnp.float32),
        jax.ShapeDtypeStruct((half, strip), jnp.bfloat16),
    )
    return vmem_call(
        "aggregate",
        kernel,
        shapes,
        (adjacency, *pieces, *ends),
        scratch=[pltpu.VMEM((depth, strip), jnp.bfloat16)],
        after=after,
        flops=2 * rows * depth * strip,
        moved=2 * (rows * depth + depth * strip + rows * strip),
    )


def dense(spot, held, arrived, weight, cotangents):
    chunks = len(held)
    rows, width = held[0].shape
    depth, cols = weight.shape
    groups = len(cotangents)
    side = rows // groups
    part = depth // groups
    quarter = part // 2

    def kernel(*refs):
        refs = list(refs)
        _, group, core = position(spot)
        held_refs = [refs.pop(0) for _ in range(chunks)]
        arrived_refs = [[refs.pop(0) for _ in range(chunks)] for _ in range(groups - 1)]
        weight_ref = refs.pop(0)
        cot_refs = [refs.pop(0) for _ in range(groups)]
        act_ref, near_ref, far_ref = refs[:3]
        back_ref = refs[3]
        agg = refs[-2]
        grad = refs[-1]
        for h in range(chunks):
            for g in range(groups):
                total = held_refs[h][g * side : (g + 1) * side].astype(jnp.float32)
                for s in range(1, groups):
                    at = (g + s) % groups
                    total = total + arrived_refs[s - 1][h][at * side : (at + 1) * side].astype(jnp.float32)
                agg[g * side : (g + 1) * side, h * width : (h + 1) * width] = total.astype(jnp.bfloat16)
        for g in range(groups):
            value = jnp.dot(agg[g * side : (g + 1) * side], weight_ref[...], preferred_element_type=jnp.float32)
            gate = jax.nn.sigmoid(value)
            if g == 0:
                act_ref[...] = (value * gate).astype(jnp.bfloat16)
            slope = gate * (1.0 + value * (1.0 - gate))
            cot = cot_refs[(groups - g) % groups][...].astype(jnp.float32)
            grad[g * side : (g + 1) * side] = (cot * slope).astype(jnp.bfloat16)
        back_ref[...] = lax.dot_general(
            grad[...], weight_ref[...], (((1,), (1,)), ((), ())), preferred_element_type=jnp.float32
        ).astype(jnp.bfloat16)
        first = group * part
        near_at = pl.multiple_of(first + core * quarter, 128)
        far_at = pl.multiple_of(first + (1 - core) * quarter, 128)
        far_ref[...] = lax.dot_general(
            agg[:, pl.ds(far_at, quarter)], grad[...], (((0,), (0,)), ((), ())), preferred_element_type=jnp.float32
        ).astype(jnp.bfloat16)
        near_ref[...] = lax.dot_general(
            agg[:, pl.ds(near_at, quarter)], grad[...], (((0,), (0,)), ((), ())), preferred_element_type=jnp.float32
        )

    shapes = [
        jax.ShapeDtypeStruct((side, cols), jnp.bfloat16),
        jax.ShapeDtypeStruct((quarter, cols), jnp.float32),
        jax.ShapeDtypeStruct((quarter, cols), jnp.bfloat16),
        jax.ShapeDtypeStruct((rows, depth), jnp.bfloat16),
    ]
    outs = vmem_call(
        "dense",
        kernel,
        shapes,
        (*held, *[a for step in arrived for a in step], weight, *cotangents),
        scratch=[pltpu.VMEM((rows, depth), jnp.bfloat16), pltpu.VMEM((rows, cols), jnp.bfloat16)],
        flops=2 * rows * cols * (2 * depth + part),
        moved=2 * (depth * cols + 6 * rows * depth),
    )
    return outs


def back_blocks(adjacency, near, far, count):
    rows, depth = adjacency.shape
    half, width = near.shape
    height = depth // count

    def kernel(adj_ref, near_ref, far_ref, *out_refs):
        held = out_refs[-1]
        held[:half] = near_ref[...]
        held[half:] = far_ref[...]
        for place in reversed(range(count)):
            block = lax.dot_general(
                adj_ref[:, place * height : (place + 1) * height],
                held[...],
                (((0,), (0,)), ((), ())),
                preferred_element_type=jnp.float32,
            ).astype(jnp.bfloat16)
            if place == count - 1:
                out_refs[place][...] = block[:, : width // 2]
                out_refs[place + 1][...] = block[:, width // 2 :]
            else:
                out_refs[place][...] = block

    shapes = [jax.ShapeDtypeStruct((height, width), jnp.bfloat16)] * (count - 1)
    shapes += [jax.ShapeDtypeStruct((height, width // 2), jnp.bfloat16)] * 2
    return vmem_call(
        "back_blocks",
        kernel,
        shapes,
        (adjacency, near, far),
        scratch=[pltpu.VMEM((rows, width), jnp.bfloat16)],
        flops=2 * rows * depth * width,
        moved=2 * (rows * depth + depth * width + rows * width),
    )


def weight_blocks(spot, near, arrived):
    count = len(spot)
    rows, cols = near.shape
    share, middle = rows // count, cols // 2

    def kernel(near_ref, arrived_ref, *refs):
        total = refs[-1]
        me, _, _ = position(spot)
        total[...] = near_ref[...] + arrived_ref[...].astype(jnp.float32)
        for place, away in enumerate(ring_slots(count)):
            at = pl.multiple_of(lax.rem(me + away, count) * share, share)
            block = total[pl.ds(at, share)].astype(jnp.bfloat16)
            if place == count - 1:
                refs[place][...] = block[:, :middle]
                refs[place + 1][...] = block[:, middle:]
            else:
                refs[place][...] = block

    shapes = [jax.ShapeDtypeStruct((share, cols), jnp.bfloat16)] * (count - 1)
    shapes += [jax.ShapeDtypeStruct((share, middle), jnp.bfloat16)] * 2
    scratch = [pltpu.VMEM(near.shape, jnp.float32)]
    return vmem_call("weight_blocks", kernel, shapes, (near, arrived), scratch=scratch, flops=near.size, moved=8 * near.size)


def add_round(pairs, finals, carried=(), after=(), flops=0):
    args = [a for group in pairs + finals for a in group] + list(carried)

    def kernel(*refs):
        ins, outs = list(refs[: len(args)]), list(refs[len(args) :])
        for _ in pairs:
            right, left, first, second = (ins.pop(0) for _ in range(4))
            width, part = right.shape[1], first.shape[1]
            out_right, out_left = outs.pop(0), outs.pop(0)
            out_right[:, :part] = right[:, :part] + first[...]
            out_left[:, width - part :] = left[:, width - part :] + second[...]
            if part < width:
                out_right[:, part:] = right[:, part:]
                out_left[:, : width - part] = left[:, : width - part]
        for _ in finals:
            own, first, second = (ins.pop(0)[...].astype(jnp.float32) for _ in range(3))
            outs.pop(0)[...] = (own + first + second).astype(jnp.bfloat16)
        for _ in carried:
            outs.pop(0)[...] = ins.pop(0)[...]

    shapes = [jax.ShapeDtypeStruct(g[0].shape, jnp.bfloat16) for g in pairs for _ in range(2)]
    shapes += [jax.ShapeDtypeStruct(g[0].shape, jnp.bfloat16) for g in finals]
    shapes += [jax.ShapeDtypeStruct(a.shape, jnp.bfloat16) for a in carried]
    moved = sum(4 * a.size for a in args)
    outs = vmem_call("add_round", kernel, shapes, args, after=after, flops=flops, moved=moved)
    return [tuple(outs[2 * k : 2 * k + 2]) for k in range(len(pairs))], outs[2 * len(pairs) :]


def stack_blocks(blocks, ends, after):
    height, width = (blocks or ends)[0].shape
    if not blocks:
        width *= 2

    def kernel(*refs):
        out_ref = refs[-1]
        for place in range(len(blocks)):
            out_ref[place * height : (place + 1) * height] = refs[place][...]
        for side in range(len(ends)):
            half = width // 2
            out_ref[len(blocks) * height :, side * half : (side + 1) * half] = refs[len(blocks) + side][...]

    total = len(blocks) + len(ends) // 2
    shape = jax.ShapeDtypeStruct((total * height, width), jnp.bfloat16)
    return vmem_call("stack_blocks", kernel, shape, (*blocks, *ends), after=after, moved=4 * total * height * width)


def join_weight(spot, groups, shape, stacks, begun=None):
    count = len(spot)
    quarter = shape[0] // (2 * groups)
    share = quarter // count
    total = sum(len(s[1]) for s in stacks)

    def kernel(*refs):
        stack_refs = refs[0 if begun is None else 1 :]
        out_ref, wide, sems = refs[-3:]
        me, group, core = position(spot)
        copies = []
        for ref, (_, aways, steps, other) in zip(stack_refs, stacks):
            back = lax.rem(group + groups - steps, groups)
            base = (back * 2 + (1 - core if other else core)) * quarter
            for place, away in enumerate(aways):
                slot = len(copies)
                wide[slot] = ref[place * share : (place + 1) * share].astype(jnp.float32)
                at = pl.multiple_of(base + lax.rem(me + away, count) * share, share)
                copies.append(pltpu.make_async_copy(wide.at[slot], out_ref.at[pl.ds(at, share)], sems.at[slot]))
                copies[-1].start()
        for copy in copies:
            copy.wait()

    out = jax.ShapeDtypeStruct(shape, jnp.float32)
    scratch = [pltpu.VMEM((total, share, shape[1]), jnp.float32), pltpu.SemaphoreType.DMA((total,))]
    args = [s[0] for s in stacks]
    moved = 6 * total * share * shape[1]
    flops = HEAVY
    if begun is None:
        return vmem_call("join_weight", kernel, out, args, scratch=scratch, hbm_out=True, flops=flops, moved=moved)
    return vmem_call("join_weight", kernel, out, [begun, *args], scratch=scratch, hbm=1, hbm_out=True, aliases={0: 0}, flops=flops, moved=moved)


def body(width, feats, weight, tile_vals, tile_rows, tile_cols, tile_count, grad_out):
    count = lax.axis_size("row")
    columns = lax.axis_size("col")
    groups = columns // 2
    rounds = count // 2
    ring = ring_of(count, width)
    spot = [0] * count
    for place, row in enumerate(ring):
        spot[row] = place

    to_right = [(ring[k], ring[(k + 1) % count]) for k in range(count)]
    to_left = [(ring[k], ring[(k - 1) % count]) for k in range(count)]
    swap = [(k, k ^ 1) for k in range(columns)]

    def go(label, right, left):
        with jax.named_scope(label):
            return lax.ppermute(right, "row", to_right), lax.ppermute(left, "row", to_left)

    def go_halves(label, right, left):
        middle = right.shape[1] // 2
        return go(label, right[:, :middle], left[:, middle:])

    def swap_core(label, value):
        with jax.named_scope(label):
            return lax.ppermute(value, "col", swap)

    def from_group(label, value, steps):
        with jax.named_scope(label):
            return lax.ppermute(value, "col", [(k, (k + 2 * steps) % columns) for k in range(columns)])

    adjacency, near_feats = place_tiles(spot, groups, tile_vals, tile_rows, tile_cols, tile_count, feats)
    cotangents = [grad_out] + [from_group("cotangent_y", grad_out, s) for s in range(1, groups)]
    pieces = [near_feats]
    moving = (feats, feats)
    for step in range(1, rounds + 1):
        if step == 2:
            moving = gate(moving, [adjacency])
        if step > 1:
            pieces += moving
        send = go if step < rounds else go_halves
        moving = send(f"feature_ring_{step}", *moving)

    held = []
    arrived = [[] for _ in range(groups - 1)]
    for h in range(STRIPS):
        near, far = aggregate(adjacency, pieces, moving, h, STRIPS, cotangents[1:])
        total = (near + swap_core(f"sum_core_{h}", far).astype(jnp.float32)).astype(jnp.bfloat16)
        held.append(total)
        for s in range(1, groups):
            arrived[s - 1].append(from_group(f"sum_y_{h}", total, s))

    activated, near_weight, far_weight, back = dense(spot, held, arrived, weight, cotangents)

    slots = ring_slots(count)
    cuts = (0, 3, count - 3, count - 1, count)
    stacks = []

    def spread_part(part, after=()):
        first, last = cuts[part], cuts[part + 1]
        stack = stack_blocks(pieces[first:last], weight_moving if last == count else (), after)
        found = []
        for s in range(groups):
            value = stack if s == 0 else from_group(f"weight_y_{part}", stack, s)
            found.append((value, slots[first:last], s, False))
            found.append((swap_core(f"weight_last_{part}", value), slots[first:last], s, True))
        stacks.append(found)

    far_weight = swap_core("weight_core", far_weight)
    far_back = swap_core("back_core", back)
    terms = weight_blocks(spot, near_weight, far_weight)
    blocks = back_blocks(adjacency, back, far_back, count)
    pieces = []
    moving = weight_moving = None
    for turn in range(2 * rounds):
        j, odd = divmod(turn, 2)
        pairs, finals, carried, after = [], [], [], []
        if 0 < turn < rounds:
            step = 2 * (rounds - turn)
            pairs.append((terms[step], terms[step - 1], *weight_moving))
        elif turn == rounds:
            finals.append((terms[0], *weight_moving))
        elif turn > rounds:
            carried = weight_moving
            if turn == 2 * rounds - 1:
                after = [found[0] for found in stacks[0]]
        if j > 0 and not odd:
            step = 2 * (rounds - j)
            pairs.append((blocks[step], blocks[step - 1], *moving))
        if turn > 0:
            sums, ends = add_round(pairs, finals, carried, after, HEAVY if odd else 0)
        label = f"weight_ring_{turn}"
        if turn == 0:
            weight_moving = go(label, terms[count - 1], terms[count])
        elif turn < rounds:
            weight_moving = go(label, *sums[0])
        elif turn == rounds:
            pieces.append(ends[0])
            weight_moving = go(label, ends[0], ends[0])
        else:
            pieces += weight_moving
            send = go if turn < 2 * rounds - 1 else go_halves
            weight_moving = send(label, *ends)
            if len(pieces) in cuts:
                spread_part(cuts.index(len(pieces)) - 1)
        label = f"back_ring_{j}"
        if turn == 0:
            moving = go(label, blocks[count - 1], blocks[count])
        elif not odd:
            moving = go(label, *sums[-1])
    _, (grad_feats,) = add_round([], [(blocks[0], *moving)])

    spread_part(3, [*moving, *(found[0] for found in stacks[1])])
    grad_weight = None
    for part in range(4):
        grad_weight = join_weight(spot, groups, weight.shape, stacks[part], grad_weight)
    return (activated, grad_feats, grad_weight)


def solution(mesh):
    spread = {d.coords[0] for d in mesh.devices.flat if hasattr(d, "coords")}
    placed = (
        P(("row", "col"), None),
        P(),
        P("row", "col", None, None, None),
        P("row", "col", None),
        P("row", "col", None),
        P("row", "col"),
        P(("row", "col"), None),
    )
    return jax.shard_map(
        functools.partial(body, max(1, len(spread))),
        mesh=mesh,
        in_specs=placed,
        out_specs=(P(("row", "col"), None), P(("row", "col"), None), P()),
        check_vma=False,
    )
```

time: 130 us -> 111 us (0.85)
  starting transfers between devices: 60.8 us -> 45.7 us
  waiting for transfers between devices: 53.6 us -> 49.2 us
  Pallas kernels: 8.87 us -> 10.9 us
    ppermute x24 -> x16, waiting for transfers between devices: 35.1 us -> 11.3 us  [go(): lax.ppermute(left, 'row', to_left)]
    ppermute x24 -> x16, waiting for transfers between devices: 8.74 us -> 22.9 us  [go(): lax.ppermute(right, 'row', to_right)]
    ppermute x24 -> x16, starting transfers between devices: 25.2 us -> 15 us  [go(): lax.ppermute(left, 'row', to_left)]
    ppermute x5 -> x7, waiting for transfers between devices: 6.89 us -> 13.2 us  [from_group(): lax.ppermute(value, 'col', [(k, (k + 2 * steps) % columns) for k in range...]
    ppermute x24 -> x16, starting transfers between devices: 25.1 us -> 19.3 us  [go(): lax.ppermute(right, 'row', to_right)]
    pallas_call x18 -> x23, Pallas kernels: 8.87 us -> 10.9 us  [vmem_call(): pl.pallas_call(inner, out_shape=out_shapes, in_specs=specs, out_specs=jax...]
    ppermute x9 -> x12, waiting for transfers between devices: 2.94 us -> 1.85 us  [swap_core(): return lax.ppermute(value, 'col', swap)]
    ppermute x5 -> x7, starting transfers between devices: 8.8 us -> 9.55 us  [from_group(): lax.ppermute(value, 'col', [(k, (k + 2 * steps) % columns) for k in range...]
  transfers between devices with their start and end apart: 62 -> 51, of which waited for: 26 -> 27; matrix products, arithmetic and copies ran while one was open for 1% -> 0% of each run, Pallas kernels for 2% -> 6%
where the time goes in v3:
time: 111 us
  waiting for transfers between devices  49.2 us (44%)
  starting transfers between devices  45.7 us (41%)
  Pallas kernels  10.9 us (10%)
  local copies, waits for them, and re-layouts  3.51 us (3%)
  between operations  1.54 us (1%)
    ppermute x16, waiting for transfers between devices, go(): lax.ppermute(right, 'row', to_right)  22.9 us
    ppermute x16, starting transfers between devices, go(): lax.ppermute(right, 'row', to_right)  19.3 us
    ppermute x16, starting transfers between devices, go(): lax.ppermute(left, 'row', to_left)  15 us
    ppermute x7, waiting for transfers between devices, from_group(): lax.ppermute(value, 'col', [(k, (k + 2 * steps) % columns) for k in range...  13.2 us
    ppermute x16, waiting for transfers between devices, go(): lax.ppermute(left, 'row', to_left)  11.3 us
    pallas_call x23, Pallas kernels, vmem_call(): pl.pallas_call(inner, out_shape=out_shapes, in_specs=specs, out_specs=jax...  10.9 us
    ppermute x7, starting transfers between devices, from_group(): lax.ppermute(value, 'col', [(k, (k + 2 * steps) % columns) for k in range...  9.55 us
    unnamed x12, local copies, waits for them, and re-layouts  3.48 us
  transfers between devices with their start and end apart: 51, of which 27 were waited for; matrix products, arithmetic and copies ran while one was open for 0% of the time, Pallas kernels for 6%

profile of v3, /device:TPU:0, one launch (start us, length us, event | category | flops | bytes accessed | tf_op | source)
XLA Modules:
  0.0 111.0 jit_solution(4337889961915036718)
XLA Ops:
  0.6 3.1 %collective-permute-start.1 = (bf16[128,1024]{1,0:T(8,128)(2,1)}, bf16[128,1024]{1,0:T(8,128)(2,1)S(1)}, u32[]{:S(2)}, u32[]{:S(2)}) collective-permute-start(bf16[128,1024]{1,0:T(8,128)(2,1)} %refs_4_.2), channel_id=1, source_target_pairs={{0,8},{4,0},{12,4},{20,12},{28,20},{24,28},{16,24},{8,16},{1,9},{5... | collective-permute-start | bytes 786440 | tf_op jit(solution)/shard_map/feature_ring_1/ppermute | solution.py:363
  8.6 1.6 %collective-permute-done.1.refs_1_ = bf16[128,1024]{1,0:T(8,128)(2,1)S(1)} collective-permute-done((bf16[128,1024]{1,0:T(8,128)(2,1)}, bf16[128,1024]{1,0:T(8,128)(2,1)S(1)}, u32[]{:S(2)}, u32[]{:S(2)}) %collective-permute-start.1) | collective-permute-done | bytes 262176 | tf_op jit(solution)/shard_map/feature_ring_1/ppermute | solution.py:363
  10.1 1.5 %collective-permute-done.refs_0_ = bf16[128,1024]{1,0:T(8,128)(2,1)S(1)} collective-permute-done((bf16[128,1024]{1,0:T(8,128)(2,1)}, bf16[128,1024]{1,0:T(8,128)(2,1)S(1)}, u32[]{:S(2)}, u32[]{:S(2)}) %collective-permute-start) | collective-permute-done | bytes 262176 | tf_op jit(solution)/shard_map/feature_ring_1/ppermute | solution.py:363
  12.0 1.7 %collective-permute-start.3 = (bf16[128,1024]{1,0:T(8,128)(2,1)S(1)}, bf16[128,1024]{1,0:T(8,128)(2,1)S(1)}, u32[]{:S(2)}, u32[]{:S(2)}) collective-permute-start(bf16[128,1024]{1,0:T(8,128)(2,1)S(1)} %get-tuple-element.55.refs_3_), channel_id=1, source_target_pairs={{0,8},{4,0},{12,4},{20,12},{28,20},{24,28},{16,24},{8,16},{1,9},{5... | collective-permute-start | bytes 786440 | tf_op jit(solution)/shard_map/feature_ring_2/ppermute | solution.py:363
  13.7 4.8 %collective-permute-done.2.refs_4_ = bf16[128,1024]{1,0:T(8,128)(2,1)S(1)} collective-permute-done((bf16[128,1024]{1,0:T(8,128)(2,1)S(1)}, bf16[128,1024]{1,0:T(8,128)(2,1)S(1)}, u32[]{:S(2)}, u32[]{:S(2)}) %collective-permute-start.2) | collective-permute-done | bytes 262176 | tf_op jit(solution)/shard_map/feature_ring_2/ppermute | solution.py:363
  20.6 1.5 %collective-permute-start.8 = (bf16[128,1024]{1,0:T(8,128)(2,1)}, bf16[128,1024]{1,0:T(8,128)(2,1)S(1)}, u32[]{:S(2)}, u32[]{:S(2)}) collective-permute-start(bf16[128,1024]{1,0:T(8,128)(2,1)} %refs_5_.1), channel_id=1, source_target_pairs={{0,2},{1,3},{2,0},{3,1},{4,6},{5,7},{6,4},{7,5},{8,10},{9,11},{10,... | collective-permute-start | bytes 786440 | tf_op jit(solution)/shard_map/cotangent_y/ppermute | solution.py:375
  22.1 3.5 %collective-permute-done.4.refs_6_ = bf16[128,1024]{1,0:T(8,128)(2,1)S(1)} collective-permute-done((bf16[128,1024]{1,0:T(8,128)(2,1)S(1)}, bf16[128,1024]{1,0:T(8,128)(2,1)S(1)}, u32[]{:S(2)}, u32[]{:S(2)}) %collective-permute-start.4) | collective-permute-done | bytes 262176 | tf_op jit(solution)/shard_map/feature_ring_3/ppermute | solution.py:363
  26.0 1.9 %collective-permute-start.7 = (bf16[128,512]{1,0:T(8,128)(2,1)S(1)}, bf16[128,512]{1,0:T(8,128)(2,1)S(1)}, u32[]{:S(2)}, u32[]{:S(2)}) collective-permute-start(bf16[128,512]{1,0:T(8,128)(2,1)S(1)} %slice.17), channel_id=1, source_target_pairs={{0,8},{4,0},{12,4},{20,12},{28,20},{24,28},{16,24},{8,16},{1,9},{5... | collective-permute-start | bytes 393224 | tf_op jit(solution)/shard_map/feature_ring_4/ppermute | solution.py:363
  27.9 2.7 %collective-permute-done.6.refs_8_ = bf16[128,512]{1,0:T(8,128)(2,1)S(1)} collective-permute-done((bf16[128,512]{1,0:T(8,128)(2,1)S(1)}, bf16[128,512]{1,0:T(8,128)(2,1)S(1)}, u32[]{:S(2)}, u32[]{:S(2)}) %collective-permute-start.6) | collective-permute-done | bytes 131104 | tf_op jit(solution)/shard_map/feature_ring_4/ppermute | solution.py:363
  33.4 1.7 %collective-permute-start.12 = (bf16[256,512]{1,0:T(8,128)(2,1)S(1)}, bf16[256,512]{1,0:T(8,128)(2,1)S(1)}, u32[]{:S(2)}, u32[]{:S(2)}) collective-permute-start(bf16[256,512]{1,0:T(8,128)(2,1)S(1)} %add_convert_fusion.refs_1_), channel_id=1, source_target_pairs={{0,2},{1,3},{2,0},{3,1},{4,6},{5,7},{6,4},{7,5},{8,10},{9,11},{10,... | collective-permute-start | bytes 786440 | tf_op jit(solution)/shard_map/sum_y_1/ppermute | solution.py:375
  36.1 6.6 %collective-permute-done.12.refs_3_ = bf16[256,512]{1,0:T(8,128)(2,1)S(1)} collective-permute-done((bf16[256,512]{1,0:T(8,128)(2,1)S(1)}, bf16[256,512]{1,0:T(8,128)(2,1)S(1)}, u32[]{:S(2)}, u32[]{:S(2)}) %collective-permute-start.12) | collective-permute-done | bytes 262176 | tf_op jit(solution)/shard_map/sum_y_1/ppermute | solution.py:375
  42.6 4.8 %collective-permute-done.11.refs_2_ = bf16[256,512]{1,0:T(8,128)(2,1)S(1)} collective-permute-done((bf16[256,512]{1,0:T(8,128)(2,1)S(1)}, bf16[256,512]{1,0:T(8,128)(2,1)S(1)}, u32[]{:S(2)}, u32[]{:S(2)}) %collective-permute-start.11) | collective-permute-done | bytes 262176 | tf_op jit(solution)/shard_map/sum_y_0/ppermute | solution.py:375
  47.5 2.0 %dense.1 = (bf16[128,1024]{1,0:T(8,128)(2,1)}, f32[256,1024]{1,0:T(8,128)S(1)}, bf16[256,1024]{1,0:T(8,128)(2,1)S(1)}, bf16[256,1024]{1,0:T(8,128)(2,1)S(1)}) custom-call(bf16[256,512]{1,0:T(8,128)(2,1)S(1)} %add_convert_fusion.1.refs_0_, bf16[256,512]{1,0:T(8,128)(2,1)S(1)} %add_convert_fusion.refs_1_, ...), custom_call_target="tpu_custom_call" | custom-call | flops 1342177280 | bytes 5242880 | tf_op jit(solution)/shard_map/dense/pallas_call | solution.py:52
  51.6 1.7 %collective-permute-start.15 = (bf16[32,512]{1,0:T(8,128)(2,1)S(1)}, bf16[32,512]{1,0:T(8,128)(2,1)S(1)}, u32[]{:S(2)}, u32[]{:S(2)}) collective-permute-start(bf16[32,512]{1,0:T(8,128)(2,1)S(1)} %get-tuple-element.73), channel_id=1, source_target_pairs={{0,4},{4,12},{12,20},{20,28},{28,24},{24,16},{16,8},{8,0},{1,5},{5... | collective-permute-start | bytes 98312 | tf_op jit(solution)/shard_map/weight_ring_0/ppermute | solution.py:363
  55.0 1.7 %collective-permute-start.19 = (bf16[128,512]{1,0:T(8,128)(2,1)S(1)}, bf16[128,512]{1,0:T(8,128)(2,1)S(1)}, u32[]{:S(2)}, u32[]{:S(2)}) collective-permute-start(bf16[128,512]{1,0:T(8,128)(2,1)S(1)} %get-tuple-element.79), channel_id=1, source_target_pairs={{0,4},{4,12},{12,20},{20,28},{28,24},{24,16},{16,8},{8,0},{1,5},{5... | collective-permute-start | bytes 393224 | tf_op jit(solution)/shard_map/back_ring_0/ppermute | solution.py:363
  57.2 1.6 %collective-permute-start.17 = (bf16[32,1024]{1,0:T(8,128)(2,1)S(1)}, bf16[32,1024]{1,0:T(8,128)(2,1)S(1)}, u32[]{:S(2)}, u32[]{:S(2)}) collective-permute-start(bf16[32,1024]{1,0:T(8,128)(2,1)S(1)} %get-tuple-element.75), channel_id=1, source_target_pairs={{0,4},{4,12},{12,20},{20,28},{28,24},{24,16},{16,8},{8,0},{1,5},{5... | collective-permute-start | bytes 196616 | tf_op jit(solution)/shard_map/weight_ring_1/ppermute | solution.py:363
  59.3 2.3 %collective-permute-done.17.refs_2_ = bf16[32,1024]{1,0:T(8,128)(2,1)S(1)} collective-permute-done((bf16[32,1024]{1,0:T(8,128)(2,1)S(1)}, bf16[32,1024]{1,0:T(8,128)(2,1)S(1)}, u32[]{:S(2)}, u32[]{:S(2)}) %collective-permute-start.17) | collective-permute-done | bytes 65568 | tf_op jit(solution)/shard_map/weight_ring_1/ppermute | solution.py:363
  61.6 1.5 %collective-permute-done.18.refs_3_ = bf16[32,1024]{1,0:T(8,128)(2,1)S(1)} collective-permute-done((bf16[32,1024]{1,0:T(8,128)(2,1)S(1)}, bf16[32,1024]{1,0:T(8,128)(2,1)S(1)}, u32[]{:S(2)}, u32[]{:S(2)}) %collective-permute-start.18) | collective-permute-done | bytes 65568 | tf_op jit(solution)/shard_map/weight_ring_1/ppermute | solution.py:363
  63.2 1.6 %collective-permute-start.23 = (bf16[32,1024]{1,0:T(8,128)(2,1)S(1)}, bf16[32,1024]{1,0:T(8,128)(2,1)S(1)}, u32[]{:S(2)}, u32[]{:S(2)}) collective-permute-start(bf16[32,1024]{1,0:T(8,128)(2,1)S(1)} %get-tuple-element.86), channel_id=1, source_target_pairs={{0,4},{4,12},{12,20},{20,28},{28,24},{24,16},{16,8},{8,0},{1,5},{5... | collective-permute-start | bytes 196616 | tf_op jit(solution)/shard_map/weight_ring_2/ppermute | solution.py:363
  65.2 1.6 %collective-permute-start.21 = (bf16[128,1024]{1,0:T(8,128)(2,1)S(1)}, bf16[128,1024]{1,0:T(8,128)(2,1)S(1)}, u32[]{:S(2)}, u32[]{:S(2)}) collective-permute-start(bf16[128,1024]{1,0:T(8,128)(2,1)S(1)} %get-tuple-element.81), channel_id=1, source_target_pairs={{0,4},{4,12},{12,20},{20,28},{28,24},{24,16},{16,8},{8,0},{1,5},{5... | collective-permute-start | bytes 786440 | tf_op jit(solution)/shard_map/back_ring_1/ppermute | solution.py:363
  68.2 1.6 %collective-permute-done.24.refs_3_ = bf16[32,1024]{1,0:T(8,128)(2,1)S(1)} collective-permute-done((bf16[32,1024]{1,0:T(8,128)(2,1)S(1)}, bf16[32,1024]{1,0:T(8,128)(2,1)S(1)}, u32[]{:S(2)}, u32[]{:S(2)}) %collective-permute-start.24) | collective-permute-done | bytes 65568 | tf_op jit(solution)/shard_map/weight_ring_2/ppermute | solution.py:363
  69.8 1.6 %collective-permute-start.25 = (bf16[32,1024]{1,0:T(8,128)(2,1)S(1)}, bf16[32,1024]{1,0:T(8,128)(2,1)S(1)}, u32[]{:S(2)}, u32[]{:S(2)}) collective-permute-start(bf16[32,1024]{1,0:T(8,128)(2,1)S(1)} %get-tuple-element.88), channel_id=1, source_target_pairs={{0,4},{4,12},{12,20},{20,28},{28,24},{24,16},{16,8},{8,0},{1,5},{5... | collective-permute-start | bytes 196616 | tf_op jit(solution)/shard_map/weight_ring_3/ppermute | solution.py:363
  71.9 2.2 %collective-permute-done.25.refs_5_ = bf16[32,1024]{1,0:T(8,128)(2,1)S(1)} collective-permute-done((bf16[32,1024]{1,0:T(8,128)(2,1)S(1)}, bf16[32,1024]{1,0:T(8,128)(2,1)S(1)}, u32[]{:S(2)}, u32[]{:S(2)}) %collective-permute-start.25) | collective-permute-done | bytes 65568 | tf_op jit(solution)/shard_map/weight_ring_3/ppermute | solution.py:363
  74.2 1.9 %collective-permute-done.26.refs_6_ = bf16[32,1024]{1,0:T(8,128)(2,1)S(1)} collective-permute-done((bf16[32,1024]{1,0:T(8,128)(2,1)S(1)}, bf16[32,1024]{1,0:T(8,128)(2,1)S(1)}, u32[]{:S(2)}, u32[]{:S(2)}) %collective-permute-start.26) | collective-permute-done | bytes 65568 | tf_op jit(solution)/shard_map/weight_ring_3/ppermute | solution.py:363
  76.7 1.6 %collective-permute-start.29 = (bf16[32,1024]{1,0:T(8,128)(2,1)S(1)}, bf16[32,1024]{1,0:T(8,128)(2,1)S(1)}, u32[]{:S(2)}, u32[]{:S(2)}) collective-permute-start(bf16[32,1024]{1,0:T(8,128)(2,1)S(1)} %get-tuple-element.92.refs_0_), channel_id=1, source_target_pairs={{0,4},{4,12},{12,20},{20,28},{28,24},{24,16},{16,8},{8,0},{1,5},{5... | collective-permute-start | bytes 196616 | tf_op jit(solution)/shard_map/weight_ring_4/ppermute | solution.py:363
  78.3 1.6 %collective-permute-start.27 = (bf16[128,1024]{1,0:T(8,128)(2,1)S(1)}, bf16[128,1024]{1,0:T(8,128)(2,1)S(1)}, u32[]{:S(2)}, u32[]{:S(2)}) collective-permute-start(bf16[128,1024]{1,0:T(8,128)(2,1)S(1)} %get-tuple-element.90), channel_id=1, source_target_pairs={{0,4},{4,12},{12,20},{20,28},{28,24},{24,16},{16,8},{8,0},{1,5},{5... | collective-permute-start | bytes 786440 | tf_op jit(solution)/shard_map/back_ring_2/ppermute | solution.py:363
  81.3 1.6 %collective-permute-start.36 = (bf16[96,1024]{1,0:T(8,128)(2,1)S(1)}, bf16[96,1024]{1,0:T(8,128)(2,1)S(1)}, u32[]{:S(2)}, u32[]{:S(2)}) collective-permute-start(bf16[96,1024]{1,0:T(8,128)(2,1)S(1)} %stack_blocks.4.refs_0_.refs_2_), channel_id=1, source_target_pairs={{0,2},{1,3},{2,0},{3,1},{4,6},{5,7},{6,4},{7,5},{8,10},{9,11},{10,... | collective-permute-start | bytes 589832 | tf_op jit(solution)/shard_map/weight_y_0/ppermute | solution.py:375
  82.9 1.7 %collective-permute-start.31 = (bf16[32,1024]{1,0:T(8,128)(2,1)S(1)}, bf16[32,1024]{1,0:T(8,128)(2,1)S(1)}, u32[]{:S(2)}, u32[]{:S(2)}) collective-permute-start(bf16[32,1024]{1,0:T(8,128)(2,1)S(1)} %get-tuple-element.93), channel_id=1, source_target_pairs={{0,4},{4,12},{12,20},{20,28},{28,24},{24,16},{16,8},{8,0},{1,5},{5... | collective-permute-start | bytes 196616 | tf_op jit(solution)/shard_map/weight_ring_5/ppermute | solution.py:363
  85.0 2.2 %collective-permute-done.31.refs_4_.refs_0_ = bf16[32,1024]{1,0:T(8,128)(2,1)S(1)} collective-permute-done((bf16[32,1024]{1,0:T(8,128)(2,1)S(1)}, bf16[32,1024]{1,0:T(8,128)(2,1)S(1)}, u32[]{:S(2)}, u32[]{:S(2)}) %collective-permute-start.31) | collective-permute-done | bytes 65568 | tf_op jit(solution)/shard_map/weight_ring_5/ppermute | solution.py:363
  91.7 2.2 %collective-permute-done.41.refs_0_ = bf16[32,1024]{1,0:T(8,128)(2,1)S(1)} collective-permute-done((bf16[32,1024]{1,0:T(8,128)(2,1)S(1)}, bf16[32,1024]{1,0:T(8,128)(2,1)S(1)}, u32[]{:S(2)}, u32[]{:S(2)}) %collective-permute-start.41) | collective-permute-done | bytes 65568 | tf_op jit(solution)/shard_map/weight_ring_6/ppermute | solution.py:363
  97.2 1.6 %collective-permute-start.44 = (bf16[64,1024]{1,0:T(8,128)(2,1)S(1)}, bf16[64,1024]{1,0:T(8,128)(2,1)S(1)}, u32[]{:S(2)}, u32[]{:S(2)}) collective-permute-start(bf16[64,1024]{1,0:T(8,128)(2,1)S(1)} %stack_blocks.6.refs_1_), channel_id=1, source_target_pairs={{0,2},{1,3},{2,0},{3,1},{4,6},{5,7},{6,4},{7,5},{8,10},{9,11},{10,... | collective-permute-start | bytes 393224 | tf_op jit(solution)/shard_map/weight_y_2/ppermute | solution.py:375
  104.3 1.6 %collective-permute-start.49 = (bf16[32,1024]{1,0:T(8,128)(2,1)S(1)}, bf16[32,1024]{1,0:T(8,128)(2,1)S(1)}, u32[]{:S(2)}, u32[]{:S(2)}) collective-permute-start(bf16[32,1024]{1,0:T(8,128)(2,1)S(1)} %stack_blocks.7.refs_1_), channel_id=1, source_target_pairs={{0,2},{1,3},{2,0},{3,1},{4,6},{5,7},{6,4},{7,5},{8,10},{9,11},{10,... | collective-permute-start | bytes 196616 | tf_op jit(solution)/shard_map/weight_y_3/ppermute | solution.py:375
  (111 shorter events, 38.4 us)
Async XLA Ops:
  0.6 9.5 %collective-permute-start.1 = (bf16[128,1024]{1,0:T(8,128)(2,1)}, bf16[128,1024]{1,0:T(8,128)(2,1)S(1)}, u32[]{:S(2)}, u32[]{:S(2)}) collective-permute-start(bf16[128,1024]{1,0:T(8,128)(2,1)} %refs_4_.2), channel_id=1, source_target_pairs={{0,8},{4,0},{12,4},{20,12},{28,20},{24,28},{16,24},{8,16},{1,9},{5... | collective-permute-start | bytes 786440 | tf_op jit(solution)/shard_map/feature_ring_1/ppermute | solution.py:363
  3.7 8.0 %collective-permute-start = (bf16[128,1024]{1,0:T(8,128)(2,1)}, bf16[128,1024]{1,0:T(8,128)(2,1)S(1)}, u32[]{:S(2)}, u32[]{:S(2)}) collective-permute-start(bf16[128,1024]{1,0:T(8,128)(2,1)} %refs_4_.2), channel_id=1, source_target_pairs={{0,4},{4,12},{12,20},{20,28},{28,24},{24,16},{16,8},{8,0},{1,5},{5... | collective-permute-start | bytes 786440 | tf_op jit(solution)/shard_map/feature_ring_1/ppermute | solution.py:363
  11.7 6.9 %collective-permute-start.2 = (bf16[128,1024]{1,0:T(8,128)(2,1)S(1)}, bf16[128,1024]{1,0:T(8,128)(2,1)S(1)}, u32[]{:S(2)}, u32[]{:S(2)}) collective-permute-start(bf16[128,1024]{1,0:T(8,128)(2,1)S(1)} %get-tuple-element.54.refs_2_), channel_id=1, source_target_pairs={{0,4},{4,12},{12,20},{20,28},{28,24},{24,16},{16,8},{8,0},{1,5},{5... | collective-permute-start | bytes 786440 | tf_op jit(solution)/shard_map/feature_ring_2/ppermute | solution.py:363
  12.0 7.2 %collective-permute-start.3 = (bf16[128,1024]{1,0:T(8,128)(2,1)S(1)}, bf16[128,1024]{1,0:T(8,128)(2,1)S(1)}, u32[]{:S(2)}, u32[]{:S(2)}) collective-permute-start(bf16[128,1024]{1,0:T(8,128)(2,1)S(1)} %get-tuple-element.55.refs_3_), channel_id=1, source_target_pairs={{0,8},{4,0},{12,4},{20,12},{28,20},{24,28},{16,24},{8,16},{1,9},{5... | collective-permute-start | bytes 786440 | tf_op jit(solution)/shard_map/feature_ring_2/ppermute | solution.py:363
  18.5 7.1 %collective-permute-start.4 = (bf16[128,1024]{1,0:T(8,128)(2,1)S(1)}, bf16[128,1024]{1,0:T(8,128)(2,1)S(1)}, u32[]{:S(2)}, u32[]{:S(2)}) collective-permute-start(bf16[128,1024]{1,0:T(8,128)(2,1)S(1)} %collective-permute-done.2.refs_4_), channel_id=1, source_target_pairs={{0,4},{4,12},{12,20},{20,28},{28,24},{24,16},{16,8},{8,0},{1,5},{5... | collective-permute-start | bytes 786440 | tf_op jit(solution)/shard_map/feature_ring_3/ppermute | solution.py:363
  19.2 6.8 %collective-permute-start.5 = (bf16[128,1024]{1,0:T(8,128)(2,1)S(1)}, bf16[128,1024]{1,0:T(8,128)(2,1)S(1)}, u32[]{:S(2)}, u32[]{:S(2)}) collective-permute-start(bf16[128,1024]{1,0:T(8,128)(2,1)S(1)} %collective-permute-done.3.refs_5_), channel_id=1, source_target_pairs={{0,8},{4,0},{12,4},{20,12},{28,20},{24,28},{16,24},{8,16},{1,9},{5... | collective-permute-start | bytes 786440 | tf_op jit(solution)/shard_map/feature_ring_3/ppermute | solution.py:363
  20.6 7.4 %collective-permute-start.8 = (bf16[128,1024]{1,0:T(8,128)(2,1)}, bf16[128,1024]{1,0:T(8,128)(2,1)S(1)}, u32[]{:S(2)}, u32[]{:S(2)}) collective-permute-start(bf16[128,1024]{1,0:T(8,128)(2,1)} %refs_5_.1), channel_id=1, source_target_pairs={{0,2},{1,3},{2,0},{3,1},{4,6},{5,7},{6,4},{7,5},{8,10},{9,11},{10,... | collective-permute-start | bytes 786440 | tf_op jit(solution)/shard_map/cotangent_y/ppermute | solution.py:375
  25.6 5.0 %collective-permute-start.6 = (bf16[128,512]{1,0:T(8,128)(2,1)S(1)}, bf16[128,512]{1,0:T(8,128)(2,1)S(1)}, u32[]{:S(2)}, u32[]{:S(2)}) collective-permute-start(bf16[128,512]{1,0:T(8,128)(2,1)S(1)} %slice.16), channel_id=1, source_target_pairs={{0,4},{4,12},{12,20},{20,28},{28,24},{24,16},{16,8},{8,0},{1,5},{5... | collective-permute-start | bytes 393224 | tf_op jit(solution)/shard_map/feature_ring_4/ppermute | solution.py:363
  26.0 5.0 %collective-permute-start.7 = (bf16[128,512]{1,0:T(8,128)(2,1)S(1)}, bf16[128,512]{1,0:T(8,128)(2,1)S(1)}, u32[]{:S(2)}, u32[]{:S(2)}) collective-permute-start(bf16[128,512]{1,0:T(8,128)(2,1)S(1)} %slice.17), channel_id=1, source_target_pairs={{0,8},{4,0},{12,4},{20,12},{28,20},{24,28},{16,24},{8,16},{1,9},{5... | collective-permute-start | bytes 393224 | tf_op jit(solution)/shard_map/feature_ring_4/ppermute | solution.py:363
  33.4 9.2 %collective-permute-start.12 = (bf16[256,512]{1,0:T(8,128)(2,1)S(1)}, bf16[256,512]{1,0:T(8,128)(2,1)S(1)}, u32[]{:S(2)}, u32[]{:S(2)}) collective-permute-start(bf16[256,512]{1,0:T(8,128)(2,1)S(1)} %add_convert_fusion.refs_1_), channel_id=1, source_target_pairs={{0,2},{1,3},{2,0},{3,1},{4,6},{5,7},{6,4},{7,5},{8,10},{9,11},{10,... | collective-permute-start | bytes 786440 | tf_op jit(solution)/shard_map/sum_y_1/ppermute | solution.py:375
  35.2 12.2 %collective-permute-start.11 = (bf16[256,512]{1,0:T(8,128)(2,1)S(1)}, bf16[256,512]{1,0:T(8,128)(2,1)S(1)}, u32[]{:S(2)}, u32[]{:S(2)}) collective-permute-start(bf16[256,512]{1,0:T(8,128)(2,1)S(1)} %add_convert_fusion.1.refs_0_), channel_id=1, source_target_pairs={{0,2},{1,3},{2,0},{3,1},{4,6},{5,7},{6,4},{7,5},{8,10},{9,11},{10,... | collective-permute-start | bytes 786440 | tf_op jit(solution)/shard_map/sum_y_0/ppermute | solution.py:375
  51.6 5.5 %collective-permute-start.15 = (bf16[32,512]{1,0:T(8,128)(2,1)S(1)}, bf16[32,512]{1,0:T(8,128)(2,1)S(1)}, u32[]{:S(2)}, u32[]{:S(2)}) collective-permute-start(bf16[32,512]{1,0:T(8,128)(2,1)S(1)} %get-tuple-element.73), channel_id=1, source_target_pairs={{0,4},{4,12},{12,20},{20,28},{28,24},{24,16},{16,8},{8,0},{1,5},{5... | collective-permute-start | bytes 98312 | tf_op jit(solution)/shard_map/weight_ring_0/ppermute | solution.py:363
  55.0 8.1 %collective-permute-start.19 = (bf16[128,512]{1,0:T(8,128)(2,1)S(1)}, bf16[128,512]{1,0:T(8,128)(2,1)S(1)}, u32[]{:S(2)}, u32[]{:S(2)}) collective-permute-start(bf16[128,512]{1,0:T(8,128)(2,1)S(1)} %get-tuple-element.79), channel_id=1, source_target_pairs={{0,4},{4,12},{12,20},{20,28},{28,24},{24,16},{16,8},{8,0},{1,5},{5... | collective-permute-start | bytes 393224 | tf_op jit(solution)/shard_map/back_ring_0/ppermute | solution.py:363
  56.7 6.4 %collective-permute-start.20 = (bf16[128,512]{1,0:T(8,128)(2,1)S(1)}, bf16[128,512]{1,0:T(8,128)(2,1)S(1)}, u32[]{:S(2)}, u32[]{:S(2)}) collective-permute-start(bf16[128,512]{1,0:T(8,128)(2,1)S(1)} %get-tuple-element.80), channel_id=1, source_target_pairs={{0,8},{4,0},{12,4},{20,12},{28,20},{24,28},{16,24},{8,16},{1,9},{5... | collective-permute-start | bytes 393224 | tf_op jit(solution)/shard_map/back_ring_0/ppermute | solution.py:363
  63.2 5.0 %collective-permute-start.23 = (bf16[32,1024]{1,0:T(8,128)(2,1)S(1)}, bf16[32,1024]{1,0:T(8,128)(2,1)S(1)}, u32[]{:S(2)}, u32[]{:S(2)}) collective-permute-start(bf16[32,1024]{1,0:T(8,128)(2,1)S(1)} %get-tuple-element.86), channel_id=1, source_target_pairs={{0,4},{4,12},{12,20},{20,28},{28,24},{24,16},{16,8},{8,0},{1,5},{5... | collective-permute-start | bytes 196616 | tf_op jit(solution)/shard_map/weight_ring_2/ppermute | solution.py:363
  64.8 5.0 %collective-permute-start.24 = (bf16[32,1024]{1,0:T(8,128)(2,1)S(1)}, bf16[32,1024]{1,0:T(8,128)(2,1)S(1)}, u32[]{:S(2)}, u32[]{:S(2)}) collective-permute-start(bf16[32,1024]{1,0:T(8,128)(2,1)S(1)} %get-tuple-element.87), channel_id=1, source_target_pairs={{0,8},{4,0},{12,4},{20,12},{28,20},{24,28},{16,24},{8,16},{1,9},{5... | collective-permute-start | bytes 196616 | tf_op jit(solution)/shard_map/weight_ring_2/ppermute | solution.py:363
  65.2 10.9 %collective-permute-start.21 = (bf16[128,1024]{1,0:T(8,128)(2,1)S(1)}, bf16[128,1024]{1,0:T(8,128)(2,1)S(1)}, u32[]{:S(2)}, u32[]{:S(2)}) collective-permute-start(bf16[128,1024]{1,0:T(8,128)(2,1)S(1)} %get-tuple-element.81), channel_id=1, source_target_pairs={{0,4},{4,12},{12,20},{20,28},{28,24},{24,16},{16,8},{8,0},{1,5},{5... | collective-permute-start | bytes 786440 | tf_op jit(solution)/shard_map/back_ring_1/ppermute | solution.py:363
  66.8 9.3 %collective-permute-start.22 = (bf16[128,1024]{1,0:T(8,128)(2,1)S(1)}, bf16[128,1024]{1,0:T(8,128)(2,1)S(1)}, u32[]{:S(2)}, u32[]{:S(2)}) collective-permute-start(bf16[128,1024]{1,0:T(8,128)(2,1)S(1)} %get-tuple-element.82), channel_id=1, source_target_pairs={{0,8},{4,0},{12,4},{20,12},{28,20},{24,28},{16,24},{8,16},{1,9},{5... | collective-permute-start | bytes 786440 | tf_op jit(solution)/shard_map/back_ring_1/ppermute | solution.py:363
  76.2 4.8 %collective-permute-start.30 = (bf16[32,1024]{1,0:T(8,128)(2,1)S(1)}, bf16[32,1024]{1,0:T(8,128)(2,1)S(1)}, u32[]{:S(2)}, u32[]{:S(2)}) collective-permute-start(bf16[32,1024]{1,0:T(8,128)(2,1)S(1)} %get-tuple-element.92.refs_0_), channel_id=1, source_target_pairs={{0,8},{4,0},{12,4},{20,12},{28,20},{24,28},{16,24},{8,16},{1,9},{5... | collective-permute-start | bytes 196616 | tf_op jit(solution)/shard_map/weight_ring_4/ppermute | solution.py:363
  78.3 11.3 %collective-permute-start.27 = (bf16[128,1024]{1,0:T(8,128)(2,1)S(1)}, bf16[128,1024]{1,0:T(8,128)(2,1)S(1)}, u32[]{:S(2)}, u32[]{:S(2)}) collective-permute-start(bf16[128,1024]{1,0:T(8,128)(2,1)S(1)} %get-tuple-element.90), channel_id=1, source_target_pairs={{0,4},{4,12},{12,20},{20,28},{28,24},{24,16},{16,8},{8,0},{1,5},{5... | collective-permute-start | bytes 786440 | tf_op jit(solution)/shard_map/back_ring_2/ppermute | solution.py:363
  79.9 9.7 %collective-permute-start.28 = (bf16[128,1024]{1,0:T(8,128)(2,1)S(1)}, bf16[128,1024]{1,0:T(8,128)(2,1)S(1)}, u32[]{:S(2)}, u32[]{:S(2)}) collective-permute-start(bf16[128,1024]{1,0:T(8,128)(2,1)S(1)} %get-tuple-element.91), channel_id=1, source_target_pairs={{0,8},{4,0},{12,4},{20,12},{28,20},{24,28},{16,24},{8,16},{1,9},{5... | collective-permute-start | bytes 786440 | tf_op jit(solution)/shard_map/back_ring_2/ppermute | solution.py:363
  81.3 5.9 %collective-permute-start.36 = (bf16[96,1024]{1,0:T(8,128)(2,1)S(1)}, bf16[96,1024]{1,0:T(8,128)(2,1)S(1)}, u32[]{:S(2)}, u32[]{:S(2)}) collective-permute-start(bf16[96,1024]{1,0:T(8,128)(2,1)S(1)} %stack_blocks.4.refs_0_.refs_2_), channel_id=1, source_target_pairs={{0,2},{1,3},{2,0},{3,1},{4,6},{5,7},{6,4},{7,5},{8,10},{9,11},{10,... | collective-permute-start | bytes 589832 | tf_op jit(solution)/shard_map/weight_y_0/ppermute | solution.py:375
  87.2 9.9 %collective-permute-start.35 = (bf16[96,1024]{1,0:T(8,128)(2,1)S(1)}, bf16[96,1024]{1,0:T(8,128)(2,1)S(1)}, u32[]{:S(2)}, u32[]{:S(2)}) collective-permute-start(bf16[96,1024]{1,0:T(8,128)(2,1)S(1)} %stack_blocks.4.refs_0_.refs_2_), channel_id=1, source_target_pairs={{0,1},{1,0},{2,3},{3,2},{4,5},{5,4},{6,7},{7,6},{8,9},{9,8},{10,11... | collective-permute-start | bytes 589832 | tf_op jit(solution)/shard_map/weight_last_0/ppermute | solution.py:371
  87.2 9.9 %collective-permute-start.37 = (bf16[96,1024]{1,0:T(8,128)(2,1)S(1)}, bf16[96,1024]{1,0:T(8,128)(2,1)S(1)}, u32[]{:S(2)}, u32[]{:S(2)}) collective-permute-start(bf16[96,1024]{1,0:T(8,128)(2,1)S(1)} %collective-permute-done.36.refs_2_.refs_4_), channel_id=1, source_target_pairs={{0,1},{1,0},{2,3},{3,2},{4,5},{5,4},{6,7},{7,6},{8,9},{9,8},{10,11... | collective-permute-start | bytes 589832 | tf_op jit(solution)/shard_map/weight_last_0/ppermute | solution.py:371
  88.8 7.1 %collective-permute-start.39 = (bf16[64,1024]{1,0:T(8,128)(2,1)S(1)}, bf16[64,1024]{1,0:T(8,128)(2,1)S(1)}, u32[]{:S(2)}, u32[]{:S(2)}) collective-permute-start(bf16[64,1024]{1,0:T(8,128)(2,1)S(1)} %stack_blocks.5.refs_1_.refs_4_), channel_id=1, source_target_pairs={{0,2},{1,3},{2,0},{3,1},{4,6},{5,7},{6,4},{7,5},{8,10},{9,11},{10,... | collective-permute-start | bytes 393224 | tf_op jit(solution)/shard_map/weight_y_1/ppermute | solution.py:375
  93.9 4.9 %collective-permute-start.38 = (bf16[64,1024]{1,0:T(8,128)(2,1)S(1)}, bf16[64,1024]{1,0:T(8,128)(2,1)S(1)}, u32[]{:S(2)}, u32[]{:S(2)}) collective-permute-start(bf16[64,1024]{1,0:T(8,128)(2,1)S(1)} %stack_blocks.5.refs_1_.refs_4_), channel_id=1, source_target_pairs={{0,1},{1,0},{2,3},{3,2},{4,5},{5,4},{6,7},{7,6},{8,9},{9,8},{10,11... | collective-permute-start | bytes 393224 | tf_op jit(solution)/shard_map/weight_last_1/ppermute | solution.py:371
  95.1 9.2 %collective-permute-start.33 = (bf16[128,1024]{1,0:T(8,128)(2,1)S(1)}, bf16[128,1024]{1,0:T(8,128)(2,1)S(1)}, u32[]{:S(2)}, u32[]{:S(2)}) collective-permute-start(bf16[128,1024]{1,0:T(8,128)(2,1)S(1)} %get-tuple-element.95), channel_id=1, source_target_pairs={{0,4},{4,12},{12,20},{20,28},{28,24},{24,16},{16,8},{8,0},{1,5},{5... | collective-permute-start | bytes 786440 | tf_op jit(solution)/shard_map/back_ring_3/ppermute | solution.py:363
  95.9 8.4 %collective-permute-start.34 = (bf16[128,1024]{1,0:T(8,128)(2,1)S(1)}, bf16[128,1024]{1,0:T(8,128)(2,1)S(1)}, u32[]{:S(2)}, u32[]{:S(2)}) collective-permute-start(bf16[128,1024]{1,0:T(8,128)(2,1)S(1)} %get-tuple-element.96), channel_id=1, source_target_pairs={{0,8},{4,0},{12,4},{20,12},{28,20},{24,28},{16,24},{8,16},{1,9},{5... | collective-permute-start | bytes 786440 | tf_op jit(solution)/shard_map/back_ring_3/ppermute | solution.py:363
  97.2 5.9 %collective-permute-start.44 = (bf16[64,1024]{1,0:T(8,128)(2,1)S(1)}, bf16[64,1024]{1,0:T(8,128)(2,1)S(1)}, u32[]{:S(2)}, u32[]{:S(2)}) collective-permute-start(bf16[64,1024]{1,0:T(8,128)(2,1)S(1)} %stack_blocks.6.refs_1_), channel_id=1, source_target_pairs={{0,2},{1,3},{2,0},{3,1},{4,6},{5,7},{6,4},{7,5},{8,10},{9,11},{10,... | collective-permute-start | bytes 393224 | tf_op jit(solution)/shard_map/weight_y_2/ppermute | solution.py:375
  98.8 5.5 %collective-permute-start.47 = (bf16[32,512]{1,0:T(8,128)(2,1)S(1)}, bf16[32,512]{1,0:T(8,128)(2,1)S(1)}, u32[]{:S(2)}, u32[]{:S(2)}) collective-permute-start(bf16[32,512]{1,0:T(8,128)(2,1)S(1)} %slice.15), channel_id=1, source_target_pairs={{0,8},{4,0},{12,4},{20,12},{28,20},{24,28},{16,24},{8,16},{1,9},{5... | collective-permute-start | bytes 98312 | tf_op jit(solution)/shard_map/weight_ring_7/ppermute | solution.py:363
  99.6 4.7 %collective-permute-start.46 = (bf16[32,512]{1,0:T(8,128)(2,1)S(1)}, bf16[32,512]{1,0:T(8,128)(2,1)S(1)}, u32[]{:S(2)}, u32[]{:S(2)}) collective-permute-start(bf16[32,512]{1,0:T(8,128)(2,1)S(1)} %slice.14), channel_id=1, source_target_pairs={{0,4},{4,12},{12,20},{20,28},{28,24},{24,16},{16,8},{8,0},{1,5},{5... | collective-permute-start | bytes 98312 | tf_op jit(solution)/shard_map/weight_ring_7/ppermute | solution.py:363
  103.1 5.8 %collective-permute-start.43 = (bf16[64,1024]{1,0:T(8,128)(2,1)S(1)}, bf16[64,1024]{1,0:T(8,128)(2,1)S(1)}, u32[]{:S(2)}, u32[]{:S(2)}) collective-permute-start(bf16[64,1024]{1,0:T(8,128)(2,1)S(1)} %stack_blocks.6.refs_1_), channel_id=1, source_target_pairs={{0,1},{1,0},{2,3},{3,2},{4,5},{5,4},{6,7},{7,6},{8,9},{9,8},{10,11... | collective-permute-start | bytes 393224 | tf_op jit(solution)/shard_map/weight_last_2/ppermute | solution.py:371
  (25 other events, 105.8 us)

commit v4 on v3

v4 whole, which is shorter than its diff:
```python
import functools

import jax
import jax.numpy as jnp
from jax import lax
from jax.experimental import pallas as pl
from jax.experimental.pallas import tpu as pltpu
from jax.sharding import PartitionSpec as P

LONG = 20_000_000_000
VMEM_LIMIT = 48 * 1024 * 1024


def ring_of(count, width):
    height = count // width
    if count % width or width % 2 or height < 2:
        return list(range(count))
    walk = [(0, x) for x in range(width)]
    for turn, x in enumerate(reversed(range(width))):
        down = range(1, height) if turn % 2 == 0 else range(height - 1, 0, -1)
        walk += [(z, x) for z in down]
    return [z * width + x for z, x in walk]


def ring_slots(count):
    return [0] + [away for step in range(1, count // 2) for away in (count - step, step)] + [count // 2]


def pick(index, table):
    value = jnp.int32(table[0])
    for at in range(1, len(table)):
        value = jnp.where(index == at, jnp.int32(table[at]), value)
    return value


def position(spot):
    column = lax.axis_index("col")
    return pick(lax.axis_index("row"), spot), lax.div(column, jnp.int32(2)), lax.rem(column, jnp.int32(2))


def vmem_call(name, kernel, out_shapes, args, scratch=(), hbm=0, hbm_out=False, after=(), aliases=None, flops=0, moved=0):
    vmem = pl.BlockSpec(memory_space=pltpu.VMEM)
    anywhere = pl.BlockSpec(memory_space=pl.ANY)
    far = pl.BlockSpec(memory_space=pltpu.HBM)
    specs = [far] * hbm + [vmem] * (len(args) - hbm) + [anywhere] * len(after)
    count = len(args)

    def inner(*refs):
        kernel(*refs[:count], *refs[count + len(after) :])

    return pl.pallas_call(
        inner,
        out_shape=out_shapes,
        in_specs=specs,
        out_specs=jax.tree.map(lambda _: far if hbm_out else vmem, out_shapes),
        scratch_shapes=list(scratch),
        input_output_aliases=aliases or {},
        name=name,
        compiler_params=pltpu.CompilerParams(vmem_limit_bytes=VMEM_LIMIT),
        cost_estimate=pl.CostEstimate(flops=flops, bytes_accessed=moved, transcendentals=0),
    )(*args, *after)


def place_tiles(spot, groups, vals, tile_rows, tile_cols, tile_count, feats):
    slots, side = vals.shape[2], vals.shape[-1]
    count = len(spot)

    def kernel(row_hbm, col_hbm, live_hbm, vals_hbm, feats_hbm, out_ref, feats_ref, row_ref, col_ref, live_ref, held, sems):
        sources = (row_hbm, col_hbm, live_hbm, vals_hbm.at[0, 0], feats_hbm)
        targets = (row_ref, col_ref, live_ref, held, feats_ref)
        copies = [pltpu.make_async_copy(a, b, sems.at[k]) for k, (a, b) in enumerate(zip(sources, targets))]
        for copy in copies:
            copy.start()
        me, group, core = position(spot)
        out_ref[...] = jnp.zeros_like(out_ref)
        for copy in copies:
            copy.wait()

        def put(slot, carry):
            row = row_ref[0, 0, slot]
            other = lax.rem(row, 2) ^ core
            along = lax.rem(lax.div(row, 2) + groups - group, groups)
            top = pl.multiple_of((other * groups + along) * side, side)
            away = lax.rem(pick(col_ref[0, 0, slot], spot) + count - me, count)
            col = jnp.where(away < count // 2, 2 * away, 2 * (count - away) - 1)
            left = pl.multiple_of(col * side, side)
            out_ref[pl.ds(top, side), pl.ds(left, side)] = held[slot]
            return carry

        lax.fori_loop(0, live_ref[0, 0], put, 0)

    shapes = (
        jax.ShapeDtypeStruct((2 * groups * side, count * side), vals.dtype),
        jax.ShapeDtypeStruct(feats.shape, feats.dtype),
    )
    args = (tile_rows, tile_cols, tile_count, vals, feats)
    scratch = [pltpu.SMEM(a.shape, a.dtype) for a in args[:3]]
    scratch += [pltpu.VMEM((slots, side, side), vals.dtype), pltpu.SemaphoreType.DMA((5,))]
    return vmem_call("place_tiles", kernel, shapes, args, scratch=scratch, hbm=5, moved=4 * vals.size)


def gate(values, after):
    def kernel(*refs):
        del refs

    shapes = [jax.ShapeDtypeStruct(v.shape, v.dtype) for v in values]
    return vmem_call("gate", kernel, shapes, values, after=after, aliases={k: k for k in range(len(values))})


def aggregate(adjacency, pieces):
    rows, depth = adjacency.shape
    height, width = pieces[0].shape
    known = len(pieces) * height

    def kernel(*refs):
        adj_ref, out_ref, held = refs[0], refs[-2], refs[-1]
        for place in range(len(pieces)):
            held[place * height : (place + 1) * height] = refs[1 + place][...]
        out_ref[...] = jnp.dot(adj_ref[:, :known], held[...], preferred_element_type=jnp.float32)

    return vmem_call(
        "aggregate",
        kernel,
        jax.ShapeDtypeStruct((rows, width), jnp.float32),
        (adjacency, *pieces),
        scratch=[pltpu.VMEM((known, width), jnp.bfloat16)],
        flops=2 * rows * known * width,
        moved=2 * (rows * depth + known * width + 2 * rows * width),
    )


def aggregate_last(adjacency, known, ends, side, after):
    rows, depth = adjacency.shape
    height, middle = ends[0].shape
    half = rows // 2

    def kernel(adj_ref, known_ref, right_ref, left_ref, near_own, near_rest, far_own, far_rest):
        last = slice(depth - height, depth)
        for first, count, out_ref in (
            (half + side, half - side, far_rest),
            (half, side, far_own),
            (side, half - side, near_rest),
            (0, side, near_own),
        ):
            here = slice(first, first + count)
            for columns, end_ref in ((slice(0, middle), right_ref), (slice(middle, 2 * middle), left_ref)):
                term = jnp.dot(adj_ref[here, last], end_ref[...], preferred_element_type=jnp.float32)
                out_ref[:, columns] = (known_ref[here, columns] + term).astype(out_ref.dtype)

    shapes = [jax.ShapeDtypeStruct((n, 2 * middle), t) for t in (jnp.float32, jnp.bfloat16) for n in (side, half - side)]
    flops = 4 * rows * height * middle
    return vmem_call(
        "aggregate_last", kernel, shapes, (adjacency, known, *ends), after=after, flops=flops, moved=16 * rows * middle
    )


def slopes(value, cotangent):
    gate = jax.nn.sigmoid(value)
    slope = gate * (1.0 + value * (1.0 - gate))
    return gate, (cotangent.astype(jnp.float32) * slope).astype(jnp.bfloat16)


def times_transposed(left, right):
    return lax.dot_general(left, right, (((1,), (1,)), ((), ())), preferred_element_type=jnp.float32).astype(jnp.bfloat16)


def dense_own(held, arrived, weight, cotangent):
    side, depth = held.shape
    cols = weight.shape[1]

    def kernel(*refs):
        held_ref, weight_ref, cot_ref = refs[0], refs[-6], refs[-5]
        act_ref, agg_ref, grad_ref, back_ref = refs[-4:]
        total = held_ref[...].astype(jnp.float32)
        for ref in refs[1 : 1 + len(arrived)]:
            total = total + ref[...].astype(jnp.float32)
        agg_ref[...] = total.astype(jnp.bfloat16)
        value = jnp.dot(agg_ref[...], weight_ref[...], preferred_element_type=jnp.float32)
        gate, grad = slopes(value, cot_ref[...])
        act_ref[...] = (value * gate).astype(jnp.bfloat16)
        grad_ref[...] = grad
        back_ref[...] = times_transposed(grad, weight_ref[...])

    shapes = [jax.ShapeDtypeStruct((side, n), jnp.bfloat16) for n in (cols, depth, cols, depth)]
    return vmem_call(
        "dense_own",
        kernel,
        shapes,
        (held, *arrived, weight, cotangent),
        flops=4 * side * cols * depth,
        moved=2 * (depth * cols + 6 * side * depth),
    )


def dense_rest(spot, held, arrived, weight, cotangents, agg_own, grad_own):
    rows, depth = held.shape
    side = agg_own.shape[0]
    cols = weight.shape[1]
    part = depth // (rows // side + 1)
    quarter = part // 2

    def kernel(*refs):
        held_ref, weight_ref = refs[0], refs[1 + len(arrived)]
        cot_refs = refs[2 + len(arrived) : 2 + len(arrived) + len(cotangents)]
        agg_ref, grad_ref, near_ref, far_ref, back_ref, agg, grad = refs[-7:]
        _, group, core = position(spot)
        total = held_ref[...].astype(jnp.float32)
        for ref in refs[1 : 1 + len(arrived)]:
            total = total + ref[...].astype(jnp.float32)
        agg[:side] = agg_ref[...]
        grad[:side] = grad_ref[...]
        agg[side:] = total.astype(jnp.bfloat16)
        value = jnp.dot(agg[side:], weight_ref[...], preferred_element_type=jnp.float32)
        for g, cot_ref in enumerate(cot_refs):
            _, piece = slopes(value[g * side : (g + 1) * side], cot_ref[...])
            grad[(g + 1) * side : (g + 2) * side] = piece
        first = group * part
        far_at = pl.multiple_of(first + (1 - core) * quarter, 128)
        near_at = pl.multiple_of(first + core * quarter, 128)
        far_ref[...] = lax.dot_general(
            agg[:, pl.ds(far_at, quarter)], grad[...], (((0,), (0,)), ((), ())), preferred_element_type=jnp.float32
        ).astype(jnp.bfloat16)
        near_ref[...] = lax.dot_general(
            agg[:, pl.ds(near_at, quarter)], grad[...], (((0,), (0,)), ((), ())), preferred_element_type=jnp.float32
        )
        back_ref[...] = times_transposed(grad[side:], weight_ref[...])

    shapes = [
        jax.ShapeDtypeStruct((quarter, cols), jnp.float32),
        jax.ShapeDtypeStruct((quarter, cols), jnp.bfloat16),
        jax.ShapeDtypeStruct((rows, depth), jnp.bfloat16),
    ]
    return vmem_call(
        "dense_rest",
        kernel,
        shapes,
        (held, *arrived, weight, *cotangents, agg_own, grad_own),
        scratch=[pltpu.VMEM((side + rows, depth), jnp.bfloat16), pltpu.VMEM((side + rows, cols), jnp.bfloat16)],
        flops=4 * rows * cols * depth + 2 * (rows + side) * part * cols,
        moved=2 * (depth * cols + 6 * rows * depth),
    )


def back_blocks(adjacency, parts, count):
    rows, depth = adjacency.shape
    width = parts[0].shape[1]
    height = depth // count

    def kernel(adj_ref, *refs):
        out_refs, held = refs[len(parts) :], refs[-1]
        first = 0
        for ref in refs[: len(parts)]:
            held[first : first + ref.shape[0]] = ref[...]
            first += ref.shape[0]
        for place in reversed(range(count)):
            block = lax.dot_general(
                adj_ref[:, place * height : (place + 1) * height],
                held[...],
                (((0,), (0,)), ((), ())),
                preferred_element_type=jnp.float32,
            ).astype(jnp.bfloat16)
            if place == count - 1:
                out_refs[place][...] = block[:, : width // 2]
                out_refs[place + 1][...] = block[:, width // 2 :]
            else:
                out_refs[place][...] = block

    shapes = [jax.ShapeDtypeStruct((height, width), jnp.bfloat16)] * (count - 1)
    shapes += [jax.ShapeDtypeStruct((height, width // 2), jnp.bfloat16)] * 2
    return vmem_call(
        "back_blocks",
        kernel,
        shapes,
        (adjacency, *parts),
        scratch=[pltpu.VMEM((rows, width), jnp.bfloat16)],
        flops=2 * rows * depth * width,
        moved=2 * (rows * depth + depth * width + rows * width),
    )


def weight_blocks(spot, near, arrived):
    count = len(spot)
    rows, cols = near.shape
    share, middle = rows // count, cols // 2

    def kernel(near_ref, arrived_ref, *refs):
        total = refs[-1]
        me, _, _ = position(spot)
        total[...] = near_ref[...] + arrived_ref[...].astype(jnp.float32)
        for place, away in enumerate(ring_slots(count)):
            at = pl.multiple_of(lax.rem(me + away, count) * share, share)
            block = total[pl.ds(at, share)].astype(jnp.bfloat16)
            if place == count - 1:
                refs[place][...] = block[:, :middle]
                refs[place + 1][...] = block[:, middle:]
            else:
                refs[place][...] = block

    shapes = [jax.ShapeDtypeStruct((share, cols), jnp.bfloat16)] * (count - 1)
    shapes += [jax.ShapeDtypeStruct((share, middle), jnp.bfloat16)] * 2
    scratch = [pltpu.VMEM(near.shape, jnp.float32)]
    return vmem_call("weight_blocks", kernel, shapes, (near, arrived), scratch=scratch, flops=near.size, moved=8 * near.size)


def add_round(sums, carried, after, flops):
    args = [a for entry in sums for a in entry[:2]] + list(carried)

    def kernel(*refs):
        ins, outs = list(refs[: len(args)]), list(refs[len(args) :])
        for _, _, side in sums:
            block, arrived, out = ins.pop(0), ins.pop(0), outs.pop(0)
            width, part = block.shape[1], arrived.shape[1]
            first = (width - part) * side
            if part < width:
                out[...] = block[...]
            out[:, first : first + part] = block[:, first : first + part] + arrived[...]
        for _ in carried:
            outs.pop(0)[...] = ins.pop(0)[...]

    shapes = [jax.ShapeDtypeStruct(entry[0].shape, jnp.bfloat16) for entry in sums]
    shapes += [jax.ShapeDtypeStruct(a.shape, jnp.bfloat16) for a in carried]
    moved = sum(4 * a.size for a in args)
    return vmem_call("add_round", kernel, shapes, args, after=after, flops=flops, moved=moved)


def end_sum(own, first, second, flops):
    def kernel(own_ref, first_ref, second_ref, out_ref):
        total = own_ref[...].astype(jnp.float32) + first_ref[...].astype(jnp.float32) + second_ref[...].astype(jnp.float32)
        out_ref[...] = total.astype(jnp.bfloat16)

    shape = jax.ShapeDtypeStruct(own.shape, jnp.bfloat16)
    return vmem_call("end_sum", kernel, shape, (own, first, second), flops=flops, moved=8 * own.size)


def stack_blocks(blocks, ends=(), after=(), flops=0):
    height, width = (blocks or ends)[0].shape
    if not blocks:
        width *= 2

    def kernel(*refs):
        out_ref = refs[-1]
        for place in range(len(blocks)):
            out_ref[place * height : (place + 1) * height] = refs[place][...]
        for side in range(len(ends)):
            half = width // 2
            out_ref[len(blocks) * height :, side * half : (side + 1) * half] = refs[len(blocks) + side][...]

    total = len(blocks) + len(ends) // 2
    shape = jax.ShapeDtypeStruct((total * height, width), jnp.bfloat16)
    return vmem_call("stack_blocks", kernel, shape, (*blocks, *ends), flops=flops, after=after, moved=4 * total * height * width)


def join_weight(spot, groups, shape, stacks, begun, flops):
    count = len(spot)
    quarter = shape[0] // (2 * groups)
    share = quarter // count
    total = sum(len(s[1]) for s in stacks)
    args = [s[0] for s in stacks]
    out = jax.ShapeDtypeStruct(shape, jnp.float32)
    scratch = [pltpu.VMEM((total, share, shape[1]), jnp.float32), pltpu.SemaphoreType.DMA((total,))]

    def kernel(*refs):
        refs = refs[0 if begun is None else 1 :]
        out_ref, wide, sems = refs[-3:]
        me, group, core = position(spot)
        copies = []
        for ref, (_, aways, steps, other) in zip(refs, stacks):
            back = lax.rem(group + groups - steps, groups)
            base = (back * 2 + (1 - core if other else core)) * quarter
            for place, away in enumerate(aways):
                slot = len(copies)
                wide[slot] = ref[place * share : (place + 1) * share].astype(jnp.float32)
                at = pl.multiple_of(base + lax.rem(me + away, count) * share, share)
                copies.append(pltpu.make_async_copy(wide.at[slot], out_ref.at[pl.ds(at, share)], sems.at[slot]))
                copies[-1].start()
        for copy in copies:
            copy.wait()

    hbm = 0 if begun is None else 1
    return vmem_call(
        "join_weight",
        kernel,
        out,
        [begun] * hbm + args,
        scratch=scratch,
        hbm=hbm,
        hbm_out=True,
        aliases={0: 0} if hbm else None,
        flops=flops,
        moved=6 * total * share * shape[1],
    )


def body(width, feats, weight, tile_vals, tile_rows, tile_cols, tile_count, grad_out):
    count = lax.axis_size("row")
    columns = lax.axis_size("col")
    groups = columns // 2
    rounds = count // 2
    ring = ring_of(count, width)
    spot = [0] * count
    for place, row in enumerate(ring):
        spot[row] = place

    to_right = [(ring[k], ring[(k + 1) % count]) for k in range(count)]
    to_left = [(ring[k], ring[(k - 1) % count]) for k in range(count)]
    swap = [(k, k ^ 1) for k in range(columns)]

    def go(label, right, left):
        with jax.named_scope(label):
            return lax.ppermute(right, "row", to_right), lax.ppermute(left, "row", to_left)

    def go_halves(label, right, left):
        middle = right.shape[1] // 2
        return go(label, right[:, :middle], left[:, middle:])

    def swap_core(label, value):
        with jax.named_scope(label):
            return lax.ppermute(value, "col", swap)

    def from_group(label, value, steps):
        with jax.named_scope(label):
            return lax.ppermute(value, "col", [(k, (k + 2 * steps) % columns) for k in range(columns)])

    adjacency, near_feats = place_tiles(spot, groups, tile_vals, tile_rows, tile_cols, tile_count, feats)
    cotangents = [grad_out] + [from_group("cotangent_y", grad_out, s) for s in range(1, groups)]
    pieces = [near_feats]
    moving = (feats, feats)
    for step in range(1, rounds + 1):
        if step == 2:
            moving = gate(moving, [adjacency])
        if step > 1:
            pieces += moving
        send = go if step < rounds else go_halves
        moving = send(f"feature_ring_{step}", *moving)

    known = aggregate(adjacency, pieces)
    near_own, near_rest, far_own, far_rest = aggregate_last(adjacency, known, moving, feats.shape[0], cotangents[1:])
    rest = (near_rest + swap_core("sum_core_rest", far_rest).astype(jnp.float32)).astype(jnp.bfloat16)
    own = (near_own + swap_core("sum_core_own", far_own).astype(jnp.float32)).astype(jnp.bfloat16)
    side = feats.shape[0]
    parts = [own] + [rest[g * side : (g + 1) * side] for g in range(groups - 1)]
    arrived_own = [from_group(f"sum_y_own_{s}", parts[s], s) for s in range(1, groups)]
    arrived_rest = []
    for s in range(1, groups):
        sent = [parts[(s + g) % groups] for g in range(1, groups)]
        arrived_rest.append(from_group(f"sum_y_rest_{s}", jnp.concatenate(sent) if len(sent) > 1 else sent[0], s))
    activated, agg_own, grad_own, back_own = dense_own(own, arrived_own, weight, cotangents[0])
    turned = [cotangents[groups - g] for g in range(1, groups)]
    near_weight, far_weight, back_rest = dense_rest(spot, rest, arrived_rest, weight, turned, agg_own, grad_own)

    far_weight = swap_core("weight_core", far_weight)
    far_back = [swap_core("back_core_own", back_own), swap_core("back_core_rest", back_rest)]
    terms = weight_blocks(spot, near_weight, far_weight)
    blocks = back_blocks(adjacency, [back_own, back_rest, *far_back], count)
    slots = ring_slots(count)
    starts = [(2 * k * (2 * rounds - 1) + rounds - 1) // (2 * rounds - 2) for k in range(rounds)]
    pieces = []
    weight_moving = [terms[count - 1], terms[count]]
    moving = [blocks[count - 1], blocks[count]]
    early = early_from = None
    ordered = []
    for turn in range(2 * rounds):
        flops = 0 if turn % 2 else LONG
        sums = carried = back_sums = ()
        if 0 < turn < rounds:
            sums = [(terms[2 * (rounds - turn) - side], weight_moving[side], side) for side in range(2)]
        elif turn == rounds:
            weight_moving = [end_sum(terms[0], *weight_moving, flops)] * 2
            pieces.append(weight_moving[0])
        elif turn > rounds:
            carried = weight_moving
            pieces += weight_moving
        begins = turn in starts[1:]
        if begins:
            step = 2 * (rounds - starts.index(turn))
            back_sums = [(blocks[step - side], moving[side], side) for side in range(2)]
        if begins and turn < 2 * rounds - 1:
            apart = turn < rounds
            outs = list(add_round([*sums, *(() if apart else back_sums)], carried, ordered, flops))
            weight_moving = outs[-2:] if sums or carried else weight_moving
            moving = list(add_round(back_sums, (), weight_moving, 0)) if apart else outs[:2]
            ordered = moving[:1] if apart else []
        elif turn > 0 and turn != rounds:
            for side in range(2):
                mine = [*sums[side : side + 1], *back_sums[side : side + 1]]
                outs = add_round(mine, carried[side : side + 1], ordered, 0 if side else flops)
                weight_moving[side] = outs[0] if sums else outs[-1]
                if begins:
                    moving[side] = outs[1] if sums else outs[0]
            ordered = []
        send = go_halves if turn == 2 * rounds - 1 else go
        weight_moving = list(send(f"weight_ring_{turn}", *weight_moving))
        if turn in starts:
            moving = list(go(f"back_ring_{starts.index(turn)}", *moving))
        if turn == 2 * rounds - 2:
            early = stack_blocks(pieces)
            early_from = [from_group(f"weight_y_early_{s}", early, s) for s in range(1, groups)]
    grad_feats = end_sum(blocks[0], *moving, 0)

    late = stack_blocks(pieces[count - 3 :], weight_moving, early_from, LONG)
    late_from = [from_group(f"weight_y_late_{s}", late, s) for s in range(1, groups)]

    def placed(values, steps, part):
        return [
            entry
            for s, value in zip(steps, values)
            for entry in ((value, part, s, False), (swap_core("weight_last", value), part, s, True))
        ]

    along = range(1, groups)
    stacks = placed([early, *early_from], range(groups), slots[: count - 3]) + placed([late], [0], slots[count - 3 :])
    grad_weight = join_weight(spot, groups, weight.shape, stacks, None, LONG)
    grad_weight = join_weight(spot, groups, weight.shape, placed(late_from, along, slots[count - 3 :]), grad_weight, 0)
    return (activated, grad_feats, grad_weight)


def solution(mesh):
    spread = {d.coords[0] for d in mesh.devices.flat if hasattr(d, "coords")}
    placed = (
        P(("row", "col"), None),
        P(),
        P("row", "col", None, None, None),
        P("row", "col", None),
        P("row", "col", None),
        P("row", "col"),
        P(("row", "col"), None),
    )
    return jax.shard_map(
        functools.partial(body, max(1, len(spread))),
        mesh=mesh,
        in_specs=placed,
        out_specs=(P(("row", "col"), None), P(("row", "col"), None), P()),
        check_vma=False,
    )
```

time: 111 us -> 105 us (0.946)
  starting transfers between devices: 45.7 us -> 42.3 us
  waiting for transfers between devices: 49.2 us -> 46.2 us
    ppermute x16, starting transfers between devices: 15 us -> 25 us  [go(): lax.ppermute(left, 'row', to_left)]
    ppermute x16, starting transfers between devices: 19.3 us -> 10.7 us  [go(): lax.ppermute(right, 'row', to_right)]
    ppermute x7 -> x5, starting transfers between devices: 9.55 us -> 5.41 us  [from_group(): lax.ppermute(value, 'col', [(k, (k + 2 * steps) % columns) for k in range...]
    ppermute x7 -> x5, waiting for transfers between devices: 13.2 us -> 10.1 us  [from_group(): lax.ppermute(value, 'col', [(k, (k + 2 * steps) % columns) for k in range...]
    ppermute x12 -> x9, waiting for transfers between devices: 1.85 us -> 2.36 us  [swap_core(): return lax.ppermute(value, 'col', swap)]
    pallas_call x23 -> x25, Pallas kernels: 10.9 us -> 11.2 us  [vmem_call(): pl.pallas_call(inner, out_shape=out_shapes, in_specs=specs, out_specs=jax...]
  transfers between devices with their start and end apart: 51 -> 46, of which waited for: 27 -> 24; matrix products, arithmetic and copies ran while one was open for 0% -> 0% of each run, Pallas kernels for 6% -> 8%
where the time goes in v4:
time: 105 us
  waiting for transfers between devices  46.2 us (44%)
  starting transfers between devices  42.3 us (40%)
  Pallas kernels  11.2 us (11%)
  local copies, waits for them, and re-layouts  3.51 us (3%)
  between operations  1.53 us (1%)
    ppermute x16, starting transfers between devices, go(): lax.ppermute(left, 'row', to_left)  25 us
    ppermute x16, waiting for transfers between devices, go(): lax.ppermute(right, 'row', to_right)  22.4 us
    ppermute x16, waiting for transfers between devices, go(): lax.ppermute(left, 'row', to_left)  11.4 us
    pallas_call x25, Pallas kernels, vmem_call(): pl.pallas_call(inner, out_shape=out_shapes, in_specs=specs, out_specs=jax...  11.2 us
    ppermute x16, starting transfers between devices, go(): lax.ppermute(right, 'row', to_right)  10.7 us
    ppermute x5, waiting for transfers between devices, from_group(): lax.ppermute(value, 'col', [(k, (k + 2 * steps) % columns) for k in range...  10.1 us
    ppermute x5, starting transfers between devices, from_group(): lax.ppermute(value, 'col', [(k, (k + 2 * steps) % columns) for k in range...  5.41 us
    unnamed x12, local copies, waits for them, and re-layouts  3.48 us
  transfers between devices with their start and end apart: 46, of which 24 were waited for; matrix products, arithmetic and copies ran while one was open for 0% of the time, Pallas kernels for 8%

profile of v4, /device:TPU:0, one launch (start us, length us, event | category | flops | bytes accessed | tf_op | source)
XLA Modules:
  0.0 104.9 jit_solution(3003283012244348652)
XLA Ops:
  0.6 3.1 %collective-permute-start.1 = (bf16[128,1024]{1,0:T(8,128)(2,1)}, bf16[128,1024]{1,0:T(8,128)(2,1)S(1)}, u32[]{:S(2)}, u32[]{:S(2)}) collective-permute-start(bf16[128,1024]{1,0:T(8,128)(2,1)} %refs_4_.1), channel_id=1, source_target_pairs={{0,8},{4,0},{12,4},{20,12},{28,20},{24,28},{16,24},{8,16},{1,9},{5... | collective-permute-start | bytes 786440 | tf_op jit(solution)/shard_map/feature_ring_1/ppermute | solution.py:410
  8.7 1.4 %collective-permute-done.1.refs_1_ = bf16[128,1024]{1,0:T(8,128)(2,1)S(1)} collective-permute-done((bf16[128,1024]{1,0:T(8,128)(2,1)}, bf16[128,1024]{1,0:T(8,128)(2,1)S(1)}, u32[]{:S(2)}, u32[]{:S(2)}) %collective-permute-start.1) | collective-permute-done | bytes 262176 | tf_op jit(solution)/shard_map/feature_ring_1/ppermute | solution.py:410
  10.1 1.5 %collective-permute-done.refs_0_ = bf16[128,1024]{1,0:T(8,128)(2,1)S(1)} collective-permute-done((bf16[128,1024]{1,0:T(8,128)(2,1)}, bf16[128,1024]{1,0:T(8,128)(2,1)S(1)}, u32[]{:S(2)}, u32[]{:S(2)}) %collective-permute-start) | collective-permute-done | bytes 262176 | tf_op jit(solution)/shard_map/feature_ring_1/ppermute | solution.py:410
  12.0 1.7 %collective-permute-start.3 = (bf16[128,1024]{1,0:T(8,128)(2,1)S(1)}, bf16[128,1024]{1,0:T(8,128)(2,1)S(1)}, u32[]{:S(2)}, u32[]{:S(2)}) collective-permute-start(bf16[128,1024]{1,0:T(8,128)(2,1)S(1)} %get-tuple-element.51.refs_3_), channel_id=1, source_target_pairs={{0,8},{4,0},{12,4},{20,12},{28,20},{24,28},{16,24},{8,16},{1,9},{5... | collective-permute-start | bytes 786440 | tf_op jit(solution)/shard_map/feature_ring_2/ppermute | solution.py:410
  13.7 4.8 %collective-permute-done.2.refs_4_ = bf16[128,1024]{1,0:T(8,128)(2,1)S(1)} collective-permute-done((bf16[128,1024]{1,0:T(8,128)(2,1)S(1)}, bf16[128,1024]{1,0:T(8,128)(2,1)S(1)}, u32[]{:S(2)}, u32[]{:S(2)}) %collective-permute-start.2) | collective-permute-done | bytes 262176 | tf_op jit(solution)/shard_map/feature_ring_2/ppermute | solution.py:410
  20.6 1.5 %collective-permute-start.8 = (bf16[128,1024]{1,0:T(8,128)(2,1)}, bf16[128,1024]{1,0:T(8,128)(2,1)S(1)}, u32[]{:S(2)}, u32[]{:S(2)}) collective-permute-start(bf16[128,1024]{1,0:T(8,128)(2,1)} %refs_3_.3), channel_id=1, source_target_pairs={{0,2},{1,3},{2,0},{3,1},{4,6},{5,7},{6,4},{7,5},{8,10},{9,11},{10,... | collective-permute-start | bytes 786440 | tf_op jit(solution)/shard_map/cotangent_y/ppermute | solution.py:422
  22.1 3.5 %collective-permute-done.4.refs_6_ = bf16[128,1024]{1,0:T(8,128)(2,1)S(1)} collective-permute-done((bf16[128,1024]{1,0:T(8,128)(2,1)S(1)}, bf16[128,1024]{1,0:T(8,128)(2,1)S(1)}, u32[]{:S(2)}, u32[]{:S(2)}) %collective-permute-start.4) | collective-permute-done | bytes 262176 | tf_op jit(solution)/shard_map/feature_ring_3/ppermute | solution.py:410
  26.0 1.9 %collective-permute-start.7 = (bf16[128,512]{1,0:T(8,128)(2,1)S(1)}, bf16[128,512]{1,0:T(8,128)(2,1)S(1)}, u32[]{:S(2)}, u32[]{:S(2)}) collective-permute-start(bf16[128,512]{1,0:T(8,128)(2,1)S(1)} %slice.17), channel_id=1, source_target_pairs={{0,8},{4,0},{12,4},{20,12},{28,20},{24,28},{16,24},{8,16},{1,9},{5... | collective-permute-start | bytes 393224 | tf_op jit(solution)/shard_map/feature_ring_4/ppermute | solution.py:410
  29.2 1.5 %collective-permute-done.6.refs_2_ = bf16[128,512]{1,0:T(8,128)(2,1)S(1)} collective-permute-done((bf16[128,512]{1,0:T(8,128)(2,1)S(1)}, bf16[128,512]{1,0:T(8,128)(2,1)S(1)}, u32[]{:S(2)}, u32[]{:S(2)}) %collective-permute-start.6) | collective-permute-done | bytes 131104 | tf_op jit(solution)/shard_map/feature_ring_4/ppermute | solution.py:410
  33.1 1.7 %collective-permute-start.11 = (bf16[128,1024]{1,0:T(8,128)(2,1)S(1)}, bf16[128,1024]{1,0:T(8,128)(2,1)S(1)}, u32[]{:S(2)}, u32[]{:S(2)}) collective-permute-start(bf16[128,1024]{1,0:T(8,128)(2,1)S(1)} %add_convert_fusion.refs_0_), channel_id=1, source_target_pairs={{0,2},{1,3},{2,0},{3,1},{4,6},{5,7},{6,4},{7,5},{8,10},{9,11},{10,... | collective-permute-start | bytes 786440 | tf_op jit(solution)/shard_map/sum_y_own_1/ppermute | solution.py:422
  35.3 7.0 %collective-permute-done.11.refs_1_ = bf16[128,1024]{1,0:T(8,128)(2,1)S(1)} collective-permute-done((bf16[128,1024]{1,0:T(8,128)(2,1)S(1)}, bf16[128,1024]{1,0:T(8,128)(2,1)S(1)}, u32[]{:S(2)}, u32[]{:S(2)}) %collective-permute-start.11) | collective-permute-done | bytes 262176 | tf_op jit(solution)/shard_map/sum_y_own_1/ppermute | solution.py:422
  42.3 1.7 %dense_own.1 = (bf16[128,1024]{1,0:T(8,128)(2,1)}, bf16[128,1024]{1,0:T(8,128)(2,1)S(1)}, bf16[128,1024]{1,0:T(8,128)(2,1)S(1)}, bf16[128,1024]{1,0:T(8,128)(2,1)S(1)}) custom-call(bf16[128,1024]{1,0:T(8,128)(2,1)S(1)} %add_convert_fusion.1.refs_0_, bf16[128,1024]{1,0:T(8,128)(2,1)S(1)} %collective-permute-done.11.refs_1_, bf16[1024,1024]{1,0:T(8,128)(2,1)S(1)} %copy-done, ...), custom_call_target="tpu_custom_call" | custom-call | flops 536870912 | bytes 3670016 | tf_op jit(solution)/shard_map/dense_own/pallas_call | solution.py:51
  44.0 3.1 %collective-permute-done.12.refs_1_ = bf16[128,1024]{1,0:T(8,128)(2,1)S(1)} collective-permute-done((bf16[128,1024]{1,0:T(8,128)(2,1)S(1)}, bf16[128,1024]{1,0:T(8,128)(2,1)S(1)}, u32[]{:S(2)}, u32[]{:S(2)}) %collective-permute-start.12) | collective-permute-done | bytes 262176 | tf_op jit(solution)/shard_map/sum_y_rest_1/ppermute | solution.py:422
  47.1 1.5 %dense_rest.1 = (f32[256,1024]{1,0:T(8,128)S(1)}, bf16[256,1024]{1,0:T(8,128)(2,1)S(1)}, bf16[128,1024]{1,0:T(8,128)(2,1)S(1)}) custom-call(bf16[128,1024]{1,0:T(8,128)(2,1)S(1)} %add_convert_fusion.refs_0_, bf16[128,1024]{1,0:T(8,128)(2,1)S(1)} %collective-permute-done.12.refs_1_, bf16[1024,1024]{1,0:T(8,128)(2,1)S(1)} %copy-done, ...), custom_call_target="tpu_custom_call" | custom-call | flops 805306368 | bytes 3670016 | tf_op jit(solution)/shard_map/dense_rest/pallas_call | solution.py:51
  50.8 1.9 %collective-permute-start.20 = (bf16[32,512]{1,0:T(8,128)(2,1)S(1)}, bf16[32,512]{1,0:T(8,128)(2,1)S(1)}, u32[]{:S(2)}, u32[]{:S(2)}) collective-permute-start(bf16[32,512]{1,0:T(8,128)(2,1)S(1)} %get-tuple-element.75), channel_id=1, source_target_pairs={{0,8},{4,0},{12,4},{20,12},{28,20},{24,28},{16,24},{8,16},{1,9},{5... | collective-permute-start | bytes 98312 | tf_op jit(solution)/shard_map/weight_ring_0/ppermute | solution.py:410
  52.9 1.9 %collective-permute-done.20.refs_1_ = bf16[32,512]{1,0:T(8,128)(2,1)S(1)} collective-permute-done((bf16[32,512]{1,0:T(8,128)(2,1)S(1)}, bf16[32,512]{1,0:T(8,128)(2,1)S(1)}, u32[]{:S(2)}, u32[]{:S(2)}) %collective-permute-start.20) | collective-permute-done | bytes 32800 | tf_op jit(solution)/shard_map/weight_ring_0/ppermute | solution.py:410
  54.8 1.9 %collective-permute-start.21 = (bf16[32,1024]{1,0:T(8,128)(2,1)S(1)}, bf16[32,1024]{1,0:T(8,128)(2,1)S(1)}, u32[]{:S(2)}, u32[]{:S(2)}) collective-permute-start(bf16[32,1024]{1,0:T(8,128)(2,1)S(1)} %add_round.12), channel_id=1, source_target_pairs={{0,8},{4,0},{12,4},{20,12},{28,20},{24,28},{16,24},{8,16},{1,9},{5... | collective-permute-start | bytes 196616 | tf_op jit(solution)/shard_map/weight_ring_1/ppermute | solution.py:410
  58.2 1.7 %collective-permute-start.15 = (bf16[128,512]{1,0:T(8,128)(2,1)S(1)}, bf16[128,512]{1,0:T(8,128)(2,1)S(1)}, u32[]{:S(2)}, u32[]{:S(2)}) collective-permute-start(bf16[128,512]{1,0:T(8,128)(2,1)S(1)} %get-tuple-element.65), channel_id=1, source_target_pairs={{0,4},{4,12},{12,20},{20,28},{28,24},{24,16},{16,8},{8,0},{1,5},{5... | collective-permute-start | bytes 393224 | tf_op jit(solution)/shard_map/back_ring_0/ppermute | solution.py:410
  62.0 1.6 %collective-permute-start.26 = (bf16[32,1024]{1,0:T(8,128)(2,1)S(1)}, bf16[32,1024]{1,0:T(8,128)(2,1)S(1)}, u32[]{:S(2)}, u32[]{:S(2)}) collective-permute-start(bf16[32,1024]{1,0:T(8,128)(2,1)S(1)} %get-tuple-element.77.refs_5_), channel_id=1, source_target_pairs={{0,8},{4,0},{12,4},{20,12},{28,20},{24,28},{16,24},{8,16},{1,9},{5... | collective-permute-start | bytes 196616 | tf_op jit(solution)/shard_map/weight_ring_2/ppermute | solution.py:410
  66.6 2.0 %collective-permute-start.27 = (bf16[32,1024]{1,0:T(8,128)(2,1)S(1)}, bf16[32,1024]{1,0:T(8,128)(2,1)S(1)}, u32[]{:S(2)}, u32[]{:S(2)}) collective-permute-start(bf16[32,1024]{1,0:T(8,128)(2,1)S(1)} %add_round.16), channel_id=1, source_target_pairs={{0,8},{4,0},{12,4},{20,12},{28,20},{24,28},{16,24},{8,16},{1,9},{5... | collective-permute-start | bytes 196616 | tf_op jit(solution)/shard_map/weight_ring_3/ppermute | solution.py:410
  68.7 2.0 %collective-permute-start.23 = (bf16[128,1024]{1,0:T(8,128)(2,1)S(1)}, bf16[128,1024]{1,0:T(8,128)(2,1)S(1)}, u32[]{:S(2)}, u32[]{:S(2)}) collective-permute-start(bf16[128,1024]{1,0:T(8,128)(2,1)S(1)} %get-tuple-element.80), channel_id=1, source_target_pairs={{0,8},{4,0},{12,4},{20,12},{28,20},{24,28},{16,24},{8,16},{1,9},{5... | collective-permute-start | bytes 786440 | tf_op jit(solution)/shard_map/back_ring_1/ppermute | solution.py:410
  73.8 2.8 %collective-permute-done.29.refs_5_.refs_2_ = bf16[32,1024]{1,0:T(8,128)(2,1)S(1)} collective-permute-done((bf16[32,1024]{1,0:T(8,128)(2,1)S(1)}, bf16[32,1024]{1,0:T(8,128)(2,1)S(1)}, u32[]{:S(2)}, u32[]{:S(2)}) %collective-permute-start.29) | collective-permute-done | bytes 65568 | tf_op jit(solution)/shard_map/weight_ring_4/ppermute | solution.py:410
  78.5 1.6 %collective-permute-start.35 = (bf16[32,1024]{1,0:T(8,128)(2,1)S(1)}, bf16[32,1024]{1,0:T(8,128)(2,1)S(1)}, u32[]{:S(2)}, u32[]{:S(2)}) collective-permute-start(bf16[32,1024]{1,0:T(8,128)(2,1)S(1)} %get-tuple-element.89), channel_id=1, source_target_pairs={{0,8},{4,0},{12,4},{20,12},{28,20},{24,28},{16,24},{8,16},{1,9},{5... | collective-permute-start | bytes 196616 | tf_op jit(solution)/shard_map/weight_ring_5/ppermute | solution.py:410
  80.5 1.6 %collective-permute-start.34 = (bf16[128,1024]{1,0:T(8,128)(2,1)S(1)}, bf16[128,1024]{1,0:T(8,128)(2,1)S(1)}, u32[]{:S(2)}, u32[]{:S(2)}) collective-permute-start(bf16[128,1024]{1,0:T(8,128)(2,1)S(1)} %get-tuple-element.88), channel_id=1, source_target_pairs={{0,8},{4,0},{12,4},{20,12},{28,20},{24,28},{16,24},{8,16},{1,9},{5... | collective-permute-start | bytes 786440 | tf_op jit(solution)/shard_map/back_ring_2/ppermute | solution.py:410
  84.4 1.6 %collective-permute-start.32 = (bf16[32,1024]{1,0:T(8,128)(2,1)S(1)}, bf16[32,1024]{1,0:T(8,128)(2,1)S(1)}, u32[]{:S(2)}, u32[]{:S(2)}) collective-permute-start(bf16[32,1024]{1,0:T(8,128)(2,1)S(1)} %add_round.18), channel_id=1, source_target_pairs={{0,4},{4,12},{12,20},{20,28},{28,24},{24,16},{16,8},{8,0},{1,5},{5... | collective-permute-start | bytes 196616 | tf_op jit(solution)/shard_map/weight_ring_6/ppermute | solution.py:410
  86.4 2.2 %collective-permute-done.32.refs_2_.refs_0_ = bf16[32,1024]{1,0:T(8,128)(2,1)S(1)} collective-permute-done((bf16[32,1024]{1,0:T(8,128)(2,1)S(1)}, bf16[32,1024]{1,0:T(8,128)(2,1)S(1)}, u32[]{:S(2)}, u32[]{:S(2)}) %collective-permute-start.32) | collective-permute-done | bytes 65568 | tf_op jit(solution)/shard_map/weight_ring_6/ppermute | solution.py:410
  88.7 1.7 %collective-permute-start.41 = (bf16[32,512]{1,0:T(8,128)(2,1)S(1)}, bf16[32,512]{1,0:T(8,128)(2,1)S(1)}, u32[]{:S(2)}, u32[]{:S(2)}) collective-permute-start(bf16[32,512]{1,0:T(8,128)(2,1)S(1)} %slice.14), channel_id=1, source_target_pairs={{0,4},{4,12},{12,20},{20,28},{28,24},{24,16},{16,8},{8,0},{1,5},{5... | collective-permute-start | bytes 98312 | tf_op jit(solution)/shard_map/weight_ring_7/ppermute | solution.py:410
  90.9 1.6 %collective-permute-start.33 = (bf16[128,1024]{1,0:T(8,128)(2,1)S(1)}, bf16[128,1024]{1,0:T(8,128)(2,1)S(1)}, u32[]{:S(2)}, u32[]{:S(2)}) collective-permute-start(bf16[128,1024]{1,0:T(8,128)(2,1)S(1)} %get-tuple-element.86), channel_id=1, source_target_pairs={{0,4},{4,12},{12,20},{20,28},{28,24},{24,16},{16,8},{8,0},{1,5},{5... | collective-permute-start | bytes 786440 | tf_op jit(solution)/shard_map/back_ring_3/ppermute | solution.py:410
  92.7 1.6 %collective-permute-start.37 = (bf16[128,1024]{1,0:T(8,128)(2,1)S(1)}, bf16[128,1024]{1,0:T(8,128)(2,1)S(1)}, u32[]{:S(2)}, u32[]{:S(2)}) collective-permute-start(bf16[128,1024]{1,0:T(8,128)(2,1)S(1)} %get-tuple-element.90), channel_id=1, source_target_pairs={{0,8},{4,0},{12,4},{20,12},{28,20},{24,28},{16,24},{8,16},{1,9},{5... | collective-permute-start | bytes 786440 | tf_op jit(solution)/shard_map/back_ring_3/ppermute | solution.py:410
  95.1 4.5 %collective-permute-done.33.refs_1_ = bf16[128,1024]{1,0:T(8,128)(2,1)S(1)} collective-permute-done((bf16[128,1024]{1,0:T(8,128)(2,1)S(1)}, bf16[128,1024]{1,0:T(8,128)(2,1)S(1)}, u32[]{:S(2)}, u32[]{:S(2)}) %collective-permute-start.33) | collective-permute-done | bytes 262176 | tf_op jit(solution)/shard_map/back_ring_3/ppermute | solution.py:410
  99.6 1.5 %collective-permute-done.37.refs_2_ = bf16[128,1024]{1,0:T(8,128)(2,1)S(1)} collective-permute-done((bf16[128,1024]{1,0:T(8,128)(2,1)S(1)}, bf16[128,1024]{1,0:T(8,128)(2,1)S(1)}, u32[]{:S(2)}, u32[]{:S(2)}) %collective-permute-start.37) | collective-permute-done | bytes 262176 | tf_op jit(solution)/shard_map/back_ring_3/ppermute | solution.py:410
  101.9 2.0 %join_weight.2.refs_0_ = f32[1024,1024]{1,0:T(8,128)} custom-call(bf16[160,1024]{1,0:T(8,128)(2,1)S(1)} %stack_blocks.2.refs_0_, bf16[160,1024]{1,0:T(8,128)(2,1)S(1)} %collective-permute-done.38.refs_1_, bf16[160,1024]{1,0:T(8,128)(2,1)S(1)} %collective-permute-done.39.refs_4_.refs_2_, bf16[160,1024]{1,0:T(8,128)(2,1)S(1)} %collective-permute-done.40.refs_3_, ...), custom_call_target="tpu_custom_call" | custom-call | flops 20000000000 | bytes 5111808 | tf_op jit(solution)/shard_map/join_weight/pallas_call | solution.py:51
  (103 shorter events, 31.6 us)
Async XLA Ops:
  0.6 9.5 %collective-permute-start.1 = (bf16[128,1024]{1,0:T(8,128)(2,1)}, bf16[128,1024]{1,0:T(8,128)(2,1)S(1)}, u32[]{:S(2)}, u32[]{:S(2)}) collective-permute-start(bf16[128,1024]{1,0:T(8,128)(2,1)} %refs_4_.1), channel_id=1, source_target_pairs={{0,8},{4,0},{12,4},{20,12},{28,20},{24,28},{16,24},{8,16},{1,9},{5... | collective-permute-start | bytes 786440 | tf_op jit(solution)/shard_map/feature_ring_1/ppermute | solution.py:410
  3.7 8.0 %collective-permute-start = (bf16[128,1024]{1,0:T(8,128)(2,1)}, bf16[128,1024]{1,0:T(8,128)(2,1)S(1)}, u32[]{:S(2)}, u32[]{:S(2)}) collective-permute-start(bf16[128,1024]{1,0:T(8,128)(2,1)} %refs_4_.1), channel_id=1, source_target_pairs={{0,4},{4,12},{12,20},{20,28},{28,24},{24,16},{16,8},{8,0},{1,5},{5... | collective-permute-start | bytes 786440 | tf_op jit(solution)/shard_map/feature_ring_1/ppermute | solution.py:410
  11.7 6.9 %collective-permute-start.2 = (bf16[128,1024]{1,0:T(8,128)(2,1)S(1)}, bf16[128,1024]{1,0:T(8,128)(2,1)S(1)}, u32[]{:S(2)}, u32[]{:S(2)}) collective-permute-start(bf16[128,1024]{1,0:T(8,128)(2,1)S(1)} %get-tuple-element.50.refs_2_), channel_id=1, source_target_pairs={{0,4},{4,12},{12,20},{20,28},{28,24},{24,16},{16,8},{8,0},{1,5},{5... | collective-permute-start | bytes 786440 | tf_op jit(solution)/shard_map/feature_ring_2/ppermute | solution.py:410
  12.0 7.2 %collective-permute-start.3 = (bf16[128,1024]{1,0:T(8,128)(2,1)S(1)}, bf16[128,1024]{1,0:T(8,128)(2,1)S(1)}, u32[]{:S(2)}, u32[]{:S(2)}) collective-permute-start(bf16[128,1024]{1,0:T(8,128)(2,1)S(1)} %get-tuple-element.51.refs_3_), channel_id=1, source_target_pairs={{0,8},{4,0},{12,4},{20,12},{28,20},{24,28},{16,24},{8,16},{1,9},{5... | collective-permute-start | bytes 786440 | tf_op jit(solution)/shard_map/feature_ring_2/ppermute | solution.py:410
  18.5 7.1 %collective-permute-start.4 = (bf16[128,1024]{1,0:T(8,128)(2,1)S(1)}, bf16[128,1024]{1,0:T(8,128)(2,1)S(1)}, u32[]{:S(2)}, u32[]{:S(2)}) collective-permute-start(bf16[128,1024]{1,0:T(8,128)(2,1)S(1)} %collective-permute-done.2.refs_4_), channel_id=1, source_target_pairs={{0,4},{4,12},{12,20},{20,28},{28,24},{24,16},{16,8},{8,0},{1,5},{5... | collective-permute-start | bytes 786440 | tf_op jit(solution)/shard_map/feature_ring_3/ppermute | solution.py:410
  19.2 6.8 %collective-permute-start.5 = (bf16[128,1024]{1,0:T(8,128)(2,1)S(1)}, bf16[128,1024]{1,0:T(8,128)(2,1)S(1)}, u32[]{:S(2)}, u32[]{:S(2)}) collective-permute-start(bf16[128,1024]{1,0:T(8,128)(2,1)S(1)} %collective-permute-done.3.refs_5_), channel_id=1, source_target_pairs={{0,8},{4,0},{12,4},{20,12},{28,20},{24,28},{16,24},{8,16},{1,9},{5... | collective-permute-start | bytes 786440 | tf_op jit(solution)/shard_map/feature_ring_3/ppermute | solution.py:410
  20.6 8.6 %collective-permute-start.8 = (bf16[128,1024]{1,0:T(8,128)(2,1)}, bf16[128,1024]{1,0:T(8,128)(2,1)S(1)}, u32[]{:S(2)}, u32[]{:S(2)}) collective-permute-start(bf16[128,1024]{1,0:T(8,128)(2,1)} %refs_3_.3), channel_id=1, source_target_pairs={{0,2},{1,3},{2,0},{3,1},{4,6},{5,7},{6,4},{7,5},{8,10},{9,11},{10,... | collective-permute-start | bytes 786440 | tf_op jit(solution)/shard_map/cotangent_y/ppermute | solution.py:422
  25.6 5.0 %collective-permute-start.6 = (bf16[128,512]{1,0:T(8,128)(2,1)S(1)}, bf16[128,512]{1,0:T(8,128)(2,1)S(1)}, u32[]{:S(2)}, u32[]{:S(2)}) collective-permute-start(bf16[128,512]{1,0:T(8,128)(2,1)S(1)} %slice.16), channel_id=1, source_target_pairs={{0,4},{4,12},{12,20},{20,28},{28,24},{24,16},{16,8},{8,0},{1,5},{5... | collective-permute-start | bytes 393224 | tf_op jit(solution)/shard_map/feature_ring_4/ppermute | solution.py:410
  26.0 5.0 %collective-permute-start.7 = (bf16[128,512]{1,0:T(8,128)(2,1)S(1)}, bf16[128,512]{1,0:T(8,128)(2,1)S(1)}, u32[]{:S(2)}, u32[]{:S(2)}) collective-permute-start(bf16[128,512]{1,0:T(8,128)(2,1)S(1)} %slice.17), channel_id=1, source_target_pairs={{0,8},{4,0},{12,4},{20,12},{28,20},{24,28},{16,24},{8,16},{1,9},{5... | collective-permute-start | bytes 393224 | tf_op jit(solution)/shard_map/feature_ring_4/ppermute | solution.py:410
  33.1 9.2 %collective-permute-start.11 = (bf16[128,1024]{1,0:T(8,128)(2,1)S(1)}, bf16[128,1024]{1,0:T(8,128)(2,1)S(1)}, u32[]{:S(2)}, u32[]{:S(2)}) collective-permute-start(bf16[128,1024]{1,0:T(8,128)(2,1)S(1)} %add_convert_fusion.refs_0_), channel_id=1, source_target_pairs={{0,2},{1,3},{2,0},{3,1},{4,6},{5,7},{6,4},{7,5},{8,10},{9,11},{10,... | collective-permute-start | bytes 786440 | tf_op jit(solution)/shard_map/sum_y_own_1/ppermute | solution.py:422
  34.9 12.2 %collective-permute-start.12 = (bf16[128,1024]{1,0:T(8,128)(2,1)S(1)}, bf16[128,1024]{1,0:T(8,128)(2,1)S(1)}, u32[]{:S(2)}, u32[]{:S(2)}) collective-permute-start(bf16[128,1024]{1,0:T(8,128)(2,1)S(1)} %add_convert_fusion.1.refs_0_), channel_id=1, source_target_pairs={{0,2},{1,3},{2,0},{3,1},{4,6},{5,7},{6,4},{7,5},{8,10},{9,11},{10,... | collective-permute-start | bytes 786440 | tf_op jit(solution)/shard_map/sum_y_rest_1/ppermute | solution.py:422
  48.7 8.2 %collective-permute-start.13 = (bf16[128,1024]{1,0:T(8,128)(2,1)S(1)}, bf16[128,1024]{1,0:T(8,128)(2,1)S(1)}, u32[]{:S(2)}, u32[]{:S(2)}) collective-permute-start(bf16[128,1024]{1,0:T(8,128)(2,1)S(1)} %get-tuple-element.57.refs_1_), channel_id=1, source_target_pairs={{0,1},{1,0},{2,3},{3,2},{4,5},{5,4},{6,7},{7,6},{8,9},{9,8},{10,11... | collective-permute-start | bytes 786440 | tf_op jit(solution)/shard_map/back_core_own/ppermute | solution.py:418
  49.2 7.7 %collective-permute-start.14 = (bf16[128,1024]{1,0:T(8,128)(2,1)S(1)}, bf16[128,1024]{1,0:T(8,128)(2,1)S(1)}, u32[]{:S(2)}, u32[]{:S(2)}) collective-permute-start(bf16[128,1024]{1,0:T(8,128)(2,1)S(1)} %get-tuple-element.60.refs_2_), channel_id=1, source_target_pairs={{0,1},{1,0},{2,3},{3,2},{4,5},{5,4},{6,7},{7,6},{8,9},{9,8},{10,11... | collective-permute-start | bytes 786440 | tf_op jit(solution)/shard_map/back_core_rest/ppermute | solution.py:418
  54.8 5.6 %collective-permute-start.21 = (bf16[32,1024]{1,0:T(8,128)(2,1)S(1)}, bf16[32,1024]{1,0:T(8,128)(2,1)S(1)}, u32[]{:S(2)}, u32[]{:S(2)}) collective-permute-start(bf16[32,1024]{1,0:T(8,128)(2,1)S(1)} %add_round.12), channel_id=1, source_target_pairs={{0,8},{4,0},{12,4},{20,12},{28,20},{24,28},{16,24},{8,16},{1,9},{5... | collective-permute-start | bytes 196616 | tf_op jit(solution)/shard_map/weight_ring_1/ppermute | solution.py:410
  56.7 4.8 %collective-permute-start.19 = (bf16[32,1024]{1,0:T(8,128)(2,1)S(1)}, bf16[32,1024]{1,0:T(8,128)(2,1)S(1)}, u32[]{:S(2)}, u32[]{:S(2)}) collective-permute-start(bf16[32,1024]{1,0:T(8,128)(2,1)S(1)} %add_round.11), channel_id=1, source_target_pairs={{0,4},{4,12},{12,20},{20,28},{28,24},{24,16},{16,8},{8,0},{1,5},{5... | collective-permute-start | bytes 196616 | tf_op jit(solution)/shard_map/weight_ring_1/ppermute | solution.py:410
  58.2 5.4 %collective-permute-start.15 = (bf16[128,512]{1,0:T(8,128)(2,1)S(1)}, bf16[128,512]{1,0:T(8,128)(2,1)S(1)}, u32[]{:S(2)}, u32[]{:S(2)}) collective-permute-start(bf16[128,512]{1,0:T(8,128)(2,1)S(1)} %get-tuple-element.65), channel_id=1, source_target_pairs={{0,4},{4,12},{12,20},{20,28},{28,24},{24,16},{16,8},{8,0},{1,5},{5... | collective-permute-start | bytes 393224 | tf_op jit(solution)/shard_map/back_ring_0/ppermute | solution.py:410
  59.9 5.0 %collective-permute-start.16 = (bf16[128,512]{1,0:T(8,128)(2,1)S(1)}, bf16[128,512]{1,0:T(8,128)(2,1)S(1)}, u32[]{:S(2)}, u32[]{:S(2)}) collective-permute-start(bf16[128,512]{1,0:T(8,128)(2,1)S(1)} %get-tuple-element.67), channel_id=1, source_target_pairs={{0,8},{4,0},{12,4},{20,12},{28,20},{24,28},{16,24},{8,16},{1,9},{5... | collective-permute-start | bytes 393224 | tf_op jit(solution)/shard_map/back_ring_0/ppermute | solution.py:410
  61.6 4.8 %collective-permute-start.24 = (bf16[32,1024]{1,0:T(8,128)(2,1)S(1)}, bf16[32,1024]{1,0:T(8,128)(2,1)S(1)}, u32[]{:S(2)}, u32[]{:S(2)}) collective-permute-start(bf16[32,1024]{1,0:T(8,128)(2,1)S(1)} %get-tuple-element.76.refs_4_), channel_id=1, source_target_pairs={{0,4},{4,12},{12,20},{20,28},{28,24},{24,16},{16,8},{8,0},{1,5},{5... | collective-permute-start | bytes 196616 | tf_op jit(solution)/shard_map/weight_ring_2/ppermute | solution.py:410
  66.6 5.1 %collective-permute-start.27 = (bf16[32,1024]{1,0:T(8,128)(2,1)S(1)}, bf16[32,1024]{1,0:T(8,128)(2,1)S(1)}, u32[]{:S(2)}, u32[]{:S(2)}) collective-permute-start(bf16[32,1024]{1,0:T(8,128)(2,1)S(1)} %add_round.16), channel_id=1, source_target_pairs={{0,8},{4,0},{12,4},{20,12},{28,20},{24,28},{16,24},{8,16},{1,9},{5... | collective-permute-start | bytes 196616 | tf_op jit(solution)/shard_map/weight_ring_3/ppermute | solution.py:410
  68.6 9.3 %collective-permute-start.22 = (bf16[128,1024]{1,0:T(8,128)(2,1)S(1)}, bf16[128,1024]{1,0:T(8,128)(2,1)S(1)}, u32[]{:S(2)}, u32[]{:S(2)}) collective-permute-start(bf16[128,1024]{1,0:T(8,128)(2,1)S(1)} %get-tuple-element.78.refs_2_), channel_id=1, source_target_pairs={{0,4},{4,12},{12,20},{20,28},{28,24},{24,16},{16,8},{8,0},{1,5},{5... | collective-permute-start | bytes 786440 | tf_op jit(solution)/shard_map/back_ring_1/ppermute | solution.py:410
  68.7 9.2 %collective-permute-start.23 = (bf16[128,1024]{1,0:T(8,128)(2,1)S(1)}, bf16[128,1024]{1,0:T(8,128)(2,1)S(1)}, u32[]{:S(2)}, u32[]{:S(2)}) collective-permute-start(bf16[128,1024]{1,0:T(8,128)(2,1)S(1)} %get-tuple-element.80), channel_id=1, source_target_pairs={{0,8},{4,0},{12,4},{20,12},{28,20},{24,28},{16,24},{8,16},{1,9},{5... | collective-permute-start | bytes 786440 | tf_op jit(solution)/shard_map/back_ring_1/ppermute | solution.py:410
  71.7 4.9 %collective-permute-start.29 = (bf16[32,1024]{1,0:T(8,128)(2,1)S(1)}, bf16[32,1024]{1,0:T(8,128)(2,1)S(1)}, u32[]{:S(2)}, u32[]{:S(2)}) collective-permute-start(bf16[32,1024]{1,0:T(8,128)(2,1)S(1)} %end_sum.2.refs_0_), channel_id=1, source_target_pairs={{0,8},{4,0},{12,4},{20,12},{28,20},{24,28},{16,24},{8,16},{1,9},{5... | collective-permute-start | bytes 196616 | tf_op jit(solution)/shard_map/weight_ring_4/ppermute | solution.py:410
  73.0 4.9 %collective-permute-start.28 = (bf16[32,1024]{1,0:T(8,128)(2,1)S(1)}, bf16[32,1024]{1,0:T(8,128)(2,1)S(1)}, u32[]{:S(2)}, u32[]{:S(2)}) collective-permute-start(bf16[32,1024]{1,0:T(8,128)(2,1)S(1)} %end_sum.2.refs_0_), channel_id=1, source_target_pairs={{0,4},{4,12},{12,20},{20,28},{28,24},{24,16},{16,8},{8,0},{1,5},{5... | collective-permute-start | bytes 196616 | tf_op jit(solution)/shard_map/weight_ring_4/ppermute | solution.py:410
  78.5 4.9 %collective-permute-start.35 = (bf16[32,1024]{1,0:T(8,128)(2,1)S(1)}, bf16[32,1024]{1,0:T(8,128)(2,1)S(1)}, u32[]{:S(2)}, u32[]{:S(2)}) collective-permute-start(bf16[32,1024]{1,0:T(8,128)(2,1)S(1)} %get-tuple-element.89), channel_id=1, source_target_pairs={{0,8},{4,0},{12,4},{20,12},{28,20},{24,28},{16,24},{8,16},{1,9},{5... | collective-permute-start | bytes 196616 | tf_op jit(solution)/shard_map/weight_ring_5/ppermute | solution.py:410
  80.1 8.6 %collective-permute-start.30 = (bf16[128,1024]{1,0:T(8,128)(2,1)S(1)}, bf16[128,1024]{1,0:T(8,128)(2,1)S(1)}, u32[]{:S(2)}, u32[]{:S(2)}) collective-permute-start(bf16[128,1024]{1,0:T(8,128)(2,1)S(1)} %get-tuple-element.84), channel_id=1, source_target_pairs={{0,4},{4,12},{12,20},{20,28},{28,24},{24,16},{16,8},{8,0},{1,5},{5... | collective-permute-start | bytes 786440 | tf_op jit(solution)/shard_map/back_ring_2/ppermute | solution.py:410
  80.5 9.9 %collective-permute-start.34 = (bf16[128,1024]{1,0:T(8,128)(2,1)S(1)}, bf16[128,1024]{1,0:T(8,128)(2,1)S(1)}, u32[]{:S(2)}, u32[]{:S(2)}) collective-permute-start(bf16[128,1024]{1,0:T(8,128)(2,1)S(1)} %get-tuple-element.88), channel_id=1, source_target_pairs={{0,8},{4,0},{12,4},{20,12},{28,20},{24,28},{16,24},{8,16},{1,9},{5... | collective-permute-start | bytes 786440 | tf_op jit(solution)/shard_map/back_ring_2/ppermute | solution.py:410
  83.4 10.9 %collective-permute-start.39 = (bf16[160,1024]{1,0:T(8,128)(2,1)S(1)}, bf16[160,1024]{1,0:T(8,128)(2,1)S(1)}, u32[]{:S(2)}, u32[]{:S(2)}) collective-permute-start(bf16[160,1024]{1,0:T(8,128)(2,1)S(1)} %stack_blocks.2.refs_0_), channel_id=1, source_target_pairs={{0,2},{1,3},{2,0},{3,1},{4,6},{5,7},{6,4},{7,5},{8,10},{9,11},{10,... | collective-permute-start | bytes 983048 | tf_op jit(solution)/shard_map/weight_y_early_1/ppermute | solution.py:422
  90.9 11.0 %collective-permute-start.38 = (bf16[160,1024]{1,0:T(8,128)(2,1)S(1)}, bf16[160,1024]{1,0:T(8,128)(2,1)S(1)}, u32[]{:S(2)}, u32[]{:S(2)}) collective-permute-start(bf16[160,1024]{1,0:T(8,128)(2,1)S(1)} %stack_blocks.2.refs_0_), channel_id=1, source_target_pairs={{0,1},{1,0},{2,3},{3,2},{4,5},{5,4},{6,7},{7,6},{8,9},{9,8},{10,11... | collective-permute-start | bytes 983048 | tf_op jit(solution)/shard_map/weight_last/ppermute | solution.py:418
  90.9 8.7 %collective-permute-start.33 = (bf16[128,1024]{1,0:T(8,128)(2,1)S(1)}, bf16[128,1024]{1,0:T(8,128)(2,1)S(1)}, u32[]{:S(2)}, u32[]{:S(2)}) collective-permute-start(bf16[128,1024]{1,0:T(8,128)(2,1)S(1)} %get-tuple-element.86), channel_id=1, source_target_pairs={{0,4},{4,12},{12,20},{20,28},{28,24},{24,16},{16,8},{8,0},{1,5},{5... | collective-permute-start | bytes 786440 | tf_op jit(solution)/shard_map/back_ring_3/ppermute | solution.py:410
  92.7 8.5 %collective-permute-start.37 = (bf16[128,1024]{1,0:T(8,128)(2,1)S(1)}, bf16[128,1024]{1,0:T(8,128)(2,1)S(1)}, u32[]{:S(2)}, u32[]{:S(2)}) collective-permute-start(bf16[128,1024]{1,0:T(8,128)(2,1)S(1)} %get-tuple-element.90), channel_id=1, source_target_pairs={{0,8},{4,0},{12,4},{20,12},{28,20},{24,28},{16,24},{8,16},{1,9},{5... | collective-permute-start | bytes 786440 | tf_op jit(solution)/shard_map/back_ring_3/ppermute | solution.py:410
  94.2 7.7 %collective-permute-start.40 = (bf16[160,1024]{1,0:T(8,128)(2,1)S(1)}, bf16[160,1024]{1,0:T(8,128)(2,1)S(1)}, u32[]{:S(2)}, u32[]{:S(2)}) collective-permute-start(bf16[160,1024]{1,0:T(8,128)(2,1)S(1)} %collective-permute-done.39.refs_4_.refs_2_), channel_id=1, source_target_pairs={{0,1},{1,0},{2,3},{3,2},{4,5},{5,4},{6,7},{7,6},{8,9},{9,8},{10,11... | collective-permute-start | bytes 983048 | tf_op jit(solution)/shard_map/weight_last/ppermute | solution.py:418
  94.4 7.5 %collective-permute-start.44 = (bf16[96,1024]{1,0:T(8,128)(2,1)S(1)}, bf16[96,1024]{1,0:T(8,128)(2,1)S(1)}, u32[]{:S(2)}, u32[]{:S(2)}) collective-permute-start(bf16[96,1024]{1,0:T(8,128)(2,1)S(1)} %stack_blocks.3.refs_4_), channel_id=1, source_target_pairs={{0,2},{1,3},{2,0},{3,1},{4,6},{5,7},{6,4},{7,5},{8,10},{9,11},{10,... | collective-permute-start | bytes 589832 | tf_op jit(solution)/shard_map/weight_y_late_1/ppermute | solution.py:422
  (20 other events, 81.2 us)

commit v5 on v4

--- a/solution.py
+++ b/solution.py
@@ -202,7 +202,7 @@
     def kernel(*refs):
         held_ref, weight_ref = refs[0], refs[1 + len(arrived)]
         cot_refs = refs[2 + len(arrived) : 2 + len(arrived) + len(cotangents)]
-        agg_ref, grad_ref, near_ref, far_ref, back_ref, agg, grad = refs[-7:]
+        agg_ref, grad_ref, near_ref, far_ref, rest_ref, agg, grad = refs[-7:]
         _, group, core = position(spot)
         total = held_ref[...].astype(jnp.float32)
         for ref in refs[1 : 1 + len(arrived)]:
@@ -223,12 +223,12 @@
         near_ref[...] = lax.dot_general(
             agg[:, pl.ds(near_at, quarter)], grad[...], (((0,), (0,)), ((), ())), preferred_element_type=jnp.float32
         )
-        back_ref[...] = times_transposed(grad[side:], weight_ref[...])
+        rest_ref[...] = grad[side:]
 
     shapes = [
         jax.ShapeDtypeStruct((quarter, cols), jnp.float32),
         jax.ShapeDtypeStruct((quarter, cols), jnp.bfloat16),
-        jax.ShapeDtypeStruct((rows, depth), jnp.bfloat16),
+        jax.ShapeDtypeStruct((rows, cols), jnp.bfloat16),
     ]
     return vmem_call(
         "dense_rest",
@@ -239,6 +239,14 @@
         flops=4 * rows * cols * depth + 2 * (rows + side) * part * cols,
         moved=2 * (depth * cols + 6 * rows * depth),
     )
+
+
+def back_of(grad, weight):
+    def kernel(grad_ref, weight_ref, out_ref):
+        out_ref[...] = times_transposed(grad_ref[...], weight_ref[...])
+
+    shape = jax.ShapeDtypeStruct((grad.shape[0], weight.shape[0]), jnp.bfloat16)
+    return vmem_call("back_of", kernel, shape, (grad, weight), flops=2 * grad.size * weight.shape[0], moved=2 * weight.size)
 
 
 def back_blocks(adjacency, parts, count):
@@ -446,9 +454,10 @@
         arrived_rest.append(from_group(f"sum_y_rest_{s}", jnp.concatenate(sent) if len(sent) > 1 else sent[0], s))
     activated, agg_own, grad_own, back_own = dense_own(own, arrived_own, weight, cotangents[0])
     turned = [cotangents[groups - g] for g in range(1, groups)]
-    near_weight, far_weight, back_rest = dense_rest(spot, rest, arrived_rest, weight, turned, agg_own, grad_own)
+    near_weight, far_weight, grad_rest = dense_rest(spot, rest, arrived_rest, weight, turned, agg_own, grad_own)
 
     far_weight = swap_core("weight_core", far_weight)
+    back_rest = back_of(grad_rest, weight)
     far_back = [swap_core("back_core_own", back_own), swap_core("back_core_rest", back_rest)]
     terms = weight_blocks(spot, near_weight, far_weight)
     blocks = back_blocks(adjacency, [back_own, back_rest, *far_back], count)
@@ -483,7 +492,7 @@
         elif turn > 0 and turn != rounds:
             for side in range(2):
                 mine = [*sums[side : side + 1], *back_sums[side : side + 1]]
-                outs = add_round(mine, carried[side : side + 1], ordered, 0 if side else flops)
+                outs = add_round(mine, carried[side : side + 1], ordered, flops)
                 weight_moving[side] = outs[0] if sums else outs[-1]
                 if begins:
                     moving[side] = outs[1] if sums else outs[0]

time: 105 us -> 103 us (0.981)
  waiting for transfers between devices: 46.2 us -> 43.2 us
    ppermute x16, starting transfers between devices: 10.7 us -> 7.56 us  [go(): lax.ppermute(right, 'row', to_right)]
    ppermute x16, starting transfers between devices: 25 us -> 27.6 us  [go(): lax.ppermute(left, 'row', to_left)]
    ppermute x16, waiting for transfers between devices: 11.4 us -> 9.38 us  [go(): lax.ppermute(left, 'row', to_left)]
    ppermute x5, starting transfers between devices: 5.41 us -> 6.85 us  [from_group(): lax.ppermute(value, 'col', [(k, (k + 2 * steps) % columns) for k in range...]
    pallas_call x25 -> x26, Pallas kernels: 11.2 us -> 11.3 us  [vmem_call(): pl.pallas_call(inner, out_shape=out_shapes, in_specs=specs, out_specs=jax...]
  transfers between devices with their start and end apart: 46 -> 46, of which waited for: 24 -> 25; matrix products, arithmetic and copies ran while one was open for 0% -> 0% of each run, Pallas kernels for 8% -> 9%
where the time goes in v5:
time: 103 us
  starting transfers between devices  43.3 us (42%)
  waiting for transfers between devices  43.2 us (42%)
  Pallas kernels  11.3 us (11%)
  local copies, waits for them, and re-layouts  3.51 us (3%)
  between operations  1.52 us (1%)
    ppermute x16, starting transfers between devices, go(): lax.ppermute(left, 'row', to_left)  27.6 us
    ppermute x16, waiting for transfers between devices, go(): lax.ppermute(right, 'row', to_right)  21.7 us
    pallas_call x26, Pallas kernels, vmem_call(): pl.pallas_call(inner, out_shape=out_shapes, in_specs=specs, out_specs=jax...  11.3 us
    ppermute x5, waiting for transfers between devices, from_group(): lax.ppermute(value, 'col', [(k, (k + 2 * steps) % columns) for k in range...  10.5 us
    ppermute x16, waiting for transfers between devices, go(): lax.ppermute(left, 'row', to_left)  9.38 us
    ppermute x16, starting transfers between devices, go(): lax.ppermute(right, 'row', to_right)  7.56 us
    ppermute x5, starting transfers between devices, from_group(): lax.ppermute(value, 'col', [(k, (k + 2 * steps) % columns) for k in range...  6.85 us
    unnamed x12, local copies, waits for them, and re-layouts  3.48 us
  transfers between devices with their start and end apart: 46, of which 25 were waited for; matrix products, arithmetic and copies ran while one was open for 0% of the time, Pallas kernels for 9%

profile of v5, /device:TPU:0, one launch (start us, length us, event | category | flops | bytes accessed | tf_op | source)
XLA Modules:
  0.0 102.9 jit_solution(18239557677242171743)
XLA Ops:
  0.6 3.1 %collective-permute-start.1 = (bf16[128,1024]{1,0:T(8,128)(2,1)}, bf16[128,1024]{1,0:T(8,128)(2,1)S(1)}, u32[]{:S(2)}, u32[]{:S(2)}) collective-permute-start(bf16[128,1024]{1,0:T(8,128)(2,1)} %refs_4_.1), channel_id=1, source_target_pairs={{0,8},{4,0},{12,4},{20,12},{28,20},{24,28},{16,24},{8,16},{1,9},{5... | collective-permute-start | bytes 786440 | tf_op jit(solution)/shard_map/feature_ring_1/ppermute | solution.py:418
  8.7 1.5 %collective-permute-done.1.refs_1_ = bf16[128,1024]{1,0:T(8,128)(2,1)S(1)} collective-permute-done((bf16[128,1024]{1,0:T(8,128)(2,1)}, bf16[128,1024]{1,0:T(8,128)(2,1)S(1)}, u32[]{:S(2)}, u32[]{:S(2)}) %collective-permute-start.1) | collective-permute-done | bytes 262176 | tf_op jit(solution)/shard_map/feature_ring_1/ppermute | solution.py:418
  10.1 1.5 %collective-permute-done.refs_0_ = bf16[128,1024]{1,0:T(8,128)(2,1)S(1)} collective-permute-done((bf16[128,1024]{1,0:T(8,128)(2,1)}, bf16[128,1024]{1,0:T(8,128)(2,1)S(1)}, u32[]{:S(2)}, u32[]{:S(2)}) %collective-permute-start) | collective-permute-done | bytes 262176 | tf_op jit(solution)/shard_map/feature_ring_1/ppermute | solution.py:418
  12.0 1.7 %collective-permute-start.3 = (bf16[128,1024]{1,0:T(8,128)(2,1)S(1)}, bf16[128,1024]{1,0:T(8,128)(2,1)S(1)}, u32[]{:S(2)}, u32[]{:S(2)}) collective-permute-start(bf16[128,1024]{1,0:T(8,128)(2,1)S(1)} %get-tuple-element.51.refs_3_), channel_id=1, source_target_pairs={{0,8},{4,0},{12,4},{20,12},{28,20},{24,28},{16,24},{8,16},{1,9},{5... | collective-permute-start | bytes 786440 | tf_op jit(solution)/shard_map/feature_ring_2/ppermute | solution.py:418
  13.7 4.8 %collective-permute-done.2.refs_4_ = bf16[128,1024]{1,0:T(8,128)(2,1)S(1)} collective-permute-done((bf16[128,1024]{1,0:T(8,128)(2,1)S(1)}, bf16[128,1024]{1,0:T(8,128)(2,1)S(1)}, u32[]{:S(2)}, u32[]{:S(2)}) %collective-permute-start.2) | collective-permute-done | bytes 262176 | tf_op jit(solution)/shard_map/feature_ring_2/ppermute | solution.py:418
  20.6 1.5 %collective-permute-start.8 = (bf16[128,1024]{1,0:T(8,128)(2,1)}, bf16[128,1024]{1,0:T(8,128)(2,1)S(1)}, u32[]{:S(2)}, u32[]{:S(2)}) collective-permute-start(bf16[128,1024]{1,0:T(8,128)(2,1)} %refs_3_.3), channel_id=1, source_target_pairs={{0,2},{1,3},{2,0},{3,1},{4,6},{5,7},{6,4},{7,5},{8,10},{9,11},{10,... | collective-permute-start | bytes 786440 | tf_op jit(solution)/shard_map/cotangent_y/ppermute | solution.py:430
  22.1 3.5 %collective-permute-done.4.refs_6_ = bf16[128,1024]{1,0:T(8,128)(2,1)S(1)} collective-permute-done((bf16[128,1024]{1,0:T(8,128)(2,1)S(1)}, bf16[128,1024]{1,0:T(8,128)(2,1)S(1)}, u32[]{:S(2)}, u32[]{:S(2)}) %collective-permute-start.4) | collective-permute-done | bytes 262176 | tf_op jit(solution)/shard_map/feature_ring_3/ppermute | solution.py:418
  26.0 1.9 %collective-permute-start.7 = (bf16[128,512]{1,0:T(8,128)(2,1)S(1)}, bf16[128,512]{1,0:T(8,128)(2,1)S(1)}, u32[]{:S(2)}, u32[]{:S(2)}) collective-permute-start(bf16[128,512]{1,0:T(8,128)(2,1)S(1)} %slice.17), channel_id=1, source_target_pairs={{0,8},{4,0},{12,4},{20,12},{28,20},{24,28},{16,24},{8,16},{1,9},{5... | collective-permute-start | bytes 393224 | tf_op jit(solution)/shard_map/feature_ring_4/ppermute | solution.py:418
  29.2 1.5 %collective-permute-done.6.refs_2_ = bf16[128,512]{1,0:T(8,128)(2,1)S(1)} collective-permute-done((bf16[128,512]{1,0:T(8,128)(2,1)S(1)}, bf16[128,512]{1,0:T(8,128)(2,1)S(1)}, u32[]{:S(2)}, u32[]{:S(2)}) %collective-permute-start.6) | collective-permute-done | bytes 131104 | tf_op jit(solution)/shard_map/feature_ring_4/ppermute | solution.py:418
  33.1 1.7 %collective-permute-start.11 = (bf16[128,1024]{1,0:T(8,128)(2,1)S(1)}, bf16[128,1024]{1,0:T(8,128)(2,1)S(1)}, u32[]{:S(2)}, u32[]{:S(2)}) collective-permute-start(bf16[128,1024]{1,0:T(8,128)(2,1)S(1)} %add_convert_fusion.refs_0_), channel_id=1, source_target_pairs={{0,2},{1,3},{2,0},{3,1},{4,6},{5,7},{6,4},{7,5},{8,10},{9,11},{10,... | collective-permute-start | bytes 786440 | tf_op jit(solution)/shard_map/sum_y_own_1/ppermute | solution.py:430
  35.3 7.0 %collective-permute-done.11.refs_1_ = bf16[128,1024]{1,0:T(8,128)(2,1)S(1)} collective-permute-done((bf16[128,1024]{1,0:T(8,128)(2,1)S(1)}, bf16[128,1024]{1,0:T(8,128)(2,1)S(1)}, u32[]{:S(2)}, u32[]{:S(2)}) %collective-permute-start.11) | collective-permute-done | bytes 262176 | tf_op jit(solution)/shard_map/sum_y_own_1/ppermute | solution.py:430
  42.3 1.7 %dense_own.1 = (bf16[128,1024]{1,0:T(8,128)(2,1)}, bf16[128,1024]{1,0:T(8,128)(2,1)S(1)}, bf16[128,1024]{1,0:T(8,128)(2,1)S(1)}, bf16[128,1024]{1,0:T(8,128)(2,1)S(1)}) custom-call(bf16[128,1024]{1,0:T(8,128)(2,1)S(1)} %add_convert_fusion.1.refs_0_, bf16[128,1024]{1,0:T(8,128)(2,1)S(1)} %collective-permute-done.11.refs_1_, bf16[1024,1024]{1,0:T(8,128)(2,1)S(1)} %copy-done, ...), custom_call_target="tpu_custom_call" | custom-call | flops 536870912 | bytes 3670016 | tf_op jit(solution)/shard_map/dense_own/pallas_call | solution.py:51
  44.0 3.1 %collective-permute-done.12.refs_1_ = bf16[128,1024]{1,0:T(8,128)(2,1)S(1)} collective-permute-done((bf16[128,1024]{1,0:T(8,128)(2,1)S(1)}, bf16[128,1024]{1,0:T(8,128)(2,1)S(1)}, u32[]{:S(2)}, u32[]{:S(2)}) %collective-permute-start.12) | collective-permute-done | bytes 262176 | tf_op jit(solution)/shard_map/sum_y_rest_1/ppermute | solution.py:430
  50.2 1.9 %collective-permute-start.20 = (bf16[32,512]{1,0:T(8,128)(2,1)S(1)}, bf16[32,512]{1,0:T(8,128)(2,1)S(1)}, u32[]{:S(2)}, u32[]{:S(2)}) collective-permute-start(bf16[32,512]{1,0:T(8,128)(2,1)S(1)} %get-tuple-element.75), channel_id=1, source_target_pairs={{0,8},{4,0},{12,4},{20,12},{28,20},{24,28},{16,24},{8,16},{1,9},{5... | collective-permute-start | bytes 98312 | tf_op jit(solution)/shard_map/weight_ring_0/ppermute | solution.py:418
  52.3 1.9 %collective-permute-done.20.refs_1_ = bf16[32,512]{1,0:T(8,128)(2,1)S(1)} collective-permute-done((bf16[32,512]{1,0:T(8,128)(2,1)S(1)}, bf16[32,512]{1,0:T(8,128)(2,1)S(1)}, u32[]{:S(2)}, u32[]{:S(2)}) %collective-permute-start.20) | collective-permute-done | bytes 32800 | tf_op jit(solution)/shard_map/weight_ring_0/ppermute | solution.py:418
  54.2 1.9 %collective-permute-start.21 = (bf16[32,1024]{1,0:T(8,128)(2,1)S(1)}, bf16[32,1024]{1,0:T(8,128)(2,1)S(1)}, u32[]{:S(2)}, u32[]{:S(2)}) collective-permute-start(bf16[32,1024]{1,0:T(8,128)(2,1)S(1)} %add_round.12), channel_id=1, source_target_pairs={{0,8},{4,0},{12,4},{20,12},{28,20},{24,28},{16,24},{8,16},{1,9},{5... | collective-permute-start | bytes 196616 | tf_op jit(solution)/shard_map/weight_ring_1/ppermute | solution.py:418
  57.6 1.7 %collective-permute-start.15 = (bf16[128,512]{1,0:T(8,128)(2,1)S(1)}, bf16[128,512]{1,0:T(8,128)(2,1)S(1)}, u32[]{:S(2)}, u32[]{:S(2)}) collective-permute-start(bf16[128,512]{1,0:T(8,128)(2,1)S(1)} %get-tuple-element.65), channel_id=1, source_target_pairs={{0,4},{4,12},{12,20},{20,28},{28,24},{24,16},{16,8},{8,0},{1,5},{5... | collective-permute-start | bytes 393224 | tf_op jit(solution)/shard_map/back_ring_0/ppermute | solution.py:418
  61.4 1.6 %collective-permute-start.26 = (bf16[32,1024]{1,0:T(8,128)(2,1)S(1)}, bf16[32,1024]{1,0:T(8,128)(2,1)S(1)}, u32[]{:S(2)}, u32[]{:S(2)}) collective-permute-start(bf16[32,1024]{1,0:T(8,128)(2,1)S(1)} %get-tuple-element.77.refs_5_), channel_id=1, source_target_pairs={{0,8},{4,0},{12,4},{20,12},{28,20},{24,28},{16,24},{8,16},{1,9},{5... | collective-permute-start | bytes 196616 | tf_op jit(solution)/shard_map/weight_ring_2/ppermute | solution.py:418
  64.3 1.4 %collective-permute-done.24.refs_1_ = bf16[32,1024]{1,0:T(8,128)(2,1)S(1)} collective-permute-done((bf16[32,1024]{1,0:T(8,128)(2,1)S(1)}, bf16[32,1024]{1,0:T(8,128)(2,1)S(1)}, u32[]{:S(2)}, u32[]{:S(2)}) %collective-permute-start.24) | collective-permute-done | bytes 65568 | tf_op jit(solution)/shard_map/weight_ring_2/ppermute | solution.py:418
  66.0 2.0 %collective-permute-start.27 = (bf16[32,1024]{1,0:T(8,128)(2,1)S(1)}, bf16[32,1024]{1,0:T(8,128)(2,1)S(1)}, u32[]{:S(2)}, u32[]{:S(2)}) collective-permute-start(bf16[32,1024]{1,0:T(8,128)(2,1)S(1)} %add_round.16), channel_id=1, source_target_pairs={{0,8},{4,0},{12,4},{20,12},{28,20},{24,28},{16,24},{8,16},{1,9},{5... | collective-permute-start | bytes 196616 | tf_op jit(solution)/shard_map/weight_ring_3/ppermute | solution.py:418
  68.1 2.0 %collective-permute-start.23 = (bf16[128,1024]{1,0:T(8,128)(2,1)S(1)}, bf16[128,1024]{1,0:T(8,128)(2,1)S(1)}, u32[]{:S(2)}, u32[]{:S(2)}) collective-permute-start(bf16[128,1024]{1,0:T(8,128)(2,1)S(1)} %get-tuple-element.80), channel_id=1, source_target_pairs={{0,8},{4,0},{12,4},{20,12},{28,20},{24,28},{16,24},{8,16},{1,9},{5... | collective-permute-start | bytes 786440 | tf_op jit(solution)/shard_map/back_ring_1/ppermute | solution.py:418
  73.2 2.7 %collective-permute-done.29.refs_5_.refs_2_ = bf16[32,1024]{1,0:T(8,128)(2,1)S(1)} collective-permute-done((bf16[32,1024]{1,0:T(8,128)(2,1)S(1)}, bf16[32,1024]{1,0:T(8,128)(2,1)S(1)}, u32[]{:S(2)}, u32[]{:S(2)}) %collective-permute-start.29) | collective-permute-done | bytes 65568 | tf_op jit(solution)/shard_map/weight_ring_4/ppermute | solution.py:418
  75.9 1.4 %collective-permute-done.28.refs_4_.refs_1_ = bf16[32,1024]{1,0:T(8,128)(2,1)S(1)} collective-permute-done((bf16[32,1024]{1,0:T(8,128)(2,1)S(1)}, bf16[32,1024]{1,0:T(8,128)(2,1)S(1)}, u32[]{:S(2)}, u32[]{:S(2)}) %collective-permute-start.28) | collective-permute-done | bytes 65568 | tf_op jit(solution)/shard_map/weight_ring_4/ppermute | solution.py:418
  77.9 1.6 %collective-permute-start.35 = (bf16[32,1024]{1,0:T(8,128)(2,1)S(1)}, bf16[32,1024]{1,0:T(8,128)(2,1)S(1)}, u32[]{:S(2)}, u32[]{:S(2)}) collective-permute-start(bf16[32,1024]{1,0:T(8,128)(2,1)S(1)} %get-tuple-element.89), channel_id=1, source_target_pairs={{0,8},{4,0},{12,4},{20,12},{28,20},{24,28},{16,24},{8,16},{1,9},{5... | collective-permute-start | bytes 196616 | tf_op jit(solution)/shard_map/weight_ring_5/ppermute | solution.py:418
  79.9 1.6 %collective-permute-start.34 = (bf16[128,1024]{1,0:T(8,128)(2,1)S(1)}, bf16[128,1024]{1,0:T(8,128)(2,1)S(1)}, u32[]{:S(2)}, u32[]{:S(2)}) collective-permute-start(bf16[128,1024]{1,0:T(8,128)(2,1)S(1)} %get-tuple-element.88), channel_id=1, source_target_pairs={{0,8},{4,0},{12,4},{20,12},{28,20},{24,28},{16,24},{8,16},{1,9},{5... | collective-permute-start | bytes 786440 | tf_op jit(solution)/shard_map/back_ring_2/ppermute | solution.py:418
  82.2 1.6 %collective-permute-start.39 = (bf16[160,1024]{1,0:T(8,128)(2,1)S(1)}, bf16[160,1024]{1,0:T(8,128)(2,1)S(1)}, u32[]{:S(2)}, u32[]{:S(2)}) collective-permute-start(bf16[160,1024]{1,0:T(8,128)(2,1)S(1)} %stack_blocks.2.refs_0_), channel_id=1, source_target_pairs={{0,2},{1,3},{2,0},{3,1},{4,6},{5,7},{6,4},{7,5},{8,10},{9,11},{10,... | collective-permute-start | bytes 983048 | tf_op jit(solution)/shard_map/weight_y_early_1/ppermute | solution.py:430
  83.8 1.6 %collective-permute-start.36 = (bf16[32,1024]{1,0:T(8,128)(2,1)S(1)}, bf16[32,1024]{1,0:T(8,128)(2,1)S(1)}, u32[]{:S(2)}, u32[]{:S(2)}) collective-permute-start(bf16[32,1024]{1,0:T(8,128)(2,1)S(1)} %add_round.20), channel_id=1, source_target_pairs={{0,8},{4,0},{12,4},{20,12},{28,20},{24,28},{16,24},{8,16},{1,9},{5... | collective-permute-start | bytes 196616 | tf_op jit(solution)/shard_map/weight_ring_6/ppermute | solution.py:418
  88.1 1.6 %collective-permute-start.42 = (bf16[32,512]{1,0:T(8,128)(2,1)S(1)}, bf16[32,512]{1,0:T(8,128)(2,1)S(1)}, u32[]{:S(2)}, u32[]{:S(2)}) collective-permute-start(bf16[32,512]{1,0:T(8,128)(2,1)S(1)} %slice.15), channel_id=1, source_target_pairs={{0,8},{4,0},{12,4},{20,12},{28,20},{24,28},{16,24},{8,16},{1,9},{5... | collective-permute-start | bytes 98312 | tf_op jit(solution)/shard_map/weight_ring_7/ppermute | solution.py:418
  90.5 1.9 %collective-permute-start.37 = (bf16[128,1024]{1,0:T(8,128)(2,1)S(1)}, bf16[128,1024]{1,0:T(8,128)(2,1)S(1)}, u32[]{:S(2)}, u32[]{:S(2)}) collective-permute-start(bf16[128,1024]{1,0:T(8,128)(2,1)S(1)} %get-tuple-element.90), channel_id=1, source_target_pairs={{0,8},{4,0},{12,4},{20,12},{28,20},{24,28},{16,24},{8,16},{1,9},{5... | collective-permute-start | bytes 786440 | tf_op jit(solution)/shard_map/back_ring_3/ppermute | solution.py:418
  92.4 1.6 %collective-permute-start.44 = (bf16[96,1024]{1,0:T(8,128)(2,1)S(1)}, bf16[96,1024]{1,0:T(8,128)(2,1)S(1)}, u32[]{:S(2)}, u32[]{:S(2)}) collective-permute-start(bf16[96,1024]{1,0:T(8,128)(2,1)S(1)} %stack_blocks.3.refs_4_), channel_id=1, source_target_pairs={{0,2},{1,3},{2,0},{3,1},{4,6},{5,7},{6,4},{7,5},{8,10},{9,11},{10,... | collective-permute-start | bytes 589832 | tf_op jit(solution)/shard_map/weight_y_late_1/ppermute | solution.py:430
  94.0 4.5 %collective-permute-done.33.refs_1_ = bf16[128,1024]{1,0:T(8,128)(2,1)S(1)} collective-permute-done((bf16[128,1024]{1,0:T(8,128)(2,1)S(1)}, bf16[128,1024]{1,0:T(8,128)(2,1)S(1)}, u32[]{:S(2)}, u32[]{:S(2)}) %collective-permute-start.33) | collective-permute-done | bytes 262176 | tf_op jit(solution)/shard_map/back_ring_3/ppermute | solution.py:418
  100.0 2.0 %join_weight.2.refs_0_ = f32[1024,1024]{1,0:T(8,128)} custom-call(bf16[160,1024]{1,0:T(8,128)(2,1)S(1)} %stack_blocks.2.refs_0_, bf16[160,1024]{1,0:T(8,128)(2,1)S(1)} %collective-permute-done.38.refs_1_, bf16[160,1024]{1,0:T(8,128)(2,1)S(1)} %collective-permute-done.39.refs_4_.refs_2_, bf16[160,1024]{1,0:T(8,128)(2,1)S(1)} %collective-permute-done.40.refs_3_, ...), custom_call_target="tpu_custom_call" | custom-call | flops 20000000000 | bytes 5111808 | tf_op jit(solution)/shard_map/join_weight/pallas_call | solution.py:51
  (104 shorter events, 30.3 us)
Async XLA Ops:
  0.6 9.5 %collective-permute-start.1 = (bf16[128,1024]{1,0:T(8,128)(2,1)}, bf16[128,1024]{1,0:T(8,128)(2,1)S(1)}, u32[]{:S(2)}, u32[]{:S(2)}) collective-permute-start(bf16[128,1024]{1,0:T(8,128)(2,1)} %refs_4_.1), channel_id=1, source_target_pairs={{0,8},{4,0},{12,4},{20,12},{28,20},{24,28},{16,24},{8,16},{1,9},{5... | collective-permute-start | bytes 786440 | tf_op jit(solution)/shard_map/feature_ring_1/ppermute | solution.py:418
  3.7 8.0 %collective-permute-start = (bf16[128,1024]{1,0:T(8,128)(2,1)}, bf16[128,1024]{1,0:T(8,128)(2,1)S(1)}, u32[]{:S(2)}, u32[]{:S(2)}) collective-permute-start(bf16[128,1024]{1,0:T(8,128)(2,1)} %refs_4_.1), channel_id=1, source_target_pairs={{0,4},{4,12},{12,20},{20,28},{28,24},{24,16},{16,8},{8,0},{1,5},{5... | collective-permute-start | bytes 786440 | tf_op jit(solution)/shard_map/feature_ring_1/ppermute | solution.py:418
  11.7 6.9 %collective-permute-start.2 = (bf16[128,1024]{1,0:T(8,128)(2,1)S(1)}, bf16[128,1024]{1,0:T(8,128)(2,1)S(1)}, u32[]{:S(2)}, u32[]{:S(2)}) collective-permute-start(bf16[128,1024]{1,0:T(8,128)(2,1)S(1)} %get-tuple-element.50.refs_2_), channel_id=1, source_target_pairs={{0,4},{4,12},{12,20},{20,28},{28,24},{24,16},{16,8},{8,0},{1,5},{5... | collective-permute-start | bytes 786440 | tf_op jit(solution)/shard_map/feature_ring_2/ppermute | solution.py:418
  12.0 7.2 %collective-permute-start.3 = (bf16[128,1024]{1,0:T(8,128)(2,1)S(1)}, bf16[128,1024]{1,0:T(8,128)(2,1)S(1)}, u32[]{:S(2)}, u32[]{:S(2)}) collective-permute-start(bf16[128,1024]{1,0:T(8,128)(2,1)S(1)} %get-tuple-element.51.refs_3_), channel_id=1, source_target_pairs={{0,8},{4,0},{12,4},{20,12},{28,20},{24,28},{16,24},{8,16},{1,9},{5... | collective-permute-start | bytes 786440 | tf_op jit(solution)/shard_map/feature_ring_2/ppermute | solution.py:418
  18.5 7.1 %collective-permute-start.4 = (bf16[128,1024]{1,0:T(8,128)(2,1)S(1)}, bf16[128,1024]{1,0:T(8,128)(2,1)S(1)}, u32[]{:S(2)}, u32[]{:S(2)}) collective-permute-start(bf16[128,1024]{1,0:T(8,128)(2,1)S(1)} %collective-permute-done.2.refs_4_), channel_id=1, source_target_pairs={{0,4},{4,12},{12,20},{20,28},{28,24},{24,16},{16,8},{8,0},{1,5},{5... | collective-permute-start | bytes 786440 | tf_op jit(solution)/shard_map/feature_ring_3/ppermute | solution.py:418
  19.2 6.8 %collective-permute-start.5 = (bf16[128,1024]{1,0:T(8,128)(2,1)S(1)}, bf16[128,1024]{1,0:T(8,128)(2,1)S(1)}, u32[]{:S(2)}, u32[]{:S(2)}) collective-permute-start(bf16[128,1024]{1,0:T(8,128)(2,1)S(1)} %collective-permute-done.3.refs_5_), channel_id=1, source_target_pairs={{0,8},{4,0},{12,4},{20,12},{28,20},{24,28},{16,24},{8,16},{1,9},{5... | collective-permute-start | bytes 786440 | tf_op jit(solution)/shard_map/feature_ring_3/ppermute | solution.py:418
  20.6 8.6 %collective-permute-start.8 = (bf16[128,1024]{1,0:T(8,128)(2,1)}, bf16[128,1024]{1,0:T(8,128)(2,1)S(1)}, u32[]{:S(2)}, u32[]{:S(2)}) collective-permute-start(bf16[128,1024]{1,0:T(8,128)(2,1)} %refs_3_.3), channel_id=1, source_target_pairs={{0,2},{1,3},{2,0},{3,1},{4,6},{5,7},{6,4},{7,5},{8,10},{9,11},{10,... | collective-permute-start | bytes 786440 | tf_op jit(solution)/shard_map/cotangent_y/ppermute | solution.py:430
  25.6 5.0 %collective-permute-start.6 = (bf16[128,512]{1,0:T(8,128)(2,1)S(1)}, bf16[128,512]{1,0:T(8,128)(2,1)S(1)}, u32[]{:S(2)}, u32[]{:S(2)}) collective-permute-start(bf16[128,512]{1,0:T(8,128)(2,1)S(1)} %slice.16), channel_id=1, source_target_pairs={{0,4},{4,12},{12,20},{20,28},{28,24},{24,16},{16,8},{8,0},{1,5},{5... | collective-permute-start | bytes 393224 | tf_op jit(solution)/shard_map/feature_ring_4/ppermute | solution.py:418
  26.0 5.0 %collective-permute-start.7 = (bf16[128,512]{1,0:T(8,128)(2,1)S(1)}, bf16[128,512]{1,0:T(8,128)(2,1)S(1)}, u32[]{:S(2)}, u32[]{:S(2)}) collective-permute-start(bf16[128,512]{1,0:T(8,128)(2,1)S(1)} %slice.17), channel_id=1, source_target_pairs={{0,8},{4,0},{12,4},{20,12},{28,20},{24,28},{16,24},{8,16},{1,9},{5... | collective-permute-start | bytes 393224 | tf_op jit(solution)/shard_map/feature_ring_4/ppermute | solution.py:418
  33.1 9.2 %collective-permute-start.11 = (bf16[128,1024]{1,0:T(8,128)(2,1)S(1)}, bf16[128,1024]{1,0:T(8,128)(2,1)S(1)}, u32[]{:S(2)}, u32[]{:S(2)}) collective-permute-start(bf16[128,1024]{1,0:T(8,128)(2,1)S(1)} %add_convert_fusion.refs_0_), channel_id=1, source_target_pairs={{0,2},{1,3},{2,0},{3,1},{4,6},{5,7},{6,4},{7,5},{8,10},{9,11},{10,... | collective-permute-start | bytes 786440 | tf_op jit(solution)/shard_map/sum_y_own_1/ppermute | solution.py:430
  34.9 12.2 %collective-permute-start.12 = (bf16[128,1024]{1,0:T(8,128)(2,1)S(1)}, bf16[128,1024]{1,0:T(8,128)(2,1)S(1)}, u32[]{:S(2)}, u32[]{:S(2)}) collective-permute-start(bf16[128,1024]{1,0:T(8,128)(2,1)S(1)} %add_convert_fusion.1.refs_0_), channel_id=1, source_target_pairs={{0,2},{1,3},{2,0},{3,1},{4,6},{5,7},{6,4},{7,5},{8,10},{9,11},{10,... | collective-permute-start | bytes 786440 | tf_op jit(solution)/shard_map/sum_y_rest_1/ppermute | solution.py:430
  48.1 8.2 %collective-permute-start.13 = (bf16[128,1024]{1,0:T(8,128)(2,1)S(1)}, bf16[128,1024]{1,0:T(8,128)(2,1)S(1)}, u32[]{:S(2)}, u32[]{:S(2)}) collective-permute-start(bf16[128,1024]{1,0:T(8,128)(2,1)S(1)} %get-tuple-element.57.refs_1_), channel_id=1, source_target_pairs={{0,1},{1,0},{2,3},{3,2},{4,5},{5,4},{6,7},{7,6},{8,9},{9,8},{10,11... | collective-permute-start | bytes 786440 | tf_op jit(solution)/shard_map/back_core_own/ppermute | solution.py:426
  49.4 6.9 %collective-permute-start.14 = (bf16[128,1024]{1,0:T(8,128)(2,1)S(1)}, bf16[128,1024]{1,0:T(8,128)(2,1)S(1)}, u32[]{:S(2)}, u32[]{:S(2)}) collective-permute-start(bf16[128,1024]{1,0:T(8,128)(2,1)S(1)} %back_of.1.refs_2_), channel_id=1, source_target_pairs={{0,1},{1,0},{2,3},{3,2},{4,5},{5,4},{6,7},{7,6},{8,9},{9,8},{10,11... | collective-permute-start | bytes 786440 | tf_op jit(solution)/shard_map/back_core_rest/ppermute | solution.py:426
  54.2 5.6 %collective-permute-start.21 = (bf16[32,1024]{1,0:T(8,128)(2,1)S(1)}, bf16[32,1024]{1,0:T(8,128)(2,1)S(1)}, u32[]{:S(2)}, u32[]{:S(2)}) collective-permute-start(bf16[32,1024]{1,0:T(8,128)(2,1)S(1)} %add_round.12), channel_id=1, source_target_pairs={{0,8},{4,0},{12,4},{20,12},{28,20},{24,28},{16,24},{8,16},{1,9},{5... | collective-permute-start | bytes 196616 | tf_op jit(solution)/shard_map/weight_ring_1/ppermute | solution.py:418
  56.1 4.8 %collective-permute-start.19 = (bf16[32,1024]{1,0:T(8,128)(2,1)S(1)}, bf16[32,1024]{1,0:T(8,128)(2,1)S(1)}, u32[]{:S(2)}, u32[]{:S(2)}) collective-permute-start(bf16[32,1024]{1,0:T(8,128)(2,1)S(1)} %add_round.11), channel_id=1, source_target_pairs={{0,4},{4,12},{12,20},{20,28},{28,24},{24,16},{16,8},{8,0},{1,5},{5... | collective-permute-start | bytes 196616 | tf_op jit(solution)/shard_map/weight_ring_1/ppermute | solution.py:418
  57.6 5.4 %collective-permute-start.15 = (bf16[128,512]{1,0:T(8,128)(2,1)S(1)}, bf16[128,512]{1,0:T(8,128)(2,1)S(1)}, u32[]{:S(2)}, u32[]{:S(2)}) collective-permute-start(bf16[128,512]{1,0:T(8,128)(2,1)S(1)} %get-tuple-element.65), channel_id=1, source_target_pairs={{0,4},{4,12},{12,20},{20,28},{28,24},{24,16},{16,8},{8,0},{1,5},{5... | collective-permute-start | bytes 393224 | tf_op jit(solution)/shard_map/back_ring_0/ppermute | solution.py:418
  59.3 5.0 %collective-permute-start.16 = (bf16[128,512]{1,0:T(8,128)(2,1)S(1)}, bf16[128,512]{1,0:T(8,128)(2,1)S(1)}, u32[]{:S(2)}, u32[]{:S(2)}) collective-permute-start(bf16[128,512]{1,0:T(8,128)(2,1)S(1)} %get-tuple-element.67), channel_id=1, source_target_pairs={{0,8},{4,0},{12,4},{20,12},{28,20},{24,28},{16,24},{8,16},{1,9},{5... | collective-permute-start | bytes 393224 | tf_op jit(solution)/shard_map/back_ring_0/ppermute | solution.py:418
  61.0 4.8 %collective-permute-start.24 = (bf16[32,1024]{1,0:T(8,128)(2,1)S(1)}, bf16[32,1024]{1,0:T(8,128)(2,1)S(1)}, u32[]{:S(2)}, u32[]{:S(2)}) collective-permute-start(bf16[32,1024]{1,0:T(8,128)(2,1)S(1)} %get-tuple-element.76.refs_4_), channel_id=1, source_target_pairs={{0,4},{4,12},{12,20},{20,28},{28,24},{24,16},{16,8},{8,0},{1,5},{5... | collective-permute-start | bytes 196616 | tf_op jit(solution)/shard_map/weight_ring_2/ppermute | solution.py:418
  66.0 5.1 %collective-permute-start.27 = (bf16[32,1024]{1,0:T(8,128)(2,1)S(1)}, bf16[32,1024]{1,0:T(8,128)(2,1)S(1)}, u32[]{:S(2)}, u32[]{:S(2)}) collective-permute-start(bf16[32,1024]{1,0:T(8,128)(2,1)S(1)} %add_round.16), channel_id=1, source_target_pairs={{0,8},{4,0},{12,4},{20,12},{28,20},{24,28},{16,24},{8,16},{1,9},{5... | collective-permute-start | bytes 196616 | tf_op jit(solution)/shard_map/weight_ring_3/ppermute | solution.py:418
  68.0 9.3 %collective-permute-start.22 = (bf16[128,1024]{1,0:T(8,128)(2,1)S(1)}, bf16[128,1024]{1,0:T(8,128)(2,1)S(1)}, u32[]{:S(2)}, u32[]{:S(2)}) collective-permute-start(bf16[128,1024]{1,0:T(8,128)(2,1)S(1)} %get-tuple-element.78.refs_2_), channel_id=1, source_target_pairs={{0,4},{4,12},{12,20},{20,28},{28,24},{24,16},{16,8},{8,0},{1,5},{5... | collective-permute-start | bytes 786440 | tf_op jit(solution)/shard_map/back_ring_1/ppermute | solution.py:418
  68.1 9.2 %collective-permute-start.23 = (bf16[128,1024]{1,0:T(8,128)(2,1)S(1)}, bf16[128,1024]{1,0:T(8,128)(2,1)S(1)}, u32[]{:S(2)}, u32[]{:S(2)}) collective-permute-start(bf16[128,1024]{1,0:T(8,128)(2,1)S(1)} %get-tuple-element.80), channel_id=1, source_target_pairs={{0,8},{4,0},{12,4},{20,12},{28,20},{24,28},{16,24},{8,16},{1,9},{5... | collective-permute-start | bytes 786440 | tf_op jit(solution)/shard_map/back_ring_1/ppermute | solution.py:418
  71.1 4.8 %collective-permute-start.29 = (bf16[32,1024]{1,0:T(8,128)(2,1)S(1)}, bf16[32,1024]{1,0:T(8,128)(2,1)S(1)}, u32[]{:S(2)}, u32[]{:S(2)}) collective-permute-start(bf16[32,1024]{1,0:T(8,128)(2,1)S(1)} %end_sum.2.refs_0_), channel_id=1, source_target_pairs={{0,8},{4,0},{12,4},{20,12},{28,20},{24,28},{16,24},{8,16},{1,9},{5... | collective-permute-start | bytes 196616 | tf_op jit(solution)/shard_map/weight_ring_4/ppermute | solution.py:418
  72.4 4.9 %collective-permute-start.28 = (bf16[32,1024]{1,0:T(8,128)(2,1)S(1)}, bf16[32,1024]{1,0:T(8,128)(2,1)S(1)}, u32[]{:S(2)}, u32[]{:S(2)}) collective-permute-start(bf16[32,1024]{1,0:T(8,128)(2,1)S(1)} %end_sum.2.refs_0_), channel_id=1, source_target_pairs={{0,4},{4,12},{12,20},{20,28},{28,24},{24,16},{16,8},{8,0},{1,5},{5... | collective-permute-start | bytes 196616 | tf_op jit(solution)/shard_map/weight_ring_4/ppermute | solution.py:418
  79.5 7.1 %collective-permute-start.30 = (bf16[128,1024]{1,0:T(8,128)(2,1)S(1)}, bf16[128,1024]{1,0:T(8,128)(2,1)S(1)}, u32[]{:S(2)}, u32[]{:S(2)}) collective-permute-start(bf16[128,1024]{1,0:T(8,128)(2,1)S(1)} %get-tuple-element.84), channel_id=1, source_target_pairs={{0,4},{4,12},{12,20},{20,28},{28,24},{24,16},{16,8},{8,0},{1,5},{5... | collective-permute-start | bytes 786440 | tf_op jit(solution)/shard_map/back_ring_2/ppermute | solution.py:418
  79.9 8.1 %collective-permute-start.34 = (bf16[128,1024]{1,0:T(8,128)(2,1)S(1)}, bf16[128,1024]{1,0:T(8,128)(2,1)S(1)}, u32[]{:S(2)}, u32[]{:S(2)}) collective-permute-start(bf16[128,1024]{1,0:T(8,128)(2,1)S(1)} %get-tuple-element.88), channel_id=1, source_target_pairs={{0,8},{4,0},{12,4},{20,12},{28,20},{24,28},{16,24},{8,16},{1,9},{5... | collective-permute-start | bytes 786440 | tf_op jit(solution)/shard_map/back_ring_2/ppermute | solution.py:418
  81.7 4.8 %collective-permute-start.32 = (bf16[32,1024]{1,0:T(8,128)(2,1)S(1)}, bf16[32,1024]{1,0:T(8,128)(2,1)S(1)}, u32[]{:S(2)}, u32[]{:S(2)}) collective-permute-start(bf16[32,1024]{1,0:T(8,128)(2,1)S(1)} %add_round.18), channel_id=1, source_target_pairs={{0,4},{4,12},{12,20},{20,28},{28,24},{24,16},{16,8},{8,0},{1,5},{5... | collective-permute-start | bytes 196616 | tf_op jit(solution)/shard_map/weight_ring_6/ppermute | solution.py:418
  82.2 10.2 %collective-permute-start.39 = (bf16[160,1024]{1,0:T(8,128)(2,1)S(1)}, bf16[160,1024]{1,0:T(8,128)(2,1)S(1)}, u32[]{:S(2)}, u32[]{:S(2)}) collective-permute-start(bf16[160,1024]{1,0:T(8,128)(2,1)S(1)} %stack_blocks.2.refs_0_), channel_id=1, source_target_pairs={{0,2},{1,3},{2,0},{3,1},{4,6},{5,7},{6,4},{7,5},{8,10},{9,11},{10,... | collective-permute-start | bytes 983048 | tf_op jit(solution)/shard_map/weight_y_early_1/ppermute | solution.py:430
  89.7 10.1 %collective-permute-start.38 = (bf16[160,1024]{1,0:T(8,128)(2,1)S(1)}, bf16[160,1024]{1,0:T(8,128)(2,1)S(1)}, u32[]{:S(2)}, u32[]{:S(2)}) collective-permute-start(bf16[160,1024]{1,0:T(8,128)(2,1)S(1)} %stack_blocks.2.refs_0_), channel_id=1, source_target_pairs={{0,1},{1,0},{2,3},{3,2},{4,5},{5,4},{6,7},{7,6},{8,9},{9,8},{10,11... | collective-permute-start | bytes 983048 | tf_op jit(solution)/shard_map/weight_last/ppermute | solution.py:426
  89.7 8.8 %collective-permute-start.33 = (bf16[128,1024]{1,0:T(8,128)(2,1)S(1)}, bf16[128,1024]{1,0:T(8,128)(2,1)S(1)}, u32[]{:S(2)}, u32[]{:S(2)}) collective-permute-start(bf16[128,1024]{1,0:T(8,128)(2,1)S(1)} %get-tuple-element.86), channel_id=1, source_target_pairs={{0,4},{4,12},{12,20},{20,28},{28,24},{24,16},{16,8},{8,0},{1,5},{5... | collective-permute-start | bytes 786440 | tf_op jit(solution)/shard_map/back_ring_3/ppermute | solution.py:418
  90.5 8.1 %collective-permute-start.37 = (bf16[128,1024]{1,0:T(8,128)(2,1)S(1)}, bf16[128,1024]{1,0:T(8,128)(2,1)S(1)}, u32[]{:S(2)}, u32[]{:S(2)}) collective-permute-start(bf16[128,1024]{1,0:T(8,128)(2,1)S(1)} %get-tuple-element.90), channel_id=1, source_target_pairs={{0,8},{4,0},{12,4},{20,12},{28,20},{24,28},{16,24},{8,16},{1,9},{5... | collective-permute-start | bytes 786440 | tf_op jit(solution)/shard_map/back_ring_3/ppermute | solution.py:418
  92.4 7.6 %collective-permute-start.40 = (bf16[160,1024]{1,0:T(8,128)(2,1)S(1)}, bf16[160,1024]{1,0:T(8,128)(2,1)S(1)}, u32[]{:S(2)}, u32[]{:S(2)}) collective-permute-start(bf16[160,1024]{1,0:T(8,128)(2,1)S(1)} %collective-permute-done.39.refs_4_.refs_2_), channel_id=1, source_target_pairs={{0,1},{1,0},{2,3},{3,2},{4,5},{5,4},{6,7},{7,6},{8,9},{9,8},{10,11... | collective-permute-start | bytes 983048 | tf_op jit(solution)/shard_map/weight_last/ppermute | solution.py:426
  92.4 7.4 %collective-permute-start.44 = (bf16[96,1024]{1,0:T(8,128)(2,1)S(1)}, bf16[96,1024]{1,0:T(8,128)(2,1)S(1)}, u32[]{:S(2)}, u32[]{:S(2)}) collective-permute-start(bf16[96,1024]{1,0:T(8,128)(2,1)S(1)} %stack_blocks.3.refs_4_), channel_id=1, source_target_pairs={{0,2},{1,3},{2,0},{3,1},{4,6},{5,7},{6,4},{7,5},{8,10},{9,11},{10,... | collective-permute-start | bytes 589832 | tf_op jit(solution)/shard_map/weight_y_late_1/ppermute | solution.py:430
  (20 other events, 80.8 us)

commit v6 on v5

--- a/solution.py
+++ b/solution.py
@@ -358,18 +358,22 @@
     return vmem_call("stack_blocks", kernel, shape, (*blocks, *ends), flops=flops, after=after, moved=4 * total * height * width)
 
 
-def join_weight(spot, groups, shape, stacks, begun, flops):
+def join_weight(spot, groups, shape, stacks, begun, last, flops):
     count = len(spot)
     quarter = shape[0] // (2 * groups)
     share = quarter // count
     total = sum(len(s[1]) for s in stacks)
-    args = [s[0] for s in stacks]
-    out = jax.ShapeDtypeStruct(shape, jnp.float32)
-    scratch = [pltpu.VMEM((total, share, shape[1]), jnp.float32), pltpu.SemaphoreType.DMA((total,))]
+    args = [s[0] for s in stacks] + list(last)
+    outs = [jax.ShapeDtypeStruct(shape, jnp.float32)]
+    scratch = [pltpu.VMEM((total, share, shape[1]), jnp.float32), pltpu.SemaphoreType.DMA((total + 1,))]
+    if last:
+        outs.append(jax.ShapeDtypeStruct(last[0].shape, jnp.bfloat16))
+        scratch.append(pltpu.VMEM(last[0].shape, jnp.bfloat16))
 
     def kernel(*refs):
         refs = refs[0 if begun is None else 1 :]
-        out_ref, wide, sems = refs[-3:]
+        out_refs = refs[len(args) : len(args) + len(outs)]
+        wide, sems = refs[len(args) + len(outs) : len(args) + len(outs) + 2]
         me, group, core = position(spot)
         copies = []
         for ref, (_, aways, steps, other) in zip(refs, stacks):
@@ -379,8 +383,13 @@
                 slot = len(copies)
                 wide[slot] = ref[place * share : (place + 1) * share].astype(jnp.float32)
                 at = pl.multiple_of(base + lax.rem(me + away, count) * share, share)
-                copies.append(pltpu.make_async_copy(wide.at[slot], out_ref.at[pl.ds(at, share)], sems.at[slot]))
+                copies.append(pltpu.make_async_copy(wide.at[slot], out_refs[0].at[pl.ds(at, share)], sems.at[slot]))
                 copies[-1].start()
+        if last:
+            own, first, second = (ref[...].astype(jnp.float32) for ref in refs[len(stacks) : len(args)])
+            refs[-1][...] = (own + first + second).astype(jnp.bfloat16)
+            copies.append(pltpu.make_async_copy(refs[-1], out_refs[1], sems.at[total]))
+            copies[-1].start()
         for copy in copies:
             copy.wait()
 
@@ -388,7 +397,7 @@
     return vmem_call(
         "join_weight",
         kernel,
-        out,
+        outs,
         [begun] * hbm + args,
         scratch=scratch,
         hbm=hbm,
@@ -435,7 +444,7 @@
     moving = (feats, feats)
     for step in range(1, rounds + 1):
         if step == 2:
-            moving = gate(moving, [adjacency])
+            moving = [gate([value], [adjacency])[0] for value in moving]
         if step > 1:
             pieces += moving
         send = go if step < rounds else go_halves
@@ -504,7 +513,6 @@
         if turn == 2 * rounds - 2:
             early = stack_blocks(pieces)
             early_from = [from_group(f"weight_y_early_{s}", early, s) for s in range(1, groups)]
-    grad_feats = end_sum(blocks[0], *moving, 0)
 
     late = stack_blocks(pieces[count - 3 :], weight_moving, early_from, LONG)
     late_from = [from_group(f"weight_y_late_{s}", late, s) for s in range(1, groups)]
@@ -518,8 +526,9 @@
 
     along = range(1, groups)
     stacks = placed([early, *early_from], range(groups), slots[: count - 3]) + placed([late], [0], slots[count - 3 :])
-    grad_weight = join_weight(spot, groups, weight.shape, stacks, None, LONG)
-    grad_weight = join_weight(spot, groups, weight.shape, placed(late_from, along, slots[count - 3 :]), grad_weight, 0)
+    grad_weight, grad_feats = join_weight(spot, groups, weight.shape, stacks, None, (blocks[0], *moving), LONG)
+    stacks = placed(late_from, along, slots[count - 3 :])
+    (grad_weight,) = join_weight(spot, groups, weight.shape, stacks, grad_weight, (), 0)
     return (activated, grad_feats, grad_weight)
 
 

time: 103 us -> 102 us (level)
  starting transfers between devices: 43.3 us -> 41.2 us
  waiting for transfers between devices: 43.2 us -> 45.1 us
    ppermute x16, starting transfers between devices: 27.6 us -> 7.74 us  [go(): lax.ppermute(left, 'row', to_left)]
    ppermute x16, starting transfers between devices: 7.56 us -> 26.4 us  [go(): lax.ppermute(right, 'row', to_right)]
    ppermute x16, waiting for transfers between devices: 21.7 us -> 15.9 us  [go(): lax.ppermute(right, 'row', to_right)]
    ppermute x5, waiting for transfers between devices: 10.5 us -> 15.5 us  [from_group(): lax.ppermute(value, 'col', [(k, (k + 2 * steps) % columns) for k in range...]
    ppermute x16, waiting for transfers between devices: 9.38 us -> 12.2 us  [go(): lax.ppermute(left, 'row', to_left)]
    ppermute x5, starting transfers between devices: 6.85 us -> 5.74 us  [from_group(): lax.ppermute(value, 'col', [(k, (k + 2 * steps) % columns) for k in range...]
  transfers between devices with their start and end apart: 46 -> 46, of which waited for: 25 -> 23; matrix products, arithmetic and copies ran while one was open for 0% -> 0% of each run, Pallas kernels for 9% -> 8%
where the time goes in v6:
time: 102 us
  waiting for transfers between devices  45.1 us (44%)
  starting transfers between devices  41.2 us (40%)
  Pallas kernels  10.8 us (11%)
  local copies, waits for them, and re-layouts  3.51 us (3%)
  between operations  1.53 us (2%)
    ppermute x16, starting transfers between devices, go(): lax.ppermute(right, 'row', to_right)  26.4 us
    ppermute x16, waiting for transfers between devices, go(): lax.ppermute(right, 'row', to_right)  15.9 us
    ppermute x5, waiting for transfers between devices, from_group(): lax.ppermute(value, 'col', [(k, (k + 2 * steps) % columns) for k in range...  15.5 us
    ppermute x16, waiting for transfers between devices, go(): lax.ppermute(left, 'row', to_left)  12.2 us
    pallas_call x26, Pallas kernels, vmem_call(): pl.pallas_call(inner, out_shape=out_shapes, in_specs=specs, out_specs=jax...  10.8 us
    ppermute x16, starting transfers between devices, go(): lax.ppermute(left, 'row', to_left)  7.74 us
    ppermute x5, starting transfers between devices, from_group(): lax.ppermute(value, 'col', [(k, (k + 2 * steps) % columns) for k in range...  5.74 us
    unnamed x12, local copies, waits for them, and re-layouts  3.48 us
  transfers between devices with their start and end apart: 46, of which 23 were waited for; matrix products, arithmetic and copies ran while one was open for 0% of the time, Pallas kernels for 8%

profile of v6, /device:TPU:0, one launch (start us, length us, event | category | flops | bytes accessed | tf_op | source)
XLA Modules:
  0.0 102.2 jit_solution(15635791186623271946)
XLA Ops:
  0.6 3.0 %collective-permute-start = (bf16[128,1024]{1,0:T(8,128)(2,1)}, bf16[128,1024]{1,0:T(8,128)(2,1)S(1)}, u32[]{:S(2)}, u32[]{:S(2)}) collective-permute-start(bf16[128,1024]{1,0:T(8,128)(2,1)} %refs_4_.1), channel_id=1, source_target_pairs={{0,4},{4,12},{12,20},{20,28},{28,24},{24,16},{16,8},{8,0},{1,5},{5... | collective-permute-start | bytes 786440 | tf_op jit(solution)/shard_map/feature_ring_1/ppermute | solution.py:427
  10.2 1.7 %collective-permute-start.2 = (bf16[128,1024]{1,0:T(8,128)(2,1)S(1)}, bf16[128,1024]{1,0:T(8,128)(2,1)S(1)}, u32[]{:S(2)}, u32[]{:S(2)}) collective-permute-start(bf16[128,1024]{1,0:T(8,128)(2,1)S(1)} %gate.2.refs_2_), channel_id=1, source_target_pairs={{0,4},{4,12},{12,20},{20,28},{28,24},{24,16},{16,8},{8,0},{1,5},{5... | collective-permute-start | bytes 786440 | tf_op jit(solution)/shard_map/feature_ring_2/ppermute | solution.py:427
  12.3 5.5 %collective-permute-done.2.refs_4_ = bf16[128,1024]{1,0:T(8,128)(2,1)S(1)} collective-permute-done((bf16[128,1024]{1,0:T(8,128)(2,1)S(1)}, bf16[128,1024]{1,0:T(8,128)(2,1)S(1)}, u32[]{:S(2)}, u32[]{:S(2)}) %collective-permute-start.2) | collective-permute-done | bytes 262176 | tf_op jit(solution)/shard_map/feature_ring_2/ppermute | solution.py:427
  21.1 3.2 %collective-permute-done.4.refs_6_ = bf16[128,1024]{1,0:T(8,128)(2,1)S(1)} collective-permute-done((bf16[128,1024]{1,0:T(8,128)(2,1)S(1)}, bf16[128,1024]{1,0:T(8,128)(2,1)S(1)}, u32[]{:S(2)}, u32[]{:S(2)}) %collective-permute-start.4) | collective-permute-done | bytes 262176 | tf_op jit(solution)/shard_map/feature_ring_3/ppermute | solution.py:427
  24.3 1.6 %collective-permute-start.6 = (bf16[128,512]{1,0:T(8,128)(2,1)S(1)}, bf16[128,512]{1,0:T(8,128)(2,1)S(1)}, u32[]{:S(2)}, u32[]{:S(2)}) collective-permute-start(bf16[128,512]{1,0:T(8,128)(2,1)S(1)} %slice.16), channel_id=1, source_target_pairs={{0,4},{4,12},{12,20},{20,28},{28,24},{24,16},{16,8},{8,0},{1,5},{5... | collective-permute-start | bytes 393224 | tf_op jit(solution)/shard_map/feature_ring_4/ppermute | solution.py:427
  27.7 1.6 %collective-permute-done.6.refs_2_ = bf16[128,512]{1,0:T(8,128)(2,1)S(1)} collective-permute-done((bf16[128,512]{1,0:T(8,128)(2,1)S(1)}, bf16[128,512]{1,0:T(8,128)(2,1)S(1)}, u32[]{:S(2)}, u32[]{:S(2)}) %collective-permute-start.6) | collective-permute-done | bytes 131104 | tf_op jit(solution)/shard_map/feature_ring_4/ppermute | solution.py:427
  29.3 1.6 %collective-permute-done.7.refs_3_ = bf16[128,512]{1,0:T(8,128)(2,1)S(1)} collective-permute-done((bf16[128,512]{1,0:T(8,128)(2,1)S(1)}, bf16[128,512]{1,0:T(8,128)(2,1)S(1)}, u32[]{:S(2)}, u32[]{:S(2)}) %collective-permute-start.7) | collective-permute-done | bytes 131104 | tf_op jit(solution)/shard_map/feature_ring_4/ppermute | solution.py:427
  33.0 1.6 %collective-permute-start.11 = (bf16[128,1024]{1,0:T(8,128)(2,1)S(1)}, bf16[128,1024]{1,0:T(8,128)(2,1)S(1)}, u32[]{:S(2)}, u32[]{:S(2)}) collective-permute-start(bf16[128,1024]{1,0:T(8,128)(2,1)S(1)} %add_convert_fusion.refs_0_), channel_id=1, source_target_pairs={{0,2},{1,3},{2,0},{3,1},{4,6},{5,7},{6,4},{7,5},{8,10},{9,11},{10,... | collective-permute-start | bytes 786440 | tf_op jit(solution)/shard_map/sum_y_own_1/ppermute | solution.py:439
  35.2 7.0 %collective-permute-done.11.refs_1_ = bf16[128,1024]{1,0:T(8,128)(2,1)S(1)} collective-permute-done((bf16[128,1024]{1,0:T(8,128)(2,1)S(1)}, bf16[128,1024]{1,0:T(8,128)(2,1)S(1)}, u32[]{:S(2)}, u32[]{:S(2)}) %collective-permute-start.11) | collective-permute-done | bytes 262176 | tf_op jit(solution)/shard_map/sum_y_own_1/ppermute | solution.py:439
  42.2 1.7 %dense_own.1 = (bf16[128,1024]{1,0:T(8,128)(2,1)}, bf16[128,1024]{1,0:T(8,128)(2,1)S(1)}, bf16[128,1024]{1,0:T(8,128)(2,1)S(1)}, bf16[128,1024]{1,0:T(8,128)(2,1)S(1)}) custom-call(bf16[128,1024]{1,0:T(8,128)(2,1)S(1)} %add_convert_fusion.1.refs_0_, bf16[128,1024]{1,0:T(8,128)(2,1)S(1)} %collective-permute-done.11.refs_1_, bf16[1024,1024]{1,0:T(8,128)(2,1)S(1)} %copy-done, ...), custom_call_target="tpu_custom_call" | custom-call | flops 536870912 | bytes 3670016 | tf_op jit(solution)/shard_map/dense_own/pallas_call | solution.py:51
  43.9 3.1 %collective-permute-done.12.refs_1_ = bf16[128,1024]{1,0:T(8,128)(2,1)S(1)} collective-permute-done((bf16[128,1024]{1,0:T(8,128)(2,1)S(1)}, bf16[128,1024]{1,0:T(8,128)(2,1)S(1)}, u32[]{:S(2)}, u32[]{:S(2)}) %collective-permute-start.12) | collective-permute-done | bytes 262176 | tf_op jit(solution)/shard_map/sum_y_rest_1/ppermute | solution.py:439
  50.6 1.5 %collective-permute-start.14 = (bf16[32,512]{1,0:T(8,128)(2,1)S(1)}, bf16[32,512]{1,0:T(8,128)(2,1)S(1)}, u32[]{:S(2)}, u32[]{:S(2)}) collective-permute-start(bf16[32,512]{1,0:T(8,128)(2,1)S(1)} %get-tuple-element.63), channel_id=1, source_target_pairs={{0,4},{4,12},{12,20},{20,28},{28,24},{24,16},{16,8},{8,0},{1,5},{5... | collective-permute-start | bytes 98312 | tf_op jit(solution)/shard_map/weight_ring_0/ppermute | solution.py:427
  52.1 1.9 %collective-permute-done.16.refs_1_ = bf16[32,512]{1,0:T(8,128)(2,1)S(1)} collective-permute-done((bf16[32,512]{1,0:T(8,128)(2,1)S(1)}, bf16[32,512]{1,0:T(8,128)(2,1)S(1)}, u32[]{:S(2)}, u32[]{:S(2)}) %collective-permute-start.16) | collective-permute-done | bytes 32800 | tf_op jit(solution)/shard_map/weight_ring_0/ppermute | solution.py:427
  54.6 1.6 %collective-permute-start.15 = (bf16[32,1024]{1,0:T(8,128)(2,1)S(1)}, bf16[32,1024]{1,0:T(8,128)(2,1)S(1)}, u32[]{:S(2)}, u32[]{:S(2)}) collective-permute-start(bf16[32,1024]{1,0:T(8,128)(2,1)S(1)} %add_round.11), channel_id=1, source_target_pairs={{0,4},{4,12},{12,20},{20,28},{28,24},{24,16},{16,8},{8,0},{1,5},{5... | collective-permute-start | bytes 196616 | tf_op jit(solution)/shard_map/weight_ring_1/ppermute | solution.py:427
  57.5 1.6 %collective-permute-start.21 = (bf16[128,512]{1,0:T(8,128)(2,1)S(1)}, bf16[128,512]{1,0:T(8,128)(2,1)S(1)}, u32[]{:S(2)}, u32[]{:S(2)}) collective-permute-start(bf16[128,512]{1,0:T(8,128)(2,1)S(1)} %get-tuple-element.71), channel_id=1, source_target_pairs={{0,4},{4,12},{12,20},{20,28},{28,24},{24,16},{16,8},{8,0},{1,5},{5... | collective-permute-start | bytes 393224 | tf_op jit(solution)/shard_map/back_ring_0/ppermute | solution.py:427
  59.6 1.6 %collective-permute-start.18 = (bf16[32,1024]{1,0:T(8,128)(2,1)S(1)}, bf16[32,1024]{1,0:T(8,128)(2,1)S(1)}, u32[]{:S(2)}, u32[]{:S(2)}) collective-permute-start(bf16[32,1024]{1,0:T(8,128)(2,1)S(1)} %get-tuple-element.67.refs_4_), channel_id=1, source_target_pairs={{0,4},{4,12},{12,20},{20,28},{28,24},{24,16},{16,8},{8,0},{1,5},{5... | collective-permute-start | bytes 196616 | tf_op jit(solution)/shard_map/weight_ring_2/ppermute | solution.py:427
  62.5 1.6 %collective-permute-done.22.refs_3_ = bf16[128,512]{1,0:T(8,128)(2,1)S(1)} collective-permute-done((bf16[128,512]{1,0:T(8,128)(2,1)S(1)}, bf16[128,512]{1,0:T(8,128)(2,1)S(1)}, u32[]{:S(2)}, u32[]{:S(2)}) %collective-permute-start.22) | collective-permute-done | bytes 131104 | tf_op jit(solution)/shard_map/back_ring_0/ppermute | solution.py:427
  64.2 1.6 %collective-permute-start.23 = (bf16[32,1024]{1,0:T(8,128)(2,1)S(1)}, bf16[32,1024]{1,0:T(8,128)(2,1)S(1)}, u32[]{:S(2)}, u32[]{:S(2)}) collective-permute-start(bf16[32,1024]{1,0:T(8,128)(2,1)S(1)} %add_round.15), channel_id=1, source_target_pairs={{0,4},{4,12},{12,20},{20,28},{28,24},{24,16},{16,8},{8,0},{1,5},{5... | collective-permute-start | bytes 196616 | tf_op jit(solution)/shard_map/weight_ring_3/ppermute | solution.py:427
  66.4 1.5 %collective-permute-start.28 = (bf16[128,1024]{1,0:T(8,128)(2,1)S(1)}, bf16[128,1024]{1,0:T(8,128)(2,1)S(1)}, u32[]{:S(2)}, u32[]{:S(2)}) collective-permute-start(bf16[128,1024]{1,0:T(8,128)(2,1)S(1)} %get-tuple-element.75.refs_2_), channel_id=1, source_target_pairs={{0,4},{4,12},{12,20},{20,28},{28,24},{24,16},{16,8},{8,0},{1,5},{5... | collective-permute-start | bytes 786440 | tf_op jit(solution)/shard_map/back_ring_1/ppermute | solution.py:427
  69.3 1.6 %collective-permute-done.25.refs_2_ = bf16[32,1024]{1,0:T(8,128)(2,1)S(1)} collective-permute-done((bf16[32,1024]{1,0:T(8,128)(2,1)S(1)}, bf16[32,1024]{1,0:T(8,128)(2,1)S(1)}, u32[]{:S(2)}, u32[]{:S(2)}) %collective-permute-start.25) | collective-permute-done | bytes 65568 | tf_op jit(solution)/shard_map/weight_ring_3/ppermute | solution.py:427
  71.5 1.5 %collective-permute-start.26 = (bf16[32,1024]{1,0:T(8,128)(2,1)S(1)}, bf16[32,1024]{1,0:T(8,128)(2,1)S(1)}, u32[]{:S(2)}, u32[]{:S(2)}) collective-permute-start(bf16[32,1024]{1,0:T(8,128)(2,1)S(1)} %end_sum.1.refs_0_), channel_id=1, source_target_pairs={{0,4},{4,12},{12,20},{20,28},{28,24},{24,16},{16,8},{8,0},{1,5},{5... | collective-permute-start | bytes 196616 | tf_op jit(solution)/shard_map/weight_ring_4/ppermute | solution.py:427
  73.0 2.2 %collective-permute-done.27.refs_5_.refs_2_ = bf16[32,1024]{1,0:T(8,128)(2,1)S(1)} collective-permute-done((bf16[32,1024]{1,0:T(8,128)(2,1)S(1)}, bf16[32,1024]{1,0:T(8,128)(2,1)S(1)}, u32[]{:S(2)}, u32[]{:S(2)}) %collective-permute-start.27) | collective-permute-done | bytes 65568 | tf_op jit(solution)/shard_map/weight_ring_4/ppermute | solution.py:427
  76.2 1.5 %collective-permute-start.30 = (bf16[32,1024]{1,0:T(8,128)(2,1)S(1)}, bf16[32,1024]{1,0:T(8,128)(2,1)S(1)}, u32[]{:S(2)}, u32[]{:S(2)}) collective-permute-start(bf16[32,1024]{1,0:T(8,128)(2,1)S(1)} %get-tuple-element.80), channel_id=1, source_target_pairs={{0,4},{4,12},{12,20},{20,28},{28,24},{24,16},{16,8},{8,0},{1,5},{5... | collective-permute-start | bytes 196616 | tf_op jit(solution)/shard_map/weight_ring_5/ppermute | solution.py:427
  78.3 1.5 %collective-permute-start.37 = (bf16[128,1024]{1,0:T(8,128)(2,1)S(1)}, bf16[128,1024]{1,0:T(8,128)(2,1)S(1)}, u32[]{:S(2)}, u32[]{:S(2)}) collective-permute-start(bf16[128,1024]{1,0:T(8,128)(2,1)S(1)} %get-tuple-element.83), channel_id=1, source_target_pairs={{0,4},{4,12},{12,20},{20,28},{28,24},{24,16},{16,8},{8,0},{1,5},{5... | collective-permute-start | bytes 786440 | tf_op jit(solution)/shard_map/back_ring_2/ppermute | solution.py:427
  80.6 1.4 %collective-permute-start.35 = (bf16[32,1024]{1,0:T(8,128)(2,1)S(1)}, bf16[32,1024]{1,0:T(8,128)(2,1)S(1)}, u32[]{:S(2)}, u32[]{:S(2)}) collective-permute-start(bf16[32,1024]{1,0:T(8,128)(2,1)S(1)} %add_round.18), channel_id=1, source_target_pairs={{0,4},{4,12},{12,20},{20,28},{28,24},{24,16},{16,8},{8,0},{1,5},{5... | collective-permute-start | bytes 196616 | tf_op jit(solution)/shard_map/weight_ring_6/ppermute | solution.py:427
  82.1 1.6 %collective-permute-start.33 = (bf16[160,1024]{1,0:T(8,128)(2,1)S(1)}, bf16[160,1024]{1,0:T(8,128)(2,1)S(1)}, u32[]{:S(2)}, u32[]{:S(2)}) collective-permute-start(bf16[160,1024]{1,0:T(8,128)(2,1)S(1)} %stack_blocks.2.refs_0_), channel_id=1, source_target_pairs={{0,2},{1,3},{2,0},{3,1},{4,6},{5,7},{6,4},{7,5},{8,10},{9,11},{10,... | collective-permute-start | bytes 983048 | tf_op jit(solution)/shard_map/weight_y_early_1/ppermute | solution.py:439
  84.2 1.4 %collective-permute-done.35.refs_2_.refs_0_ = bf16[32,1024]{1,0:T(8,128)(2,1)S(1)} collective-permute-done((bf16[32,1024]{1,0:T(8,128)(2,1)S(1)}, bf16[32,1024]{1,0:T(8,128)(2,1)S(1)}, u32[]{:S(2)}, u32[]{:S(2)}) %collective-permute-start.35) | collective-permute-done | bytes 65568 | tf_op jit(solution)/shard_map/weight_ring_6/ppermute | solution.py:427
  85.7 1.6 %collective-permute-start.38 = (bf16[32,512]{1,0:T(8,128)(2,1)S(1)}, bf16[32,512]{1,0:T(8,128)(2,1)S(1)}, u32[]{:S(2)}, u32[]{:S(2)}) collective-permute-start(bf16[32,512]{1,0:T(8,128)(2,1)S(1)} %slice.14), channel_id=1, source_target_pairs={{0,4},{4,12},{12,20},{20,28},{28,24},{24,16},{16,8},{8,0},{1,5},{5... | collective-permute-start | bytes 98312 | tf_op jit(solution)/shard_map/weight_ring_7/ppermute | solution.py:427
  88.6 1.9 %collective-permute-start.42 = (bf16[128,1024]{1,0:T(8,128)(2,1)S(1)}, bf16[128,1024]{1,0:T(8,128)(2,1)S(1)}, u32[]{:S(2)}, u32[]{:S(2)}) collective-permute-start(bf16[128,1024]{1,0:T(8,128)(2,1)S(1)} %get-tuple-element.89), channel_id=1, source_target_pairs={{0,4},{4,12},{12,20},{20,28},{28,24},{24,16},{16,8},{8,0},{1,5},{5... | collective-permute-start | bytes 786440 | tf_op jit(solution)/shard_map/back_ring_3/ppermute | solution.py:427
  90.9 1.4 %collective-permute-done.40.refs_3_ = bf16[32,512]{1,0:T(8,128)(2,1)S(1)} collective-permute-done((bf16[32,512]{1,0:T(8,128)(2,1)S(1)}, bf16[32,512]{1,0:T(8,128)(2,1)S(1)}, u32[]{:S(2)}, u32[]{:S(2)}) %collective-permute-start.40) | collective-permute-done | bytes 32800 | tf_op jit(solution)/shard_map/weight_ring_7/ppermute | solution.py:427
  92.9 5.4 %collective-permute-done.44.refs_1_ = bf16[96,1024]{1,0:T(8,128)(2,1)S(1)} collective-permute-done((bf16[96,1024]{1,0:T(8,128)(2,1)S(1)}, bf16[96,1024]{1,0:T(8,128)(2,1)S(1)}, u32[]{:S(2)}, u32[]{:S(2)}) %collective-permute-start.44) | collective-permute-done | bytes 196640 | tf_op jit(solution)/shard_map/weight_y_late_1/ppermute | solution.py:439
  99.1 2.1 %join_weight.2 = (f32[1024,1024]{1,0:T(8,128)}, bf16[128,1024]{1,0:T(8,128)(2,1)}) custom-call(bf16[160,1024]{1,0:T(8,128)(2,1)S(1)} %stack_blocks.2.refs_0_, bf16[160,1024]{1,0:T(8,128)(2,1)S(1)} %collective-permute-done.32.refs_1_, bf16[160,1024]{1,0:T(8,128)(2,1)S(1)} %collective-permute-done.33.refs_4_.refs_2_, ...), custom_call_target="tpu_custom_call" | custom-call | flops 20000000000 | bytes 5111808 | tf_op jit(solution)/shard_map/join_weight/pallas_call | solution.py:51
  (104 shorter events, 31.2 us)
Async XLA Ops:
  0.6 9.6 %collective-permute-start = (bf16[128,1024]{1,0:T(8,128)(2,1)}, bf16[128,1024]{1,0:T(8,128)(2,1)S(1)}, u32[]{:S(2)}, u32[]{:S(2)}) collective-permute-start(bf16[128,1024]{1,0:T(8,128)(2,1)} %refs_4_.1), channel_id=1, source_target_pairs={{0,4},{4,12},{12,20},{20,28},{28,24},{24,16},{16,8},{8,0},{1,5},{5... | collective-permute-start | bytes 786440 | tf_op jit(solution)/shard_map/feature_ring_1/ppermute | solution.py:427
  3.6 8.3 %collective-permute-start.1 = (bf16[128,1024]{1,0:T(8,128)(2,1)}, bf16[128,1024]{1,0:T(8,128)(2,1)S(1)}, u32[]{:S(2)}, u32[]{:S(2)}) collective-permute-start(bf16[128,1024]{1,0:T(8,128)(2,1)} %refs_4_.1), channel_id=1, source_target_pairs={{0,8},{4,0},{12,4},{20,12},{28,20},{24,28},{16,24},{8,16},{1,9},{5... | collective-permute-start | bytes 786440 | tf_op jit(solution)/shard_map/feature_ring_1/ppermute | solution.py:427
  10.2 7.5 %collective-permute-start.2 = (bf16[128,1024]{1,0:T(8,128)(2,1)S(1)}, bf16[128,1024]{1,0:T(8,128)(2,1)S(1)}, u32[]{:S(2)}, u32[]{:S(2)}) collective-permute-start(bf16[128,1024]{1,0:T(8,128)(2,1)S(1)} %gate.2.refs_2_), channel_id=1, source_target_pairs={{0,4},{4,12},{12,20},{20,28},{28,24},{24,16},{16,8},{8,0},{1,5},{5... | collective-permute-start | bytes 786440 | tf_op jit(solution)/shard_map/feature_ring_2/ppermute | solution.py:427
  11.9 7.2 %collective-permute-start.3 = (bf16[128,1024]{1,0:T(8,128)(2,1)S(1)}, bf16[128,1024]{1,0:T(8,128)(2,1)S(1)}, u32[]{:S(2)}, u32[]{:S(2)}) collective-permute-start(bf16[128,1024]{1,0:T(8,128)(2,1)S(1)} %gate.3.refs_3_), channel_id=1, source_target_pairs={{0,8},{4,0},{12,4},{20,12},{28,20},{24,28},{16,24},{8,16},{1,9},{5... | collective-permute-start | bytes 786440 | tf_op jit(solution)/shard_map/feature_ring_2/ppermute | solution.py:427
  17.7 6.6 %collective-permute-start.4 = (bf16[128,1024]{1,0:T(8,128)(2,1)S(1)}, bf16[128,1024]{1,0:T(8,128)(2,1)S(1)}, u32[]{:S(2)}, u32[]{:S(2)}) collective-permute-start(bf16[128,1024]{1,0:T(8,128)(2,1)S(1)} %collective-permute-done.2.refs_4_), channel_id=1, source_target_pairs={{0,4},{4,12},{12,20},{20,28},{28,24},{24,16},{16,8},{8,0},{1,5},{5... | collective-permute-start | bytes 786440 | tf_op jit(solution)/shard_map/feature_ring_3/ppermute | solution.py:427
  19.1 6.8 %collective-permute-start.5 = (bf16[128,1024]{1,0:T(8,128)(2,1)S(1)}, bf16[128,1024]{1,0:T(8,128)(2,1)S(1)}, u32[]{:S(2)}, u32[]{:S(2)}) collective-permute-start(bf16[128,1024]{1,0:T(8,128)(2,1)S(1)} %collective-permute-done.3.refs_5_), channel_id=1, source_target_pairs={{0,8},{4,0},{12,4},{20,12},{28,20},{24,28},{16,24},{8,16},{1,9},{5... | collective-permute-start | bytes 786440 | tf_op jit(solution)/shard_map/feature_ring_3/ppermute | solution.py:427
  19.8 8.0 %collective-permute-start.8 = (bf16[128,1024]{1,0:T(8,128)(2,1)S(1)}, bf16[128,1024]{1,0:T(8,128)(2,1)S(1)}, u32[]{:S(2)}, u32[]{:S(2)}) collective-permute-start(bf16[128,1024]{1,0:T(8,128)(2,1)S(1)} %copy-done.3), channel_id=1, source_target_pairs={{0,2},{1,3},{2,0},{3,1},{4,6},{5,7},{6,4},{7,5},{8,10},{9,11},{10,... | collective-permute-start | bytes 786440 | tf_op jit(solution)/shard_map/cotangent_y/ppermute | solution.py:439
  24.3 5.0 %collective-permute-start.6 = (bf16[128,512]{1,0:T(8,128)(2,1)S(1)}, bf16[128,512]{1,0:T(8,128)(2,1)S(1)}, u32[]{:S(2)}, u32[]{:S(2)}) collective-permute-start(bf16[128,512]{1,0:T(8,128)(2,1)S(1)} %slice.16), channel_id=1, source_target_pairs={{0,4},{4,12},{12,20},{20,28},{28,24},{24,16},{16,8},{8,0},{1,5},{5... | collective-permute-start | bytes 393224 | tf_op jit(solution)/shard_map/feature_ring_4/ppermute | solution.py:427
  25.9 5.0 %collective-permute-start.7 = (bf16[128,512]{1,0:T(8,128)(2,1)S(1)}, bf16[128,512]{1,0:T(8,128)(2,1)S(1)}, u32[]{:S(2)}, u32[]{:S(2)}) collective-permute-start(bf16[128,512]{1,0:T(8,128)(2,1)S(1)} %slice.17), channel_id=1, source_target_pairs={{0,8},{4,0},{12,4},{20,12},{28,20},{24,28},{16,24},{8,16},{1,9},{5... | collective-permute-start | bytes 393224 | tf_op jit(solution)/shard_map/feature_ring_4/ppermute | solution.py:427
  33.0 9.2 %collective-permute-start.11 = (bf16[128,1024]{1,0:T(8,128)(2,1)S(1)}, bf16[128,1024]{1,0:T(8,128)(2,1)S(1)}, u32[]{:S(2)}, u32[]{:S(2)}) collective-permute-start(bf16[128,1024]{1,0:T(8,128)(2,1)S(1)} %add_convert_fusion.refs_0_), channel_id=1, source_target_pairs={{0,2},{1,3},{2,0},{3,1},{4,6},{5,7},{6,4},{7,5},{8,10},{9,11},{10,... | collective-permute-start | bytes 786440 | tf_op jit(solution)/shard_map/sum_y_own_1/ppermute | solution.py:439
  34.6 12.4 %collective-permute-start.12 = (bf16[128,1024]{1,0:T(8,128)(2,1)S(1)}, bf16[128,1024]{1,0:T(8,128)(2,1)S(1)}, u32[]{:S(2)}, u32[]{:S(2)}) collective-permute-start(bf16[128,1024]{1,0:T(8,128)(2,1)S(1)} %add_convert_fusion.1.refs_0_), channel_id=1, source_target_pairs={{0,2},{1,3},{2,0},{3,1},{4,6},{5,7},{6,4},{7,5},{8,10},{9,11},{10,... | collective-permute-start | bytes 786440 | tf_op jit(solution)/shard_map/sum_y_rest_1/ppermute | solution.py:439
  48.0 8.2 %collective-permute-start.19 = (bf16[128,1024]{1,0:T(8,128)(2,1)S(1)}, bf16[128,1024]{1,0:T(8,128)(2,1)S(1)}, u32[]{:S(2)}, u32[]{:S(2)}) collective-permute-start(bf16[128,1024]{1,0:T(8,128)(2,1)S(1)} %get-tuple-element.68.refs_1_), channel_id=1, source_target_pairs={{0,1},{1,0},{2,3},{3,2},{4,5},{5,4},{6,7},{7,6},{8,9},{9,8},{10,11... | collective-permute-start | bytes 786440 | tf_op jit(solution)/shard_map/back_core_own/ppermute | solution.py:435
  49.3 6.9 %collective-permute-start.20 = (bf16[128,1024]{1,0:T(8,128)(2,1)S(1)}, bf16[128,1024]{1,0:T(8,128)(2,1)S(1)}, u32[]{:S(2)}, u32[]{:S(2)}) collective-permute-start(bf16[128,1024]{1,0:T(8,128)(2,1)S(1)} %back_of.1.refs_2_), channel_id=1, source_target_pairs={{0,1},{1,0},{2,3},{3,2},{4,5},{5,4},{6,7},{7,6},{8,9},{9,8},{10,11... | collective-permute-start | bytes 786440 | tf_op jit(solution)/shard_map/back_core_rest/ppermute | solution.py:435
  54.0 5.5 %collective-permute-start.17 = (bf16[32,1024]{1,0:T(8,128)(2,1)S(1)}, bf16[32,1024]{1,0:T(8,128)(2,1)S(1)}, u32[]{:S(2)}, u32[]{:S(2)}) collective-permute-start(bf16[32,1024]{1,0:T(8,128)(2,1)S(1)} %add_round.12), channel_id=1, source_target_pairs={{0,8},{4,0},{12,4},{20,12},{28,20},{24,28},{16,24},{8,16},{1,9},{5... | collective-permute-start | bytes 196616 | tf_op jit(solution)/shard_map/weight_ring_1/ppermute | solution.py:427
  54.6 5.0 %collective-permute-start.15 = (bf16[32,1024]{1,0:T(8,128)(2,1)S(1)}, bf16[32,1024]{1,0:T(8,128)(2,1)S(1)}, u32[]{:S(2)}, u32[]{:S(2)}) collective-permute-start(bf16[32,1024]{1,0:T(8,128)(2,1)S(1)} %add_round.11), channel_id=1, source_target_pairs={{0,4},{4,12},{12,20},{20,28},{28,24},{24,16},{16,8},{8,0},{1,5},{5... | collective-permute-start | bytes 196616 | tf_op jit(solution)/shard_map/weight_ring_1/ppermute | solution.py:427
  57.5 5.0 %collective-permute-start.21 = (bf16[128,512]{1,0:T(8,128)(2,1)S(1)}, bf16[128,512]{1,0:T(8,128)(2,1)S(1)}, u32[]{:S(2)}, u32[]{:S(2)}) collective-permute-start(bf16[128,512]{1,0:T(8,128)(2,1)S(1)} %get-tuple-element.71), channel_id=1, source_target_pairs={{0,4},{4,12},{12,20},{20,28},{28,24},{24,16},{16,8},{8,0},{1,5},{5... | collective-permute-start | bytes 393224 | tf_op jit(solution)/shard_map/back_ring_0/ppermute | solution.py:427
  59.1 5.0 %collective-permute-start.22 = (bf16[128,512]{1,0:T(8,128)(2,1)S(1)}, bf16[128,512]{1,0:T(8,128)(2,1)S(1)}, u32[]{:S(2)}, u32[]{:S(2)}) collective-permute-start(bf16[128,512]{1,0:T(8,128)(2,1)S(1)} %get-tuple-element.73), channel_id=1, source_target_pairs={{0,8},{4,0},{12,4},{20,12},{28,20},{24,28},{16,24},{8,16},{1,9},{5... | collective-permute-start | bytes 393224 | tf_op jit(solution)/shard_map/back_ring_0/ppermute | solution.py:427
  64.2 5.1 %collective-permute-start.23 = (bf16[32,1024]{1,0:T(8,128)(2,1)S(1)}, bf16[32,1024]{1,0:T(8,128)(2,1)S(1)}, u32[]{:S(2)}, u32[]{:S(2)}) collective-permute-start(bf16[32,1024]{1,0:T(8,128)(2,1)S(1)} %add_round.15), channel_id=1, source_target_pairs={{0,4},{4,12},{12,20},{20,28},{28,24},{24,16},{16,8},{8,0},{1,5},{5... | collective-permute-start | bytes 196616 | tf_op jit(solution)/shard_map/weight_ring_3/ppermute | solution.py:427
  65.8 5.1 %collective-permute-start.25 = (bf16[32,1024]{1,0:T(8,128)(2,1)S(1)}, bf16[32,1024]{1,0:T(8,128)(2,1)S(1)}, u32[]{:S(2)}, u32[]{:S(2)}) collective-permute-start(bf16[32,1024]{1,0:T(8,128)(2,1)S(1)} %add_round.16), channel_id=1, source_target_pairs={{0,8},{4,0},{12,4},{20,12},{28,20},{24,28},{16,24},{8,16},{1,9},{5... | collective-permute-start | bytes 196616 | tf_op jit(solution)/shard_map/weight_ring_3/ppermute | solution.py:427
  66.4 9.8 %collective-permute-start.28 = (bf16[128,1024]{1,0:T(8,128)(2,1)S(1)}, bf16[128,1024]{1,0:T(8,128)(2,1)S(1)}, u32[]{:S(2)}, u32[]{:S(2)}) collective-permute-start(bf16[128,1024]{1,0:T(8,128)(2,1)S(1)} %get-tuple-element.75.refs_2_), channel_id=1, source_target_pairs={{0,4},{4,12},{12,20},{20,28},{28,24},{24,16},{16,8},{8,0},{1,5},{5... | collective-permute-start | bytes 786440 | tf_op jit(solution)/shard_map/back_ring_1/ppermute | solution.py:427
  67.9 8.3 %collective-permute-start.29 = (bf16[128,1024]{1,0:T(8,128)(2,1)S(1)}, bf16[128,1024]{1,0:T(8,128)(2,1)S(1)}, u32[]{:S(2)}, u32[]{:S(2)}) collective-permute-start(bf16[128,1024]{1,0:T(8,128)(2,1)S(1)} %get-tuple-element.79), channel_id=1, source_target_pairs={{0,8},{4,0},{12,4},{20,12},{28,20},{24,28},{16,24},{8,16},{1,9},{5... | collective-permute-start | bytes 786440 | tf_op jit(solution)/shard_map/back_ring_1/ppermute | solution.py:427
  71.5 4.7 %collective-permute-start.26 = (bf16[32,1024]{1,0:T(8,128)(2,1)S(1)}, bf16[32,1024]{1,0:T(8,128)(2,1)S(1)}, u32[]{:S(2)}, u32[]{:S(2)}) collective-permute-start(bf16[32,1024]{1,0:T(8,128)(2,1)S(1)} %end_sum.1.refs_0_), channel_id=1, source_target_pairs={{0,4},{4,12},{12,20},{20,28},{28,24},{24,16},{16,8},{8,0},{1,5},{5... | collective-permute-start | bytes 196616 | tf_op jit(solution)/shard_map/weight_ring_4/ppermute | solution.py:427
  78.3 7.3 %collective-permute-start.37 = (bf16[128,1024]{1,0:T(8,128)(2,1)S(1)}, bf16[128,1024]{1,0:T(8,128)(2,1)S(1)}, u32[]{:S(2)}, u32[]{:S(2)}) collective-permute-start(bf16[128,1024]{1,0:T(8,128)(2,1)S(1)} %get-tuple-element.83), channel_id=1, source_target_pairs={{0,4},{4,12},{12,20},{20,28},{28,24},{24,16},{16,8},{8,0},{1,5},{5... | collective-permute-start | bytes 786440 | tf_op jit(solution)/shard_map/back_ring_2/ppermute | solution.py:427
  79.9 8.4 %collective-permute-start.39 = (bf16[128,1024]{1,0:T(8,128)(2,1)S(1)}, bf16[128,1024]{1,0:T(8,128)(2,1)S(1)}, u32[]{:S(2)}, u32[]{:S(2)}) collective-permute-start(bf16[128,1024]{1,0:T(8,128)(2,1)S(1)} %get-tuple-element.86), channel_id=1, source_target_pairs={{0,8},{4,0},{12,4},{20,12},{28,20},{24,28},{16,24},{8,16},{1,9},{5... | collective-permute-start | bytes 786440 | tf_op jit(solution)/shard_map/back_ring_2/ppermute | solution.py:427
  80.6 5.1 %collective-permute-start.35 = (bf16[32,1024]{1,0:T(8,128)(2,1)S(1)}, bf16[32,1024]{1,0:T(8,128)(2,1)S(1)}, u32[]{:S(2)}, u32[]{:S(2)}) collective-permute-start(bf16[32,1024]{1,0:T(8,128)(2,1)S(1)} %add_round.18), channel_id=1, source_target_pairs={{0,4},{4,12},{12,20},{20,28},{28,24},{24,16},{16,8},{8,0},{1,5},{5... | collective-permute-start | bytes 196616 | tf_op jit(solution)/shard_map/weight_ring_6/ppermute | solution.py:427
  82.1 8.8 %collective-permute-start.33 = (bf16[160,1024]{1,0:T(8,128)(2,1)S(1)}, bf16[160,1024]{1,0:T(8,128)(2,1)S(1)}, u32[]{:S(2)}, u32[]{:S(2)}) collective-permute-start(bf16[160,1024]{1,0:T(8,128)(2,1)S(1)} %stack_blocks.2.refs_0_), channel_id=1, source_target_pairs={{0,2},{1,3},{2,0},{3,1},{4,6},{5,7},{6,4},{7,5},{8,10},{9,11},{10,... | collective-permute-start | bytes 983048 | tf_op jit(solution)/shard_map/weight_y_early_1/ppermute | solution.py:439
  85.7 4.8 %collective-permute-start.38 = (bf16[32,512]{1,0:T(8,128)(2,1)S(1)}, bf16[32,512]{1,0:T(8,128)(2,1)S(1)}, u32[]{:S(2)}, u32[]{:S(2)}) collective-permute-start(bf16[32,512]{1,0:T(8,128)(2,1)S(1)} %slice.14), channel_id=1, source_target_pairs={{0,4},{4,12},{12,20},{20,28},{28,24},{24,16},{16,8},{8,0},{1,5},{5... | collective-permute-start | bytes 98312 | tf_op jit(solution)/shard_map/weight_ring_7/ppermute | solution.py:427
  88.6 9.7 %collective-permute-start.42 = (bf16[128,1024]{1,0:T(8,128)(2,1)S(1)}, bf16[128,1024]{1,0:T(8,128)(2,1)S(1)}, u32[]{:S(2)}, u32[]{:S(2)}) collective-permute-start(bf16[128,1024]{1,0:T(8,128)(2,1)S(1)} %get-tuple-element.89), channel_id=1, source_target_pairs={{0,4},{4,12},{12,20},{20,28},{28,24},{24,16},{16,8},{8,0},{1,5},{5... | collective-permute-start | bytes 786440 | tf_op jit(solution)/shard_map/back_ring_3/ppermute | solution.py:427
  90.5 8.6 %collective-permute-start.43 = (bf16[128,1024]{1,0:T(8,128)(2,1)S(1)}, bf16[128,1024]{1,0:T(8,128)(2,1)S(1)}, u32[]{:S(2)}, u32[]{:S(2)}) collective-permute-start(bf16[128,1024]{1,0:T(8,128)(2,1)S(1)} %get-tuple-element.90), channel_id=1, source_target_pairs={{0,8},{4,0},{12,4},{20,12},{28,20},{24,28},{16,24},{8,16},{1,9},{5... | collective-permute-start | bytes 786440 | tf_op jit(solution)/shard_map/back_ring_3/ppermute | solution.py:427
  90.9 8.2 %collective-permute-start.34 = (bf16[160,1024]{1,0:T(8,128)(2,1)S(1)}, bf16[160,1024]{1,0:T(8,128)(2,1)S(1)}, u32[]{:S(2)}, u32[]{:S(2)}) collective-permute-start(bf16[160,1024]{1,0:T(8,128)(2,1)S(1)} %collective-permute-done.33.refs_4_.refs_2_), channel_id=1, source_target_pairs={{0,1},{1,0},{2,3},{3,2},{4,5},{5,4},{6,7},{7,6},{8,9},{9,8},{10,11... | collective-permute-start | bytes 983048 | tf_op jit(solution)/shard_map/weight_last/ppermute | solution.py:435
  92.3 6.0 %collective-permute-start.44 = (bf16[96,1024]{1,0:T(8,128)(2,1)S(1)}, bf16[96,1024]{1,0:T(8,128)(2,1)S(1)}, u32[]{:S(2)}, u32[]{:S(2)}) collective-permute-start(bf16[96,1024]{1,0:T(8,128)(2,1)S(1)} %stack_blocks.3.refs_4_), channel_id=1, source_target_pairs={{0,2},{1,3},{2,0},{3,1},{4,6},{5,7},{6,4},{7,5},{8,10},{9,11},{10,... | collective-permute-start | bytes 589832 | tf_op jit(solution)/shard_map/weight_y_late_1/ppermute | solution.py:439
  92.9 6.2 %collective-permute-start.41 = (bf16[96,1024]{1,0:T(8,128)(2,1)S(1)}, bf16[96,1024]{1,0:T(8,128)(2,1)S(1)}, u32[]{:S(2)}, u32[]{:S(2)}) collective-permute-start(bf16[96,1024]{1,0:T(8,128)(2,1)S(1)} %stack_blocks.3.refs_4_), channel_id=1, source_target_pairs={{0,1},{1,0},{2,3},{3,2},{4,5},{5,4},{6,7},{7,6},{8,9},{9,8},{10,11... | collective-permute-start | bytes 589832 | tf_op jit(solution)/shard_map/weight_last/ppermute | solution.py:435
  (20 other events, 83.6 us)

commit v7 on v6

--- a/solution.py
+++ b/solution.py
@@ -202,7 +202,7 @@
     def kernel(*refs):
         held_ref, weight_ref = refs[0], refs[1 + len(arrived)]
         cot_refs = refs[2 + len(arrived) : 2 + len(arrived) + len(cotangents)]
-        agg_ref, grad_ref, near_ref, far_ref, rest_ref, agg, grad = refs[-7:]
+        agg_ref, grad_ref, far_ref, rest_ref, agg, grad = refs[-6:]
         _, group, core = position(spot)
         total = held_ref[...].astype(jnp.float32)
         for ref in refs[1 : 1 + len(arrived)]:
@@ -216,29 +216,40 @@
             grad[(g + 1) * side : (g + 2) * side] = piece
         first = group * part
         far_at = pl.multiple_of(first + (1 - core) * quarter, 128)
-        near_at = pl.multiple_of(first + core * quarter, 128)
         far_ref[...] = lax.dot_general(
             agg[:, pl.ds(far_at, quarter)], grad[...], (((0,), (0,)), ((), ())), preferred_element_type=jnp.float32
         ).astype(jnp.bfloat16)
-        near_ref[...] = lax.dot_general(
-            agg[:, pl.ds(near_at, quarter)], grad[...], (((0,), (0,)), ((), ())), preferred_element_type=jnp.float32
-        )
         rest_ref[...] = grad[side:]
 
     shapes = [
-        jax.ShapeDtypeStruct((quarter, cols), jnp.float32),
         jax.ShapeDtypeStruct((quarter, cols), jnp.bfloat16),
         jax.ShapeDtypeStruct((rows, cols), jnp.bfloat16),
+        jax.ShapeDtypeStruct((side + rows, depth), jnp.bfloat16),
+        jax.ShapeDtypeStruct((side + rows, cols), jnp.bfloat16),
     ]
     return vmem_call(
         "dense_rest",
         kernel,
         shapes,
         (held, *arrived, weight, *cotangents, agg_own, grad_own),
-        scratch=[pltpu.VMEM((side + rows, depth), jnp.bfloat16), pltpu.VMEM((side + rows, cols), jnp.bfloat16)],
         flops=4 * rows * cols * depth + 2 * (rows + side) * part * cols,
         moved=2 * (depth * cols + 6 * rows * depth),
     )
+
+
+def own_share(spot, agg, grad, groups):
+    depth, cols = agg.shape[1], grad.shape[1]
+    quarter = depth // (2 * groups)
+
+    def kernel(agg_ref, grad_ref, out_ref):
+        _, group, core = position(spot)
+        at = pl.multiple_of((group * 2 + core) * quarter, 128)
+        out_ref[...] = lax.dot_general(
+            agg_ref[:, pl.ds(at, quarter)], grad_ref[...], (((0,), (0,)), ((), ())), preferred_element_type=jnp.float32
+        )
+
+    shape = jax.ShapeDtypeStruct((quarter, cols), jnp.float32)
+    return vmem_call("own_share", kernel, shape, (agg, grad), flops=2 * agg.shape[0] * quarter * cols, moved=4 * agg.size)
 
 
 def back_of(grad, weight):
@@ -463,8 +474,9 @@
         arrived_rest.append(from_group(f"sum_y_rest_{s}", jnp.concatenate(sent) if len(sent) > 1 else sent[0], s))
     activated, agg_own, grad_own, back_own = dense_own(own, arrived_own, weight, cotangents[0])
     turned = [cotangents[groups - g] for g in range(1, groups)]
-    near_weight, far_weight, grad_rest = dense_rest(spot, rest, arrived_rest, weight, turned, agg_own, grad_own)
-
+    far_weight, grad_rest, agg, grad = dense_rest(spot, rest, arrived_rest, weight, turned, agg_own, grad_own)
+
+    near_weight = own_share(spot, agg, grad, groups)
     far_weight = swap_core("weight_core", far_weight)
     back_rest = back_of(grad_rest, weight)
     far_back = [swap_core("back_core_own", back_own), swap_core("back_core_rest", back_rest)]

time: 102 us -> 102 us (level)
  waiting for transfers between devices: 45.1 us -> 42.9 us
  starting transfers between devices: 41.2 us -> 42.6 us
    ppermute x16, waiting for transfers between devices: 12.2 us -> 10.5 us  [go(): lax.ppermute(left, 'row', to_left)]
    pallas_call x26 -> x27, Pallas kernels: 10.8 us -> 11 us  [vmem_call(): pl.pallas_call(inner, out_shape=out_shapes, in_specs=specs, out_specs=jax...]
  transfers between devices with their start and end apart: 46 -> 46, of which waited for: 23 -> 23; matrix products, arithmetic and copies ran while one was open for 0% -> 0% of each run, Pallas kernels for 8% -> 9%
where the time goes in v7:
time: 102 us
  waiting for transfers between devices  42.9 us (42%)
  starting transfers between devices  42.6 us (42%)
  Pallas kernels  11 us (11%)
  local copies, waits for them, and re-layouts  3.51 us (3%)
  between operations  1.53 us (2%)
    ppermute x16, starting transfers between devices, go(): lax.ppermute(right, 'row', to_right)  27.1 us
    ppermute x5, waiting for transfers between devices, from_group(): lax.ppermute(value, 'col', [(k, (k + 2 * steps) % columns) for k in range...  15.7 us
    ppermute x16, waiting for transfers between devices, go(): lax.ppermute(right, 'row', to_right)  15.6 us
    pallas_call x27, Pallas kernels, vmem_call(): pl.pallas_call(inner, out_shape=out_shapes, in_specs=specs, out_specs=jax...  11 us
    ppermute x16, waiting for transfers between devices, go(): lax.ppermute(left, 'row', to_left)  10.5 us
    ppermute x16, starting transfers between devices, go(): lax.ppermute(left, 'row', to_left)  7.95 us
    ppermute x5, starting transfers between devices, from_group(): lax.ppermute(value, 'col', [(k, (k + 2 * steps) % columns) for k in range...  6.12 us
    unnamed x12, local copies, waits for them, and re-layouts  3.48 us
  transfers between devices with their start and end apart: 46, of which 23 were waited for; matrix products, arithmetic and copies ran while one was open for 0% of the time, Pallas kernels for 9%

profile of v7, /device:TPU:0, one launch (start us, length us, event | category | flops | bytes accessed | tf_op | source)
XLA Modules:
  0.0 101.6 jit_solution(8853321353202405056)
XLA Ops:
  0.6 3.0 %collective-permute-start = (bf16[128,1024]{1,0:T(8,128)(2,1)}, bf16[128,1024]{1,0:T(8,128)(2,1)S(1)}, u32[]{:S(2)}, u32[]{:S(2)}) collective-permute-start(bf16[128,1024]{1,0:T(8,128)(2,1)} %refs_4_.1), channel_id=1, source_target_pairs={{0,4},{4,12},{12,20},{20,28},{28,24},{24,16},{16,8},{8,0},{1,5},{5... | collective-permute-start | bytes 786440 | tf_op jit(solution)/shard_map/feature_ring_1/ppermute | solution.py:438
  8.8 1.4 %collective-permute-done.refs_0_ = bf16[128,1024]{1,0:T(8,128)(2,1)S(1)} collective-permute-done((bf16[128,1024]{1,0:T(8,128)(2,1)}, bf16[128,1024]{1,0:T(8,128)(2,1)S(1)}, u32[]{:S(2)}, u32[]{:S(2)}) %collective-permute-start) | collective-permute-done | bytes 262176 | tf_op jit(solution)/shard_map/feature_ring_1/ppermute | solution.py:438
  10.2 1.7 %collective-permute-start.2 = (bf16[128,1024]{1,0:T(8,128)(2,1)S(1)}, bf16[128,1024]{1,0:T(8,128)(2,1)S(1)}, u32[]{:S(2)}, u32[]{:S(2)}) collective-permute-start(bf16[128,1024]{1,0:T(8,128)(2,1)S(1)} %gate.2.refs_2_), channel_id=1, source_target_pairs={{0,4},{4,12},{12,20},{20,28},{28,24},{24,16},{16,8},{8,0},{1,5},{5... | collective-permute-start | bytes 786440 | tf_op jit(solution)/shard_map/feature_ring_2/ppermute | solution.py:438
  12.3 5.5 %collective-permute-done.2.refs_4_ = bf16[128,1024]{1,0:T(8,128)(2,1)S(1)} collective-permute-done((bf16[128,1024]{1,0:T(8,128)(2,1)S(1)}, bf16[128,1024]{1,0:T(8,128)(2,1)S(1)}, u32[]{:S(2)}, u32[]{:S(2)}) %collective-permute-start.2) | collective-permute-done | bytes 262176 | tf_op jit(solution)/shard_map/feature_ring_2/ppermute | solution.py:438
  21.1 3.2 %collective-permute-done.4.refs_6_ = bf16[128,1024]{1,0:T(8,128)(2,1)S(1)} collective-permute-done((bf16[128,1024]{1,0:T(8,128)(2,1)S(1)}, bf16[128,1024]{1,0:T(8,128)(2,1)S(1)}, u32[]{:S(2)}, u32[]{:S(2)}) %collective-permute-start.4) | collective-permute-done | bytes 262176 | tf_op jit(solution)/shard_map/feature_ring_3/ppermute | solution.py:438
  24.3 1.6 %collective-permute-start.6 = (bf16[128,512]{1,0:T(8,128)(2,1)S(1)}, bf16[128,512]{1,0:T(8,128)(2,1)S(1)}, u32[]{:S(2)}, u32[]{:S(2)}) collective-permute-start(bf16[128,512]{1,0:T(8,128)(2,1)S(1)} %slice.16), channel_id=1, source_target_pairs={{0,4},{4,12},{12,20},{20,28},{28,24},{24,16},{16,8},{8,0},{1,5},{5... | collective-permute-start | bytes 393224 | tf_op jit(solution)/shard_map/feature_ring_4/ppermute | solution.py:438
  27.7 1.6 %collective-permute-done.6.refs_2_ = bf16[128,512]{1,0:T(8,128)(2,1)S(1)} collective-permute-done((bf16[128,512]{1,0:T(8,128)(2,1)S(1)}, bf16[128,512]{1,0:T(8,128)(2,1)S(1)}, u32[]{:S(2)}, u32[]{:S(2)}) %collective-permute-start.6) | collective-permute-done | bytes 131104 | tf_op jit(solution)/shard_map/feature_ring_4/ppermute | solution.py:438
  29.3 1.6 %collective-permute-done.7.refs_3_ = bf16[128,512]{1,0:T(8,128)(2,1)S(1)} collective-permute-done((bf16[128,512]{1,0:T(8,128)(2,1)S(1)}, bf16[128,512]{1,0:T(8,128)(2,1)S(1)}, u32[]{:S(2)}, u32[]{:S(2)}) %collective-permute-start.7) | collective-permute-done | bytes 131104 | tf_op jit(solution)/shard_map/feature_ring_4/ppermute | solution.py:438
  33.0 1.6 %collective-permute-start.11 = (bf16[128,1024]{1,0:T(8,128)(2,1)S(1)}, bf16[128,1024]{1,0:T(8,128)(2,1)S(1)}, u32[]{:S(2)}, u32[]{:S(2)}) collective-permute-start(bf16[128,1024]{1,0:T(8,128)(2,1)S(1)} %add_convert_fusion.refs_0_), channel_id=1, source_target_pairs={{0,2},{1,3},{2,0},{3,1},{4,6},{5,7},{6,4},{7,5},{8,10},{9,11},{10,... | collective-permute-start | bytes 786440 | tf_op jit(solution)/shard_map/sum_y_own_1/ppermute | solution.py:450
  35.2 7.0 %collective-permute-done.11.refs_1_ = bf16[128,1024]{1,0:T(8,128)(2,1)S(1)} collective-permute-done((bf16[128,1024]{1,0:T(8,128)(2,1)S(1)}, bf16[128,1024]{1,0:T(8,128)(2,1)S(1)}, u32[]{:S(2)}, u32[]{:S(2)}) %collective-permute-start.11) | collective-permute-done | bytes 262176 | tf_op jit(solution)/shard_map/sum_y_own_1/ppermute | solution.py:450
  42.2 1.7 %dense_own.1 = (bf16[128,1024]{1,0:T(8,128)(2,1)}, bf16[128,1024]{1,0:T(8,128)(2,1)S(1)}, bf16[128,1024]{1,0:T(8,128)(2,1)S(1)}, bf16[128,1024]{1,0:T(8,128)(2,1)S(1)}) custom-call(bf16[128,1024]{1,0:T(8,128)(2,1)S(1)} %add_convert_fusion.1.refs_0_, bf16[128,1024]{1,0:T(8,128)(2,1)S(1)} %collective-permute-done.11.refs_1_, bf16[1024,1024]{1,0:T(8,128)(2,1)S(1)} %copy-done, ...), custom_call_target="tpu_custom_call" | custom-call | flops 536870912 | bytes 3670016 | tf_op jit(solution)/shard_map/dense_own/pallas_call | solution.py:51
  43.9 3.1 %collective-permute-done.12.refs_1_ = bf16[128,1024]{1,0:T(8,128)(2,1)S(1)} collective-permute-done((bf16[128,1024]{1,0:T(8,128)(2,1)S(1)}, bf16[128,1024]{1,0:T(8,128)(2,1)S(1)}, u32[]{:S(2)}, u32[]{:S(2)}) %collective-permute-start.12) | collective-permute-done | bytes 262176 | tf_op jit(solution)/shard_map/sum_y_rest_1/ppermute | solution.py:450
  50.5 1.5 %collective-permute-start.14 = (bf16[32,512]{1,0:T(8,128)(2,1)S(1)}, bf16[32,512]{1,0:T(8,128)(2,1)S(1)}, u32[]{:S(2)}, u32[]{:S(2)}) collective-permute-start(bf16[32,512]{1,0:T(8,128)(2,1)S(1)} %get-tuple-element.65), channel_id=1, source_target_pairs={{0,4},{4,12},{12,20},{20,28},{28,24},{24,16},{16,8},{8,0},{1,5},{5... | collective-permute-start | bytes 98312 | tf_op jit(solution)/shard_map/weight_ring_0/ppermute | solution.py:438
  52.0 1.9 %collective-permute-done.16.refs_1_ = bf16[32,512]{1,0:T(8,128)(2,1)S(1)} collective-permute-done((bf16[32,512]{1,0:T(8,128)(2,1)S(1)}, bf16[32,512]{1,0:T(8,128)(2,1)S(1)}, u32[]{:S(2)}, u32[]{:S(2)}) %collective-permute-start.16) | collective-permute-done | bytes 32800 | tf_op jit(solution)/shard_map/weight_ring_0/ppermute | solution.py:438
  54.5 1.6 %collective-permute-start.15 = (bf16[32,1024]{1,0:T(8,128)(2,1)S(1)}, bf16[32,1024]{1,0:T(8,128)(2,1)S(1)}, u32[]{:S(2)}, u32[]{:S(2)}) collective-permute-start(bf16[32,1024]{1,0:T(8,128)(2,1)S(1)} %add_round.11), channel_id=1, source_target_pairs={{0,4},{4,12},{12,20},{20,28},{28,24},{24,16},{16,8},{8,0},{1,5},{5... | collective-permute-start | bytes 196616 | tf_op jit(solution)/shard_map/weight_ring_1/ppermute | solution.py:438
  57.4 1.6 %collective-permute-start.21 = (bf16[128,512]{1,0:T(8,128)(2,1)S(1)}, bf16[128,512]{1,0:T(8,128)(2,1)S(1)}, u32[]{:S(2)}, u32[]{:S(2)}) collective-permute-start(bf16[128,512]{1,0:T(8,128)(2,1)S(1)} %get-tuple-element.73), channel_id=1, source_target_pairs={{0,4},{4,12},{12,20},{20,28},{28,24},{24,16},{16,8},{8,0},{1,5},{5... | collective-permute-start | bytes 393224 | tf_op jit(solution)/shard_map/back_ring_0/ppermute | solution.py:438
  59.5 1.6 %collective-permute-start.18 = (bf16[32,1024]{1,0:T(8,128)(2,1)S(1)}, bf16[32,1024]{1,0:T(8,128)(2,1)S(1)}, u32[]{:S(2)}, u32[]{:S(2)}) collective-permute-start(bf16[32,1024]{1,0:T(8,128)(2,1)S(1)} %get-tuple-element.69.refs_4_), channel_id=1, source_target_pairs={{0,4},{4,12},{12,20},{20,28},{28,24},{24,16},{16,8},{8,0},{1,5},{5... | collective-permute-start | bytes 196616 | tf_op jit(solution)/shard_map/weight_ring_2/ppermute | solution.py:438
  62.4 1.6 %collective-permute-done.22.refs_3_ = bf16[128,512]{1,0:T(8,128)(2,1)S(1)} collective-permute-done((bf16[128,512]{1,0:T(8,128)(2,1)S(1)}, bf16[128,512]{1,0:T(8,128)(2,1)S(1)}, u32[]{:S(2)}, u32[]{:S(2)}) %collective-permute-start.22) | collective-permute-done | bytes 131104 | tf_op jit(solution)/shard_map/back_ring_0/ppermute | solution.py:438
  64.0 1.6 %collective-permute-start.23 = (bf16[32,1024]{1,0:T(8,128)(2,1)S(1)}, bf16[32,1024]{1,0:T(8,128)(2,1)S(1)}, u32[]{:S(2)}, u32[]{:S(2)}) collective-permute-start(bf16[32,1024]{1,0:T(8,128)(2,1)S(1)} %add_round.15), channel_id=1, source_target_pairs={{0,4},{4,12},{12,20},{20,28},{28,24},{24,16},{16,8},{8,0},{1,5},{5... | collective-permute-start | bytes 196616 | tf_op jit(solution)/shard_map/weight_ring_3/ppermute | solution.py:438
  66.2 1.6 %collective-permute-start.28 = (bf16[128,1024]{1,0:T(8,128)(2,1)S(1)}, bf16[128,1024]{1,0:T(8,128)(2,1)S(1)}, u32[]{:S(2)}, u32[]{:S(2)}) collective-permute-start(bf16[128,1024]{1,0:T(8,128)(2,1)S(1)} %get-tuple-element.77.refs_2_), channel_id=1, source_target_pairs={{0,4},{4,12},{12,20},{20,28},{28,24},{24,16},{16,8},{8,0},{1,5},{5... | collective-permute-start | bytes 786440 | tf_op jit(solution)/shard_map/back_ring_1/ppermute | solution.py:438
  69.1 1.6 %collective-permute-done.25.refs_2_ = bf16[32,1024]{1,0:T(8,128)(2,1)S(1)} collective-permute-done((bf16[32,1024]{1,0:T(8,128)(2,1)S(1)}, bf16[32,1024]{1,0:T(8,128)(2,1)S(1)}, u32[]{:S(2)}, u32[]{:S(2)}) %collective-permute-start.25) | collective-permute-done | bytes 65568 | tf_op jit(solution)/shard_map/weight_ring_3/ppermute | solution.py:438
  71.3 1.6 %collective-permute-start.26 = (bf16[32,1024]{1,0:T(8,128)(2,1)S(1)}, bf16[32,1024]{1,0:T(8,128)(2,1)S(1)}, u32[]{:S(2)}, u32[]{:S(2)}) collective-permute-start(bf16[32,1024]{1,0:T(8,128)(2,1)S(1)} %end_sum.1.refs_0_), channel_id=1, source_target_pairs={{0,4},{4,12},{12,20},{20,28},{28,24},{24,16},{16,8},{8,0},{1,5},{5... | collective-permute-start | bytes 196616 | tf_op jit(solution)/shard_map/weight_ring_4/ppermute | solution.py:438
  72.9 2.2 %collective-permute-done.27.refs_5_.refs_2_ = bf16[32,1024]{1,0:T(8,128)(2,1)S(1)} collective-permute-done((bf16[32,1024]{1,0:T(8,128)(2,1)S(1)}, bf16[32,1024]{1,0:T(8,128)(2,1)S(1)}, u32[]{:S(2)}, u32[]{:S(2)}) %collective-permute-start.27) | collective-permute-done | bytes 65568 | tf_op jit(solution)/shard_map/weight_ring_4/ppermute | solution.py:438
  75.7 1.8 %collective-permute-start.30 = (bf16[32,1024]{1,0:T(8,128)(2,1)S(1)}, bf16[32,1024]{1,0:T(8,128)(2,1)S(1)}, u32[]{:S(2)}, u32[]{:S(2)}) collective-permute-start(bf16[32,1024]{1,0:T(8,128)(2,1)S(1)} %get-tuple-element.82), channel_id=1, source_target_pairs={{0,4},{4,12},{12,20},{20,28},{28,24},{24,16},{16,8},{8,0},{1,5},{5... | collective-permute-start | bytes 196616 | tf_op jit(solution)/shard_map/weight_ring_5/ppermute | solution.py:438
  77.9 1.6 %collective-permute-start.37 = (bf16[128,1024]{1,0:T(8,128)(2,1)S(1)}, bf16[128,1024]{1,0:T(8,128)(2,1)S(1)}, u32[]{:S(2)}, u32[]{:S(2)}) collective-permute-start(bf16[128,1024]{1,0:T(8,128)(2,1)S(1)} %get-tuple-element.85), channel_id=1, source_target_pairs={{0,4},{4,12},{12,20},{20,28},{28,24},{24,16},{16,8},{8,0},{1,5},{5... | collective-permute-start | bytes 786440 | tf_op jit(solution)/shard_map/back_ring_2/ppermute | solution.py:438
  80.1 1.6 %collective-permute-start.35 = (bf16[32,1024]{1,0:T(8,128)(2,1)S(1)}, bf16[32,1024]{1,0:T(8,128)(2,1)S(1)}, u32[]{:S(2)}, u32[]{:S(2)}) collective-permute-start(bf16[32,1024]{1,0:T(8,128)(2,1)S(1)} %add_round.18), channel_id=1, source_target_pairs={{0,4},{4,12},{12,20},{20,28},{28,24},{24,16},{16,8},{8,0},{1,5},{5... | collective-permute-start | bytes 196616 | tf_op jit(solution)/shard_map/weight_ring_6/ppermute | solution.py:438
  81.8 1.6 %collective-permute-start.33 = (bf16[160,1024]{1,0:T(8,128)(2,1)S(1)}, bf16[160,1024]{1,0:T(8,128)(2,1)S(1)}, u32[]{:S(2)}, u32[]{:S(2)}) collective-permute-start(bf16[160,1024]{1,0:T(8,128)(2,1)S(1)} %stack_blocks.2.refs_0_), channel_id=1, source_target_pairs={{0,2},{1,3},{2,0},{3,1},{4,6},{5,7},{6,4},{7,5},{8,10},{9,11},{10,... | collective-permute-start | bytes 983048 | tf_op jit(solution)/shard_map/weight_y_early_1/ppermute | solution.py:450
  83.8 1.5 %collective-permute-done.35.refs_2_.refs_0_ = bf16[32,1024]{1,0:T(8,128)(2,1)S(1)} collective-permute-done((bf16[32,1024]{1,0:T(8,128)(2,1)S(1)}, bf16[32,1024]{1,0:T(8,128)(2,1)S(1)}, u32[]{:S(2)}, u32[]{:S(2)}) %collective-permute-start.35) | collective-permute-done | bytes 65568 | tf_op jit(solution)/shard_map/weight_ring_6/ppermute | solution.py:438
  85.4 1.7 %collective-permute-start.38 = (bf16[32,512]{1,0:T(8,128)(2,1)S(1)}, bf16[32,512]{1,0:T(8,128)(2,1)S(1)}, u32[]{:S(2)}, u32[]{:S(2)}) collective-permute-start(bf16[32,512]{1,0:T(8,128)(2,1)S(1)} %slice.14), channel_id=1, source_target_pairs={{0,4},{4,12},{12,20},{20,28},{28,24},{24,16},{16,8},{8,0},{1,5},{5... | collective-permute-start | bytes 98312 | tf_op jit(solution)/shard_map/weight_ring_7/ppermute | solution.py:438
  88.2 1.8 %collective-permute-start.42 = (bf16[128,1024]{1,0:T(8,128)(2,1)S(1)}, bf16[128,1024]{1,0:T(8,128)(2,1)S(1)}, u32[]{:S(2)}, u32[]{:S(2)}) collective-permute-start(bf16[128,1024]{1,0:T(8,128)(2,1)S(1)} %get-tuple-element.91), channel_id=1, source_target_pairs={{0,4},{4,12},{12,20},{20,28},{28,24},{24,16},{16,8},{8,0},{1,5},{5... | collective-permute-start | bytes 786440 | tf_op jit(solution)/shard_map/back_ring_3/ppermute | solution.py:438
  92.8 5.6 %collective-permute-done.44.refs_1_ = bf16[96,1024]{1,0:T(8,128)(2,1)S(1)} collective-permute-done((bf16[96,1024]{1,0:T(8,128)(2,1)S(1)}, bf16[96,1024]{1,0:T(8,128)(2,1)S(1)}, u32[]{:S(2)}, u32[]{:S(2)}) %collective-permute-start.44) | collective-permute-done | bytes 196640 | tf_op jit(solution)/shard_map/weight_y_late_1/ppermute | solution.py:450
  98.6 2.1 %join_weight.2 = (f32[1024,1024]{1,0:T(8,128)}, bf16[128,1024]{1,0:T(8,128)(2,1)}) custom-call(bf16[160,1024]{1,0:T(8,128)(2,1)S(1)} %stack_blocks.2.refs_0_, bf16[160,1024]{1,0:T(8,128)(2,1)S(1)} %collective-permute-done.32.refs_1_, bf16[160,1024]{1,0:T(8,128)(2,1)S(1)} %collective-permute-done.33.refs_4_.refs_2_, ...), custom_call_target="tpu_custom_call" | custom-call | flops 20000000000 | bytes 5111808 | tf_op jit(solution)/shard_map/join_weight/pallas_call | solution.py:51
  (105 shorter events, 29.6 us)
Async XLA Ops:
  0.6 9.6 %collective-permute-start = (bf16[128,1024]{1,0:T(8,128)(2,1)}, bf16[128,1024]{1,0:T(8,128)(2,1)S(1)}, u32[]{:S(2)}, u32[]{:S(2)}) collective-permute-start(bf16[128,1024]{1,0:T(8,128)(2,1)} %refs_4_.1), channel_id=1, source_target_pairs={{0,4},{4,12},{12,20},{20,28},{28,24},{24,16},{16,8},{8,0},{1,5},{5... | collective-permute-start | bytes 786440 | tf_op jit(solution)/shard_map/feature_ring_1/ppermute | solution.py:438
  3.6 8.3 %collective-permute-start.1 = (bf16[128,1024]{1,0:T(8,128)(2,1)}, bf16[128,1024]{1,0:T(8,128)(2,1)S(1)}, u32[]{:S(2)}, u32[]{:S(2)}) collective-permute-start(bf16[128,1024]{1,0:T(8,128)(2,1)} %refs_4_.1), channel_id=1, source_target_pairs={{0,8},{4,0},{12,4},{20,12},{28,20},{24,28},{16,24},{8,16},{1,9},{5... | collective-permute-start | bytes 786440 | tf_op jit(solution)/shard_map/feature_ring_1/ppermute | solution.py:438
  10.2 7.5 %collective-permute-start.2 = (bf16[128,1024]{1,0:T(8,128)(2,1)S(1)}, bf16[128,1024]{1,0:T(8,128)(2,1)S(1)}, u32[]{:S(2)}, u32[]{:S(2)}) collective-permute-start(bf16[128,1024]{1,0:T(8,128)(2,1)S(1)} %gate.2.refs_2_), channel_id=1, source_target_pairs={{0,4},{4,12},{12,20},{20,28},{28,24},{24,16},{16,8},{8,0},{1,5},{5... | collective-permute-start | bytes 786440 | tf_op jit(solution)/shard_map/feature_ring_2/ppermute | solution.py:438
  11.9 7.2 %collective-permute-start.3 = (bf16[128,1024]{1,0:T(8,128)(2,1)S(1)}, bf16[128,1024]{1,0:T(8,128)(2,1)S(1)}, u32[]{:S(2)}, u32[]{:S(2)}) collective-permute-start(bf16[128,1024]{1,0:T(8,128)(2,1)S(1)} %gate.3.refs_3_), channel_id=1, source_target_pairs={{0,8},{4,0},{12,4},{20,12},{28,20},{24,28},{16,24},{8,16},{1,9},{5... | collective-permute-start | bytes 786440 | tf_op jit(solution)/shard_map/feature_ring_2/ppermute | solution.py:438
  17.7 6.6 %collective-permute-start.4 = (bf16[128,1024]{1,0:T(8,128)(2,1)S(1)}, bf16[128,1024]{1,0:T(8,128)(2,1)S(1)}, u32[]{:S(2)}, u32[]{:S(2)}) collective-permute-start(bf16[128,1024]{1,0:T(8,128)(2,1)S(1)} %collective-permute-done.2.refs_4_), channel_id=1, source_target_pairs={{0,4},{4,12},{12,20},{20,28},{28,24},{24,16},{16,8},{8,0},{1,5},{5... | collective-permute-start | bytes 786440 | tf_op jit(solution)/shard_map/feature_ring_3/ppermute | solution.py:438
  19.1 6.8 %collective-permute-start.5 = (bf16[128,1024]{1,0:T(8,128)(2,1)S(1)}, bf16[128,1024]{1,0:T(8,128)(2,1)S(1)}, u32[]{:S(2)}, u32[]{:S(2)}) collective-permute-start(bf16[128,1024]{1,0:T(8,128)(2,1)S(1)} %collective-permute-done.3.refs_5_), channel_id=1, source_target_pairs={{0,8},{4,0},{12,4},{20,12},{28,20},{24,28},{16,24},{8,16},{1,9},{5... | collective-permute-start | bytes 786440 | tf_op jit(solution)/shard_map/feature_ring_3/ppermute | solution.py:438
  19.8 8.0 %collective-permute-start.8 = (bf16[128,1024]{1,0:T(8,128)(2,1)S(1)}, bf16[128,1024]{1,0:T(8,128)(2,1)S(1)}, u32[]{:S(2)}, u32[]{:S(2)}) collective-permute-start(bf16[128,1024]{1,0:T(8,128)(2,1)S(1)} %copy-done.3), channel_id=1, source_target_pairs={{0,2},{1,3},{2,0},{3,1},{4,6},{5,7},{6,4},{7,5},{8,10},{9,11},{10,... | collective-permute-start | bytes 786440 | tf_op jit(solution)/shard_map/cotangent_y/ppermute | solution.py:450
  24.3 5.0 %collective-permute-start.6 = (bf16[128,512]{1,0:T(8,128)(2,1)S(1)}, bf16[128,512]{1,0:T(8,128)(2,1)S(1)}, u32[]{:S(2)}, u32[]{:S(2)}) collective-permute-start(bf16[128,512]{1,0:T(8,128)(2,1)S(1)} %slice.16), channel_id=1, source_target_pairs={{0,4},{4,12},{12,20},{20,28},{28,24},{24,16},{16,8},{8,0},{1,5},{5... | collective-permute-start | bytes 393224 | tf_op jit(solution)/shard_map/feature_ring_4/ppermute | solution.py:438
  25.9 5.0 %collective-permute-start.7 = (bf16[128,512]{1,0:T(8,128)(2,1)S(1)}, bf16[128,512]{1,0:T(8,128)(2,1)S(1)}, u32[]{:S(2)}, u32[]{:S(2)}) collective-permute-start(bf16[128,512]{1,0:T(8,128)(2,1)S(1)} %slice.17), channel_id=1, source_target_pairs={{0,8},{4,0},{12,4},{20,12},{28,20},{24,28},{16,24},{8,16},{1,9},{5... | collective-permute-start | bytes 393224 | tf_op jit(solution)/shard_map/feature_ring_4/ppermute | solution.py:438
  33.0 9.2 %collective-permute-start.11 = (bf16[128,1024]{1,0:T(8,128)(2,1)S(1)}, bf16[128,1024]{1,0:T(8,128)(2,1)S(1)}, u32[]{:S(2)}, u32[]{:S(2)}) collective-permute-start(bf16[128,1024]{1,0:T(8,128)(2,1)S(1)} %add_convert_fusion.refs_0_), channel_id=1, source_target_pairs={{0,2},{1,3},{2,0},{3,1},{4,6},{5,7},{6,4},{7,5},{8,10},{9,11},{10,... | collective-permute-start | bytes 786440 | tf_op jit(solution)/shard_map/sum_y_own_1/ppermute | solution.py:450
  34.6 12.4 %collective-permute-start.12 = (bf16[128,1024]{1,0:T(8,128)(2,1)S(1)}, bf16[128,1024]{1,0:T(8,128)(2,1)S(1)}, u32[]{:S(2)}, u32[]{:S(2)}) collective-permute-start(bf16[128,1024]{1,0:T(8,128)(2,1)S(1)} %add_convert_fusion.1.refs_0_), channel_id=1, source_target_pairs={{0,2},{1,3},{2,0},{3,1},{4,6},{5,7},{6,4},{7,5},{8,10},{9,11},{10,... | collective-permute-start | bytes 786440 | tf_op jit(solution)/shard_map/sum_y_rest_1/ppermute | solution.py:450
  47.9 8.2 %collective-permute-start.19 = (bf16[128,1024]{1,0:T(8,128)(2,1)S(1)}, bf16[128,1024]{1,0:T(8,128)(2,1)S(1)}, u32[]{:S(2)}, u32[]{:S(2)}) collective-permute-start(bf16[128,1024]{1,0:T(8,128)(2,1)S(1)} %get-tuple-element.70.refs_1_), channel_id=1, source_target_pairs={{0,1},{1,0},{2,3},{3,2},{4,5},{5,4},{6,7},{7,6},{8,9},{9,8},{10,11... | collective-permute-start | bytes 786440 | tf_op jit(solution)/shard_map/back_core_own/ppermute | solution.py:446
  49.2 6.9 %collective-permute-start.20 = (bf16[128,1024]{1,0:T(8,128)(2,1)S(1)}, bf16[128,1024]{1,0:T(8,128)(2,1)S(1)}, u32[]{:S(2)}, u32[]{:S(2)}) collective-permute-start(bf16[128,1024]{1,0:T(8,128)(2,1)S(1)} %back_of.1.refs_2_), channel_id=1, source_target_pairs={{0,1},{1,0},{2,3},{3,2},{4,5},{5,4},{6,7},{7,6},{8,9},{9,8},{10,11... | collective-permute-start | bytes 786440 | tf_op jit(solution)/shard_map/back_core_rest/ppermute | solution.py:446
  53.9 5.5 %collective-permute-start.17 = (bf16[32,1024]{1,0:T(8,128)(2,1)S(1)}, bf16[32,1024]{1,0:T(8,128)(2,1)S(1)}, u32[]{:S(2)}, u32[]{:S(2)}) collective-permute-start(bf16[32,1024]{1,0:T(8,128)(2,1)S(1)} %add_round.12), channel_id=1, source_target_pairs={{0,8},{4,0},{12,4},{20,12},{28,20},{24,28},{16,24},{8,16},{1,9},{5... | collective-permute-start | bytes 196616 | tf_op jit(solution)/shard_map/weight_ring_1/ppermute | solution.py:438
  54.5 5.0 %collective-permute-start.15 = (bf16[32,1024]{1,0:T(8,128)(2,1)S(1)}, bf16[32,1024]{1,0:T(8,128)(2,1)S(1)}, u32[]{:S(2)}, u32[]{:S(2)}) collective-permute-start(bf16[32,1024]{1,0:T(8,128)(2,1)S(1)} %add_round.11), channel_id=1, source_target_pairs={{0,4},{4,12},{12,20},{20,28},{28,24},{24,16},{16,8},{8,0},{1,5},{5... | collective-permute-start | bytes 196616 | tf_op jit(solution)/shard_map/weight_ring_1/ppermute | solution.py:438
  57.4 5.0 %collective-permute-start.21 = (bf16[128,512]{1,0:T(8,128)(2,1)S(1)}, bf16[128,512]{1,0:T(8,128)(2,1)S(1)}, u32[]{:S(2)}, u32[]{:S(2)}) collective-permute-start(bf16[128,512]{1,0:T(8,128)(2,1)S(1)} %get-tuple-element.73), channel_id=1, source_target_pairs={{0,4},{4,12},{12,20},{20,28},{28,24},{24,16},{16,8},{8,0},{1,5},{5... | collective-permute-start | bytes 393224 | tf_op jit(solution)/shard_map/back_ring_0/ppermute | solution.py:438
  59.0 5.0 %collective-permute-start.22 = (bf16[128,512]{1,0:T(8,128)(2,1)S(1)}, bf16[128,512]{1,0:T(8,128)(2,1)S(1)}, u32[]{:S(2)}, u32[]{:S(2)}) collective-permute-start(bf16[128,512]{1,0:T(8,128)(2,1)S(1)} %get-tuple-element.75), channel_id=1, source_target_pairs={{0,8},{4,0},{12,4},{20,12},{28,20},{24,28},{16,24},{8,16},{1,9},{5... | collective-permute-start | bytes 393224 | tf_op jit(solution)/shard_map/back_ring_0/ppermute | solution.py:438
  61.1 4.6 %collective-permute-start.24 = (bf16[32,1024]{1,0:T(8,128)(2,1)S(1)}, bf16[32,1024]{1,0:T(8,128)(2,1)S(1)}, u32[]{:S(2)}, u32[]{:S(2)}) collective-permute-start(bf16[32,1024]{1,0:T(8,128)(2,1)S(1)} %get-tuple-element.76.refs_5_), channel_id=1, source_target_pairs={{0,8},{4,0},{12,4},{20,12},{28,20},{24,28},{16,24},{8,16},{1,9},{5... | collective-permute-start | bytes 196616 | tf_op jit(solution)/shard_map/weight_ring_2/ppermute | solution.py:438
  64.0 5.1 %collective-permute-start.23 = (bf16[32,1024]{1,0:T(8,128)(2,1)S(1)}, bf16[32,1024]{1,0:T(8,128)(2,1)S(1)}, u32[]{:S(2)}, u32[]{:S(2)}) collective-permute-start(bf16[32,1024]{1,0:T(8,128)(2,1)S(1)} %add_round.15), channel_id=1, source_target_pairs={{0,4},{4,12},{12,20},{20,28},{28,24},{24,16},{16,8},{8,0},{1,5},{5... | collective-permute-start | bytes 196616 | tf_op jit(solution)/shard_map/weight_ring_3/ppermute | solution.py:438
  65.7 5.1 %collective-permute-start.25 = (bf16[32,1024]{1,0:T(8,128)(2,1)S(1)}, bf16[32,1024]{1,0:T(8,128)(2,1)S(1)}, u32[]{:S(2)}, u32[]{:S(2)}) collective-permute-start(bf16[32,1024]{1,0:T(8,128)(2,1)S(1)} %add_round.16), channel_id=1, source_target_pairs={{0,8},{4,0},{12,4},{20,12},{28,20},{24,28},{16,24},{8,16},{1,9},{5... | collective-permute-start | bytes 196616 | tf_op jit(solution)/shard_map/weight_ring_3/ppermute | solution.py:438
  66.2 9.4 %collective-permute-start.28 = (bf16[128,1024]{1,0:T(8,128)(2,1)S(1)}, bf16[128,1024]{1,0:T(8,128)(2,1)S(1)}, u32[]{:S(2)}, u32[]{:S(2)}) collective-permute-start(bf16[128,1024]{1,0:T(8,128)(2,1)S(1)} %get-tuple-element.77.refs_2_), channel_id=1, source_target_pairs={{0,4},{4,12},{12,20},{20,28},{28,24},{24,16},{16,8},{8,0},{1,5},{5... | collective-permute-start | bytes 786440 | tf_op jit(solution)/shard_map/back_ring_1/ppermute | solution.py:438
  67.8 7.9 %collective-permute-start.29 = (bf16[128,1024]{1,0:T(8,128)(2,1)S(1)}, bf16[128,1024]{1,0:T(8,128)(2,1)S(1)}, u32[]{:S(2)}, u32[]{:S(2)}) collective-permute-start(bf16[128,1024]{1,0:T(8,128)(2,1)S(1)} %get-tuple-element.81), channel_id=1, source_target_pairs={{0,8},{4,0},{12,4},{20,12},{28,20},{24,28},{16,24},{8,16},{1,9},{5... | collective-permute-start | bytes 786440 | tf_op jit(solution)/shard_map/back_ring_1/ppermute | solution.py:438
  77.9 7.4 %collective-permute-start.37 = (bf16[128,1024]{1,0:T(8,128)(2,1)S(1)}, bf16[128,1024]{1,0:T(8,128)(2,1)S(1)}, u32[]{:S(2)}, u32[]{:S(2)}) collective-permute-start(bf16[128,1024]{1,0:T(8,128)(2,1)S(1)} %get-tuple-element.85), channel_id=1, source_target_pairs={{0,4},{4,12},{12,20},{20,28},{28,24},{24,16},{16,8},{8,0},{1,5},{5... | collective-permute-start | bytes 786440 | tf_op jit(solution)/shard_map/back_ring_2/ppermute | solution.py:438
  79.5 8.2 %collective-permute-start.39 = (bf16[128,1024]{1,0:T(8,128)(2,1)S(1)}, bf16[128,1024]{1,0:T(8,128)(2,1)S(1)}, u32[]{:S(2)}, u32[]{:S(2)}) collective-permute-start(bf16[128,1024]{1,0:T(8,128)(2,1)S(1)} %get-tuple-element.88), channel_id=1, source_target_pairs={{0,8},{4,0},{12,4},{20,12},{28,20},{24,28},{16,24},{8,16},{1,9},{5... | collective-permute-start | bytes 786440 | tf_op jit(solution)/shard_map/back_ring_2/ppermute | solution.py:438
  80.1 5.2 %collective-permute-start.35 = (bf16[32,1024]{1,0:T(8,128)(2,1)S(1)}, bf16[32,1024]{1,0:T(8,128)(2,1)S(1)}, u32[]{:S(2)}, u32[]{:S(2)}) collective-permute-start(bf16[32,1024]{1,0:T(8,128)(2,1)S(1)} %add_round.18), channel_id=1, source_target_pairs={{0,4},{4,12},{12,20},{20,28},{28,24},{24,16},{16,8},{8,0},{1,5},{5... | collective-permute-start | bytes 196616 | tf_op jit(solution)/shard_map/weight_ring_6/ppermute | solution.py:438
  81.8 9.2 %collective-permute-start.33 = (bf16[160,1024]{1,0:T(8,128)(2,1)S(1)}, bf16[160,1024]{1,0:T(8,128)(2,1)S(1)}, u32[]{:S(2)}, u32[]{:S(2)}) collective-permute-start(bf16[160,1024]{1,0:T(8,128)(2,1)S(1)} %stack_blocks.2.refs_0_), channel_id=1, source_target_pairs={{0,2},{1,3},{2,0},{3,1},{4,6},{5,7},{6,4},{7,5},{8,10},{9,11},{10,... | collective-permute-start | bytes 983048 | tf_op jit(solution)/shard_map/weight_y_early_1/ppermute | solution.py:450
  85.4 4.6 %collective-permute-start.38 = (bf16[32,512]{1,0:T(8,128)(2,1)S(1)}, bf16[32,512]{1,0:T(8,128)(2,1)S(1)}, u32[]{:S(2)}, u32[]{:S(2)}) collective-permute-start(bf16[32,512]{1,0:T(8,128)(2,1)S(1)} %slice.14), channel_id=1, source_target_pairs={{0,4},{4,12},{12,20},{20,28},{28,24},{24,16},{16,8},{8,0},{1,5},{5... | collective-permute-start | bytes 98312 | tf_op jit(solution)/shard_map/weight_ring_7/ppermute | solution.py:438
  88.2 10.2 %collective-permute-start.42 = (bf16[128,1024]{1,0:T(8,128)(2,1)S(1)}, bf16[128,1024]{1,0:T(8,128)(2,1)S(1)}, u32[]{:S(2)}, u32[]{:S(2)}) collective-permute-start(bf16[128,1024]{1,0:T(8,128)(2,1)S(1)} %get-tuple-element.91), channel_id=1, source_target_pairs={{0,4},{4,12},{12,20},{20,28},{28,24},{24,16},{16,8},{8,0},{1,5},{5... | collective-permute-start | bytes 786440 | tf_op jit(solution)/shard_map/back_ring_3/ppermute | solution.py:438
  90.0 8.6 %collective-permute-start.43 = (bf16[128,1024]{1,0:T(8,128)(2,1)S(1)}, bf16[128,1024]{1,0:T(8,128)(2,1)S(1)}, u32[]{:S(2)}, u32[]{:S(2)}) collective-permute-start(bf16[128,1024]{1,0:T(8,128)(2,1)S(1)} %get-tuple-element.92), channel_id=1, source_target_pairs={{0,8},{4,0},{12,4},{20,12},{28,20},{24,28},{16,24},{8,16},{1,9},{5... | collective-permute-start | bytes 786440 | tf_op jit(solution)/shard_map/back_ring_3/ppermute | solution.py:438
  91.0 7.6 %collective-permute-start.34 = (bf16[160,1024]{1,0:T(8,128)(2,1)S(1)}, bf16[160,1024]{1,0:T(8,128)(2,1)S(1)}, u32[]{:S(2)}, u32[]{:S(2)}) collective-permute-start(bf16[160,1024]{1,0:T(8,128)(2,1)S(1)} %collective-permute-done.33.refs_4_.refs_2_), channel_id=1, source_target_pairs={{0,1},{1,0},{2,3},{3,2},{4,5},{5,4},{6,7},{7,6},{8,9},{9,8},{10,11... | collective-permute-start | bytes 983048 | tf_op jit(solution)/shard_map/weight_last/ppermute | solution.py:446
  91.7 6.6 %collective-permute-start.44 = (bf16[96,1024]{1,0:T(8,128)(2,1)S(1)}, bf16[96,1024]{1,0:T(8,128)(2,1)S(1)}, u32[]{:S(2)}, u32[]{:S(2)}) collective-permute-start(bf16[96,1024]{1,0:T(8,128)(2,1)S(1)} %stack_blocks.3.refs_4_), channel_id=1, source_target_pairs={{0,2},{1,3},{2,0},{3,1},{4,6},{5,7},{6,4},{7,5},{8,10},{9,11},{10,... | collective-permute-start | bytes 589832 | tf_op jit(solution)/shard_map/weight_y_late_1/ppermute | solution.py:450
  92.7 5.8 %collective-permute-start.41 = (bf16[96,1024]{1,0:T(8,128)(2,1)S(1)}, bf16[96,1024]{1,0:T(8,128)(2,1)S(1)}, u32[]{:S(2)}, u32[]{:S(2)}) collective-permute-start(bf16[96,1024]{1,0:T(8,128)(2,1)S(1)} %stack_blocks.3.refs_4_), channel_id=1, source_target_pairs={{0,1},{1,0},{2,3},{3,2},{4,5},{5,4},{6,7},{7,6},{8,9},{9,8},{10,11... | collective-permute-start | bytes 589832 | tf_op jit(solution)/shard_map/weight_last/ppermute | solution.py:446
  (20 other events, 82.8 us)
